TPU v7x, 32 devices: a whole 2x2x4 slice. The times are simulated.
32 devices in a mesh: patch: 16 (over z, y, core), fsdp: 2 (over x).
Axes of the slice: x: 2, y: 2, z: 4, core: 2. Of those that a mesh axis runs over, the one named last changes fastest.
Arguments:
- image: bfloat16 [2048, 3072], P('patch'), may hold values from -6 to 6
- mod_shift: float32 [3072], replicated, may hold values from -3 to 3
- mod_scale: float32 [3072], replicated, may hold values from -2.5 to 2.5
- mod_gate: float32 [3072], replicated, may hold values from -4 to 4
- w_query: bfloat16 [3072, 2048], P('patch', 'fsdp'), may hold values from -0.109375 to 0.109375
- w_key: bfloat16 [3072, 2048], P('patch', 'fsdp'), may hold values from -0.109375 to 0.109375
- w_value: bfloat16 [3072, 2048], P('patch', 'fsdp'), may hold values from -0.109375 to 0.109375
- query_gain: float32 [128], replicated, may hold values from 1.5 to 160
- key_gain: float32 [128], replicated, may hold values from 0.1 to 1.9
- text_keys: bfloat16 [512, 2048], P(None, 'fsdp'), may hold values from -6 to 6
- text_values: bfloat16 [512, 2048], P(None, 'fsdp'), may hold values from -6 to 6
- stale_keys: bfloat16 [2048, 2048], P('patch', 'fsdp'), may hold values from -6 to 6
- stale_values: bfloat16 [2048, 2048], P('patch', 'fsdp'), may hold values from -6 to 6
- w_out: bfloat16 [2048, 3072], P('fsdp', 'patch'), may hold values from -0.125 to 0.125
Outputs:
- hidden: bfloat16 [2048, 3072], P('patch', 'fsdp')
- fresh_keys: bfloat16 [2048, 2048], P('patch', 'fsdp')
- fresh_values: bfloat16 [2048, 2048], P('patch', 'fsdp')
All inputs are finite; a program needn't handle non-finite values.
Results may differ from a plain program's by a relative error of at most 0.013.
Values may be sent and summed in bfloat16 or wider, within the bound.
No kernel may reach another device: no remote copies, remote signals or barrier semaphores. Data moves between devices by JAX's collectives and lax.ppermute only.
A program may use at most 128 MiB of HBM per device.

v0:
```python
import math

import jax
import jax.numpy as jnp
from jax import lax
from jax.sharding import PartitionSpec as P


def modulate(image, mod_shift, mod_scale):
    values = image.astype(jnp.float32)
    center = jnp.mean(values, axis=-1, keepdims=True)
    spread = jnp.mean(jnp.square(values - center), axis=-1, keepdims=True)
    normed = (values - center) * lax.rsqrt(spread + 1e-06)
    return ((1.0 + mod_scale) * normed + mod_shift).astype(jnp.bfloat16)


def head_norm(projected, gain, head_size):
    count = projected.shape[0]
    shaped = projected.reshape(count, -1, head_size)
    power = jnp.mean(shaped * shaped, axis=-1, keepdims=True)
    return (shaped * lax.rsqrt(power + 1e-06) * gain).astype(jnp.bfloat16).reshape(count, -1)


def on_device(
    image,
    mod_shift,
    mod_scale,
    mod_gate,
    w_query,
    w_key,
    w_value,
    query_gain,
    key_gain,
    text_keys,
    text_values,
    stale_keys,
    stale_values,
    w_out,
):
    head_size = query_gain.shape[0]
    row_count = image.shape[0]
    model_width = image.shape[1]
    local_width = w_query.shape[1]
    head_count = local_width // head_size
    modded = modulate(image, mod_shift, mod_scale)
    pieces = (
        lax.all_gather(w_query, "patch", axis=0, tiled=True),
        lax.all_gather(w_key, "patch", axis=0, tiled=True),
        lax.all_gather(w_value, "patch", axis=0, tiled=True),
    )
    query_proj, key_proj, value_proj = tuple(
        (jnp.dot(modded, piece, preferred_element_type=jnp.float32) for piece in pieces)
    )
    queries = head_norm(query_proj, query_gain, head_size)
    key_new = head_norm(key_proj, key_gain, head_size)
    value_new = value_proj.astype(jnp.bfloat16)
    query_heads = queries.reshape(row_count, head_count, head_size)
    own_start = lax.axis_index("patch") * row_count

    def score_piece(piece):
        return jnp.einsum(
            "rhd,khd->hrk",
            query_heads,
            piece.reshape(piece.shape[0], head_count, head_size),
            preferred_element_type=jnp.float32,
        )

    text_scores = score_piece(text_keys)
    own_scores = score_piece(key_new)
    key_rows, value_rows = (
        lax.all_gather(stale_keys, "patch", axis=0, tiled=True),
        lax.all_gather(stale_values, "patch", axis=0, tiled=True),
    )
    image_scores = score_piece(key_rows)
    image_scores = lax.dynamic_update_slice(image_scores, own_scores, (0, 0, own_start))
    value_rows = lax.dynamic_update_slice_in_dim(value_rows, value_new, own_start, 0)
    factor = 1.0 / math.sqrt(head_size)
    text_scores = text_scores * factor
    image_scores = image_scores * factor
    largest = jnp.maximum(
        jnp.max(text_scores, axis=-1, keepdims=True), jnp.max(image_scores, axis=-1, keepdims=True)
    )
    text_expos = jnp.exp(text_scores - largest)
    image_expos = jnp.exp(image_scores - largest)
    totals = jnp.sum(text_expos, axis=-1, keepdims=True) + jnp.sum(
        image_expos, axis=-1, keepdims=True
    )
    text_weights = (text_expos / totals).astype(jnp.bfloat16)
    image_weights = (image_expos / totals).astype(jnp.bfloat16)
    mixture = jnp.einsum(
        "hrk,khd->rhd",
        text_weights,
        text_values.reshape(-1, head_count, head_size),
        preferred_element_type=jnp.float32,
    )
    mixture = mixture + jnp.einsum(
        "hrk,khd->rhd",
        image_weights,
        value_rows.reshape(-1, head_count, head_size),
        preferred_element_type=jnp.float32,
    )
    attended = mixture.astype(jnp.bfloat16).reshape(row_count, local_width)
    fsdp_count = lax.axis_size("fsdp")
    fsdp_index = lax.axis_index("fsdp")
    share_width = model_width // fsdp_count
    partial_out = jnp.dot(
        attended,
        lax.all_gather(w_out, "patch", axis=1, tiled=True),
        preferred_element_type=jnp.float32,
    )
    summed = lax.psum_scatter(
        partial_out.astype(jnp.bfloat16), "fsdp", scatter_dimension=1, tiled=True
    ).astype(jnp.float32)
    col_start = fsdp_index * share_width
    image_part = lax.dynamic_slice_in_dim(image, col_start, share_width, 1).astype(jnp.float32)
    gate_part = lax.dynamic_slice_in_dim(mod_gate, col_start, share_width, 0)
    hidden = (image_part + gate_part * summed).astype(jnp.bfloat16)
    return (hidden, key_new, value_new)


def solution(mesh):
    return jax.shard_map(
        on_device,
        mesh=mesh,
        in_specs=(
            P("patch", None),
            P(),
            P(),
            P(),
            P("patch", "fsdp"),
            P("patch", "fsdp"),
            P("patch", "fsdp"),
            P(),
            P(),
            P(None, "fsdp"),
            P(None, "fsdp"),
            P("patch", "fsdp"),
            P("patch", "fsdp"),
            P("fsdp", "patch"),
        ),
        out_specs=(P("patch", "fsdp"), P("patch", "fsdp"), P("patch", "fsdp")),
        check_vma=False,
    )
```

profile of v0, /device:TPU:0, one launch (start us, length us, event | category | flops | bytes accessed | tf_op | source)
XLA Modules:
  0.0 399.0 jit_solution(5096100544951035050)
XLA Ops:
  7.3 0.7 all-gather.13.cloned.1.call-update
  8.0 0.7 all-gather.15.cloned.1.call-update
  8.7 0.7 all-gather.11.cloned.1.call-update
  9.5 0.5 all-gather.7.cloned.1.call-update
  10.1 1.8 copy.47
  11.9 0.5 all-gather.17.cloned.1.call-update
  12.5 2.3 copy.59
  15.0 0.4 fusion.5
  15.4 48.1 %all-gather.13.cloned.1.call-done = bf16[2048,1024]{1,0:T(8,128)(2,1)} async-done(((bf16[128,1024]{1,0:T(8,128)(2,1)}), bf16[2048,1024]{1,0:T(8,128)(2,1)}) %all-gather.13.cloned.1.call-update) | async-done | bytes 4194320 | tf_op jit(solution)/shard_map/all_gather | solution.py:72
  63.5 62.7 %all-gather.15.cloned.1.call-done = bf16[3072,1024]{1,0:T(8,128)(2,1)} async-done(((bf16[192,1024]{1,0:T(8,128)(2,1)}), bf16[3072,1024]{1,0:T(8,128)(2,1)}) %all-gather.15.cloned.1.call-update) | async-done | bytes 6291472 | tf_op jit(solution)/shard_map/all_gather | solution.py:49
  126.2 4.6 %constant_dynamic-update-slice_fusion = (bf16[2048,1024]{1,0:T(8,128)(2,1)}, bf16[128,1024]{1,0:T(8,128)(2,1)}) fusion(bf16[2048,1024]{1,0:T(8,128)(2,1)} %all-gather.13.cloned.1.call-done, s32[]{:T(128)S(6)} %select_n.9, bf16[3072,1024]{1,0:T(8,128)(2,1)} %all-gather.15.cloned.1.call-done, bf16[128,3072]{1,0:T(8,128)(2,1)S(1)} %copy-done.1, ...), kind=kOutput, calls=%fused_computation.45 | convolution fusion | flops 807796736 | bytes 7627780 | tf_op jit(solution)/shard_map/dot_general | solution.py:52
  130.8 6.5 %copy.60 = bf16[2048,1024]{0,1:T(8,128)(2,1)} copy(bf16[2048,1024]{1,0:T(8,128)(2,1)} %get-tuple-element.3) | data formatting | bytes 8388608 | tf_op jit(solution)/shard_map/reshape | solution.py:99
  137.3 51.6 %all-gather.11.cloned.1.call-done = bf16[3072,1024]{1,0:T(8,128)(2,1)} async-done(((bf16[192,1024]{1,0:T(8,128)(2,1)}), bf16[3072,1024]{1,0:T(8,128)(2,1)}) %all-gather.11.cloned.1.call-update) | async-done | bytes 6291472 | tf_op jit(solution)/shard_map/all_gather | solution.py:48
  188.9 3.8 fusion.25
  192.8 0.8 copy-done.3
  194.1 57.5 %all-gather.7.cloned.1.call-done = bf16[3072,1024]{1,0:T(8,128)(2,1)} async-done(((bf16[192,1024]{1,0:T(8,128)(2,1)}), bf16[3072,1024]{1,0:T(8,128)(2,1)}) %all-gather.7.cloned.1.call-update) | async-done | bytes 6291472 | tf_op jit(solution)/shard_map/all_gather | solution.py:47
  251.5 3.8 convolution_bitcast_fusion.1
  255.9 0.3 multiply_convert_fusion
  256.2 49.7 %all-gather.9.cloned.1.call-done = bf16[2048,1024]{0,1:T(8,128)(2,1)} async-done(((bf16[128,1024]{0,1:T(8,128)(2,1)}), bf16[2048,1024]{0,1:T(8,128)(2,1)}) %all-gather.9.cloned.1.call-update) | async-done | bytes 4194320 | tf_op jit(solution)/shard_map/all_gather | solution.py:71
  306.0 3.4 fusion.19
  309.7 0.5 multiply_reduce_fusion.1
  310.3 0.7 multiply_reduce_fusion
  310.9 0.6 fusion.4
  311.5 1.6 fusion
  313.2 0.6 copy-done.2
  313.8 3.0 fusion.10
  316.8 0.8 fusion.11
  317.6 50.6 %all-gather.17.cloned.1.call-done = bf16[1024,3072]{0,1:T(8,128)(2,1)} async-done(((bf16[1024,192]{0,1:T(8,128)(2,1)}), bf16[1024,3072]{0,1:T(8,128)(2,1)}) %all-gather.17.cloned.1.call-update) | async-done | bytes 6291472 | tf_op jit(solution)/shard_map/all_gather | solution.py:108
  368.2 6.0 %convolution_convert_fusion = bf16[128,3072]{1,0:T(8,128)(2,1)} fusion(bf16[128,1024]{0,1:T(8,128)(2,1)S(1)} %bitcast.52, bf16[1024,3072]{0,1:T(8,128)(2,1)} %all-gather.17.cloned.1.call-done), kind=kOutput, calls=%fused_computation.5 | convolution fusion | flops 805699584 | bytes 7340032 | tf_op jit(solution)/shard_map/dot_general | solution.py:106
  374.4 0.8 fusion.16
  375.3 15.1 %reduce-scatter.2.cloned.1.call-done = bf16[128,1536]{1,0:T(8,128)(2,1)} async-done(((bf16[128,3072]{1,0:T(8,128)(2,1)}), bf16[128,1536]{1,0:T(8,128)(2,1)}) %reduce-scatter.2.cloned.1.call-update) | async-done | bytes 393232 | tf_op jit(solution)/shard_map/reduce_scatter | solution.py:111
  390.3 1.9 add_convert_fusion
  (49 shorter events, 2.1 us)
Async XLA Ops:
  7.2 302.5 %copy-start = (bf16[512,1024]{1,0:T(8,128)(2,1)S(1)}, bf16[512,1024]{1,0:T(8,128)(2,1)}, u32[]{:S(2)}) copy-start(bf16[512,1024]{1,0:T(8,128)(2,1)} %param.23) | copy-start | bytes 3145732
  7.2 7.6 %copy-start.1 = (bf16[128,3072]{1,0:T(8,128)(2,1)S(1)}, bf16[128,3072]{1,0:T(8,128)(2,1)}, u32[]{:S(2)}) copy-start(bf16[128,3072]{1,0:T(8,128)(2,1)} %param.14) | copy-start | bytes 2359300
  7.2 8.2 %copy-start.6 = (f32[3072]{0:T(1024)S(1)}, f32[3072]{0:T(1024)}, u32[]{:S(2)}) copy-start(f32[3072]{0:T(1024)} %param.16) | copy-start | bytes 36868
  7.2 119.0 %copy-start.10 = (f32[3072]{0:T(1024)S(1)}, f32[3072]{0:T(1024)}, u32[]{:S(2)}) copy-start(f32[3072]{0:T(1024)} %param.15) | copy-start | bytes 36868
  7.2 56.3 %all-gather.13.cloned.1.call-start = ((), (), s32[]{:S(2)}) async-start(), calls=%async_computation.4 | async-start | bytes 4456448 | tf_op jit(solution)/shard_map/all_gather | solution.py:72
  7.9 118.2 %all-gather.15.cloned.1.call-start = ((), (), s32[]{:S(2)}) async-start(), calls=%async_computation.5 | async-start | bytes 6684672 | tf_op jit(solution)/shard_map/all_gather | solution.py:49
  8.7 180.2 %all-gather.11.cloned.1.call-start = ((), (), s32[]{:S(2)}) async-start(), calls=%async_computation.3 | async-start | bytes 6684672 | tf_op jit(solution)/shard_map/all_gather | solution.py:48
  9.4 242.1 %all-gather.7.cloned.1.call-start = ((), (), s32[]{:S(2)}) async-start(), calls=%async_computation.1 | async-start | bytes 6684672 | tf_op jit(solution)/shard_map/all_gather | solution.py:47
  10.0 296.0 %all-gather.9.cloned.1.call-start = ((), (), s32[]{:S(2)}) async-start(), calls=%async_computation.2 | async-start | bytes 4456448 | tf_op jit(solution)/shard_map/all_gather | solution.py:71
  11.9 356.3 %all-gather.17.cloned.1.call-start = ((), (), s32[]{:S(2)}) async-start(), calls=%async_computation.6 | async-start | bytes 6684672 | tf_op jit(solution)/shard_map/all_gather | solution.py:108
  12.4 377.9 %reduce-scatter.2.cloned.1.call-start = ((), (), s32[]{:S(2)}) async-start(), calls=%async_computation.7 | async-start | bytes 1179648 | tf_op jit(solution)/shard_map/reduce_scatter | solution.py:111
  192.8 0.8 copy-start.3
  194.1 61.8 %copy-start.8 = (f32[128]{0:T(128)S(1)}, f32[128]{0:T(128)}, u32[]{:S(2)}) copy-start(f32[128]{0:T(128)} %param.22) | copy-start | bytes 1540
  194.1 61.8 %copy-start.9 = (f32[128]{0:T(128)S(1)}, f32[128]{0:T(128)}, u32[]{:S(2)}) copy-start(f32[128]{0:T(128)} %param.21) | copy-start | bytes 1540
  311.5 2.3 copy-start.2
  313.8 3.0 copy-start.5
  317.6 56.6 %copy-start.7 = (f32[3072]{0:T(1024)S(1)}, f32[3072]{0:T(1024)}, u32[]{:S(2)}) copy-start(f32[3072]{0:T(1024)} %param.17) | copy-start | bytes 36868
  368.2 6.3 %copy-start.4 = (f32[128,1024]{1,0:T(8,128)S(1)}, f32[128,1024]{1,0:T(8,128)}, u32[]{:S(2)}) copy-start(f32[128,1024]{1,0:T(8,128)} %copy-done.3) | copy-start | bytes 1572868
Sparse Core Ops, SparseCore 0:
  10.2 53.2 all-gather.12
  65.8 60.3 all-gather.14
  128.4 60.4 all-gather.10
  191.1 60.4 all-gather.6
  254.1 51.8 all-gather.8
  308.1 59.9 all-gather.16
  374.2 16.0 reduce-scatter.1
where the time goes:
time: 400 us; the launch traced here: 399 us
  waiting for transfers between devices  338 us (84%)
  matrix products  26.3 us (7%)
  between operations  14.4 us (4%)
  local copies, waits for them, and re-layouts  12.9 us (3%)
  other arithmetic  6.93 us (2%)
    all_gather x1, waiting for transfers between devices, on_device(): lax.all_gather(w_value, 'patch', axis=0, tiled=True)  62.7 us
    all_gather x1, waiting for transfers between devices, on_device(): lax.all_gather(w_query, 'patch', axis=0, tiled=True)  57.5 us
    all_gather x1, waiting for transfers between devices, on_device(): lax.all_gather(w_key, 'patch', axis=0, tiled=True)  51.6 us
    all_gather x1, waiting for transfers between devices, on_device(): lax.all_gather(w_out, 'patch', axis=1, tiled=True)  50.6 us
    all_gather x1, waiting for transfers between devices, on_device(): lax.all_gather(stale_keys, 'patch', axis=0, tiled=True)  49.7 us
    all_gather x1, waiting for transfers between devices, on_device(): lax.all_gather(stale_values, 'patch', axis=0, tiled=True)  48.1 us
    reduce_scatter x1, waiting for transfers between devices, on_device(): lax.psum_scatter(partial_out.astype(jnp.bfloat16), 'fsdp', scatter_dimens...  15.1 us
    dot_general x3, matrix products, on_device(): jnp.dot(modded, piece, preferred_element_type=jnp.float32)  12.3 us
  transfers between devices with their start and end apart: 7, of which 7 were waited for; matrix products, arithmetic and copies ran while one was open for 9% of the time, Pallas kernels for 0%

commit v1 on v0

v1 whole, which is shorter than its diff:
```python
import functools
import math

import jax
import jax.numpy as jnp
from jax import lax
from jax.experimental import pallas as pl
from jax.experimental.pallas import tpu as pltpu
from jax.sharding import PartitionSpec as P

INNER = 4
VMEM_BYTES = 60 * 1024 * 1024


def modulate(image, mod_shift, mod_scale):
    values = image.astype(jnp.float32)
    center = jnp.mean(values, axis=-1, keepdims=True)
    spread = jnp.mean(jnp.square(values - center), axis=-1, keepdims=True)
    normed = (values - center) * lax.rsqrt(spread + 1e-06)
    return ((1.0 + mod_scale) * normed + mod_shift).astype(jnp.bfloat16)


def after(x, *deps):
    return lax.optimization_barrier((x,) + deps)[0]


def nt_dot(a, b):
    return lax.dot_general(a, b, (((1,), (1,)), ((), ())), preferred_element_type=jnp.float32)


def patch_kernel(depth, head_size, n_pieces, counts, where_ref, *refs):
    n_shares, n_patches = sum(counts), len(counts)
    shares, refs = refs[:n_shares], refs[n_shares:]
    tk_ref, tv_ref, qg_ref, kg_ref = refs[:4]
    pieces, refs = refs[4 : 4 + n_pieces], refs[4 + n_pieces :]
    att_refs, kv_refs = refs[:n_patches], refs[n_patches : 2 * n_patches]
    held, scores, expos, sems = refs[2 * n_patches :]
    rows, width = att_refs[0].shape
    groups = [slice(g * rows, (g + 1) * rows) for g in range(n_patches)]
    owns, firsts, at = [], [], 1 + n_pieces
    for count in counts:
        owns.append(where_ref[at])
        firsts.append([where_ref[at + 1 + i] for i in range(count)])
        at += 1 + count
    copies = [
        pltpu.make_async_copy(piece, held.at[where_ref[1 + i]], sems.at[i])
        for i, piece in enumerate(pieces)
    ]
    for copy in copies:
        copy.start()

    def put(refs, cols, value):
        for g, group in enumerate(groups):
            share = rows // counts[g]
            for i, first in enumerate(firsts[g]):
                start = group.start + i * share
                refs[g][pl.ds(pl.multiple_of(first, 16), share), cols] = value[start : start + share]

    chunk = INNER * depth
    proj = [jnp.zeros((n_patches * rows, width), jnp.float32) for _ in range(3)]
    if chunk % 128 == 0:
        for first in range(0, n_pieces, INNER):
            for copy in copies[first : first + INNER]:
                copy.wait()
            place = where_ref[1 + first] // INNER
            cols = pl.ds(pl.multiple_of(place * chunk, 128), chunk)
            part = jnp.concatenate([x[:, cols] for x in shares], axis=0)
            for i in range(3):
                weight = held[pl.ds(place * INNER, INNER), i * depth : (i + 1) * depth, :]
                proj[i] += jnp.dot(
                    part, weight.reshape(chunk, width), preferred_element_type=jnp.float32
                )
    else:
        for copy in copies:
            copy.wait()
        part = jnp.concatenate([x[...] for x in shares], axis=0)
        for i in range(3):
            weight = held[:, i * depth : (i + 1) * depth, :]
            proj[i] += jnp.dot(
                part, weight.reshape(n_pieces * depth, width), preferred_element_type=jnp.float32
            )
    q_proj, k_proj, v_proj = proj

    def norm(x, gain):
        power = jnp.mean(x * x, axis=-1, keepdims=True)
        return (x * lax.rsqrt(power + 1e-06) * gain).astype(jnp.bfloat16)

    v_new = v_proj.astype(jnp.bfloat16)
    put(kv_refs, slice(width, 2 * width), v_new)
    k0, v0 = 3 * depth, 3 * depth + rows
    scale = math.log2(math.e) / math.sqrt(head_size)
    for h in range(width // head_size):
        cols = slice(h * head_size, (h + 1) * head_size)
        key = norm(k_proj[:, cols], kg_ref[...])
        put(kv_refs, cols, key)
        query = norm(q_proj[:, cols], qg_ref[...])
        value = v_new[:, cols]
        keys = held[:, k0 : k0 + rows, cols].reshape(n_pieces * rows, head_size)
        values = held[:, v0 : v0 + rows, cols].reshape(n_pieces * rows, head_size)
        scores[...] = nt_dot(query, keys)
        own_cols = [pl.ds(pl.multiple_of(own * rows, 128), rows) for own in owns]
        for g, group in enumerate(groups):
            scores[group, own_cols[g]] = nt_dot(query[group], key[group])
        text_s = nt_dot(query, tk_ref[:, cols])
        image_s = scores[...]
        largest = jnp.maximum(
            jnp.max(text_s, axis=-1, keepdims=True), jnp.max(image_s, axis=-1, keepdims=True)
        )
        text_e = jnp.exp2((text_s - largest) * scale)
        image_e = jnp.exp2((image_s - largest) * scale)
        total = jnp.sum(text_e, axis=-1, keepdims=True) + jnp.sum(image_e, axis=-1, keepdims=True)
        expos[...] = image_e.astype(jnp.bfloat16)
        fresh_mix = []
        for g, group in enumerate(groups):
            fresh_mix.append(
                jnp.dot(expos[group, own_cols[g]], value[group], preferred_element_type=jnp.float32)
            )
            expos[group, own_cols[g]] = jnp.zeros((rows, rows), jnp.bfloat16)
        mixture = (
            jnp.dot(text_e.astype(jnp.bfloat16), tv_ref[:, cols], preferred_element_type=jnp.float32)
            + jnp.dot(expos[...], values, preferred_element_type=jnp.float32)
            + jnp.concatenate(fresh_mix, axis=0)
        )
        put(att_refs, cols, (mixture / total).astype(jnp.bfloat16))


def attend_patches(where, patches, text_keys, text_values, query_gain, key_gain, pieces, depth, width):
    shares = [x for patch in patches for x in patch]
    model_width = shares[0].shape[1]
    rows = sum(x.shape[0] for x in patches[0])
    n = len(patches)
    head_size = query_gain.shape[0]
    texts = text_keys.shape[0]
    n_pieces = len(pieces)
    whole = lambda i, w: (0, 0)
    outs = [width] * n + [2 * width] * n
    out = pl.pallas_call(
        functools.partial(patch_kernel, depth, head_size, n_pieces, [len(x) for x in patches]),
        grid_spec=pltpu.PrefetchScalarGridSpec(
            num_scalar_prefetch=1,
            grid=(1,),
            in_specs=[pl.BlockSpec(x.shape, whole) for x in shares]
            + [
                pl.BlockSpec((texts, width), lambda i, w: (0, w[0])),
                pl.BlockSpec((texts, width), lambda i, w: (0, w[0])),
                pl.BlockSpec((1, head_size), whole),
                pl.BlockSpec((1, head_size), whole),
            ]
            + [pl.BlockSpec(memory_space=pl.ANY)] * n_pieces,
            out_specs=[pl.BlockSpec((rows, x), whole) for x in outs],
            scratch_shapes=[
                pltpu.VMEM((n_pieces,) + pieces[0].shape, jnp.bfloat16),
                pltpu.VMEM((n * rows, n_pieces * rows), jnp.float32),
                pltpu.VMEM((n * rows, n_pieces * rows), jnp.bfloat16),
                pltpu.SemaphoreType.DMA((n_pieces,)),
            ],
        ),
        out_shape=[jax.ShapeDtypeStruct((rows, x), jnp.bfloat16) for x in outs],
        compiler_params=pltpu.CompilerParams(vmem_limit_bytes=VMEM_BYTES),
        cost_estimate=pl.CostEstimate(
            flops=2 * n * rows * (model_width * 3 * width + 2 * (texts + n_pieces * rows) * width),
            bytes_accessed=2 * n_pieces * pieces[0].size,
            transcendentals=n * rows * (texts + n_pieces * rows) * (width // head_size),
        ),
    )(
        where,
        *shares,
        text_keys,
        text_values,
        query_gain.reshape(1, -1),
        key_gain.reshape(1, -1),
        *pieces,
    )
    return out[:n], out[n:]


def deal_kernel(n_arrays, team, member_ref, *refs):
    arrays, outs = refs[:n_arrays], refs[n_arrays:]
    width = outs[0].shape[1]
    for k in range(team):
        at = lax.rem(member_ref[0] + k, team)
        cols = pl.ds(pl.multiple_of(at * width, 128), width)
        first = 0
        for x in arrays:
            rows = x.shape[0]
            outs[k][first : first + rows, :] = x[:, cols]
            first += rows


def deal(member, arrays, team):
    width = arrays[0].shape[1] // team
    shape = jax.ShapeDtypeStruct((sum(x.shape[0] for x in arrays), width), jnp.bfloat16)
    return pl.pallas_call(
        functools.partial(deal_kernel, len(arrays), team),
        in_specs=[pl.BlockSpec(memory_space=pltpu.SMEM)]
        + [pl.BlockSpec(memory_space=pltpu.VMEM)] * len(arrays),
        out_specs=[pl.BlockSpec(memory_space=pltpu.VMEM)] * team,
        out_shape=[shape] * team,
        compiler_params=pltpu.CompilerParams(vmem_limit_bytes=VMEM_BYTES),
    )(member.reshape(1), *arrays)


def collect_kernel(team, member_ref, *refs):
    packs, outs = refs[:team], refs[team:]
    width = outs[0].shape[1] // team
    for s in range(team):
        at = lax.rem(member_ref[0] + s, team)
        cols = pl.ds(pl.multiple_of(at * width, 128), width)
        for i, out in enumerate(outs):
            out[:, cols] = packs[s][:, i * width : (i + 1) * width]


def collect(member, packs):
    team = len(packs)
    rows, double = packs[0].shape
    shape = jax.ShapeDtypeStruct((rows, double // 2 * team), jnp.bfloat16)
    return pl.pallas_call(
        functools.partial(collect_kernel, team),
        in_specs=[pl.BlockSpec(memory_space=pltpu.SMEM)]
        + [pl.BlockSpec(memory_space=pltpu.VMEM)] * team,
        out_specs=[pl.BlockSpec(memory_space=pltpu.VMEM)] * 2,
        out_shape=[shape, shape],
        compiler_params=pltpu.CompilerParams(vmem_limit_bytes=VMEM_BYTES),
    )(member.reshape(1), *packs)


def project_kernel(team, where_ref, *refs):
    packs, w_ref, out_ref = refs[:team], refs[team], refs[team + 1]
    width = w_ref.shape[1] // team
    total = jnp.zeros(out_ref.shape, jnp.float32)
    for s in range(team):
        at = lax.rem(where_ref[0] + s, team)
        cols = pl.ds(pl.multiple_of(at * width, 128), width)
        total += nt_dot(packs[s][...], w_ref[:, cols])
    out_ref[...] = total.astype(out_ref.dtype)


def project(where, packs, w_rows, share, dtype):
    rows, width = packs[0].shape
    local_width = w_rows.shape[1]
    steps = 3 if share % (3 * 256) == 0 else 1
    block = share // steps
    return pl.pallas_call(
        functools.partial(project_kernel, len(packs)),
        grid_spec=pltpu.PrefetchScalarGridSpec(
            num_scalar_prefetch=1,
            grid=(steps,),
            in_specs=[pl.BlockSpec((rows, width), lambda i, w: (0, 0))] * len(packs)
            + [pl.BlockSpec((block, local_width), lambda i, w: (w[1] * steps + i, 0))],
            out_specs=pl.BlockSpec((rows, block), lambda i, w: (0, i)),
        ),
        out_shape=jax.ShapeDtypeStruct((rows, share), dtype),
        compiler_params=pltpu.CompilerParams(vmem_limit_bytes=VMEM_BYTES),
        cost_estimate=pl.CostEstimate(
            flops=2 * rows * share * local_width,
            bytes_accessed=2 * share * local_width,
            transcendentals=0,
        ),
    )(where, *packs, w_rows)


def on_device(
    image,
    mod_shift,
    mod_scale,
    mod_gate,
    w_query,
    w_key,
    w_value,
    query_gain,
    key_gain,
    text_keys,
    text_values,
    stale_keys,
    stale_values,
    w_out,
):
    head_size = query_gain.shape[0]
    rows, model_width = image.shape
    depth, local_width = w_query.shape
    heads = local_width // head_size
    patches = lax.axis_size("patch")
    fsdp = lax.axis_size("fsdp")
    outer = patches // INNER
    team = math.gcd(outer, heads)
    width = local_width // team
    me = lax.axis_index("patch")
    mine = lax.axis_index("fsdp")
    place, seat = me // INNER, me % INNER
    member = place % team

    def along_outer(x, step):
        return lax.ppermute(
            x, "patch", [(p, (p + step * INNER) % patches) for p in range(patches)]
        )

    def along_team(x, step):
        pairs = []
        for p in range(patches):
            z = p // INNER
            to = z - z % team + (z % team + step) % team
            pairs.append((p, to * INNER + p % INNER))
        return lax.ppermute(x, "patch", pairs)

    def flip(x, bit):
        return lax.ppermute(x, "patch", [(p, p ^ bit) for p in range(patches)])

    def along_fsdp(x, step):
        return lax.ppermute(x, "fsdp", [(i, (i + step) % fsdp) for i in range(fsdp)])

    def steps_of(count):
        return sorted(range(1, count), key=lambda s: (min(s, count - s), s))

    w_rows = lax.all_gather(w_out.T, "patch", axis=0, tiled=True)
    dealt = deal(member, (w_query, w_key, w_value, stale_keys, stale_values), team)
    modded = modulate(image, mod_shift, mod_scale)
    share = rows // fsdp
    part = lax.dynamic_slice_in_dim(modded, mine * share, share, axis=0)

    pieces, origins, sent, incoming = {}, {}, [], {0: [modded]}

    def send_rows(s):
        got = along_team(after(part, *sent[-2:-1]), s)
        sent.append(got)
        incoming[s] = [got] + [along_fsdp(got, i) for i in range(1, fsdp)]

    def spread(s, piece):
        side = flip(piece, 2)
        pieces[s] = [piece, side, flip(piece, 1), flip(side, 1)]
        source = (place + (outer - s)) % outer
        origins[s] = [source * INNER + (seat ^ bits) for bits in (0, 2, 1, 3)]

    team_order, order = steps_of(team), steps_of(outer)
    for s in team_order[:-1]:
        send_rows(s)
    spread(0, dealt[0])
    for s in order:
        piece = along_outer(after(dealt[s % team], *sent[-2:-1]), s)
        sent.append(piece)
        spread(s, piece)
    for s in team_order[-1:]:
        send_rows(s)

    all_pieces = [x for s in [0] + order for x in pieces[s]]
    all_origins = [o for s in [0] + order for o in origins[s]]
    attended, fresh = {}, {}
    last = []
    for batch in ([0] + team_order[:-1], team_order[-1:]):
        if not batch:
            continue
        where = [member] + all_origins
        for s in batch:
            where.append((place - member + (member + team - s) % team) * INNER + seat)
            where += [((mine + (fsdp - i)) % fsdp) * share for i in range(fsdp)] if s else [0 * mine]
        att, kv = attend_patches(
            after(jnp.stack(where).astype(jnp.int32), *last),
            [incoming[s] for s in batch],
            text_keys,
            text_values,
            query_gain,
            key_gain,
            all_pieces,
            depth,
            width,
        )
        for s, a, f in zip(batch, att, kv):
            attended[s] = along_team(a, team - s) if s else a
            fresh[s] = along_team(f, team - s) if s else f
            last += [attended[s], fresh[s]]
    packs = [attended[s] for s in range(team)]
    out_share = model_width // fsdp
    received = []
    for i in range(1, fsdp):
        where = jnp.stack([member, (mine + i) % fsdp]).astype(jnp.int32)
        received.append(along_fsdp(project(where, packs, w_rows, out_share, jnp.bfloat16), i))
    where = jnp.stack([member, mine]).astype(jnp.int32)
    summed = project(where, packs, w_rows, out_share, jnp.float32)
    fresh = [fresh[s] for s in range(team)]
    key_out, value_out = collect(member, [after(fresh[0], summed)] + fresh[1:])
    for x in received:
        summed = summed + x.astype(jnp.float32)
    col_start = mine * out_share
    image_part = lax.dynamic_slice_in_dim(image, col_start, out_share, 1).astype(jnp.float32)
    gate_part = lax.dynamic_slice_in_dim(mod_gate, col_start, out_share, 0)
    hidden = (image_part + gate_part * summed).astype(jnp.bfloat16)
    return (hidden, key_out, value_out)


def solution(mesh):
    return jax.shard_map(
        on_device,
        mesh=mesh,
        in_specs=(
            P("patch", None),
            P(),
            P(),
            P(),
            P("patch", "fsdp"),
            P("patch", "fsdp"),
            P("patch", "fsdp"),
            P(),
            P(),
            P(None, "fsdp"),
            P(None, "fsdp"),
            P("patch", "fsdp"),
            P("patch", "fsdp"),
            P("fsdp", "patch"),
        ),
        out_specs=(P("patch", "fsdp"), P("patch", "fsdp"), P("patch", "fsdp")),
        check_vma=False,
    )
```

time: 400 us -> 197 us (0.49)
  waiting for transfers between devices: 338 us -> 103 us
  starting transfers between devices: 0.27 us -> 35.9 us
  Pallas kernels: 0 us -> 34.6 us
  matrix products: 26.3 us -> 0 us
  local copies, waits for them, and re-layouts: 12.9 us -> 3.86 us
    all_gather x6 -> x1, waiting for transfers between devices: 320 us -> 0.01 us  [on_device(): w_rows = lax.all_gather(w_out.T, 'patch', axis=0, tiled=True)]
    ppermute x0 -> x28, waiting for transfers between devices: none -> 102 us  [the longest x9 52.5 us: along_team(): return lax.ppermute(x, 'patch', pairs)]
    ppermute x0 -> x28, starting transfers between devices: none -> 35.9 us  [the longest x12 16 us: flip(): return lax.ppermute(x, 'patch', [(p, p ^ bit) for p in range(patches)])]
    pallas_call x0 -> x6, Pallas kernels: none -> 34.6 us  [the longest x2 20.1 us: attend_patches(): pl.pallas_call(functools.partial(patch_kernel, depth, head_size, n_pieces...]
    dot_general x9 -> x0, matrix products: 26.3 us -> none  [the longest x3 12.3 us: on_device(): jnp.dot(modded, piece, preferred_element_type=jnp.float32)]
    reduce_scatter x1 -> x0, waiting for transfers between devices: 15.1 us -> none  [on_device(): lax.psum_scatter(partial_out.astype(jnp.bfloat16), 'fsdp', scatter_dimens...]
    reshape x2 -> x0, local copies, waits for them, and re-layouts: 8.83 us -> none  [the longest x1 6.51 us: on_device(): value_rows.reshape(-1, head_count, head_size)]
  transfers between devices with their start and end apart: 7 -> 29, of which waited for: 7 -> 13; matrix products, arithmetic and copies ran while one was open for 9% -> 2% of each run, Pallas kernels for 0% -> 15%
where the time goes in v1:
time: 197 us
  waiting for transfers between devices  103 us (52%)
  starting transfers between devices  35.9 us (18%)
  Pallas kernels  34.6 us (18%)
  between operations  14.3 us (7%)
  other arithmetic  5.29 us (3%)
  local copies, waits for them, and re-layouts  3.86 us (2%)
    ppermute x9, waiting for transfers between devices, along_team(): return lax.ppermute(x, 'patch', pairs)  52.5 us
    ppermute x3, waiting for transfers between devices, along_outer(): lax.ppermute(x, 'patch', [(p, (p + step * INNER) % patches) for p in rang...  38 us
    pallas_call x2, Pallas kernels, attend_patches(): pl.pallas_call(functools.partial(patch_kernel, depth, head_size, n_pieces...  20.1 us
    ppermute x12, starting transfers between devices, flip(): return lax.ppermute(x, 'patch', [(p, p ^ bit) for p in range(patches)])  16 us
    ppermute x9, starting transfers between devices, along_team(): return lax.ppermute(x, 'patch', pairs)  13.3 us
    ppermute x4, waiting for transfers between devices, along_fsdp(): lax.ppermute(x, 'fsdp', [(i, (i + step) % fsdp) for i in range(fsdp)])  10.1 us
    pallas_call x2, Pallas kernels, project(): pl.pallas_call(functools.partial(project_kernel, len(packs)), grid_spec=p...  9.76 us
  transfers between devices with their start and end apart: 29, of which 13 were waited for; matrix products, arithmetic and copies ran while one was open for 2% of the time, Pallas kernels for 15%

profile of v1, /device:TPU:0, one launch (start us, length us, event | category | flops | bytes accessed | tf_op | source)
XLA Modules:
  0.0 197.0 jit_solution(8872279678395229817)
XLA Ops:
  7.9 1.3 convert_reduce_fusion
  10.1 3.1 %collective-permute-start = (bf16[64,3072]{1,0:T(8,128)(2,1)S(1)}, bf16[64,3072]{1,0:T(8,128)(2,1)S(1)}, u32[]{:S(2)}, u32[]{:S(2)}) collective-permute-start(bf16[64,3072]{1,0:T(8,128)(2,1)S(1)} %constant_dynamic-slice_fusion), channel_id=1, source_target_pairs={{0,8},{2,10},{4,12},{6,14},{8,16},{10,18},{12,20},{14,22},{16,24},... | collective-permute-start | bytes 1179656 | tf_op jit(solution)/shard_map/ppermute | solution.py:303
  13.2 2.8 %shard_map.157 = (bf16[832,256]{1,0:T(8,128)(2,1)}, bf16[832,256]{1,0:T(8,128)(2,1)}, bf16[832,256]{1,0:T(8,128)(2,1)}, bf16[832,256]{1,0:T(8,128)(2,1)}) custom-call(s32[1]{0:T(128)} %bitcast.member_ref, bf16[192,1024]{1,0:T(8,128)(2,1)} %refs_0_.1, bf16[192,1024]{1,0:T(8,128)(2,1)} %refs_1_.1, bf16[192,1024]{1,0:T(8,128)(2,1)} %refs_2_.2, ...), custom_call_target="tpu_custom_call" | custom-call | tf_op jit(solution)/shard_map/pallas_call | solution.py:193
  16.0 8.3 %collective-permute-done.refs_1_ = bf16[64,3072]{1,0:T(8,128)(2,1)S(1)} collective-permute-done((bf16[64,3072]{1,0:T(8,128)(2,1)S(1)}, bf16[64,3072]{1,0:T(8,128)(2,1)S(1)}, u32[]{:S(2)}, u32[]{:S(2)}) %collective-permute-start) | collective-permute-done | bytes 393248 | tf_op jit(solution)/shard_map/ppermute | solution.py:303
  24.4 0.7 copy-done.8
  25.1 3.8 %collective-permute-start.2 = (bf16[64,3072]{1,0:T(8,128)(2,1)S(1)}, bf16[64,3072]{1,0:T(8,128)(2,1)S(1)}, u32[]{:S(2)}, u32[]{:S(2)}) collective-permute-start(bf16[64,3072]{1,0:T(8,128)(2,1)S(1)} %constant_dynamic-slice_fusion), channel_id=1, source_target_pairs={{0,24},{2,26},{4,28},{6,30},{8,0},{10,2},{12,4},{14,6},{16,8},{18,... | collective-permute-start | bytes 1179656 | tf_op jit(solution)/shard_map/ppermute | solution.py:303
  28.9 1.5 collective-permute-start.4
  30.5 24.1 %collective-permute-done.2.refs_3_ = bf16[64,3072]{1,0:T(8,128)(2,1)S(1)} collective-permute-done((bf16[64,3072]{1,0:T(8,128)(2,1)S(1)}, bf16[64,3072]{1,0:T(8,128)(2,1)S(1)}, u32[]{:S(2)}, u32[]{:S(2)}) %collective-permute-start.2) | collective-permute-done | bytes 393248 | tf_op jit(solution)/shard_map/ppermute | solution.py:303
  54.5 1.8 collective-permute-start.11
  56.4 0.9 collective-permute-start.15
  57.3 1.5 collective-permute-start.1
  59.4 10.1 %collective-permute-done.1.refs_2_ = bf16[64,3072]{1,0:T(8,128)(2,1)S(1)} collective-permute-done((bf16[64,3072]{1,0:T(8,128)(2,1)}, bf16[64,3072]{1,0:T(8,128)(2,1)S(1)}, u32[]{:S(2)}, u32[]{:S(2)}) %collective-permute-start.1) | collective-permute-done | bytes 393248 | tf_op jit(solution)/shard_map/ppermute | solution.py:309
  69.5 1.5 collective-permute-start.8
  70.9 11.6 %collective-permute-done.11.refs_17_.refs_14_ = bf16[832,256]{1,0:T(8,128)(2,1)S(1)} collective-permute-done((bf16[832,256]{1,0:T(8,128)(2,1)}, bf16[832,256]{1,0:T(8,128)(2,1)S(1)}, u32[]{:S(2)}, u32[]{:S(2)}) %collective-permute-start.11) | collective-permute-done | bytes 426016 | tf_op jit(solution)/shard_map/ppermute | solution.py:293
  82.5 1.5 collective-permute-start.12
  84.1 26.4 %collective-permute-done.15.refs_21_.refs_18_ = bf16[832,256]{1,0:T(8,128)(2,1)} collective-permute-done((bf16[832,256]{1,0:T(8,128)(2,1)}, bf16[832,256]{1,0:T(8,128)(2,1)}, u32[]{:S(2)}, u32[]{:S(2)}) %collective-permute-start.15) | collective-permute-done | bytes 426016 | tf_op jit(solution)/shard_map/ppermute | solution.py:293
  110.6 10.0 %collective-permute-start.16 = (bf16[832,256]{1,0:T(8,128)(2,1)}, bf16[832,256]{1,0:T(8,128)(2,1)}, u32[]{:S(2)}, u32[]{:S(2)}) collective-permute-start(bf16[832,256]{1,0:T(8,128)(2,1)} %collective-permute-done.15.refs_21_.refs_18_), channel_id=1, source_target_pairs={{0,4},{2,6},{4,0},{6,2},{8,12},{10,14},{12,8},{14,10},{16,20},{18,... | collective-permute-start | bytes 1277960 | tf_op jit(solution)/shard_map/ppermute | solution.py:306
  120.6 8.9 %collective-permute-done.23.refs_0_ = bf16[64,3072]{1,0:T(8,128)(2,1)S(1)} collective-permute-done((bf16[64,3072]{1,0:T(8,128)(2,1)}, bf16[64,3072]{1,0:T(8,128)(2,1)S(1)}, u32[]{:S(2)}, u32[]{:S(2)}) %collective-permute-start.23) | collective-permute-done | bytes 393248 | tf_op jit(solution)/shard_map/ppermute | solution.py:303
  134.0 12.3 %shard_map.158 = (bf16[128,256]{1,0:T(8,128)(2,1)}, bf16[128,256]{1,0:T(8,128)(2,1)}, bf16[128,256]{1,0:T(8,128)(2,1)}, bf16[128,512]{1,0:T(8,128)(2,1)}, bf16[1...) custom-call(s32[25]{0:T(128)} %stack.134.where_ref, bf16[128,3072]{1,0:T(8,128)(2,1)} %copy-done.1, ...), custom_call_target="tpu_custom_call" | custom-call | flops 2818572288 | bytes 6815744 | tf_op jit(solution)/shard_map/pallas_call | solution.py:137
  146.4 1.5 collective-permute-start.20
  148.4 3.2 %collective-permute-start.19 = (bf16[128,256]{1,0:T(8,128)(2,1)}, bf16[128,256]{1,0:T(8,128)(2,1)S(1)}, u32[]{:S(2)}, u32[]{:S(2)}) collective-permute-start(bf16[128,256]{1,0:T(8,128)(2,1)} %get-tuple-element.31), channel_id=1, source_target_pairs={{0,24},{2,26},{4,28},{6,30},{8,0},{10,2},{12,4},{14,6},{16,8},{18,... | collective-permute-start | bytes 196616 | tf_op jit(solution)/shard_map/ppermute | solution.py:303
  152.3 4.7 %collective-permute-done.19.refs_1_ = bf16[128,256]{1,0:T(8,128)(2,1)S(1)} collective-permute-done((bf16[128,256]{1,0:T(8,128)(2,1)}, bf16[128,256]{1,0:T(8,128)(2,1)S(1)}, u32[]{:S(2)}, u32[]{:S(2)}) %collective-permute-start.19) | collective-permute-done | bytes 65568 | tf_op jit(solution)/shard_map/ppermute | solution.py:303
  157.1 0.9 collective-permute-done.21.refs_3_
  158.0 7.8 %shard_map.159 = (bf16[128,256]{1,0:T(8,128)(2,1)}, bf16[128,512]{1,0:T(8,128)(2,1)}) custom-call(s32[20]{0:T(128)} %stack.136.where_ref, bf16[64,3072]{1,0:T(8,128)(2,1)} %copy-done.9, bf16[64,3072]{1,0:T(8,128)(2,1)} %collective-permute-done.24.refs_1_, bf16[512,1024]{1,0:T(8,128)(2,1)} %refs_2_.3, bf16[512,1024]{1,0:T(8,128)(2,1)} %refs_3_.3, ...), custom_call_target="tpu_custom_call" | custom-call | flops 939524096 | bytes 6815744 | tf_op jit(solution)/shard_map/pallas_call | solution.py:137
  165.8 1.0 collective-permute-start.25
  167.4 3.8 %collective-permute-done.25.refs_2_ = bf16[128,256]{1,0:T(8,128)(2,1)S(1)} collective-permute-done((bf16[128,256]{1,0:T(8,128)(2,1)}, bf16[128,256]{1,0:T(8,128)(2,1)S(1)}, u32[]{:S(2)}, u32[]{:S(2)}) %collective-permute-start.25) | collective-permute-done | bytes 65568 | tf_op jit(solution)/shard_map/ppermute | solution.py:303
  171.9 4.8 %shard_map.161 = bf16[128,1536]{1,0:T(8,128)(2,1)} custom-call(s32[2]{0:T(128)} %pad_add_fusion.1.where_ref, bf16[128,256]{1,0:T(8,128)(2,1)} %get-tuple-element.30.refs_0_, bf16[128,256]{1,0:T(8,128)(2,1)} %copy-done.14, bf16[128,256]{1,0:T(8,128)(2,1)} %copy-done.16, bf16[128,256]{1,0:T(8,128)(2,1)} %copy-done.15, ...), custom_call_target="tpu_custom_call" | custom-call | flops 402653184 | bytes 3145728 | tf_op jit(solution)/shard_map/pallas_call | solution.py:243
  176.7 1.5 collective-permute-start.26
  178.9 4.9 %shard_map.160 = f32[128,1536]{1,0:T(8,128)} custom-call(s32[2]{0:T(128)} %pad_add_fusion.where_ref, bf16[128,256]{1,0:T(8,128)(2,1)} %get-tuple-element.30.refs_0_, bf16[128,256]{1,0:T(8,128)(2,1)} %copy-done.14, bf16[128,256]{1,0:T(8,128)(2,1)} %copy-done.16, bf16[128,256]{1,0:T(8,128)(2,1)} %copy-done.15, ...), custom_call_target="tpu_custom_call" | custom-call | flops 402653184 | bytes 3145728 | tf_op jit(solution)/shard_map/pallas_call | solution.py:243
  183.8 1.7 collective-permute-done.27.refs_2_
  186.2 1.9 shard_map.162
  188.1 2.0 %add_convert_fusion = bf16[128,1536]{1,0:T(8,128)(2,1)} fusion(f32[128,1536]{1,0:T(8,128)} %shard_map.160, bf16[128,1536]{1,0:T(8,128)(2,1)S(1)} %collective-permute-done.26, f32[1536]{0:T(1024)S(1)} %dynamic_slice.10, bf16[128,3072]{1,0:T(8,128)(2,1)S(1)} %copy-done, s32[]{:T(128)S(6)} %select_n.72), kind=kLoop, calls=%fused_computation.8 | loop fusion | flops 1179648 | bytes 1972228 | tf_op jit(solution)/shard_map/convert_element_type | solution.py:385
  (94 shorter events, 10.6 us)
Async XLA Ops:
  7.2 164.1 %all-gather.2.cloned.1.call-start = ((), (), s32[]{:S(2)}) async-start(), calls=%async_computation | async-start | bytes 6684672 | tf_op jit(solution)/shard_map/all_gather | solution.py:314
  10.1 124.0 %copy-start.1 = (bf16[128,3072]{1,0:T(8,128)(2,1)}, bf16[128,3072]{1,0:T(8,128)(2,1)S(1)}, u32[]{:S(2)}) copy-start(bf16[128,3072]{1,0:T(8,128)(2,1)S(1)} %fusion.5.refs_0_) | copy-start | bytes 2359300
  10.1 14.2 %collective-permute-start = (bf16[64,3072]{1,0:T(8,128)(2,1)S(1)}, bf16[64,3072]{1,0:T(8,128)(2,1)S(1)}, u32[]{:S(2)}, u32[]{:S(2)}) collective-permute-start(bf16[64,3072]{1,0:T(8,128)(2,1)S(1)} %constant_dynamic-slice_fusion), channel_id=1, source_target_pairs={{0,8},{2,10},{4,12},{6,14},{8,16},{10,18},{12,20},{14,22},{16,24},... | collective-permute-start | bytes 1179656 | tf_op jit(solution)/shard_map/ppermute | solution.py:303
  25.1 31.3 %collective-permute-start.7 = (bf16[832,256]{1,0:T(8,128)(2,1)}, bf16[832,256]{1,0:T(8,128)(2,1)S(1)}, u32[]{:S(2)}, u32[]{:S(2)}) collective-permute-start(bf16[832,256]{1,0:T(8,128)(2,1)} %get-tuple-element.25), channel_id=1, source_target_pairs={{0,8},{2,10},{4,12},{6,14},{8,16},{10,18},{12,20},{14,22},{16,24},... | collective-permute-start | bytes 1277960 | tf_op jit(solution)/shard_map/ppermute | solution.py:293
  25.1 29.4 %collective-permute-start.2 = (bf16[64,3072]{1,0:T(8,128)(2,1)S(1)}, bf16[64,3072]{1,0:T(8,128)(2,1)S(1)}, u32[]{:S(2)}, u32[]{:S(2)}) collective-permute-start(bf16[64,3072]{1,0:T(8,128)(2,1)S(1)} %constant_dynamic-slice_fusion), channel_id=1, source_target_pairs={{0,24},{2,26},{4,28},{6,30},{8,0},{10,2},{12,4},{14,6},{16,8},{18,... | collective-permute-start | bytes 1179656 | tf_op jit(solution)/shard_map/ppermute | solution.py:303
  28.9 28.3 %collective-permute-start.4 = (bf16[832,256]{1,0:T(8,128)(2,1)}, bf16[832,256]{1,0:T(8,128)(2,1)S(1)}, u32[]{:S(2)}, u32[]{:S(2)}) collective-permute-start(bf16[832,256]{1,0:T(8,128)(2,1)} %get-tuple-element.23.refs_9_.refs_6_), channel_id=1, source_target_pairs={{0,4},{2,6},{4,0},{6,2},{8,12},{10,14},{12,8},{14,10},{16,20},{18,... | collective-permute-start | bytes 1277960 | tf_op jit(solution)/shard_map/ppermute | solution.py:306
  30.5 28.3 %collective-permute-start.5 = (bf16[832,256]{1,0:T(8,128)(2,1)}, bf16[832,256]{1,0:T(8,128)(2,1)S(1)}, u32[]{:S(2)}, u32[]{:S(2)}) collective-permute-start(bf16[832,256]{1,0:T(8,128)(2,1)} %get-tuple-element.23.refs_9_.refs_6_), channel_id=1, source_target_pairs={{0,2},{2,0},{4,6},{6,4},{8,10},{10,8},{12,14},{14,12},{16,18},{18,... | collective-permute-start | bytes 1277960 | tf_op jit(solution)/shard_map/ppermute | solution.py:306
  54.5 28.0 %collective-permute-start.11 = (bf16[832,256]{1,0:T(8,128)(2,1)}, bf16[832,256]{1,0:T(8,128)(2,1)S(1)}, u32[]{:S(2)}, u32[]{:S(2)}) collective-permute-start(bf16[832,256]{1,0:T(8,128)(2,1)} %get-tuple-element.27), channel_id=1, source_target_pairs={{0,24},{2,26},{4,28},{6,30},{8,0},{10,2},{12,4},{14,6},{16,8},{18,... | collective-permute-start | bytes 1277960 | tf_op jit(solution)/shard_map/ppermute | solution.py:293
  56.4 77.6 %copy-start.2 = (bf16[832,256]{1,0:T(8,128)(2,1)}, bf16[832,256]{1,0:T(8,128)(2,1)S(1)}, u32[]{:S(2)}) copy-start(bf16[832,256]{1,0:T(8,128)(2,1)S(1)} %collective-permute-done.7.refs_13_.refs_10_) | copy-start | bytes 1277956
  56.4 54.2 %collective-permute-start.15 = (bf16[832,256]{1,0:T(8,128)(2,1)}, bf16[832,256]{1,0:T(8,128)(2,1)}, u32[]{:S(2)}, u32[]{:S(2)}) collective-permute-start(bf16[832,256]{1,0:T(8,128)(2,1)} %get-tuple-element.29), channel_id=1, source_target_pairs={{0,16},{2,18},{4,20},{6,22},{8,24},{10,26},{12,28},{14,30},{16,0},... | collective-permute-start | bytes 1277960 | tf_op jit(solution)/shard_map/ppermute | solution.py:293
  57.3 76.8 %copy-start.3 = (bf16[832,256]{1,0:T(8,128)(2,1)}, bf16[832,256]{1,0:T(8,128)(2,1)S(1)}, u32[]{:S(2)}) copy-start(bf16[832,256]{1,0:T(8,128)(2,1)S(1)} %collective-permute-done.4.refs_10_.refs_7_) | copy-start | bytes 1277956
  57.3 63.3 %collective-permute-start.6 = (bf16[832,256]{1,0:T(8,128)(2,1)S(1)}, bf16[832,256]{1,0:T(8,128)(2,1)S(1)}, u32[]{:S(2)}, u32[]{:S(2)}) collective-permute-start(bf16[832,256]{1,0:T(8,128)(2,1)S(1)} %collective-permute-done.4.refs_10_.refs_7_), channel_id=1, source_target_pairs={{0,2},{2,0},{4,6},{6,4},{8,10},{10,8},{12,14},{14,12},{16,18},{18,... | collective-permute-start | bytes 1277960 | tf_op jit(solution)/shard_map/ppermute | solution.py:306
  57.3 12.2 %collective-permute-start.1 = (bf16[64,3072]{1,0:T(8,128)(2,1)}, bf16[64,3072]{1,0:T(8,128)(2,1)S(1)}, u32[]{:S(2)}, u32[]{:S(2)}) collective-permute-start(bf16[64,3072]{1,0:T(8,128)(2,1)} %copy-done.8), channel_id=1, source_target_pairs={{0,1},{1,0},{2,3},{3,2},{4,5},{5,4},{6,7},{7,6},{8,9},{9,8},{10,11... | collective-permute-start | bytes 1179656 | tf_op jit(solution)/shard_map/ppermute | solution.py:309
  58.8 25.2 %collective-permute-start.3 = (bf16[64,3072]{1,0:T(8,128)(2,1)S(1)}, bf16[64,3072]{1,0:T(8,128)(2,1)S(1)}, u32[]{:S(2)}, u32[]{:S(2)}) collective-permute-start(bf16[64,3072]{1,0:T(8,128)(2,1)S(1)} %collective-permute-done.2.refs_3_), channel_id=1, source_target_pairs={{0,1},{1,0},{2,3},{3,2},{4,5},{5,4},{6,7},{7,6},{8,9},{9,8},{10,11... | collective-permute-start | bytes 1179656 | tf_op jit(solution)/shard_map/ppermute | solution.py:309
  69.5 60.0 %collective-permute-start.8 = (bf16[832,256]{1,0:T(8,128)(2,1)S(1)}, bf16[832,256]{1,0:T(8,128)(2,1)}, u32[]{:S(2)}, u32[]{:S(2)}) collective-permute-start(bf16[832,256]{1,0:T(8,128)(2,1)S(1)} %collective-permute-done.7.refs_13_.refs_10_), channel_id=1, source_target_pairs={{0,4},{2,6},{4,0},{6,2},{8,12},{10,14},{12,8},{14,10},{16,20},{18,... | collective-permute-start | bytes 1277960 | tf_op jit(solution)/shard_map/ppermute | solution.py:306
  82.5 47.5 %collective-permute-start.12 = (bf16[832,256]{1,0:T(8,128)(2,1)S(1)}, bf16[832,256]{1,0:T(8,128)(2,1)}, u32[]{:S(2)}, u32[]{:S(2)}) collective-permute-start(bf16[832,256]{1,0:T(8,128)(2,1)S(1)} %collective-permute-done.11.refs_17_.refs_14_), channel_id=1, source_target_pairs={{0,4},{2,6},{4,0},{6,2},{8,12},{10,14},{12,8},{14,10},{16,20},{18,... | collective-permute-start | bytes 1277960 | tf_op jit(solution)/shard_map/ppermute | solution.py:306
  84.0 46.0 %collective-permute-start.13 = (bf16[832,256]{1,0:T(8,128)(2,1)S(1)}, bf16[832,256]{1,0:T(8,128)(2,1)S(1)}, u32[]{:S(2)}, u32[]{:S(2)}) collective-permute-start(bf16[832,256]{1,0:T(8,128)(2,1)S(1)} %collective-permute-done.11.refs_17_.refs_14_), channel_id=1, source_target_pairs={{0,2},{2,0},{4,6},{6,4},{8,10},{10,8},{12,14},{14,12},{16,18},{18,... | collective-permute-start | bytes 1277960 | tf_op jit(solution)/shard_map/ppermute | solution.py:306
  110.6 20.3 %collective-permute-start.16 = (bf16[832,256]{1,0:T(8,128)(2,1)}, bf16[832,256]{1,0:T(8,128)(2,1)}, u32[]{:S(2)}, u32[]{:S(2)}) collective-permute-start(bf16[832,256]{1,0:T(8,128)(2,1)} %collective-permute-done.15.refs_21_.refs_18_), channel_id=1, source_target_pairs={{0,4},{2,6},{4,0},{6,2},{8,12},{10,14},{12,8},{14,10},{16,20},{18,... | collective-permute-start | bytes 1277960 | tf_op jit(solution)/shard_map/ppermute | solution.py:306
  120.5 8.9 %collective-permute-start.23 = (bf16[64,3072]{1,0:T(8,128)(2,1)}, bf16[64,3072]{1,0:T(8,128)(2,1)S(1)}, u32[]{:S(2)}, u32[]{:S(2)}) collective-permute-start(bf16[64,3072]{1,0:T(8,128)(2,1)} %copy-done.13), channel_id=1, source_target_pairs={{0,16},{2,18},{4,20},{6,22},{8,24},{10,26},{12,28},{14,30},{16,0},... | collective-permute-start | bytes 1179656 | tf_op jit(solution)/shard_map/ppermute | solution.py:303
  129.5 2.5 %collective-permute-start.9 = (bf16[832,256]{1,0:T(8,128)(2,1)S(1)}, bf16[832,256]{1,0:T(8,128)(2,1)}, u32[]{:S(2)}, u32[]{:S(2)}) collective-permute-start(bf16[832,256]{1,0:T(8,128)(2,1)S(1)} %collective-permute-done.7.refs_13_.refs_10_), channel_id=1, source_target_pairs={{0,2},{2,0},{4,6},{6,4},{8,10},{10,8},{12,14},{14,12},{16,18},{18,... | collective-permute-start | bytes 1277960 | tf_op jit(solution)/shard_map/ppermute | solution.py:306
  129.5 2.8 %collective-permute-start.17 = (bf16[832,256]{1,0:T(8,128)(2,1)}, bf16[832,256]{1,0:T(8,128)(2,1)}, u32[]{:S(2)}, u32[]{:S(2)}) collective-permute-start(bf16[832,256]{1,0:T(8,128)(2,1)} %collective-permute-done.15.refs_21_.refs_18_), channel_id=1, source_target_pairs={{0,2},{2,0},{4,6},{6,4},{8,10},{10,8},{12,14},{14,12},{16,18},{18,... | collective-permute-start | bytes 1277960 | tf_op jit(solution)/shard_map/ppermute | solution.py:306
  130.0 2.8 %collective-permute-start.10 = (bf16[832,256]{1,0:T(8,128)(2,1)}, bf16[832,256]{1,0:T(8,128)(2,1)}, u32[]{:S(2)}, u32[]{:S(2)}) collective-permute-start(bf16[832,256]{1,0:T(8,128)(2,1)} %collective-permute-done.8.refs_14_.refs_11_), channel_id=1, source_target_pairs={{0,2},{2,0},{4,6},{6,4},{8,10},{10,8},{12,14},{14,12},{16,18},{18,... | collective-permute-start | bytes 1277960 | tf_op jit(solution)/shard_map/ppermute | solution.py:306
  130.1 3.3 %collective-permute-start.14 = (bf16[832,256]{1,0:T(8,128)(2,1)}, bf16[832,256]{1,0:T(8,128)(2,1)}, u32[]{:S(2)}, u32[]{:S(2)}) collective-permute-start(bf16[832,256]{1,0:T(8,128)(2,1)} %collective-permute-done.12.refs_18_.refs_15_), channel_id=1, source_target_pairs={{0,2},{2,0},{4,6},{6,4},{8,10},{10,8},{12,14},{14,12},{16,18},{18,... | collective-permute-start | bytes 1277960 | tf_op jit(solution)/shard_map/ppermute | solution.py:306
  130.9 3.1 %collective-permute-start.18 = (bf16[832,256]{1,0:T(8,128)(2,1)}, bf16[832,256]{1,0:T(8,128)(2,1)}, u32[]{:S(2)}, u32[]{:S(2)}) collective-permute-start(bf16[832,256]{1,0:T(8,128)(2,1)} %collective-permute-done.16.refs_22_.refs_19_), channel_id=1, source_target_pairs={{0,2},{2,0},{4,6},{6,4},{8,10},{10,8},{12,14},{14,12},{16,18},{18,... | collective-permute-start | bytes 1277960 | tf_op jit(solution)/shard_map/ppermute | solution.py:306
  132.0 26.0 %collective-permute-start.24 = (bf16[64,3072]{1,0:T(8,128)(2,1)}, bf16[64,3072]{1,0:T(8,128)(2,1)}, u32[]{:S(2)}, u32[]{:S(2)}) collective-permute-start(bf16[64,3072]{1,0:T(8,128)(2,1)} %copy-done.9), channel_id=1, source_target_pairs={{0,1},{1,0},{2,3},{3,2},{4,5},{5,4},{6,7},{7,6},{8,9},{9,8},{10,11... | collective-permute-start | bytes 1179656 | tf_op jit(solution)/shard_map/ppermute | solution.py:309
  146.4 11.6 %collective-permute-start.20 = (bf16[128,512]{1,0:T(8,128)(2,1)}, bf16[128,512]{1,0:T(8,128)(2,1)S(1)}, u32[]{:S(2)}, u32[]{:S(2)}) collective-permute-start(bf16[128,512]{1,0:T(8,128)(2,1)} %get-tuple-element.33), channel_id=1, source_target_pairs={{0,24},{2,26},{4,28},{6,30},{8,0},{10,2},{12,4},{14,6},{16,8},{18,... | collective-permute-start | bytes 393224 | tf_op jit(solution)/shard_map/ppermute | solution.py:303
  147.9 10.1 %collective-permute-start.22 = (bf16[128,512]{1,0:T(8,128)(2,1)}, bf16[128,512]{1,0:T(8,128)(2,1)S(1)}, u32[]{:S(2)}, u32[]{:S(2)}) collective-permute-start(bf16[128,512]{1,0:T(8,128)(2,1)} %get-tuple-element.35), channel_id=1, source_target_pairs={{0,8},{2,10},{4,12},{6,14},{8,16},{10,18},{12,20},{14,22},{16,24},... | collective-permute-start | bytes 393224 | tf_op jit(solution)/shard_map/ppermute | solution.py:303
  148.4 8.6 %collective-permute-start.19 = (bf16[128,256]{1,0:T(8,128)(2,1)}, bf16[128,256]{1,0:T(8,128)(2,1)S(1)}, u32[]{:S(2)}, u32[]{:S(2)}) collective-permute-start(bf16[128,256]{1,0:T(8,128)(2,1)} %get-tuple-element.31), channel_id=1, source_target_pairs={{0,24},{2,26},{4,28},{6,30},{8,0},{10,2},{12,4},{14,6},{16,8},{18,... | collective-permute-start | bytes 196616 | tf_op jit(solution)/shard_map/ppermute | solution.py:303
  151.7 6.3 %collective-permute-start.21 = (bf16[128,256]{1,0:T(8,128)(2,1)}, bf16[128,256]{1,0:T(8,128)(2,1)S(1)}, u32[]{:S(2)}, u32[]{:S(2)}) collective-permute-start(bf16[128,256]{1,0:T(8,128)(2,1)} %get-tuple-element.34), channel_id=1, source_target_pairs={{0,8},{2,10},{4,12},{6,14},{8,16},{10,18},{12,20},{14,22},{16,24},... | collective-permute-start | bytes 196616 | tf_op jit(solution)/shard_map/ppermute | solution.py:303
  165.8 5.4 %collective-permute-start.25 = (bf16[128,256]{1,0:T(8,128)(2,1)}, bf16[128,256]{1,0:T(8,128)(2,1)S(1)}, u32[]{:S(2)}, u32[]{:S(2)}) collective-permute-start(bf16[128,256]{1,0:T(8,128)(2,1)} %get-tuple-element.38), channel_id=1, source_target_pairs={{0,16},{2,18},{4,20},{6,22},{8,24},{10,26},{12,28},{14,30},{16,0},... | collective-permute-start | bytes 196616 | tf_op jit(solution)/shard_map/ppermute | solution.py:303
  176.7 11.4 %collective-permute-start.26 = (bf16[128,1536]{1,0:T(8,128)(2,1)}, bf16[128,1536]{1,0:T(8,128)(2,1)S(1)}, u32[]{:S(2)}, u32[]{:S(2)}) collective-permute-start(bf16[128,1536]{1,0:T(8,128)(2,1)} %shard_map.161), channel_id=1, source_target_pairs={{0,1},{1,0},{2,3},{3,2},{4,5},{5,4},{6,7},{7,6},{8,9},{9,8},{10,11... | collective-permute-start | bytes 1179656 | tf_op jit(solution)/shard_map/ppermute | solution.py:309
  178.3 7.3 %collective-permute-start.27 = (bf16[128,512]{1,0:T(8,128)(2,1)S(1)}, bf16[128,512]{1,0:T(8,128)(2,1)S(1)}, u32[]{:S(2)}, u32[]{:S(2)}) collective-permute-start(bf16[128,512]{1,0:T(8,128)(2,1)S(1)} %copy-done.23), channel_id=1, source_target_pairs={{0,16},{2,18},{4,20},{6,22},{8,24},{10,26},{12,28},{14,30},{16,0},... | collective-permute-start | bytes 393224 | tf_op jit(solution)/shard_map/ppermute | solution.py:303
  (21 other events, 326.5 us)
Sparse Core Ops, SparseCore 0:
  10.3 94.9 all-gather.1

commit v2 on v1

--- a/solution.py
+++ b/solution.py
@@ -33,9 +33,9 @@
     shares, refs = refs[:n_shares], refs[n_shares:]
     tk_ref, tv_ref, qg_ref, kg_ref = refs[:4]
     pieces, refs = refs[4 : 4 + n_pieces], refs[4 + n_pieces :]
-    att_refs, kv_refs = refs[:n_patches], refs[n_patches : 2 * n_patches]
-    held, scores, expos, sems = refs[2 * n_patches :]
-    rows, width = att_refs[0].shape
+    att_refs, refs = refs[: n_patches // 2], refs[n_patches // 2 :]
+    kv_refs, (held, scores, expos, sems) = refs[:n_patches], refs[n_patches:]
+    rows, width = kv_refs[0].shape[0], kv_refs[0].shape[1] // 2
     groups = [slice(g * rows, (g + 1) * rows) for g in range(n_patches)]
     owns, firsts, at = [], [], 1 + n_pieces
     for count in counts:
@@ -49,12 +49,23 @@
     for copy in copies:
         copy.start()
 
-    def put(refs, cols, value):
+    def put(ref_of, cols, value):
         for g, group in enumerate(groups):
+            ref, base = ref_of(g)
             share = rows // counts[g]
             for i, first in enumerate(firsts[g]):
                 start = group.start + i * share
-                refs[g][pl.ds(pl.multiple_of(first, 16), share), cols] = value[start : start + share]
+                to = pl.ds(pl.multiple_of(base + first, 16), share)
+                ref[to, cols] = value[start : start + share]
+
+    def kv_of(g):
+        return kv_refs[g], 0
+
+    def att_of(g):
+        return att_refs[g // 2], lax.rem(owns[g] // INNER, 2) * rows
+
+    def rows_of(cols):
+        return jnp.concatenate([x[:, cols] for x in shares], axis=0)
 
     chunk = INNER * depth
     proj = [jnp.zeros((n_patches * rows, width), jnp.float32) for _ in range(3)]
@@ -64,7 +75,7 @@
                 copy.wait()
             place = where_ref[1 + first] // INNER
             cols = pl.ds(pl.multiple_of(place * chunk, 128), chunk)
-            part = jnp.concatenate([x[:, cols] for x in shares], axis=0)
+            part = rows_of(cols)
             for i in range(3):
                 weight = held[pl.ds(place * INNER, INNER), i * depth : (i + 1) * depth, :]
                 proj[i] += jnp.dot(
@@ -73,7 +84,7 @@
     else:
         for copy in copies:
             copy.wait()
-        part = jnp.concatenate([x[...] for x in shares], axis=0)
+        part = rows_of(slice(None))
         for i in range(3):
             weight = held[:, i * depth : (i + 1) * depth, :]
             proj[i] += jnp.dot(
@@ -86,13 +97,13 @@
         return (x * lax.rsqrt(power + 1e-06) * gain).astype(jnp.bfloat16)
 
     v_new = v_proj.astype(jnp.bfloat16)
-    put(kv_refs, slice(width, 2 * width), v_new)
+    put(kv_of, slice(width, 2 * width), v_new)
     k0, v0 = 3 * depth, 3 * depth + rows
     scale = math.log2(math.e) / math.sqrt(head_size)
     for h in range(width // head_size):
         cols = slice(h * head_size, (h + 1) * head_size)
         key = norm(k_proj[:, cols], kg_ref[...])
-        put(kv_refs, cols, key)
+        put(kv_of, cols, key)
         query = norm(q_proj[:, cols], qg_ref[...])
         value = v_new[:, cols]
         keys = held[:, k0 : k0 + rows, cols].reshape(n_pieces * rows, head_size)
@@ -121,7 +132,7 @@
             + jnp.dot(expos[...], values, preferred_element_type=jnp.float32)
             + jnp.concatenate(fresh_mix, axis=0)
         )
-        put(att_refs, cols, (mixture / total).astype(jnp.bfloat16))
+        put(att_of, cols, (mixture / total).astype(jnp.bfloat16))
 
 
 def attend_patches(where, patches, text_keys, text_values, query_gain, key_gain, pieces, depth, width):
@@ -133,7 +144,7 @@
     texts = text_keys.shape[0]
     n_pieces = len(pieces)
     whole = lambda i, w: (0, 0)
-    outs = [width] * n + [2 * width] * n
+    outs = [(2 * rows, width)] * (n // 2) + [(rows, 2 * width)] * n
     out = pl.pallas_call(
         functools.partial(patch_kernel, depth, head_size, n_pieces, [len(x) for x in patches]),
         grid_spec=pltpu.PrefetchScalarGridSpec(
@@ -147,7 +158,7 @@
                 pl.BlockSpec((1, head_size), whole),
             ]
             + [pl.BlockSpec(memory_space=pl.ANY)] * n_pieces,
-            out_specs=[pl.BlockSpec((rows, x), whole) for x in outs],
+            out_specs=[pl.BlockSpec(x, whole) for x in outs],
             scratch_shapes=[
                 pltpu.VMEM((n_pieces,) + pieces[0].shape, jnp.bfloat16),
                 pltpu.VMEM((n * rows, n_pieces * rows), jnp.float32),
@@ -155,7 +166,7 @@
                 pltpu.SemaphoreType.DMA((n_pieces,)),
             ],
         ),
-        out_shape=[jax.ShapeDtypeStruct((rows, x), jnp.bfloat16) for x in outs],
+        out_shape=[jax.ShapeDtypeStruct(x, jnp.bfloat16) for x in outs],
         compiler_params=pltpu.CompilerParams(vmem_limit_bytes=VMEM_BYTES),
         cost_estimate=pl.CostEstimate(
             flops=2 * n * rows * (model_width * 3 * width + 2 * (texts + n_pieces * rows) * width),
@@ -171,14 +182,14 @@
         key_gain.reshape(1, -1),
         *pieces,
     )
-    return out[:n], out[n:]
+    return out[: n // 2], out[n // 2 :]
 
 
 def deal_kernel(n_arrays, team, member_ref, *refs):
     arrays, outs = refs[:n_arrays], refs[n_arrays:]
     width = outs[0].shape[1]
     for k in range(team):
-        at = lax.rem(member_ref[0] + k, team)
+        at = member_ref[0] ^ k
         cols = pl.ds(pl.multiple_of(at * width, 128), width)
         first = 0
         for x in arrays:
@@ -204,7 +215,7 @@
     packs, outs = refs[:team], refs[team:]
     width = outs[0].shape[1] // team
     for s in range(team):
-        at = lax.rem(member_ref[0] + s, team)
+        at = member_ref[0] ^ s
         cols = pl.ds(pl.multiple_of(at * width, 128), width)
         for i, out in enumerate(outs):
             out[:, cols] = packs[s][:, i * width : (i + 1) * width]
@@ -224,39 +235,62 @@
     )(member.reshape(1), *packs)
 
 
-def project_kernel(team, where_ref, *refs):
-    packs, w_ref, out_ref = refs[:team], refs[team], refs[team + 1]
-    width = w_ref.shape[1] // team
-    total = jnp.zeros(out_ref.shape, jnp.float32)
-    for s in range(team):
-        at = lax.rem(where_ref[0] + s, team)
-        cols = pl.ds(pl.multiple_of(at * width, 128), width)
-        total += nt_dot(packs[s][...], w_ref[:, cols])
-    out_ref[...] = total.astype(out_ref.dtype)
-
-
-def project(where, packs, w_rows, share, dtype):
-    rows, width = packs[0].shape
-    local_width = w_rows.shape[1]
-    steps = 3 if share % (3 * 256) == 0 else 1
-    block = share // steps
+def project_kernel(n_packs, n_pieces, n_shares, where_ref, *refs):
+    packs, pieces = refs[:n_packs], refs[n_packs : n_packs + n_pieces]
+    refs = refs[n_packs + n_pieces :]
+    outs, held, sems = refs[:-2], refs[-2], refs[-1]
+    rows, width = packs[0].shape[0] // 2, packs[0].shape[1]
+    depth = held.shape[1]
+    copies = [
+        pltpu.make_async_copy(piece, held.at[where_ref[2 + n_shares + i]], sems.at[i])
+        for i, piece in enumerate(pieces)
+    ]
+    for copy in copies:
+        copy.start()
+    own = pl.multiple_of(where_ref[1] * rows, 16)
+    other = pl.multiple_of((1 - where_ref[1]) * rows, 16)
+    attended = [
+        jnp.concatenate([x[pl.ds(own, rows), :], x[pl.ds(other, rows), :]], axis=0) for x in packs
+    ]
+    for copy in copies:
+        copy.wait()
+    for i in reversed(range(n_shares)):
+        block = pl.ds(where_ref[2 + i] * INNER, INNER)
+        total = jnp.zeros((2 * rows, INNER * depth), jnp.float32)
+        for s in range(n_packs):
+            cols = pl.ds(pl.multiple_of((where_ref[0] ^ s) * width, 128), width)
+            total += nt_dot(attended[s], held[block, :, cols].reshape(INNER * depth, width))
+        outs[2 * i][...] = total[:rows].astype(outs[2 * i].dtype)
+        outs[2 * i + 1][...] = total[rows:].astype(outs[2 * i + 1].dtype)
+
+
+def project(where, packs, pieces, n_shares):
+    rows, width = packs[0].shape[0] // 2, packs[0].shape[1]
+    depth, local_width = pieces[0].shape
+    block = INNER * depth
+    whole = lambda i, w: (0, 0)
+    types = [jnp.float32] + [jnp.bfloat16] * (2 * n_shares - 1)
     return pl.pallas_call(
-        functools.partial(project_kernel, len(packs)),
+        functools.partial(project_kernel, len(packs), len(pieces), n_shares),
         grid_spec=pltpu.PrefetchScalarGridSpec(
             num_scalar_prefetch=1,
-            grid=(steps,),
-            in_specs=[pl.BlockSpec((rows, width), lambda i, w: (0, 0))] * len(packs)
-            + [pl.BlockSpec((block, local_width), lambda i, w: (w[1] * steps + i, 0))],
-            out_specs=pl.BlockSpec((rows, block), lambda i, w: (0, i)),
+            grid=(1,),
+            in_specs=[pl.BlockSpec((2 * rows, width), whole)] * len(packs)
+            + [pl.BlockSpec(memory_space=pl.ANY)] * len(pieces),
+            out_specs=[pl.BlockSpec((rows, block), whole)] * len(types),
+            scratch_shapes=[
+                pltpu.VMEM((len(pieces), depth, local_width), jnp.bfloat16),
+                pltpu.SemaphoreType.DMA((len(pieces),)),
+            ],
         ),
-        out_shape=jax.ShapeDtypeStruct((rows, share), dtype),
+        out_shape=[jax.ShapeDtypeStruct((rows, block), t) for t in types],
         compiler_params=pltpu.CompilerParams(vmem_limit_bytes=VMEM_BYTES),
         cost_estimate=pl.CostEstimate(
-            flops=2 * rows * share * local_width,
-            bytes_accessed=2 * share * local_width,
+            flops=4 * rows * block * n_shares * local_width,
+            bytes_accessed=2 * block * n_shares * local_width,
             transcendentals=0,
         ),
-    )(where, *packs, w_rows)
+    )(where, *packs, *pieces)
 
 
 def on_device(
@@ -284,101 +318,117 @@
     outer = patches // INNER
     team = math.gcd(outer, heads)
     width = local_width // team
+    assert outer == 2 * fsdp and team > 1 and team & (team - 1) == 0 and outer & (outer - 1) == 0
     me = lax.axis_index("patch")
     mine = lax.axis_index("fsdp")
     place, seat = me // INNER, me % INNER
-    member = place % team
-
-    def along_outer(x, step):
-        return lax.ppermute(
-            x, "patch", [(p, (p + step * INNER) % patches) for p in range(patches)]
-        )
-
-    def along_team(x, step):
-        pairs = []
-        for p in range(patches):
-            z = p // INNER
-            to = z - z % team + (z % team + step) % team
-            pairs.append((p, to * INNER + p % INNER))
-        return lax.ppermute(x, "patch", pairs)
-
-    def flip(x, bit):
-        return lax.ppermute(x, "patch", [(p, p ^ bit) for p in range(patches)])
+    member, parity = place % team, place % 2
+    chain = []
+
+    def over_outer(x, pairs):
+        if len(chain) >= 3:
+            x = after(x, chain[-3])
+        seats = range(INNER)
+        pairs = [(a * INNER + k, b * INNER + k) for a, b in pairs for k in seats]
+        chain.append(lax.ppermute(x, "patch", pairs))
+        return chain[-1]
+
+    def to_partner(x, bits):
+        return over_outer(x, [(z, z ^ bits) for z in range(outer)])
+
+    def flip(x, bits):
+        return lax.ppermute(x, "patch", [(p, p ^ bits) for p in range(patches)])
 
     def along_fsdp(x, step):
         return lax.ppermute(x, "fsdp", [(i, (i + step) % fsdp) for i in range(fsdp)])
 
-    def steps_of(count):
-        return sorted(range(1, count), key=lambda s: (min(s, count - s), s))
-
-    w_rows = lax.all_gather(w_out.T, "patch", axis=0, tiled=True)
-    dealt = deal(member, (w_query, w_key, w_value, stale_keys, stale_values), team)
+    def along_both(x, bits, step):
+        pairs = [
+            (p * fsdp + f, (p ^ (bits * INNER)) * fsdp + (f + step) % fsdp)
+            for p in range(patches)
+            for f in range(fsdp)
+        ]
+        return lax.ppermute(x, ("patch", "fsdp"), pairs)
+
+    def spread(piece):
+        side = flip(piece, 2)
+        return [piece, side, flip(piece, 1), flip(side, 1)]
+
+    def seats_of(position):
+        return [position * INNER + (seat ^ bits) for bits in (0, 2, 1, 3)]
+
     modded = modulate(image, mod_shift, mod_scale)
     share = rows // fsdp
     part = lax.dynamic_slice_in_dim(modded, mine * share, share, axis=0)
-
-    pieces, origins, sent, incoming = {}, {}, [], {0: [modded]}
-
-    def send_rows(s):
-        got = along_team(after(part, *sent[-2:-1]), s)
-        sent.append(got)
-        incoming[s] = [got] + [along_fsdp(got, i) for i in range(1, fsdp)]
-
-    def spread(s, piece):
-        side = flip(piece, 2)
-        pieces[s] = [piece, side, flip(piece, 1), flip(side, 1)]
-        source = (place + (outer - s)) % outer
-        origins[s] = [source * INNER + (seat ^ bits) for bits in (0, 2, 1, 3)]
-
-    team_order, order = steps_of(team), steps_of(outer)
-    for s in team_order[:-1]:
-        send_rows(s)
-    spread(0, dealt[0])
-    for s in order:
-        piece = along_outer(after(dealt[s % team], *sent[-2:-1]), s)
-        sent.append(piece)
-        spread(s, piece)
-    for s in team_order[-1:]:
-        send_rows(s)
-
-    all_pieces = [x for s in [0] + order for x in pieces[s]]
-    all_origins = [o for s in [0] + order for o in origins[s]]
-    attended, fresh = {}, {}
-    last = []
-    for batch in ([0] + team_order[:-1], team_order[-1:]):
-        if not batch:
-            continue
-        where = [member] + all_origins
-        for s in batch:
-            where.append((place - member + (member + team - s) % team) * INNER + seat)
-            where += [((mine + (fsdp - i)) % fsdp) * share for i in range(fsdp)] if s else [0 * mine]
-        att, kv = attend_patches(
-            after(jnp.stack(where).astype(jnp.int32), *last),
-            [incoming[s] for s in batch],
-            text_keys,
-            text_values,
-            query_gain,
-            key_gain,
-            all_pieces,
-            depth,
-            width,
-        )
-        for s, a, f in zip(batch, att, kv):
-            attended[s] = along_team(a, team - s) if s else a
-            fresh[s] = along_team(f, team - s) if s else f
-            last += [attended[s], fresh[s]]
-    packs = [attended[s] for s in range(team)]
+    dealt = deal(member, (w_query, w_key, w_value, stale_keys, stale_values), team)
+    pieces = {0: dealt[0]}
+    row_shares = {}
+    if outer == 4 and team == 4:
+        ends = [(1, 0), (2, 3)]
+        middle = [(1, 2), (2, 1)]
+        inside = jnp.logical_or(place == 1, place == 2)
+        near = to_partner(part, 1)
+        across = over_outer(part, middle)
+        pieces[1] = to_partner(dealt[1], 1)
+        far = over_outer(near, middle)
+        pieces[2] = to_partner(dealt[2], 2)
+        end_across = over_outer(across, ends)
+        pieces[3] = to_partner(dealt[3], 3)
+        end_far = over_outer(far, ends)
+        row_shares[1] = near
+        row_shares[2] = jnp.where(inside, far, end_across)
+        row_shares[3] = jnp.where(inside, across, end_far)
+    else:
+        for k in range(1, team):
+            row_shares[k] = to_partner(part, k)
+        for k in range(1, outer):
+            pieces[k] = to_partner(dealt[k % team], k)
+    out_pieces = [w_out.T] + [to_partner(w_out.T, 2 * k) for k in range(1, fsdp)]
+
+    pieces = [x for k in range(outer) for x in spread(pieces[k])]
+    origins = [o for k in range(outer) for o in seats_of(place ^ k)]
+    patch_rows = [[modded]]
+    for k in range(1, team):
+        got = row_shares[k]
+        patch_rows.append([got] + [along_fsdp(got, i) for i in range(1, fsdp)])
+    out_pieces = [x for piece in out_pieces for x in spread(piece)]
+    out_places = [o for k in range(fsdp) for o in seats_of((place ^ (2 * k)) // 2)]
+
+    where = [member] + origins
+    for k in range(team):
+        where.append((place ^ k) * INNER + seat)
+        where += [((mine + (fsdp - i)) % fsdp) * share for i in range(fsdp)] if k else [0 * mine]
+    att, kv = attend_patches(
+        jnp.stack(where).astype(jnp.int32),
+        patch_rows,
+        text_keys,
+        text_values,
+        query_gain,
+        key_gain,
+        pieces,
+        depth,
+        width,
+    )
+    def give(x, bits):
+        return lax.ppermute(x, "patch", [(p, p ^ (bits * INNER)) for p in range(patches)])
+
+    packs = [att[0]] + [give(att[k // 2], k) for k in range(1, team)]
+    where = [member, parity] + [(mine + i) % fsdp for i in range(fsdp)] + out_places
+    partial = project(jnp.stack(where).astype(jnp.int32), packs, out_pieces, fsdp)
+    own, partner = partial[0], [along_both(partial[1], 1, 0)]
+    for i in range(1, fsdp):
+        own = own + along_fsdp(partial[2 * i], i).astype(jnp.float32)
+        partner.append(along_both(partial[2 * i + 1], 1, i))
+    other = sum(x.astype(jnp.float32) for x in partner)
+    summed = jnp.where(
+        parity == 0,
+        jnp.concatenate([own, other], axis=1),
+        jnp.concatenate([other, own], axis=1),
+    )
+    fresh = [kv[0]] + [give(kv[k], k) for k in range(1, team)]
+    key_out, value_out = collect(member, [after(fresh[0], partial[0])] + fresh[1:])
+
     out_share = model_width // fsdp
-    received = []
-    for i in range(1, fsdp):
-        where = jnp.stack([member, (mine + i) % fsdp]).astype(jnp.int32)
-        received.append(along_fsdp(project(where, packs, w_rows, out_share, jnp.bfloat16), i))
-    where = jnp.stack([member, mine]).astype(jnp.int32)
-    summed = project(where, packs, w_rows, out_share, jnp.float32)
-    fresh = [fresh[s] for s in range(team)]
-    key_out, value_out = collect(member, [after(fresh[0], summed)] + fresh[1:])
-    for x in received:
-        summed = summed + x.astype(jnp.float32)
     col_start = mine * out_share
     image_part = lax.dynamic_slice_in_dim(image, col_start, out_share, 1).astype(jnp.float32)
     gate_part = lax.dynamic_slice_in_dim(mod_gate, col_start, out_share, 0)

time: 197 us -> 165 us (0.84)
  waiting for transfers between devices: 103 us -> 82.9 us
  between operations: 14.3 us -> 1.08 us
  starting transfers between devices: 35.9 us -> 48.1 us
  Pallas kernels: 34.6 us -> 24.9 us
    ppermute x24 -> x35, waiting for transfers between devices: 92.2 us -> 71.2 us  [the longest x9 46.7 us: over_outer(): chain.append(lax.ppermute(x, 'patch', pairs))]
    ppermute x24 -> x35, starting transfers between devices: 32.1 us -> 42.2 us  [the longest x9 19.6 us: over_outer(): chain.append(lax.ppermute(x, 'patch', pairs))]
    pallas_call x2 -> x1, Pallas kernels: 20.1 us -> 14.6 us  [attend_patches(): pl.pallas_call(functools.partial(patch_kernel, depth, head_size, n_pieces...]
    pallas_call x2 -> x1, Pallas kernels: 9.76 us -> 5.59 us  [project(): pl.pallas_call(functools.partial(project_kernel, len(packs), len(pieces),...]
    ppermute x4, starting transfers between devices: 3.84 us -> 5.95 us  [along_fsdp(): lax.ppermute(x, 'fsdp', [(i, (i + step) % fsdp) for i in range(fsdp)])]
  transfers between devices with their start and end apart: 29 -> 39, of which waited for: 13 -> 14; matrix products, arithmetic and copies ran while one was open for 2% -> 1% of each run, Pallas kernels for 15% -> 12%
where the time goes in v2:
time: 165 us
  waiting for transfers between devices  82.9 us (50%)
  starting transfers between devices  48.1 us (29%)
  Pallas kernels  24.9 us (15%)
  other arithmetic  4.25 us (3%)
  local copies, waits for them, and re-layouts  3.38 us (2%)
    ppermute x9, waiting for transfers between devices, over_outer(): chain.append(lax.ppermute(x, 'patch', pairs))  46.7 us
    ppermute x9, starting transfers between devices, over_outer(): chain.append(lax.ppermute(x, 'patch', pairs))  19.6 us
    ppermute x6, waiting for transfers between devices, give(): lax.ppermute(x, 'patch', [(p, p ^ bits * INNER) for p in range(patches)])  15.6 us
    pallas_call x1, Pallas kernels, attend_patches(): pl.pallas_call(functools.partial(patch_kernel, depth, head_size, n_pieces...  14.6 us
    ppermute x4, waiting for transfers between devices, along_fsdp(): lax.ppermute(x, 'fsdp', [(i, (i + step) % fsdp) for i in range(fsdp)])  11.6 us
    ppermute x18, starting transfers between devices, flip(): return lax.ppermute(x, 'patch', [(p, p ^ bits) for p in range(patches)])  10.9 us
    ppermute x6, starting transfers between devices, give(): lax.ppermute(x, 'patch', [(p, p ^ bits * INNER) for p in range(patches)])  9.02 us
    ppermute x18, waiting for transfers between devices, flip(): return lax.ppermute(x, 'patch', [(p, p ^ bits) for p in range(patches)])  8.18 us
  transfers between devices with their start and end apart: 39, of which 14 were waited for; matrix products, arithmetic and copies ran while one was open for 1% of the time, Pallas kernels for 12%

profile of v2, /device:TPU:0, one launch (start us, length us, event | category | flops | bytes accessed | tf_op | source)
XLA Modules:
  0.0 164.6 jit_solution(17824247821339235779)
XLA Ops:
  2.9 3.1 %collective-permute-start = (bf16[64,3072]{1,0:T(8,128)(2,1)S(1)}, bf16[64,3072]{1,0:T(8,128)(2,1)}, u32[]{:S(2)}, u32[]{:S(2)}) collective-permute-start(bf16[64,3072]{1,0:T(8,128)(2,1)S(1)} %constant_dynamic-slice_fusion), channel_id=1, source_target_pairs={{0,8},{2,10},{4,12},{6,14},{8,0},{10,2},{12,4},{14,6},{16,24},{18,... | collective-permute-start | bytes 1179656 | tf_op jit(solution)/shard_map/ppermute | solution.py:333
  6.0 2.8 %shard_map.157 = (bf16[832,256]{1,0:T(8,128)(2,1)}, bf16[832,256]{1,0:T(8,128)(2,1)}, bf16[832,256]{1,0:T(8,128)(2,1)}, bf16[832,256]{1,0:T(8,128)(2,1)}) custom-call(s32[1]{0:T(128)} %bitcast.member_ref, bf16[192,1024]{1,0:T(8,128)(2,1)} %refs_0_.1, bf16[192,1024]{1,0:T(8,128)(2,1)} %refs_1_.1, bf16[192,1024]{1,0:T(8,128)(2,1)} %refs_2_.1, ...), custom_call_target="tpu_custom_call" | custom-call | tf_op jit(solution)/shard_map/pallas_call | solution.py:204
  9.8 6.3 %collective-permute-done.refs_1_ = bf16[64,3072]{1,0:T(8,128)(2,1)} collective-permute-done((bf16[64,3072]{1,0:T(8,128)(2,1)S(1)}, bf16[64,3072]{1,0:T(8,128)(2,1)}, u32[]{:S(2)}, u32[]{:S(2)}) %collective-permute-start) | collective-permute-done | bytes 393248 | tf_op jit(solution)/shard_map/ppermute | solution.py:333
  16.7 2.1 %collective-permute-start.10 = (bf16[832,256]{1,0:T(8,128)(2,1)}, bf16[832,256]{1,0:T(8,128)(2,1)}, u32[]{:S(2)}, u32[]{:S(2)}) collective-permute-start(bf16[832,256]{1,0:T(8,128)(2,1)} %get-tuple-element.32.refs_11_), channel_id=1, source_target_pairs={{0,4},{2,6},{4,0},{6,2},{8,12},{10,14},{12,8},{14,10},{16,20},{18,... | collective-permute-start | bytes 1277960 | tf_op jit(solution)/shard_map/ppermute | solution.py:340
  18.8 6.9 %collective-permute-start.7 = (bf16[832,256]{1,0:T(8,128)(2,1)}, bf16[832,256]{1,0:T(8,128)(2,1)}, u32[]{:S(2)}, u32[]{:S(2)}) collective-permute-start(bf16[832,256]{1,0:T(8,128)(2,1)} %get-tuple-element.30), channel_id=1, source_target_pairs={{0,16},{2,18},{4,20},{6,22},{8,24},{10,26},{12,28},{14,30},{16,0},... | collective-permute-start | bytes 1277960 | tf_op jit(solution)/shard_map/ppermute | solution.py:333
  25.8 1.5 collective-permute-start.26
  28.6 7.0 %collective-permute-done.26.refs_5_ = bf16[192,1024]{1,0:T(8,128)(2,1)S(1)} collective-permute-done((bf16[192,1024]{1,0:T(8,128)(2,1)S(1)}, bf16[192,1024]{1,0:T(8,128)(2,1)S(1)}, u32[]{:S(2)}, u32[]{:S(2)}) %collective-permute-start.26) | collective-permute-done | bytes 393248 | tf_op jit(solution)/shard_map/ppermute | solution.py:340
  37.0 1.5 collective-permute-start.13
  38.5 18.7 %collective-permute-done.5 = bf16[64,3072]{1,0:T(8,128)(2,1)S(1)} collective-permute-done((bf16[64,3072]{1,0:T(8,128)(2,1)S(1)}, bf16[64,3072]{1,0:T(8,128)(2,1)S(1)}, u32[]{:S(2)}, u32[]{:S(2)}) %collective-permute-start.5) | collective-permute-done | bytes 393248 | tf_op jit(solution)/shard_map/ppermute | solution.py:333
  57.2 2.8 %collective-permute-start.19 = (bf16[832,256]{1,0:T(8,128)(2,1)}, bf16[832,256]{1,0:T(8,128)(2,1)}, u32[]{:S(2)}, u32[]{:S(2)}) collective-permute-start(bf16[832,256]{1,0:T(8,128)(2,1)} %get-tuple-element.34), channel_id=1, source_target_pairs={{0,24},{2,26},{4,28},{6,30},{8,16},{10,18},{12,20},{14,22},{16,8},... | collective-permute-start | bytes 1277960 | tf_op jit(solution)/shard_map/ppermute | solution.py:333
  60.0 1.6 collective-permute-start.6
  61.6 1.5 collective-permute-start.8
  63.1 2.4 %collective-permute-start.29 = (bf16[192,1024]{1,0:T(8,128)(2,1)S(1)}, bf16[192,1024]{1,0:T(8,128)(2,1)S(1)}, u32[]{:S(2)}, u32[]{:S(2)}) collective-permute-start(bf16[192,1024]{1,0:T(8,128)(2,1)S(1)} %bitcast.35), channel_id=1, source_target_pairs={{0,16},{2,18},{4,20},{6,22},{8,24},{10,26},{12,28},{14,30},{16,0},... | collective-permute-start | bytes 1179656 | tf_op jit(solution)/shard_map/ppermute | solution.py:333
  65.5 1.5 collective-permute-start.16
  67.0 4.4 %collective-permute-done.6.refs_4_ = bf16[64,3072]{1,0:T(8,128)(2,1)} collective-permute-done((bf16[64,3072]{1,0:T(8,128)(2,1)S(1)}, bf16[64,3072]{1,0:T(8,128)(2,1)}, u32[]{:S(2)}, u32[]{:S(2)}) %collective-permute-start.6) | collective-permute-done | bytes 393248 | tf_op jit(solution)/shard_map/ppermute | solution.py:343
  71.4 8.6 %collective-permute-done.8 = bf16[64,3072]{1,0:T(8,128)(2,1)S(1)} collective-permute-done((bf16[64,3072]{1,0:T(8,128)(2,1)S(1)}, bf16[64,3072]{1,0:T(8,128)(2,1)S(1)}, u32[]{:S(2)}, u32[]{:S(2)}) %collective-permute-start.8) | collective-permute-done | bytes 393248 | tf_op jit(solution)/shard_map/ppermute | solution.py:333
  80.0 1.5 collective-permute-start.20
  81.6 13.1 %collective-permute-done.29.refs_8_ = bf16[192,1024]{1,0:T(8,128)(2,1)S(1)} collective-permute-done((bf16[192,1024]{1,0:T(8,128)(2,1)S(1)}, bf16[192,1024]{1,0:T(8,128)(2,1)S(1)}, u32[]{:S(2)}, u32[]{:S(2)}) %collective-permute-start.29) | collective-permute-done | bytes 393248 | tf_op jit(solution)/shard_map/ppermute | solution.py:333
  94.7 1.5 collective-permute-start.9
  96.2 1.5 collective-permute-start.30
  98.3 7.2 %collective-permute-done.9.refs_6_ = bf16[64,3072]{1,0:T(8,128)(2,1)} collective-permute-done((bf16[64,3072]{1,0:T(8,128)(2,1)S(1)}, bf16[64,3072]{1,0:T(8,128)(2,1)}, u32[]{:S(2)}, u32[]{:S(2)}) %collective-permute-start.9) | collective-permute-done | bytes 393248 | tf_op jit(solution)/shard_map/ppermute | solution.py:343
  108.0 14.6 %shard_map.158 = (bf16[256,256]{1,0:T(8,128)(2,1)}, bf16[256,256]{1,0:T(8,128)(2,1)}, bf16[128,512]{1,0:T(8,128)(2,1)}, bf16[128,512]{1,0:T(8,128)(2,1)}, bf16[1...) custom-call(s32[28]{0:T(128)} %stack.136.where_ref, bf16[128,3072]{1,0:T(8,128)(2,1)} %copy-done.1, ...), custom_call_target="tpu_custom_call" | custom-call | flops 3758096384 | bytes 6815744 | tf_op jit(solution)/shard_map/pallas_call | solution.py:148
  123.0 2.8 %collective-permute-start.24 = (bf16[256,256]{1,0:T(8,128)(2,1)}, bf16[256,256]{1,0:T(8,128)(2,1)S(1)}, u32[]{:S(2)}, u32[]{:S(2)}) collective-permute-start(bf16[256,256]{1,0:T(8,128)(2,1)} %get-tuple-element.36), channel_id=1, source_target_pairs={{0,16},{2,18},{4,20},{6,22},{8,24},{10,26},{12,28},{14,30},{16,0},... | collective-permute-start | bytes 393224 | tf_op jit(solution)/shard_map/ppermute | solution.py:413
  127.7 3.4 %collective-permute-done.23.refs_1_ = bf16[256,256]{1,0:T(8,128)(2,1)S(1)} collective-permute-done((bf16[256,256]{1,0:T(8,128)(2,1)}, bf16[256,256]{1,0:T(8,128)(2,1)S(1)}, u32[]{:S(2)}, u32[]{:S(2)}) %collective-permute-start.23) | collective-permute-done | bytes 131104 | tf_op jit(solution)/shard_map/ppermute | solution.py:413
  131.1 5.0 %collective-permute-done.24.refs_2_ = bf16[256,256]{1,0:T(8,128)(2,1)S(1)} collective-permute-done((bf16[256,256]{1,0:T(8,128)(2,1)}, bf16[256,256]{1,0:T(8,128)(2,1)S(1)}, u32[]{:S(2)}, u32[]{:S(2)}) %collective-permute-start.24) | collective-permute-done | bytes 131104 | tf_op jit(solution)/shard_map/ppermute | solution.py:413
  137.4 5.6 %shard_map.159 = (f32[128,768]{1,0:T(8,128)}, bf16[128,768]{1,0:T(8,128)(2,1)}, bf16[128,768]{1,0:T(8,128)(2,1)}, bf16[128,768]{1,0:T(8,128)(2,1)}) custom-call(s32[12]{0:T(128)} %stack.117.where_ref, bf16[256,256]{1,0:T(8,128)(2,1)} %get-tuple-element.35.refs_0_, bf16[256,256]{1,0:T(8,128)(2,1)} %copy-done.9, bf16[256,256]{1,0:T(8,128)(2,1)} %copy-done.10, ...), custom_call_target="tpu_custom_call" | custom-call | flops 805306368 | bytes 3145728 | tf_op jit(solution)/shard_map/pallas_call | solution.py:273
  143.0 1.6 collective-permute-start.33
  144.6 2.0 %collective-permute-start.36 = (bf16[128,512]{1,0:T(8,128)(2,1)S(1)}, bf16[128,512]{1,0:T(8,128)(2,1)S(1)}, u32[]{:S(2)}, u32[]{:S(2)}) collective-permute-start(bf16[128,512]{1,0:T(8,128)(2,1)S(1)} %copy-done.27), channel_id=1, source_target_pairs={{0,8},{2,10},{4,12},{6,14},{8,0},{10,2},{12,4},{14,6},{16,24},{18,... | collective-permute-start | bytes 393224 | tf_op jit(solution)/shard_map/ppermute | solution.py:413
  147.7 1.5 collective-permute-start.38
  151.2 1.8 %collective-permute-start.34 = (bf16[128,768]{1,0:T(8,128)(2,1)}, bf16[128,768]{1,0:T(8,128)(2,1)S(1)}, u32[]{:S(2)}, u32[]{:S(2)}) collective-permute-start(bf16[128,768]{1,0:T(8,128)(2,1)} %get-tuple-element.40), channel_id=1, source_target_pairs={{0,8},{1,9},{2,10},{3,11},{4,12},{5,13},{6,14},{7,15},{8,0},{9,1},... | collective-permute-start | bytes 589832 | tf_op jit(solution)/shard_map/ppermute | solution.py:351
  153.0 5.3 %collective-permute-done.37.refs_2_ = bf16[128,512]{1,0:T(8,128)(2,1)S(1)} collective-permute-done((bf16[128,512]{1,0:T(8,128)(2,1)S(1)}, bf16[128,512]{1,0:T(8,128)(2,1)S(1)}, u32[]{:S(2)}, u32[]{:S(2)}) %collective-permute-start.37) | collective-permute-done | bytes 131104 | tf_op jit(solution)/shard_map/ppermute | solution.py:413
  159.8 1.9 %shard_map.160 = (bf16[128,1024]{1,0:T(8,128)(2,1)}, bf16[128,1024]{1,0:T(8,128)(2,1)}) custom-call(s32[1]{0:T(128)} %bitcast.member_ref, bf16[128,512]{1,0:T(8,128)(2,1)} %get-tuple-element.43.refs_0_, bf16[128,512]{1,0:T(8,128)(2,1)} %copy-done.12, bf16[128,512]{1,0:T(8,128)(2,1)} %copy-done.13, bf16[128,512]{1,0:T(8,128)(2,1)} %copy-done.14), custom_call_target="tpu_custom_call" | custom-call | tf_op jit(solution)/shard_map/pallas_call | solution.py:228
  (121 shorter events, 20.7 us)
Async XLA Ops:
  2.9 13.1 %collective-permute-start = (bf16[64,3072]{1,0:T(8,128)(2,1)S(1)}, bf16[64,3072]{1,0:T(8,128)(2,1)}, u32[]{:S(2)}, u32[]{:S(2)}) collective-permute-start(bf16[64,3072]{1,0:T(8,128)(2,1)S(1)} %constant_dynamic-slice_fusion), channel_id=1, source_target_pairs={{0,8},{2,10},{4,12},{6,14},{8,0},{10,2},{12,4},{14,6},{16,24},{18,... | collective-permute-start | bytes 1179656 | tf_op jit(solution)/shard_map/ppermute | solution.py:333
  8.8 17.0 %collective-permute-start.4 = (bf16[832,256]{1,0:T(8,128)(2,1)}, bf16[832,256]{1,0:T(8,128)(2,1)}, u32[]{:S(2)}, u32[]{:S(2)}) collective-permute-start(bf16[832,256]{1,0:T(8,128)(2,1)} %get-tuple-element.27), channel_id=1, source_target_pairs={{0,8},{2,10},{4,12},{6,14},{8,0},{10,2},{12,4},{14,6},{16,24},{18,... | collective-permute-start | bytes 1277960 | tf_op jit(solution)/shard_map/ppermute | solution.py:333
  16.1 11.2 %collective-permute-start.2 = (bf16[64,3072]{1,0:T(8,128)(2,1)}, bf16[64,3072]{1,0:T(8,128)(2,1)S(1)}, u32[]{:S(2)}, u32[]{:S(2)}) collective-permute-start(bf16[64,3072]{1,0:T(8,128)(2,1)} %collective-permute-done.refs_1_), channel_id=1, source_target_pairs={{8,16},{10,18},{12,20},{14,22},{16,8},{18,10},{20,12},{22,14},{9,1... | collective-permute-start | bytes 1179656 | tf_op jit(solution)/shard_map/ppermute | solution.py:333
  16.7 20.2 %collective-permute-start.10 = (bf16[832,256]{1,0:T(8,128)(2,1)}, bf16[832,256]{1,0:T(8,128)(2,1)}, u32[]{:S(2)}, u32[]{:S(2)}) collective-permute-start(bf16[832,256]{1,0:T(8,128)(2,1)} %get-tuple-element.32.refs_11_), channel_id=1, source_target_pairs={{0,4},{2,6},{4,0},{6,2},{8,12},{10,14},{12,8},{14,10},{16,20},{18,... | collective-permute-start | bytes 1277960 | tf_op jit(solution)/shard_map/ppermute | solution.py:340
  18.8 19.7 %collective-permute-start.11 = (bf16[832,256]{1,0:T(8,128)(2,1)}, bf16[832,256]{1,0:T(8,128)(2,1)S(1)}, u32[]{:S(2)}, u32[]{:S(2)}) collective-permute-start(bf16[832,256]{1,0:T(8,128)(2,1)} %get-tuple-element.32.refs_11_), channel_id=1, source_target_pairs={{0,2},{2,0},{4,6},{6,4},{8,10},{10,8},{12,14},{14,12},{16,18},{18,... | collective-permute-start | bytes 1277960 | tf_op jit(solution)/shard_map/ppermute | solution.py:340
  18.8 38.4 %collective-permute-start.7 = (bf16[832,256]{1,0:T(8,128)(2,1)}, bf16[832,256]{1,0:T(8,128)(2,1)}, u32[]{:S(2)}, u32[]{:S(2)}) collective-permute-start(bf16[832,256]{1,0:T(8,128)(2,1)} %get-tuple-element.30), channel_id=1, source_target_pairs={{0,16},{2,18},{4,20},{6,22},{8,24},{10,26},{12,28},{14,30},{16,0},... | collective-permute-start | bytes 1277960 | tf_op jit(solution)/shard_map/ppermute | solution.py:333
  27.3 29.9 %collective-permute-start.5 = (bf16[64,3072]{1,0:T(8,128)(2,1)S(1)}, bf16[64,3072]{1,0:T(8,128)(2,1)S(1)}, u32[]{:S(2)}, u32[]{:S(2)}) collective-permute-start(bf16[64,3072]{1,0:T(8,128)(2,1)S(1)} %collective-permute-done.3), channel_id=1, source_target_pairs={{8,0},{10,2},{12,4},{14,6},{16,24},{18,26},{20,28},{22,30},{9,1},{... | collective-permute-start | bytes 1179656 | tf_op jit(solution)/shard_map/ppermute | solution.py:333
  35.6 24.4 %collective-permute-start.1 = (bf16[64,3072]{1,0:T(8,128)(2,1)}, bf16[64,3072]{1,0:T(8,128)(2,1)S(1)}, u32[]{:S(2)}, u32[]{:S(2)}) collective-permute-start(bf16[64,3072]{1,0:T(8,128)(2,1)} %collective-permute-done.refs_1_), channel_id=1, source_target_pairs={{0,1},{1,0},{2,3},{3,2},{4,5},{5,4},{6,7},{7,6},{8,9},{9,8},{10,11... | collective-permute-start | bytes 1179656 | tf_op jit(solution)/shard_map/ppermute | solution.py:343
  37.0 26.1 %collective-permute-start.13 = (bf16[832,256]{1,0:T(8,128)(2,1)}, bf16[832,256]{1,0:T(8,128)(2,1)S(1)}, u32[]{:S(2)}, u32[]{:S(2)}) collective-permute-start(bf16[832,256]{1,0:T(8,128)(2,1)} %collective-permute-done.4.refs_15_), channel_id=1, source_target_pairs={{0,4},{2,6},{4,0},{6,2},{8,12},{10,14},{12,8},{14,10},{16,20},{18,... | collective-permute-start | bytes 1277960 | tf_op jit(solution)/shard_map/ppermute | solution.py:340
  38.5 27.0 %collective-permute-start.14 = (bf16[832,256]{1,0:T(8,128)(2,1)}, bf16[832,256]{1,0:T(8,128)(2,1)S(1)}, u32[]{:S(2)}, u32[]{:S(2)}) collective-permute-start(bf16[832,256]{1,0:T(8,128)(2,1)} %collective-permute-done.4.refs_15_), channel_id=1, source_target_pairs={{0,2},{2,0},{4,6},{6,4},{8,10},{10,8},{12,14},{14,12},{16,18},{18,... | collective-permute-start | bytes 1277960 | tf_op jit(solution)/shard_map/ppermute | solution.py:340
  57.2 22.8 %collective-permute-start.19 = (bf16[832,256]{1,0:T(8,128)(2,1)}, bf16[832,256]{1,0:T(8,128)(2,1)}, u32[]{:S(2)}, u32[]{:S(2)}) collective-permute-start(bf16[832,256]{1,0:T(8,128)(2,1)} %get-tuple-element.34), channel_id=1, source_target_pairs={{0,24},{2,26},{4,28},{6,30},{8,16},{10,18},{12,20},{14,22},{16,8},... | collective-permute-start | bytes 1277960 | tf_op jit(solution)/shard_map/ppermute | solution.py:333
  60.0 11.4 %collective-permute-start.6 = (bf16[64,3072]{1,0:T(8,128)(2,1)S(1)}, bf16[64,3072]{1,0:T(8,128)(2,1)}, u32[]{:S(2)}, u32[]{:S(2)}) collective-permute-start(bf16[64,3072]{1,0:T(8,128)(2,1)S(1)} %broadcast_select_fusion.1.refs_3_), channel_id=1, source_target_pairs={{0,1},{1,0},{2,3},{3,2},{4,5},{5,4},{6,7},{7,6},{8,9},{9,8},{10,11... | collective-permute-start | bytes 1179656 | tf_op jit(solution)/shard_map/ppermute | solution.py:343
  61.6 18.4 %collective-permute-start.8 = (bf16[64,3072]{1,0:T(8,128)(2,1)S(1)}, bf16[64,3072]{1,0:T(8,128)(2,1)S(1)}, u32[]{:S(2)}, u32[]{:S(2)}) collective-permute-start(bf16[64,3072]{1,0:T(8,128)(2,1)S(1)} %collective-permute-done.2), channel_id=1, source_target_pairs={{8,0},{10,2},{12,4},{14,6},{16,24},{18,26},{20,28},{22,30},{9,1},{... | collective-permute-start | bytes 1179656 | tf_op jit(solution)/shard_map/ppermute | solution.py:333
  63.1 31.6 %collective-permute-start.29 = (bf16[192,1024]{1,0:T(8,128)(2,1)S(1)}, bf16[192,1024]{1,0:T(8,128)(2,1)S(1)}, u32[]{:S(2)}, u32[]{:S(2)}) collective-permute-start(bf16[192,1024]{1,0:T(8,128)(2,1)S(1)} %bitcast.35), channel_id=1, source_target_pairs={{0,16},{2,18},{4,20},{6,22},{8,24},{10,26},{12,28},{14,30},{16,0},... | collective-permute-start | bytes 1179656 | tf_op jit(solution)/shard_map/ppermute | solution.py:333
  65.5 30.7 %collective-permute-start.16 = (bf16[832,256]{1,0:T(8,128)(2,1)}, bf16[832,256]{1,0:T(8,128)(2,1)}, u32[]{:S(2)}, u32[]{:S(2)}) collective-permute-start(bf16[832,256]{1,0:T(8,128)(2,1)} %collective-permute-done.7.refs_19_), channel_id=1, source_target_pairs={{0,4},{2,6},{4,0},{6,2},{8,12},{10,14},{12,8},{14,10},{16,20},{18,... | collective-permute-start | bytes 1277960 | tf_op jit(solution)/shard_map/ppermute | solution.py:340
  71.4 26.3 %collective-permute-start.17 = (bf16[832,256]{1,0:T(8,128)(2,1)}, bf16[832,256]{1,0:T(8,128)(2,1)S(1)}, u32[]{:S(2)}, u32[]{:S(2)}) collective-permute-start(bf16[832,256]{1,0:T(8,128)(2,1)} %collective-permute-done.7.refs_19_), channel_id=1, source_target_pairs={{0,2},{2,0},{4,6},{6,4},{8,10},{10,8},{12,14},{14,12},{16,18},{18,... | collective-permute-start | bytes 1277960 | tf_op jit(solution)/shard_map/ppermute | solution.py:340
  80.0 17.7 %collective-permute-start.15 = (bf16[832,256]{1,0:T(8,128)(2,1)S(1)}, bf16[832,256]{1,0:T(8,128)(2,1)S(1)}, u32[]{:S(2)}, u32[]{:S(2)}) collective-permute-start(bf16[832,256]{1,0:T(8,128)(2,1)S(1)} %collective-permute-done.13.refs_16_), channel_id=1, source_target_pairs={{0,2},{2,0},{4,6},{6,4},{8,10},{10,8},{12,14},{14,12},{16,18},{18,... | collective-permute-start | bytes 1277960 | tf_op jit(solution)/shard_map/ppermute | solution.py:340
  80.0 18.2 %collective-permute-start.20 = (bf16[832,256]{1,0:T(8,128)(2,1)}, bf16[832,256]{1,0:T(8,128)(2,1)}, u32[]{:S(2)}, u32[]{:S(2)}) collective-permute-start(bf16[832,256]{1,0:T(8,128)(2,1)} %collective-permute-done.19.refs_23_), channel_id=1, source_target_pairs={{0,4},{2,6},{4,0},{6,2},{8,12},{10,14},{12,8},{14,10},{16,20},{18,... | collective-permute-start | bytes 1277960 | tf_op jit(solution)/shard_map/ppermute | solution.py:340
  94.7 10.9 %collective-permute-start.9 = (bf16[64,3072]{1,0:T(8,128)(2,1)S(1)}, bf16[64,3072]{1,0:T(8,128)(2,1)}, u32[]{:S(2)}, u32[]{:S(2)}) collective-permute-start(bf16[64,3072]{1,0:T(8,128)(2,1)S(1)} %broadcast_select_fusion.refs_5_), channel_id=1, source_target_pairs={{0,1},{1,0},{2,3},{3,2},{4,5},{5,4},{6,7},{7,6},{8,9},{9,8},{10,11... | collective-permute-start | bytes 1179656 | tf_op jit(solution)/shard_map/ppermute | solution.py:343
  96.2 10.5 %collective-permute-start.30 = (bf16[192,1024]{1,0:T(8,128)(2,1)S(1)}, bf16[192,1024]{1,0:T(8,128)(2,1)S(1)}, u32[]{:S(2)}, u32[]{:S(2)}) collective-permute-start(bf16[192,1024]{1,0:T(8,128)(2,1)S(1)} %collective-permute-done.29.refs_8_), channel_id=1, source_target_pairs={{0,4},{2,6},{4,0},{6,2},{8,12},{10,14},{12,8},{14,10},{16,20},{18,... | collective-permute-start | bytes 1179656 | tf_op jit(solution)/shard_map/ppermute | solution.py:340
  97.7 10.2 %collective-permute-start.18 = (bf16[832,256]{1,0:T(8,128)(2,1)}, bf16[832,256]{1,0:T(8,128)(2,1)}, u32[]{:S(2)}, u32[]{:S(2)}) collective-permute-start(bf16[832,256]{1,0:T(8,128)(2,1)} %collective-permute-done.16.refs_20_), channel_id=1, source_target_pairs={{0,2},{2,0},{4,6},{6,4},{8,10},{10,8},{12,14},{14,12},{16,18},{18,... | collective-permute-start | bytes 1277960 | tf_op jit(solution)/shard_map/ppermute | solution.py:340
  105.5 17.5 %collective-permute-start.27 = (bf16[192,1024]{1,0:T(8,128)(2,1)S(1)}, bf16[192,1024]{1,0:T(8,128)(2,1)S(1)}, u32[]{:S(2)}, u32[]{:S(2)}) collective-permute-start(bf16[192,1024]{1,0:T(8,128)(2,1)S(1)} %bitcast.36), channel_id=1, source_target_pairs={{0,2},{2,0},{4,6},{6,4},{8,10},{10,8},{12,14},{14,12},{16,18},{18,... | collective-permute-start | bytes 1179656 | tf_op jit(solution)/shard_map/ppermute | solution.py:340
  106.7 19.1 %collective-permute-start.28 = (bf16[192,1024]{1,0:T(8,128)(2,1)S(1)}, bf16[192,1024]{1,0:T(8,128)(2,1)}, u32[]{:S(2)}, u32[]{:S(2)}) collective-permute-start(bf16[192,1024]{1,0:T(8,128)(2,1)S(1)} %collective-permute-done.26.refs_5_), channel_id=1, source_target_pairs={{0,2},{2,0},{4,6},{6,4},{8,10},{10,8},{12,14},{14,12},{16,18},{18,... | collective-permute-start | bytes 1179656 | tf_op jit(solution)/shard_map/ppermute | solution.py:340
  107.4 20.2 %collective-permute-start.31 = (bf16[192,1024]{1,0:T(8,128)(2,1)S(1)}, bf16[192,1024]{1,0:T(8,128)(2,1)}, u32[]{:S(2)}, u32[]{:S(2)}) collective-permute-start(bf16[192,1024]{1,0:T(8,128)(2,1)S(1)} %collective-permute-done.29.refs_8_), channel_id=1, source_target_pairs={{0,2},{2,0},{4,6},{6,4},{8,10},{10,8},{12,14},{14,12},{16,18},{18,... | collective-permute-start | bytes 1179656 | tf_op jit(solution)/shard_map/ppermute | solution.py:340
  107.9 19.8 %collective-permute-start.32 = (bf16[192,1024]{1,0:T(8,128)(2,1)S(1)}, bf16[192,1024]{1,0:T(8,128)(2,1)}, u32[]{:S(2)}, u32[]{:S(2)}) collective-permute-start(bf16[192,1024]{1,0:T(8,128)(2,1)S(1)} %collective-permute-done.30.refs_9_), channel_id=1, source_target_pairs={{0,2},{2,0},{4,6},{6,4},{8,10},{10,8},{12,14},{14,12},{16,18},{18,... | collective-permute-start | bytes 1179656 | tf_op jit(solution)/shard_map/ppermute | solution.py:340
  123.0 13.1 %collective-permute-start.24 = (bf16[256,256]{1,0:T(8,128)(2,1)}, bf16[256,256]{1,0:T(8,128)(2,1)S(1)}, u32[]{:S(2)}, u32[]{:S(2)}) collective-permute-start(bf16[256,256]{1,0:T(8,128)(2,1)} %get-tuple-element.36), channel_id=1, source_target_pairs={{0,16},{2,18},{4,20},{6,22},{8,24},{10,26},{12,28},{14,30},{16,0},... | collective-permute-start | bytes 393224 | tf_op jit(solution)/shard_map/ppermute | solution.py:413
  125.8 10.3 %collective-permute-start.25 = (bf16[256,256]{1,0:T(8,128)(2,1)}, bf16[256,256]{1,0:T(8,128)(2,1)S(1)}, u32[]{:S(2)}, u32[]{:S(2)}) collective-permute-start(bf16[256,256]{1,0:T(8,128)(2,1)} %get-tuple-element.36), channel_id=1, source_target_pairs={{0,24},{2,26},{4,28},{6,30},{8,16},{10,18},{12,20},{14,22},{16,8},... | collective-permute-start | bytes 393224 | tf_op jit(solution)/shard_map/ppermute | solution.py:413
  143.0 18.7 %collective-permute-start.33 = (bf16[128,768]{1,0:T(8,128)(2,1)}, bf16[128,768]{1,0:T(8,128)(2,1)S(1)}, u32[]{:S(2)}, u32[]{:S(2)}) collective-permute-start(bf16[128,768]{1,0:T(8,128)(2,1)} %get-tuple-element.39), channel_id=1, source_target_pairs={{0,1},{1,0},{2,3},{3,2},{4,5},{5,4},{6,7},{7,6},{8,9},{9,8},{10,11... | collective-permute-start | bytes 589832 | tf_op jit(solution)/shard_map/ppermute | solution.py:343
  146.6 11.7 %collective-permute-start.37 = (bf16[128,512]{1,0:T(8,128)(2,1)S(1)}, bf16[128,512]{1,0:T(8,128)(2,1)S(1)}, u32[]{:S(2)}, u32[]{:S(2)}) collective-permute-start(bf16[128,512]{1,0:T(8,128)(2,1)S(1)} %copy-done.26), channel_id=1, source_target_pairs={{0,16},{2,18},{4,20},{6,22},{8,24},{10,26},{12,28},{14,30},{16,0},... | collective-permute-start | bytes 393224 | tf_op jit(solution)/shard_map/ppermute | solution.py:413
  147.7 11.4 %collective-permute-start.38 = (bf16[128,512]{1,0:T(8,128)(2,1)S(1)}, bf16[128,512]{1,0:T(8,128)(2,1)S(1)}, u32[]{:S(2)}, u32[]{:S(2)}) collective-permute-start(bf16[128,512]{1,0:T(8,128)(2,1)S(1)} %copy-done.25), channel_id=1, source_target_pairs={{0,24},{2,26},{4,28},{6,30},{8,16},{10,18},{12,20},{14,22},{16,8},... | collective-permute-start | bytes 393224 | tf_op jit(solution)/shard_map/ppermute | solution.py:413
  149.3 13.5 %collective-permute-start.35 = (bf16[128,768]{1,0:T(8,128)(2,1)}, bf16[128,768]{1,0:T(8,128)(2,1)S(1)}, u32[]{:S(2)}, u32[]{:S(2)}) collective-permute-start(bf16[128,768]{1,0:T(8,128)(2,1)} %get-tuple-element.41), channel_id=1, source_target_pairs={{0,9},{1,8},{2,11},{3,10},{4,13},{5,12},{6,15},{7,14},{8,1},{9,0},... | collective-permute-start | bytes 589832 | tf_op jit(solution)/shard_map/ppermute | solution.py:351
  151.2 12.4 %collective-permute-start.34 = (bf16[128,768]{1,0:T(8,128)(2,1)}, bf16[128,768]{1,0:T(8,128)(2,1)S(1)}, u32[]{:S(2)}, u32[]{:S(2)}) collective-permute-start(bf16[128,768]{1,0:T(8,128)(2,1)} %get-tuple-element.40), channel_id=1, source_target_pairs={{0,8},{1,9},{2,10},{3,11},{4,12},{5,13},{6,14},{7,15},{8,0},{9,1},... | collective-permute-start | bytes 589832 | tf_op jit(solution)/shard_map/ppermute | solution.py:351
  (35 other events, 561.4 us)

commit v3 on v2

--- a/solution.py
+++ b/solution.py
@@ -28,41 +28,37 @@
     return lax.dot_general(a, b, (((1,), (1,)), ((), ())), preferred_element_type=jnp.float32)
 
 
-def patch_kernel(depth, head_size, n_pieces, counts, where_ref, *refs):
+def norm_heads(x, gain):
+    power = jnp.mean(x * x, axis=-1, keepdims=True)
+    return (x * lax.rsqrt(power + 1e-06) * gain).astype(jnp.bfloat16)
+
+
+def rows_kernel(depth, head_size, n_pieces, counts, where_ref, *refs):
     n_shares, n_patches = sum(counts), len(counts)
     shares, refs = refs[:n_shares], refs[n_shares:]
-    tk_ref, tv_ref, qg_ref, kg_ref = refs[:4]
-    pieces, refs = refs[4 : 4 + n_pieces], refs[4 + n_pieces :]
-    att_refs, refs = refs[: n_patches // 2], refs[n_patches // 2 :]
-    kv_refs, (held, scores, expos, sems) = refs[:n_patches], refs[n_patches:]
+    qg_ref, kg_ref = refs[:2]
+    pieces, refs = refs[2 : 2 + n_pieces], refs[2 + n_pieces :]
+    q_refs, kv_refs, (held, sems) = refs[: n_patches // 2], refs[n_patches // 2 : -2], refs[-2:]
     rows, width = kv_refs[0].shape[0], kv_refs[0].shape[1] // 2
-    groups = [slice(g * rows, (g + 1) * rows) for g in range(n_patches)]
-    owns, firsts, at = [], [], 1 + n_pieces
-    for count in counts:
-        owns.append(where_ref[at])
-        firsts.append([where_ref[at + 1 + i] for i in range(count)])
-        at += 1 + count
     copies = [
-        pltpu.make_async_copy(piece, held.at[where_ref[1 + i]], sems.at[i])
+        pltpu.make_async_copy(
+            piece.at[pl.ds(0, 3 * depth)], held.at[where_ref[i]], sems.at[i]
+        )
         for i, piece in enumerate(pieces)
     ]
     for copy in copies:
         copy.start()
 
     def put(ref_of, cols, value):
-        for g, group in enumerate(groups):
+        at = 0
+        for g, count in enumerate(counts):
+            share = rows // count
             ref, base = ref_of(g)
-            share = rows // counts[g]
-            for i, first in enumerate(firsts[g]):
-                start = group.start + i * share
-                to = pl.ds(pl.multiple_of(base + first, 16), share)
-                ref[to, cols] = value[start : start + share]
-
-    def kv_of(g):
-        return kv_refs[g], 0
-
-    def att_of(g):
-        return att_refs[g // 2], lax.rem(owns[g] // INNER, 2) * rows
+            for i in range(count):
+                first = pl.multiple_of(base + where_ref[n_pieces + at], 16)
+                start = g * rows + i * share
+                ref[pl.ds(first, share), cols] = value[start : start + share]
+                at += 1
 
     def rows_of(cols):
         return jnp.concatenate([x[:, cols] for x in shares], axis=0)
@@ -73,9 +69,8 @@
         for first in range(0, n_pieces, INNER):
             for copy in copies[first : first + INNER]:
                 copy.wait()
-            place = where_ref[1 + first] // INNER
-            cols = pl.ds(pl.multiple_of(place * chunk, 128), chunk)
-            part = rows_of(cols)
+            place = where_ref[first] // INNER
+            part = rows_of(pl.ds(pl.multiple_of(place * chunk, 128), chunk))
             for i in range(3):
                 weight = held[pl.ds(place * INNER, INNER), i * depth : (i + 1) * depth, :]
                 proj[i] += jnp.dot(
@@ -91,27 +86,77 @@
                 part, weight.reshape(n_pieces * depth, width), preferred_element_type=jnp.float32
             )
     q_proj, k_proj, v_proj = proj
-
-    def norm(x, gain):
-        power = jnp.mean(x * x, axis=-1, keepdims=True)
-        return (x * lax.rsqrt(power + 1e-06) * gain).astype(jnp.bfloat16)
-
-    v_new = v_proj.astype(jnp.bfloat16)
-    put(kv_of, slice(width, 2 * width), v_new)
-    k0, v0 = 3 * depth, 3 * depth + rows
-    scale = math.log2(math.e) / math.sqrt(head_size)
+    put(lambda g: (kv_refs[g], 0), slice(width, 2 * width), v_proj.astype(jnp.bfloat16))
     for h in range(width // head_size):
         cols = slice(h * head_size, (h + 1) * head_size)
-        key = norm(k_proj[:, cols], kg_ref[...])
-        put(kv_of, cols, key)
-        query = norm(q_proj[:, cols], qg_ref[...])
-        value = v_new[:, cols]
-        keys = held[:, k0 : k0 + rows, cols].reshape(n_pieces * rows, head_size)
-        values = held[:, v0 : v0 + rows, cols].reshape(n_pieces * rows, head_size)
+        put(lambda g: (kv_refs[g], 0), cols, norm_heads(k_proj[:, cols], kg_ref[...]))
+        put(
+            lambda g: (q_refs[g // 2], g % 2 * rows),
+            cols,
+            norm_heads(q_proj[:, cols], qg_ref[...]),
+        )
+
+
+def project_rows(where, patches, query_gain, key_gain, pieces, depth, width):
+    shares = [x for patch in patches for x in patch]
+    model_width = shares[0].shape[1]
+    rows = sum(x.shape[0] for x in patches[0])
+    n, n_pieces, head_size = len(patches), len(pieces), query_gain.shape[0]
+    whole = lambda i, w: (0, 0)
+    outs = [(2 * rows, width)] * (n // 2) + [(rows, 2 * width)] * n
+    out = pl.pallas_call(
+        functools.partial(rows_kernel, depth, head_size, n_pieces, [len(x) for x in patches]),
+        grid_spec=pltpu.PrefetchScalarGridSpec(
+            num_scalar_prefetch=1,
+            grid=(1,),
+            in_specs=[pl.BlockSpec(x.shape, whole) for x in shares]
+            + [pl.BlockSpec((1, head_size), whole)] * 2
+            + [pl.BlockSpec(memory_space=pl.ANY)] * n_pieces,
+            out_specs=[pl.BlockSpec(x, whole) for x in outs],
+            scratch_shapes=[
+                pltpu.VMEM((n_pieces, 3 * depth, width), jnp.bfloat16),
+                pltpu.SemaphoreType.DMA((n_pieces,)),
+            ],
+        ),
+        out_shape=[jax.ShapeDtypeStruct(x, jnp.bfloat16) for x in outs],
+        compiler_params=pltpu.CompilerParams(vmem_limit_bytes=VMEM_BYTES),
+        cost_estimate=pl.CostEstimate(
+            flops=2 * n * rows * model_width * 3 * width,
+            bytes_accessed=6 * n_pieces * depth * width,
+            transcendentals=0,
+        ),
+    )(where, *shares, query_gain.reshape(1, -1), key_gain.reshape(1, -1), *pieces)
+    return out[: n // 2], out[n // 2 :]
+
+
+def attend_kernel(depth, head_size, n_pieces, n_patches, where_ref, *refs):
+    q_refs, refs = refs[: n_patches // 2], refs[n_patches // 2 :]
+    kv_refs, refs = refs[:n_patches], refs[n_patches:]
+    tk_ref, tv_ref, pieces, refs = refs[0], refs[1], refs[2 : 2 + n_pieces], refs[2 + n_pieces :]
+    att_refs, (held, scores, expos, sems) = refs[:n_patches], refs[n_patches:]
+    rows, width = kv_refs[0].shape[0], kv_refs[0].shape[1] // 2
+    groups = [slice(g * rows, (g + 1) * rows) for g in range(n_patches)]
+    owns = [where_ref[1 + n_pieces + g] for g in range(n_patches)]
+    copies = [
+        pltpu.make_async_copy(
+            piece.at[pl.ds(3 * depth, 2 * rows)], held.at[where_ref[1 + i]], sems.at[i]
+        )
+        for i, piece in enumerate(pieces)
+    ]
+    for copy in copies:
+        copy.start()
+    scale = math.log2(math.e) / math.sqrt(head_size)
+    own_cols = [pl.ds(pl.multiple_of(own * rows, 128), rows) for own in owns]
+    for copy in copies:
+        copy.wait()
+    for h in range(width // head_size):
+        cols = slice(h * head_size, (h + 1) * head_size)
+        query = jnp.concatenate([x[:, cols] for x in q_refs], axis=0)
+        keys = held[:, :rows, cols].reshape(n_pieces * rows, head_size)
+        values = held[:, rows:, cols].reshape(n_pieces * rows, head_size)
         scores[...] = nt_dot(query, keys)
-        own_cols = [pl.ds(pl.multiple_of(own * rows, 128), rows) for own in owns]
         for g, group in enumerate(groups):
-            scores[group, own_cols[g]] = nt_dot(query[group], key[group])
+            scores[group, own_cols[g]] = nt_dot(query[group], kv_refs[g][:, cols])
         text_s = nt_dot(query, tk_ref[:, cols])
         image_s = scores[...]
         largest = jnp.maximum(
@@ -123,8 +168,9 @@
         expos[...] = image_e.astype(jnp.bfloat16)
         fresh_mix = []
         for g, group in enumerate(groups):
+            value = kv_refs[g][:, width + cols.start : width + cols.stop]
             fresh_mix.append(
-                jnp.dot(expos[group, own_cols[g]], value[group], preferred_element_type=jnp.float32)
+                jnp.dot(expos[group, own_cols[g]], value, preferred_element_type=jnp.float32)
             )
             expos[group, own_cols[g]] = jnp.zeros((rows, rows), jnp.bfloat16)
         mixture = (
@@ -132,57 +178,42 @@
             + jnp.dot(expos[...], values, preferred_element_type=jnp.float32)
             + jnp.concatenate(fresh_mix, axis=0)
         )
-        put(att_of, cols, (mixture / total).astype(jnp.bfloat16))
-
-
-def attend_patches(where, patches, text_keys, text_values, query_gain, key_gain, pieces, depth, width):
-    shares = [x for patch in patches for x in patch]
-    model_width = shares[0].shape[1]
-    rows = sum(x.shape[0] for x in patches[0])
-    n = len(patches)
-    head_size = query_gain.shape[0]
-    texts = text_keys.shape[0]
-    n_pieces = len(pieces)
+        attended = (mixture / total).astype(jnp.bfloat16)
+        for g, group in enumerate(groups):
+            first = pl.multiple_of(lax.rem(owns[g] // INNER, 2) * rows, 16)
+            for att_ref in att_refs[g // 2 * 2 : g // 2 * 2 + 2]:
+                att_ref[pl.ds(first, rows), cols] = attended[group]
+
+
+def attend_rows(where, queries, kv, text_keys, text_values, pieces, depth, head_size):
+    pair_rows, width = queries[0].shape
+    rows, texts, n_pieces, n = pair_rows // 2, text_keys.shape[0], len(pieces), len(kv)
     whole = lambda i, w: (0, 0)
-    outs = [(2 * rows, width)] * (n // 2) + [(rows, 2 * width)] * n
-    out = pl.pallas_call(
-        functools.partial(patch_kernel, depth, head_size, n_pieces, [len(x) for x in patches]),
+    return pl.pallas_call(
+        functools.partial(attend_kernel, depth, head_size, n_pieces, n),
         grid_spec=pltpu.PrefetchScalarGridSpec(
             num_scalar_prefetch=1,
             grid=(1,),
-            in_specs=[pl.BlockSpec(x.shape, whole) for x in shares]
-            + [
-                pl.BlockSpec((texts, width), lambda i, w: (0, w[0])),
-                pl.BlockSpec((texts, width), lambda i, w: (0, w[0])),
-                pl.BlockSpec((1, head_size), whole),
-                pl.BlockSpec((1, head_size), whole),
-            ]
+            in_specs=[pl.BlockSpec((pair_rows, width), whole)] * (n // 2)
+            + [pl.BlockSpec((rows, 2 * width), whole)] * n
+            + [pl.BlockSpec((texts, width), lambda i, w: (0, w[0]))] * 2
             + [pl.BlockSpec(memory_space=pl.ANY)] * n_pieces,
-            out_specs=[pl.BlockSpec(x, whole) for x in outs],
+            out_specs=[pl.BlockSpec((pair_rows, width), whole)] * n,
             scratch_shapes=[
-                pltpu.VMEM((n_pieces,) + pieces[0].shape, jnp.bfloat16),
+                pltpu.VMEM((n_pieces, 2 * rows, width), jnp.bfloat16),
                 pltpu.VMEM((n * rows, n_pieces * rows), jnp.float32),
                 pltpu.VMEM((n * rows, n_pieces * rows), jnp.bfloat16),
                 pltpu.SemaphoreType.DMA((n_pieces,)),
             ],
         ),
-        out_shape=[jax.ShapeDtypeStruct(x, jnp.bfloat16) for x in outs],
+        out_shape=[jax.ShapeDtypeStruct((pair_rows, width), jnp.bfloat16)] * n,
         compiler_params=pltpu.CompilerParams(vmem_limit_bytes=VMEM_BYTES),
         cost_estimate=pl.CostEstimate(
-            flops=2 * n * rows * (model_width * 3 * width + 2 * (texts + n_pieces * rows) * width),
-            bytes_accessed=2 * n_pieces * pieces[0].size,
+            flops=4 * n * rows * (texts + n_pieces * rows) * width,
+            bytes_accessed=4 * n_pieces * rows * width,
             transcendentals=n * rows * (texts + n_pieces * rows) * (width // head_size),
         ),
-    )(
-        where,
-        *shares,
-        text_keys,
-        text_values,
-        query_gain.reshape(1, -1),
-        key_gain.reshape(1, -1),
-        *pieces,
-    )
-    return out[: n // 2], out[n // 2 :]
+    )(where, *queries, *kv, text_keys, text_values, *pieces)
 
 
 def deal_kernel(n_arrays, team, member_ref, *refs):
@@ -323,15 +354,9 @@
     mine = lax.axis_index("fsdp")
     place, seat = me // INNER, me % INNER
     member, parity = place % team, place % 2
-    chain = []
-
     def over_outer(x, pairs):
-        if len(chain) >= 3:
-            x = after(x, chain[-3])
-        seats = range(INNER)
-        pairs = [(a * INNER + k, b * INNER + k) for a, b in pairs for k in seats]
-        chain.append(lax.ppermute(x, "patch", pairs))
-        return chain[-1]
+        pairs = [(a * INNER + k, b * INNER + k) for a, b in pairs for k in range(INNER)]
+        return lax.ppermute(x, "patch", pairs)
 
     def to_partner(x, bits):
         return over_outer(x, [(z, z ^ bits) for z in range(outer)])
@@ -369,12 +394,12 @@
         inside = jnp.logical_or(place == 1, place == 2)
         near = to_partner(part, 1)
         across = over_outer(part, middle)
-        pieces[1] = to_partner(dealt[1], 1)
         far = over_outer(near, middle)
-        pieces[2] = to_partner(dealt[2], 2)
+        pieces[2] = to_partner(after(dealt[2], near), 2)
+        pieces[1] = to_partner(after(dealt[1], near), 1)
         end_across = over_outer(across, ends)
-        pieces[3] = to_partner(dealt[3], 3)
         end_far = over_outer(far, ends)
+        pieces[3] = to_partner(after(dealt[3], far), 3)
         row_shares[1] = near
         row_shares[2] = jnp.where(inside, far, end_across)
         row_shares[3] = jnp.where(inside, across, end_far)
@@ -383,38 +408,48 @@
             row_shares[k] = to_partner(part, k)
         for k in range(1, outer):
             pieces[k] = to_partner(dealt[k % team], k)
-    out_pieces = [w_out.T] + [to_partner(w_out.T, 2 * k) for k in range(1, fsdp)]
+    out_piece = after(w_out.T, pieces[outer - 1])
+    out_pieces = [out_piece] + [to_partner(out_piece, 2 * k) for k in range(1, fsdp)]
 
     pieces = [x for k in range(outer) for x in spread(pieces[k])]
     origins = [o for k in range(outer) for o in seats_of(place ^ k)]
     patch_rows = [[modded]]
+    firsts = [0 * mine]
     for k in range(1, team):
         got = row_shares[k]
         patch_rows.append([got] + [along_fsdp(got, i) for i in range(1, fsdp)])
-    out_pieces = [x for piece in out_pieces for x in spread(piece)]
-    out_places = [o for k in range(fsdp) for o in seats_of((place ^ (2 * k)) // 2)]
-
-    where = [member] + origins
-    for k in range(team):
-        where.append((place ^ k) * INNER + seat)
-        where += [((mine + (fsdp - i)) % fsdp) * share for i in range(fsdp)] if k else [0 * mine]
-    att, kv = attend_patches(
-        jnp.stack(where).astype(jnp.int32),
+        firsts += [((mine + (fsdp - i)) % fsdp) * share for i in range(fsdp)]
+    queries, kv = project_rows(
+        jnp.stack(origins + firsts).astype(jnp.int32),
         patch_rows,
-        text_keys,
-        text_values,
         query_gain,
         key_gain,
         pieces,
         depth,
         width,
     )
+    out_pieces = [x for piece in out_pieces for x in spread(after(piece, queries[0]))]
+    out_places = [o for k in range(fsdp) for o in seats_of((place ^ (2 * k)) // 2)]
+
     def give(x, bits):
         return lax.ppermute(x, "patch", [(p, p ^ (bits * INNER)) for p in range(patches)])
 
-    packs = [att[0]] + [give(att[k // 2], k) for k in range(1, team)]
+    fresh = [kv[0]] + [give(kv[k], k) for k in range(1, team)]
+    where = [member] + origins + [(place ^ k) * INNER + seat for k in range(team)]
+    att = attend_rows(
+        jnp.stack(where).astype(jnp.int32),
+        queries,
+        kv,
+        text_keys,
+        text_values,
+        pieces,
+        depth,
+        head_size,
+    )
+    packs = [att[0]] + [give(att[k], k) for k in range(1, team)]
     where = [member, parity] + [(mine + i) % fsdp for i in range(fsdp)] + out_places
-    partial = project(jnp.stack(where).astype(jnp.int32), packs, out_pieces, fsdp)
+    where = after(jnp.stack(where).astype(jnp.int32), *fresh)
+    partial = project(where, packs, out_pieces, fsdp)
     own, partner = partial[0], [along_both(partial[1], 1, 0)]
     for i in range(1, fsdp):
         own = own + along_fsdp(partial[2 * i], i).astype(jnp.float32)
@@ -425,7 +460,6 @@
         jnp.concatenate([own, other], axis=1),
         jnp.concatenate([other, own], axis=1),
     )
-    fresh = [kv[0]] + [give(kv[k], k) for k in range(1, team)]
     key_out, value_out = collect(member, [after(fresh[0], partial[0])] + fresh[1:])
 
     out_share = model_width // fsdp

time: 165 us -> 164 us (level)
  waiting for transfers between devices: 82.9 us -> 69.5 us
  starting transfers between devices: 48.1 us -> 53 us
  Pallas kernels: 24.9 us -> 29.7 us
  local copies, waits for them, and re-layouts: 3.38 us -> 5.11 us
    ppermute x9, waiting for transfers between devices: 46.7 us -> 34.5 us  [over_outer(): return lax.ppermute(x, 'patch', pairs)]
    ppermute x4, waiting for transfers between devices: 11.6 us -> 1.91 us  [along_fsdp(): lax.ppermute(x, 'fsdp', [(i, (i + step) % fsdp) for i in range(fsdp)])]
    ppermute x18, waiting for transfers between devices: 8.18 us -> 16.6 us  [flip(): return lax.ppermute(x, 'patch', [(p, p ^ bits) for p in range(patches)])]
    ppermute x9, starting transfers between devices: 19.6 us -> 26.8 us  [over_outer(): return lax.ppermute(x, 'patch', pairs)]
    pallas_call x1 -> x2, Pallas kernels: 14.6 us -> 19.2 us  [the longest x1 10.7 us: attend_rows(): pl.pallas_call(functools.partial(attend_kernel, depth, head_size, n_piece...]
  transfers between devices with their start and end apart: 39 -> 39, of which waited for: 14 -> 16; matrix products, arithmetic and copies ran while one was open for 1% -> 3% of each run, Pallas kernels for 12% -> 15%
where the time goes in v3:
time: 164 us
  waiting for transfers between devices  69.5 us (42%)
  starting transfers between devices  53 us (32%)
  Pallas kernels  29.7 us (18%)
  other arithmetic  5.21 us (3%)
  local copies, waits for them, and re-layouts  5.11 us (3%)
    ppermute x9, waiting for transfers between devices, over_outer(): return lax.ppermute(x, 'patch', pairs)  34.5 us
    ppermute x9, starting transfers between devices, over_outer(): return lax.ppermute(x, 'patch', pairs)  26.8 us
    ppermute x18, waiting for transfers between devices, flip(): return lax.ppermute(x, 'patch', [(p, p ^ bits) for p in range(patches)])  16.6 us
    ppermute x6, waiting for transfers between devices, give(): lax.ppermute(x, 'patch', [(p, p ^ bits * INNER) for p in range(patches)])  15.2 us
    pallas_call x1, Pallas kernels, attend_rows(): pl.pallas_call(functools.partial(attend_kernel, depth, head_size, n_piece...  10.7 us
    ppermute x18, starting transfers between devices, flip(): return lax.ppermute(x, 'patch', [(p, p ^ bits) for p in range(patches)])  9.95 us
    pallas_call x1, Pallas kernels, project_rows(): pl.pallas_call(functools.partial(rows_kernel, depth, head_size, n_pieces,...  8.45 us
    ppermute x6, starting transfers between devices, give(): lax.ppermute(x, 'patch', [(p, p ^ bits * INNER) for p in range(patches)])  8.27 us
  transfers between devices with their start and end apart: 39, of which 16 were waited for; matrix products, arithmetic and copies ran while one was open for 3% of the time, Pallas kernels for 15%

profile of v3, /device:TPU:0, one launch (start us, length us, event | category | flops | bytes accessed | tf_op | source)
XLA Modules:
  0.0 163.7 jit_solution(11360071233122722716)
XLA Ops:
  2.9 3.1 %collective-permute-start = (bf16[64,3072]{1,0:T(8,128)(2,1)S(1)}, bf16[64,3072]{1,0:T(8,128)(2,1)}, u32[]{:S(2)}, u32[]{:S(2)}) collective-permute-start(bf16[64,3072]{1,0:T(8,128)(2,1)S(1)} %constant_dynamic-slice_fusion), channel_id=1, source_target_pairs={{0,8},{2,10},{4,12},{6,14},{8,0},{10,2},{12,4},{14,6},{16,24},{18,... | collective-permute-start | bytes 1179656 | tf_op jit(solution)/shard_map/ppermute | solution.py:359
  6.7 2.8 %shard_map.157 = (bf16[832,256]{1,0:T(8,128)(2,1)}, bf16[832,256]{1,0:T(8,128)(2,1)}, bf16[832,256]{1,0:T(8,128)(2,1)}, bf16[832,256]{1,0:T(8,128)(2,1)}) custom-call(s32[1]{0:T(128)} %bitcast.member_ref, bf16[192,1024]{1,0:T(8,128)(2,1)} %refs_0_.1, bf16[192,1024]{1,0:T(8,128)(2,1)} %refs_1_.1, bf16[192,1024]{1,0:T(8,128)(2,1)} %refs_2_.1, ...), custom_call_target="tpu_custom_call" | custom-call | tf_op jit(solution)/shard_map/pallas_call | solution.py:235
  9.5 1.5 collective-permute-start.8
  11.0 4.2 %collective-permute-done.refs_1_ = bf16[64,3072]{1,0:T(8,128)(2,1)} collective-permute-done((bf16[64,3072]{1,0:T(8,128)(2,1)S(1)}, bf16[64,3072]{1,0:T(8,128)(2,1)}, u32[]{:S(2)}, u32[]{:S(2)}) %collective-permute-start) | collective-permute-done | bytes 393248 | tf_op jit(solution)/shard_map/ppermute | solution.py:359
  17.9 4.6 %collective-permute-start.11 = (bf16[832,256]{1,0:T(8,128)(2,1)}, bf16[832,256]{1,0:T(8,128)(2,1)S(1)}, u32[]{:S(2)}, u32[]{:S(2)}) collective-permute-start(bf16[832,256]{1,0:T(8,128)(2,1)} %get-tuple-element.33), channel_id=1, source_target_pairs={{0,8},{2,10},{4,12},{6,14},{8,0},{10,2},{12,4},{14,6},{16,24},{18,... | collective-permute-start | bytes 1277960 | tf_op jit(solution)/shard_map/ppermute | solution.py:359
  22.5 7.9 %collective-permute-start.15 = (bf16[832,256]{1,0:T(8,128)(2,1)}, bf16[832,256]{1,0:T(8,128)(2,1)S(1)}, u32[]{:S(2)}, u32[]{:S(2)}) collective-permute-start(bf16[832,256]{1,0:T(8,128)(2,1)} %get-tuple-element.35), channel_id=1, source_target_pairs={{0,16},{2,18},{4,20},{6,22},{8,24},{10,26},{12,28},{14,30},{16,0},... | collective-permute-start | bytes 1277960 | tf_op jit(solution)/shard_map/ppermute | solution.py:359
  31.9 4.4 %collective-permute-done.4 = bf16[64,3072]{1,0:T(8,128)(2,1)} collective-permute-done((bf16[64,3072]{1,0:T(8,128)(2,1)S(1)}, bf16[64,3072]{1,0:T(8,128)(2,1)}, u32[]{:S(2)}, u32[]{:S(2)}) %collective-permute-start.4) | collective-permute-done | bytes 393248 | tf_op jit(solution)/shard_map/ppermute | solution.py:359
  36.3 2.1 %collective-permute-start.19 = (bf16[832,256]{1,0:T(8,128)(2,1)}, bf16[832,256]{1,0:T(8,128)(2,1)S(1)}, u32[]{:S(2)}, u32[]{:S(2)}) collective-permute-start(bf16[832,256]{1,0:T(8,128)(2,1)} %get-tuple-element.37), channel_id=1, source_target_pairs={{0,24},{2,26},{4,28},{6,30},{8,16},{10,18},{12,20},{14,22},{16,8},... | collective-permute-start | bytes 1277960 | tf_op jit(solution)/shard_map/ppermute | solution.py:359
  41.3 14.1 %collective-permute-done.11.refs_13_.refs_12_ = bf16[832,256]{1,0:T(8,128)(2,1)S(1)} collective-permute-done((bf16[832,256]{1,0:T(8,128)(2,1)}, bf16[832,256]{1,0:T(8,128)(2,1)S(1)}, u32[]{:S(2)}, u32[]{:S(2)}) %collective-permute-start.11) | collective-permute-done | bytes 426016 | tf_op jit(solution)/shard_map/ppermute | solution.py:359
  56.9 2.4 %collective-permute-done.15.refs_17_.refs_16_ = bf16[832,256]{1,0:T(8,128)(2,1)S(1)} collective-permute-done((bf16[832,256]{1,0:T(8,128)(2,1)}, bf16[832,256]{1,0:T(8,128)(2,1)S(1)}, u32[]{:S(2)}, u32[]{:S(2)}) %collective-permute-start.15) | collective-permute-done | bytes 426016 | tf_op jit(solution)/shard_map/ppermute | solution.py:359
  59.2 1.5 collective-permute-start.12
  61.7 3.9 %collective-permute-done.6 = bf16[64,3072]{1,0:T(8,128)(2,1)S(1)} collective-permute-done((bf16[64,3072]{1,0:T(8,128)(2,1)}, bf16[64,3072]{1,0:T(8,128)(2,1)S(1)}, u32[]{:S(2)}, u32[]{:S(2)}) %collective-permute-start.6) | collective-permute-done | bytes 393248 | tf_op jit(solution)/shard_map/ppermute | solution.py:359
  65.5 1.6 collective-permute-start.20
  67.2 3.7 %collective-permute-done.12.refs_14_.refs_13_ = bf16[832,256]{1,0:T(8,128)(2,1)} collective-permute-done((bf16[832,256]{1,0:T(8,128)(2,1)S(1)}, bf16[832,256]{1,0:T(8,128)(2,1)}, u32[]{:S(2)}, u32[]{:S(2)}) %collective-permute-start.12) | collective-permute-done | bytes 426016 | tf_op jit(solution)/shard_map/ppermute | solution.py:365
  72.4 7.6 %collective-permute-done.16.refs_18_.refs_17_ = bf16[832,256]{1,0:T(8,128)(2,1)} collective-permute-done((bf16[832,256]{1,0:T(8,128)(2,1)S(1)}, bf16[832,256]{1,0:T(8,128)(2,1)}, u32[]{:S(2)}, u32[]{:S(2)}) %collective-permute-start.16) | collective-permute-done | bytes 426016 | tf_op jit(solution)/shard_map/ppermute | solution.py:365
  80.5 5.2 %collective-permute-done.20.refs_22_.refs_21_ = bf16[832,256]{1,0:T(8,128)(2,1)} collective-permute-done((bf16[832,256]{1,0:T(8,128)(2,1)S(1)}, bf16[832,256]{1,0:T(8,128)(2,1)}, u32[]{:S(2)}, u32[]{:S(2)}) %collective-permute-start.20) | collective-permute-done | bytes 426016 | tf_op jit(solution)/shard_map/ppermute | solution.py:365
  86.5 4.3 %collective-permute-start.32 = (bf16[192,1024]{1,0:T(8,128)(2,1)}, bf16[192,1024]{1,0:T(8,128)(2,1)}, u32[]{:S(2)}, u32[]{:S(2)}) collective-permute-start(bf16[192,1024]{1,0:T(8,128)(2,1)} %bitcast.32.refs_4_), channel_id=1, source_target_pairs={{0,16},{2,18},{4,20},{6,22},{8,24},{10,26},{12,28},{14,30},{16,0},... | collective-permute-start | bytes 1179656 | tf_op jit(solution)/shard_map/ppermute | solution.py:359
  92.5 8.4 %shard_map.158 = (bf16[256,256]{1,0:T(8,128)(2,1)}, bf16[256,256]{1,0:T(8,128)(2,1)}, bf16[128,512]{1,0:T(8,128)(2,1)}, bf16[128,512]{1,0:T(8,128)(2,1)}, bf16[1...) custom-call(s32[23]{0:T(128)} %stack.155.where_ref, bf16[128,3072]{1,0:T(8,128)(2,1)} %copy-done.1, ...), custom_call_target="tpu_custom_call" | custom-call | flops 2415919104 | bytes 4718592 | tf_op jit(solution)/shard_map/pallas_call | solution.py:107
  100.9 1.6 collective-permute-start.29
  102.5 5.6 %collective-permute-done.32.refs_8_ = bf16[192,1024]{1,0:T(8,128)(2,1)} collective-permute-done((bf16[192,1024]{1,0:T(8,128)(2,1)}, bf16[192,1024]{1,0:T(8,128)(2,1)}, u32[]{:S(2)}, u32[]{:S(2)}) %collective-permute-start.32) | collective-permute-done | bytes 393248 | tf_op jit(solution)/shard_map/ppermute | solution.py:359
  108.1 1.5 collective-permute-start.33
  109.6 3.2 %collective-permute-start.24 = (bf16[128,512]{1,0:T(8,128)(2,1)}, bf16[128,512]{1,0:T(8,128)(2,1)S(1)}, u32[]{:S(2)}, u32[]{:S(2)}) collective-permute-start(bf16[128,512]{1,0:T(8,128)(2,1)} %get-tuple-element.40.refs_4_), channel_id=1, source_target_pairs={{0,16},{2,18},{4,20},{6,22},{8,24},{10,26},{12,28},{14,30},{16,0},... | collective-permute-start | bytes 393224 | tf_op jit(solution)/shard_map/ppermute | solution.py:435
  114.6 10.7 %shard_map.159 = (bf16[256,256]{1,0:T(8,128)(2,1)}, bf16[256,256]{1,0:T(8,128)(2,1)}, bf16[256,256]{1,0:T(8,128)(2,1)}, bf16[256,256]{1,0:T(8,128)(2,1)}) custom-call(s32[21]{0:T(128)} %stack.156.where_ref, bf16[256,256]{1,0:T(8,128)(2,1)} %get-tuple-element.43.refs_0_, bf16[256,256]{1,0:T(8,128)(2,1)} %get-tuple-element.44.refs_1_, ...), custom_call_target="tpu_custom_call" | custom-call | flops 1342177280 | bytes 2097152 | tf_op jit(solution)/shard_map/pallas_call | solution.py:192
  126.6 4.1 %collective-permute-done.26.refs_1_ = bf16[256,256]{1,0:T(8,128)(2,1)} collective-permute-done((bf16[256,256]{1,0:T(8,128)(2,1)}, bf16[256,256]{1,0:T(8,128)(2,1)}, u32[]{:S(2)}, u32[]{:S(2)}) %collective-permute-start.26) | collective-permute-done | bytes 131104 | tf_op jit(solution)/shard_map/ppermute | solution.py:435
  131.9 7.2 %collective-permute-done.27.refs_2_ = bf16[256,256]{1,0:T(8,128)(2,1)} collective-permute-done((bf16[256,256]{1,0:T(8,128)(2,1)}, bf16[256,256]{1,0:T(8,128)(2,1)}, u32[]{:S(2)}, u32[]{:S(2)}) %collective-permute-start.27) | collective-permute-done | bytes 131104 | tf_op jit(solution)/shard_map/ppermute | solution.py:435
  139.1 2.6 %collective-permute-start.28 = (bf16[256,256]{1,0:T(8,128)(2,1)}, bf16[256,256]{1,0:T(8,128)(2,1)}, u32[]{:S(2)}, u32[]{:S(2)}) collective-permute-start(bf16[256,256]{1,0:T(8,128)(2,1)} %get-tuple-element.48), channel_id=1, source_target_pairs={{0,24},{2,26},{4,28},{6,30},{8,16},{10,18},{12,20},{14,22},{16,8},... | collective-permute-start | bytes 393224 | tf_op jit(solution)/shard_map/ppermute | solution.py:435
  142.4 3.8 %collective-permute-done.28.refs_3_ = bf16[256,256]{1,0:T(8,128)(2,1)} collective-permute-done((bf16[256,256]{1,0:T(8,128)(2,1)}, bf16[256,256]{1,0:T(8,128)(2,1)}, u32[]{:S(2)}, u32[]{:S(2)}) %collective-permute-start.28) | collective-permute-done | bytes 131104 | tf_op jit(solution)/shard_map/ppermute | solution.py:435
  147.4 5.7 %shard_map.160 = (f32[128,768]{1,0:T(8,128)}, bf16[128,768]{1,0:T(8,128)(2,1)}, bf16[128,768]{1,0:T(8,128)(2,1)}, bf16[128,768]{1,0:T(8,128)(2,1)}) custom-call(s32[12]{0:T(128)} %stack.136.where_ref, bf16[256,256]{1,0:T(8,128)(2,1)} %get-tuple-element.45.refs_0_, bf16[256,256]{1,0:T(8,128)(2,1)} %collective-permute-done.26.refs_1_, ...), custom_call_target="tpu_custom_call" | custom-call | flops 805306368 | bytes 3145728 | tf_op jit(solution)/shard_map/pallas_call | solution.py:304
  153.1 1.6 collective-permute-start.36
  154.8 2.0 %collective-permute-start.37 = (bf16[128,768]{1,0:T(8,128)(2,1)}, bf16[128,768]{1,0:T(8,128)(2,1)S(1)}, u32[]{:S(2)}, u32[]{:S(2)}) collective-permute-start(bf16[128,768]{1,0:T(8,128)(2,1)} %get-tuple-element.54), channel_id=1, source_target_pairs={{0,8},{1,9},{2,10},{3,11},{4,12},{5,13},{6,14},{7,15},{8,0},{9,1},... | collective-permute-start | bytes 589832 | tf_op jit(solution)/shard_map/ppermute | solution.py:376
  156.8 1.9 %shard_map.161 = (bf16[128,1024]{1,0:T(8,128)(2,1)}, bf16[128,1024]{1,0:T(8,128)(2,1)}) custom-call(s32[1]{0:T(128)} %bitcast.member_ref, bf16[128,512]{1,0:T(8,128)(2,1)} %get-tuple-element.56.refs_2_.refs_0_, bf16[128,512]{1,0:T(8,128)(2,1)} %copy-done.25, bf16[128,512]{1,0:T(8,128)(2,1)} %copy-done.26, bf16[128,512]{1,0:T(8,128)(2,1)} %copy-done.27), custom_call_target="tpu_custom_call" | custom-call | tf_op jit(solution)/shard_map/pallas_call | solution.py:259
  158.7 1.6 collective-permute-done.36
  (129 shorter events, 26.0 us)
Async XLA Ops:
  2.9 12.3 %collective-permute-start = (bf16[64,3072]{1,0:T(8,128)(2,1)S(1)}, bf16[64,3072]{1,0:T(8,128)(2,1)}, u32[]{:S(2)}, u32[]{:S(2)}) collective-permute-start(bf16[64,3072]{1,0:T(8,128)(2,1)S(1)} %constant_dynamic-slice_fusion), channel_id=1, source_target_pairs={{0,8},{2,10},{4,12},{6,14},{8,0},{10,2},{12,4},{14,6},{16,24},{18,... | collective-permute-start | bytes 1179656 | tf_op jit(solution)/shard_map/ppermute | solution.py:359
  6.0 10.6 %collective-permute-start.3 = (bf16[64,3072]{1,0:T(8,128)(2,1)S(1)}, bf16[64,3072]{1,0:T(8,128)(2,1)S(1)}, u32[]{:S(2)}, u32[]{:S(2)}) collective-permute-start(bf16[64,3072]{1,0:T(8,128)(2,1)S(1)} %constant_dynamic-slice_fusion), channel_id=1, source_target_pairs={{8,16},{10,18},{12,20},{14,22},{16,8},{18,10},{20,12},{22,14},{9,1... | collective-permute-start | bytes 1179656 | tf_op jit(solution)/shard_map/ppermute | solution.py:359
  9.5 20.9 %collective-permute-start.8 = (bf16[832,256]{1,0:T(8,128)(2,1)}, bf16[832,256]{1,0:T(8,128)(2,1)S(1)}, u32[]{:S(2)}, u32[]{:S(2)}) collective-permute-start(bf16[832,256]{1,0:T(8,128)(2,1)} %get-tuple-element.31.refs_9_.refs_8_), channel_id=1, source_target_pairs={{0,4},{2,6},{4,0},{6,2},{8,12},{10,14},{12,8},{14,10},{16,20},{18,... | collective-permute-start | bytes 1277960 | tf_op jit(solution)/shard_map/ppermute | solution.py:365
  11.0 20.9 %collective-permute-start.9 = (bf16[832,256]{1,0:T(8,128)(2,1)}, bf16[832,256]{1,0:T(8,128)(2,1)S(1)}, u32[]{:S(2)}, u32[]{:S(2)}) collective-permute-start(bf16[832,256]{1,0:T(8,128)(2,1)} %get-tuple-element.31.refs_9_.refs_8_), channel_id=1, source_target_pairs={{0,2},{2,0},{4,6},{6,4},{8,10},{10,8},{12,14},{14,12},{16,18},{18,... | collective-permute-start | bytes 1277960 | tf_op jit(solution)/shard_map/ppermute | solution.py:365
  16.6 19.7 %collective-permute-start.4 = (bf16[64,3072]{1,0:T(8,128)(2,1)S(1)}, bf16[64,3072]{1,0:T(8,128)(2,1)}, u32[]{:S(2)}, u32[]{:S(2)}) collective-permute-start(bf16[64,3072]{1,0:T(8,128)(2,1)S(1)} %collective-permute-done.3), channel_id=1, source_target_pairs={{8,0},{10,2},{12,4},{14,6},{16,24},{18,26},{20,28},{22,30},{9,1},{... | collective-permute-start | bytes 1179656 | tf_op jit(solution)/shard_map/ppermute | solution.py:359
  17.9 37.5 %collective-permute-start.11 = (bf16[832,256]{1,0:T(8,128)(2,1)}, bf16[832,256]{1,0:T(8,128)(2,1)S(1)}, u32[]{:S(2)}, u32[]{:S(2)}) collective-permute-start(bf16[832,256]{1,0:T(8,128)(2,1)} %get-tuple-element.33), channel_id=1, source_target_pairs={{0,8},{2,10},{4,12},{6,14},{8,0},{10,2},{12,4},{14,6},{16,24},{18,... | collective-permute-start | bytes 1277960 | tf_op jit(solution)/shard_map/ppermute | solution.py:359
  22.5 36.7 %collective-permute-start.15 = (bf16[832,256]{1,0:T(8,128)(2,1)}, bf16[832,256]{1,0:T(8,128)(2,1)S(1)}, u32[]{:S(2)}, u32[]{:S(2)}) collective-permute-start(bf16[832,256]{1,0:T(8,128)(2,1)} %get-tuple-element.35), channel_id=1, source_target_pairs={{0,16},{2,18},{4,20},{6,22},{8,24},{10,26},{12,28},{14,30},{16,0},... | collective-permute-start | bytes 1277960 | tf_op jit(solution)/shard_map/ppermute | solution.py:359
  30.4 9.4 %collective-permute-start.1 = (bf16[64,3072]{1,0:T(8,128)(2,1)}, bf16[64,3072]{1,0:T(8,128)(2,1)S(1)}, u32[]{:S(2)}, u32[]{:S(2)}) collective-permute-start(bf16[64,3072]{1,0:T(8,128)(2,1)} %collective-permute-done.refs_1_), channel_id=1, source_target_pairs={{0,1},{1,0},{2,3},{3,2},{4,5},{5,4},{6,7},{7,6},{8,9},{9,8},{10,11... | collective-permute-start | bytes 1179656 | tf_op jit(solution)/shard_map/ppermute | solution.py:368
  31.9 28.8 %collective-permute-start.10 = (bf16[832,256]{1,0:T(8,128)(2,1)S(1)}, bf16[832,256]{1,0:T(8,128)(2,1)S(1)}, u32[]{:S(2)}, u32[]{:S(2)}) collective-permute-start(bf16[832,256]{1,0:T(8,128)(2,1)S(1)} %collective-permute-done.8.refs_10_.refs_9_), channel_id=1, source_target_pairs={{0,2},{2,0},{4,6},{6,4},{8,10},{10,8},{12,14},{14,12},{16,18},{18,... | collective-permute-start | bytes 1277960 | tf_op jit(solution)/shard_map/ppermute | solution.py:365
  36.3 29.2 %collective-permute-start.19 = (bf16[832,256]{1,0:T(8,128)(2,1)}, bf16[832,256]{1,0:T(8,128)(2,1)S(1)}, u32[]{:S(2)}, u32[]{:S(2)}) collective-permute-start(bf16[832,256]{1,0:T(8,128)(2,1)} %get-tuple-element.37), channel_id=1, source_target_pairs={{0,24},{2,26},{4,28},{6,30},{8,16},{10,18},{12,20},{14,22},{16,8},... | collective-permute-start | bytes 1277960 | tf_op jit(solution)/shard_map/ppermute | solution.py:359
  39.8 21.0 %collective-permute-start.5 = (bf16[64,3072]{1,0:T(8,128)(2,1)S(1)}, bf16[64,3072]{1,0:T(8,128)(2,1)S(1)}, u32[]{:S(2)}, u32[]{:S(2)}) collective-permute-start(bf16[64,3072]{1,0:T(8,128)(2,1)S(1)} %broadcast_select_fusion.1.refs_3_), channel_id=1, source_target_pairs={{0,1},{1,0},{2,3},{3,2},{4,5},{5,4},{6,7},{7,6},{8,9},{9,8},{10,11... | collective-permute-start | bytes 1179656 | tf_op jit(solution)/shard_map/ppermute | solution.py:368
  55.4 10.1 %collective-permute-start.6 = (bf16[64,3072]{1,0:T(8,128)(2,1)}, bf16[64,3072]{1,0:T(8,128)(2,1)S(1)}, u32[]{:S(2)}, u32[]{:S(2)}) collective-permute-start(bf16[64,3072]{1,0:T(8,128)(2,1)} %collective-permute-done.2), channel_id=1, source_target_pairs={{8,0},{10,2},{12,4},{14,6},{16,24},{18,26},{20,28},{22,30},{9,1},{... | collective-permute-start | bytes 1179656 | tf_op jit(solution)/shard_map/ppermute | solution.py:359
  59.2 11.6 %collective-permute-start.12 = (bf16[832,256]{1,0:T(8,128)(2,1)S(1)}, bf16[832,256]{1,0:T(8,128)(2,1)}, u32[]{:S(2)}, u32[]{:S(2)}) collective-permute-start(bf16[832,256]{1,0:T(8,128)(2,1)S(1)} %collective-permute-done.11.refs_13_.refs_12_), channel_id=1, source_target_pairs={{0,4},{2,6},{4,0},{6,2},{8,12},{10,14},{12,8},{14,10},{16,20},{18,... | collective-permute-start | bytes 1277960 | tf_op jit(solution)/shard_map/ppermute | solution.py:365
  60.8 11.6 %collective-permute-start.13 = (bf16[832,256]{1,0:T(8,128)(2,1)S(1)}, bf16[832,256]{1,0:T(8,128)(2,1)S(1)}, u32[]{:S(2)}, u32[]{:S(2)}) collective-permute-start(bf16[832,256]{1,0:T(8,128)(2,1)S(1)} %collective-permute-done.11.refs_13_.refs_12_), channel_id=1, source_target_pairs={{0,2},{2,0},{4,6},{6,4},{8,10},{10,8},{12,14},{14,12},{16,18},{18,... | collective-permute-start | bytes 1277960 | tf_op jit(solution)/shard_map/ppermute | solution.py:365
  60.9 19.1 %collective-permute-start.16 = (bf16[832,256]{1,0:T(8,128)(2,1)S(1)}, bf16[832,256]{1,0:T(8,128)(2,1)}, u32[]{:S(2)}, u32[]{:S(2)}) collective-permute-start(bf16[832,256]{1,0:T(8,128)(2,1)S(1)} %collective-permute-done.15.refs_17_.refs_16_), channel_id=1, source_target_pairs={{0,4},{2,6},{4,0},{6,2},{8,12},{10,14},{12,8},{14,10},{16,20},{18,... | collective-permute-start | bytes 1277960 | tf_op jit(solution)/shard_map/ppermute | solution.py:365
  65.5 14.5 %collective-permute-start.17 = (bf16[832,256]{1,0:T(8,128)(2,1)S(1)}, bf16[832,256]{1,0:T(8,128)(2,1)S(1)}, u32[]{:S(2)}, u32[]{:S(2)}) collective-permute-start(bf16[832,256]{1,0:T(8,128)(2,1)S(1)} %collective-permute-done.15.refs_17_.refs_16_), channel_id=1, source_target_pairs={{0,2},{2,0},{4,6},{6,4},{8,10},{10,8},{12,14},{14,12},{16,18},{18,... | collective-permute-start | bytes 1277960 | tf_op jit(solution)/shard_map/ppermute | solution.py:365
  65.5 20.2 %collective-permute-start.20 = (bf16[832,256]{1,0:T(8,128)(2,1)S(1)}, bf16[832,256]{1,0:T(8,128)(2,1)}, u32[]{:S(2)}, u32[]{:S(2)}) collective-permute-start(bf16[832,256]{1,0:T(8,128)(2,1)S(1)} %collective-permute-done.19.refs_21_.refs_20_), channel_id=1, source_target_pairs={{0,4},{2,6},{4,0},{6,2},{8,12},{10,14},{12,8},{14,10},{16,20},{18,... | collective-permute-start | bytes 1277960 | tf_op jit(solution)/shard_map/ppermute | solution.py:365
  70.9 14.9 %collective-permute-start.7 = (bf16[64,3072]{1,0:T(8,128)(2,1)S(1)}, bf16[64,3072]{1,0:T(8,128)(2,1)S(1)}, u32[]{:S(2)}, u32[]{:S(2)}) collective-permute-start(bf16[64,3072]{1,0:T(8,128)(2,1)S(1)} %broadcast_select_fusion.refs_5_), channel_id=1, source_target_pairs={{0,1},{1,0},{2,3},{3,2},{4,5},{5,4},{6,7},{7,6},{8,9},{9,8},{10,11... | collective-permute-start | bytes 1179656 | tf_op jit(solution)/shard_map/ppermute | solution.py:368
  72.3 19.1 %collective-permute-start.21 = (bf16[832,256]{1,0:T(8,128)(2,1)S(1)}, bf16[832,256]{1,0:T(8,128)(2,1)S(1)}, u32[]{:S(2)}, u32[]{:S(2)}) collective-permute-start(bf16[832,256]{1,0:T(8,128)(2,1)S(1)} %collective-permute-done.19.refs_21_.refs_20_), channel_id=1, source_target_pairs={{0,2},{2,0},{4,6},{6,4},{8,10},{10,8},{12,14},{14,12},{16,18},{18,... | collective-permute-start | bytes 1277960 | tf_op jit(solution)/shard_map/ppermute | solution.py:365
  80.0 11.5 %collective-permute-start.14 = (bf16[832,256]{1,0:T(8,128)(2,1)}, bf16[832,256]{1,0:T(8,128)(2,1)S(1)}, u32[]{:S(2)}, u32[]{:S(2)}) collective-permute-start(bf16[832,256]{1,0:T(8,128)(2,1)} %collective-permute-done.12.refs_14_.refs_13_), channel_id=1, source_target_pairs={{0,2},{2,0},{4,6},{6,4},{8,10},{10,8},{12,14},{14,12},{16,18},{18,... | collective-permute-start | bytes 1277960 | tf_op jit(solution)/shard_map/ppermute | solution.py:365
  80.0 11.5 %collective-permute-start.18 = (bf16[832,256]{1,0:T(8,128)(2,1)}, bf16[832,256]{1,0:T(8,128)(2,1)}, u32[]{:S(2)}, u32[]{:S(2)}) collective-permute-start(bf16[832,256]{1,0:T(8,128)(2,1)} %collective-permute-done.16.refs_18_.refs_17_), channel_id=1, source_target_pairs={{0,2},{2,0},{4,6},{6,4},{8,10},{10,8},{12,14},{14,12},{16,18},{18,... | collective-permute-start | bytes 1277960 | tf_op jit(solution)/shard_map/ppermute | solution.py:365
  86.5 21.6 %collective-permute-start.32 = (bf16[192,1024]{1,0:T(8,128)(2,1)}, bf16[192,1024]{1,0:T(8,128)(2,1)}, u32[]{:S(2)}, u32[]{:S(2)}) collective-permute-start(bf16[192,1024]{1,0:T(8,128)(2,1)} %bitcast.32.refs_4_), channel_id=1, source_target_pairs={{0,16},{2,18},{4,20},{6,22},{8,24},{10,26},{12,28},{14,30},{16,0},... | collective-permute-start | bytes 1179656 | tf_op jit(solution)/shard_map/ppermute | solution.py:359
  100.9 25.2 %collective-permute-start.29 = (bf16[192,1024]{1,0:T(8,128)(2,1)}, bf16[192,1024]{1,0:T(8,128)(2,1)S(1)}, u32[]{:S(2)}, u32[]{:S(2)}) collective-permute-start(bf16[192,1024]{1,0:T(8,128)(2,1)} %bitcast.32.refs_4_), channel_id=1, source_target_pairs={{0,4},{2,6},{4,0},{6,2},{8,12},{10,14},{12,8},{14,10},{16,20},{18,... | collective-permute-start | bytes 1179656 | tf_op jit(solution)/shard_map/ppermute | solution.py:365
  108.1 18.1 %collective-permute-start.33 = (bf16[192,1024]{1,0:T(8,128)(2,1)}, bf16[192,1024]{1,0:T(8,128)(2,1)S(1)}, u32[]{:S(2)}, u32[]{:S(2)}) collective-permute-start(bf16[192,1024]{1,0:T(8,128)(2,1)} %collective-permute-done.32.refs_8_), channel_id=1, source_target_pairs={{0,4},{2,6},{4,0},{6,2},{8,12},{10,14},{12,8},{14,10},{16,20},{18,... | collective-permute-start | bytes 1179656 | tf_op jit(solution)/shard_map/ppermute | solution.py:365
  109.6 15.7 %collective-permute-start.23 = (bf16[128,512]{1,0:T(8,128)(2,1)}, bf16[128,512]{1,0:T(8,128)(2,1)S(1)}, u32[]{:S(2)}, u32[]{:S(2)}) collective-permute-start(bf16[128,512]{1,0:T(8,128)(2,1)} %get-tuple-element.39.refs_3_), channel_id=1, source_target_pairs={{0,8},{2,10},{4,12},{6,14},{8,0},{10,2},{12,4},{14,6},{16,24},{18,... | collective-permute-start | bytes 393224 | tf_op jit(solution)/shard_map/ppermute | solution.py:435
  109.6 15.8 %collective-permute-start.24 = (bf16[128,512]{1,0:T(8,128)(2,1)}, bf16[128,512]{1,0:T(8,128)(2,1)S(1)}, u32[]{:S(2)}, u32[]{:S(2)}) collective-permute-start(bf16[128,512]{1,0:T(8,128)(2,1)} %get-tuple-element.40.refs_4_), channel_id=1, source_target_pairs={{0,16},{2,18},{4,20},{6,22},{8,24},{10,26},{12,28},{14,30},{16,0},... | collective-permute-start | bytes 393224 | tf_op jit(solution)/shard_map/ppermute | solution.py:435
  112.8 12.7 %collective-permute-start.25 = (bf16[128,512]{1,0:T(8,128)(2,1)}, bf16[128,512]{1,0:T(8,128)(2,1)S(1)}, u32[]{:S(2)}, u32[]{:S(2)}) collective-permute-start(bf16[128,512]{1,0:T(8,128)(2,1)} %get-tuple-element.41.refs_5_), channel_id=1, source_target_pairs={{0,24},{2,26},{4,28},{6,30},{8,16},{10,18},{12,20},{14,22},{16,8},... | collective-permute-start | bytes 393224 | tf_op jit(solution)/shard_map/ppermute | solution.py:435
  125.5 20.7 %collective-permute-start.30 = (bf16[192,1024]{1,0:T(8,128)(2,1)}, bf16[192,1024]{1,0:T(8,128)(2,1)S(1)}, u32[]{:S(2)}, u32[]{:S(2)}) collective-permute-start(bf16[192,1024]{1,0:T(8,128)(2,1)} %bitcast.32.refs_4_), channel_id=1, source_target_pairs={{0,2},{2,0},{4,6},{6,4},{8,10},{10,8},{12,14},{14,12},{16,18},{18,... | collective-permute-start | bytes 1179656 | tf_op jit(solution)/shard_map/ppermute | solution.py:365
  125.6 20.6 %collective-permute-start.34 = (bf16[192,1024]{1,0:T(8,128)(2,1)}, bf16[192,1024]{1,0:T(8,128)(2,1)S(1)}, u32[]{:S(2)}, u32[]{:S(2)}) collective-permute-start(bf16[192,1024]{1,0:T(8,128)(2,1)} %collective-permute-done.32.refs_8_), channel_id=1, source_target_pairs={{0,2},{2,0},{4,6},{6,4},{8,10},{10,8},{12,14},{14,12},{16,18},{18,... | collective-permute-start | bytes 1179656 | tf_op jit(solution)/shard_map/ppermute | solution.py:365
  126.1 20.2 %collective-permute-start.31 = (bf16[192,1024]{1,0:T(8,128)(2,1)S(1)}, bf16[192,1024]{1,0:T(8,128)(2,1)S(1)}, u32[]{:S(2)}, u32[]{:S(2)}) collective-permute-start(bf16[192,1024]{1,0:T(8,128)(2,1)S(1)} %collective-permute-done.29.refs_5_), channel_id=1, source_target_pairs={{0,2},{2,0},{4,6},{6,4},{8,10},{10,8},{12,14},{14,12},{16,18},{18,... | collective-permute-start | bytes 1179656 | tf_op jit(solution)/shard_map/ppermute | solution.py:365
  126.2 20.1 %collective-permute-start.35 = (bf16[192,1024]{1,0:T(8,128)(2,1)S(1)}, bf16[192,1024]{1,0:T(8,128)(2,1)S(1)}, u32[]{:S(2)}, u32[]{:S(2)}) collective-permute-start(bf16[192,1024]{1,0:T(8,128)(2,1)S(1)} %collective-permute-done.33.refs_9_), channel_id=1, source_target_pairs={{0,2},{2,0},{4,6},{6,4},{8,10},{10,8},{12,14},{14,12},{16,18},{18,... | collective-permute-start | bytes 1179656 | tf_op jit(solution)/shard_map/ppermute | solution.py:365
  130.7 8.4 %collective-permute-start.27 = (bf16[256,256]{1,0:T(8,128)(2,1)}, bf16[256,256]{1,0:T(8,128)(2,1)}, u32[]{:S(2)}, u32[]{:S(2)}) collective-permute-start(bf16[256,256]{1,0:T(8,128)(2,1)} %get-tuple-element.47), channel_id=1, source_target_pairs={{0,16},{2,18},{4,20},{6,22},{8,24},{10,26},{12,28},{14,30},{16,0},... | collective-permute-start | bytes 393224 | tf_op jit(solution)/shard_map/ppermute | solution.py:435
  (38 other events, 528.0 us)

commit v4 on v3

--- a/solution.py
+++ b/solution.py
@@ -154,28 +154,28 @@
         query = jnp.concatenate([x[:, cols] for x in q_refs], axis=0)
         keys = held[:, :rows, cols].reshape(n_pieces * rows, head_size)
         values = held[:, rows:, cols].reshape(n_pieces * rows, head_size)
-        scores[...] = nt_dot(query, keys)
+        scores[h] = nt_dot(query, keys)
         for g, group in enumerate(groups):
-            scores[group, own_cols[g]] = nt_dot(query[group], kv_refs[g][:, cols])
+            scores[h, group, own_cols[g]] = nt_dot(query[group], kv_refs[g][:, cols])
         text_s = nt_dot(query, tk_ref[:, cols])
-        image_s = scores[...]
+        image_s = scores[h]
         largest = jnp.maximum(
             jnp.max(text_s, axis=-1, keepdims=True), jnp.max(image_s, axis=-1, keepdims=True)
         )
         text_e = jnp.exp2((text_s - largest) * scale)
         image_e = jnp.exp2((image_s - largest) * scale)
         total = jnp.sum(text_e, axis=-1, keepdims=True) + jnp.sum(image_e, axis=-1, keepdims=True)
-        expos[...] = image_e.astype(jnp.bfloat16)
+        expos[h] = image_e.astype(jnp.bfloat16)
         fresh_mix = []
         for g, group in enumerate(groups):
             value = kv_refs[g][:, width + cols.start : width + cols.stop]
             fresh_mix.append(
-                jnp.dot(expos[group, own_cols[g]], value, preferred_element_type=jnp.float32)
+                jnp.dot(expos[h, group, own_cols[g]], value, preferred_element_type=jnp.float32)
             )
-            expos[group, own_cols[g]] = jnp.zeros((rows, rows), jnp.bfloat16)
+            expos[h, group, own_cols[g]] = jnp.zeros((rows, rows), jnp.bfloat16)
         mixture = (
             jnp.dot(text_e.astype(jnp.bfloat16), tv_ref[:, cols], preferred_element_type=jnp.float32)
-            + jnp.dot(expos[...], values, preferred_element_type=jnp.float32)
+            + jnp.dot(expos[h], values, preferred_element_type=jnp.float32)
             + jnp.concatenate(fresh_mix, axis=0)
         )
         attended = (mixture / total).astype(jnp.bfloat16)
@@ -201,8 +201,8 @@
             out_specs=[pl.BlockSpec((pair_rows, width), whole)] * n,
             scratch_shapes=[
                 pltpu.VMEM((n_pieces, 2 * rows, width), jnp.bfloat16),
-                pltpu.VMEM((n * rows, n_pieces * rows), jnp.float32),
-                pltpu.VMEM((n * rows, n_pieces * rows), jnp.bfloat16),
+                pltpu.VMEM((width // head_size, n * rows, n_pieces * rows), jnp.float32),
+                pltpu.VMEM((width // head_size, n * rows, n_pieces * rows), jnp.bfloat16),
                 pltpu.SemaphoreType.DMA((n_pieces,)),
             ],
         ),
@@ -375,9 +375,9 @@
         ]
         return lax.ppermute(x, ("patch", "fsdp"), pairs)
 
-    def spread(piece):
-        side = flip(piece, 2)
-        return [piece, side, flip(piece, 1), flip(side, 1)]
+    def spread(piece, side=None, *deps):
+        side = flip(piece, 2) if side is None else side
+        return [piece, side, flip(after(piece, *deps), 1), flip(after(side, *deps), 1)]
 
     def seats_of(position):
         return [position * INNER + (seat ^ bits) for bits in (0, 2, 1, 3)]
@@ -386,7 +386,7 @@
     share = rows // fsdp
     part = lax.dynamic_slice_in_dim(modded, mine * share, share, axis=0)
     dealt = deal(member, (w_query, w_key, w_value, stale_keys, stale_values), team)
-    pieces = {0: dealt[0]}
+    pieces, sides = {0: dealt[0]}, {}
     row_shares = {}
     if outer == 4 and team == 4:
         ends = [(1, 0), (2, 3)]
@@ -394,13 +394,16 @@
         inside = jnp.logical_or(place == 1, place == 2)
         near = to_partner(part, 1)
         across = over_outer(part, middle)
+        sides[0] = flip(pieces[0], 2)
         far = over_outer(near, middle)
-        pieces[2] = to_partner(after(dealt[2], near), 2)
-        pieces[1] = to_partner(after(dealt[1], near), 1)
+        pieces[2] = to_partner(after(dealt[2], near, across), 2)
+        pieces[1] = to_partner(after(dealt[1], near, across), 1)
         end_across = over_outer(across, ends)
-        end_far = over_outer(far, ends)
+        end_far = over_outer(after(far, sides[0]), ends)
+        sides[1] = flip(after(pieces[1], far), 2)
         pieces[3] = to_partner(after(dealt[3], far), 3)
-        row_shares[1] = near
+        sides[2] = flip(after(pieces[2], end_far, sides[1]), 2)
+        row_shares[1] = after(near, sides[1])
         row_shares[2] = jnp.where(inside, far, end_across)
         row_shares[3] = jnp.where(inside, across, end_far)
     else:
@@ -411,7 +414,8 @@
     out_piece = after(w_out.T, pieces[outer - 1])
     out_pieces = [out_piece] + [to_partner(out_piece, 2 * k) for k in range(1, fsdp)]
 
-    pieces = [x for k in range(outer) for x in spread(pieces[k])]
+    late = list(sides.values())[-1:]
+    pieces = [x for k in range(outer) for x in spread(pieces[k], sides.get(k), *late)]
     origins = [o for k in range(outer) for o in seats_of(place ^ k)]
     patch_rows = [[modded]]
     firsts = [0 * mine]
@@ -428,7 +432,6 @@
         depth,
         width,
     )
-    out_pieces = [x for piece in out_pieces for x in spread(after(piece, queries[0]))]
     out_places = [o for k in range(fsdp) for o in seats_of((place ^ (2 * k)) // 2)]
 
     def give(x, bits):
@@ -447,8 +450,11 @@
         head_size,
     )
     packs = [att[0]] + [give(att[k], k) for k in range(1, team)]
+    out_sides = [flip(after(out_pieces[0], queries[0]), 2)]
+    out_sides += [flip(after(piece, att[0], *fresh[1:]), 2) for piece in out_pieces[1:]]
+    out_pieces = [x for p, q in zip(out_pieces, out_sides) for x in spread(p, q, *packs[1:])]
     where = [member, parity] + [(mine + i) % fsdp for i in range(fsdp)] + out_places
-    where = after(jnp.stack(where).astype(jnp.int32), *fresh)
+    where = jnp.stack(where).astype(jnp.int32)
     partial = project(where, packs, out_pieces, fsdp)
     own, partner = partial[0], [along_both(partial[1], 1, 0)]
     for i in range(1, fsdp):

time: 164 us -> 163 us (level)
  starting transfers between devices: 53 us -> 48.9 us
  waiting for transfers between devices: 69.5 us -> 71.3 us
  local copies, waits for them, and re-layouts: 5.11 us -> 6.81 us
    ppermute x4, waiting for transfers between devices: 1.91 us -> 13.1 us  [along_fsdp(): lax.ppermute(x, 'fsdp', [(i, (i + step) % fsdp) for i in range(fsdp)])]
    ppermute x9, starting transfers between devices: 26.8 us -> 19.4 us  [over_outer(): return lax.ppermute(x, 'patch', pairs)]
    ppermute x6, waiting for transfers between devices: 15.2 us -> 10.8 us  [give(): lax.ppermute(x, 'patch', [(p, p ^ bits * INNER) for p in range(patches)])]
    ppermute x6, starting transfers between devices: 8.27 us -> 10.4 us  [give(): lax.ppermute(x, 'patch', [(p, p ^ bits * INNER) for p in range(patches)])]
    ppermute x9, waiting for transfers between devices: 34.5 us -> 32.5 us  [over_outer(): return lax.ppermute(x, 'patch', pairs)]
    ppermute x18, waiting for transfers between devices: 16.6 us -> 14.6 us  [flip(): return lax.ppermute(x, 'patch', [(p, p ^ bits) for p in range(patches)])]
    unnamed x62 -> x76, local copies, waits for them, and re-layouts: 3.06 us -> 4.73 us
  transfers between devices with their start and end apart: 39 -> 39, of which waited for: 16 -> 18; matrix products, arithmetic and copies ran while one was open for 3% -> 3% of each run, Pallas kernels for 15% -> 15%
where the time goes in v4:
time: 163 us
  waiting for transfers between devices  71.3 us (44%)
  starting transfers between devices  48.9 us (30%)
  Pallas kernels  29.5 us (18%)
  local copies, waits for them, and re-layouts  6.81 us (4%)
  other arithmetic  5.23 us (3%)
    ppermute x9, waiting for transfers between devices, over_outer(): return lax.ppermute(x, 'patch', pairs)  32.5 us
    ppermute x9, starting transfers between devices, over_outer(): return lax.ppermute(x, 'patch', pairs)  19.4 us
    ppermute x18, waiting for transfers between devices, flip(): return lax.ppermute(x, 'patch', [(p, p ^ bits) for p in range(patches)])  14.6 us
    ppermute x4, waiting for transfers between devices, along_fsdp(): lax.ppermute(x, 'fsdp', [(i, (i + step) % fsdp) for i in range(fsdp)])  13.1 us
    ppermute x18, starting transfers between devices, flip(): return lax.ppermute(x, 'patch', [(p, p ^ bits) for p in range(patches)])  10.8 us
    ppermute x6, waiting for transfers between devices, give(): lax.ppermute(x, 'patch', [(p, p ^ bits * INNER) for p in range(patches)])  10.8 us
    pallas_call x1, Pallas kernels, attend_rows(): pl.pallas_call(functools.partial(attend_kernel, depth, head_size, n_piece...  10.7 us
    ppermute x6, starting transfers between devices, give(): lax.ppermute(x, 'patch', [(p, p ^ bits * INNER) for p in range(patches)])  10.4 us
  transfers between devices with their start and end apart: 39, of which 18 were waited for; matrix products, arithmetic and copies ran while one was open for 3% of the time, Pallas kernels for 15%

profile of v4, /device:TPU:0, one launch (start us, length us, event | category | flops | bytes accessed | tf_op | source)
XLA Modules:
  0.0 162.8 jit_solution(3805843348573221865)
XLA Ops:
  2.9 3.1 %collective-permute-start = (bf16[64,3072]{1,0:T(8,128)(2,1)S(1)}, bf16[64,3072]{1,0:T(8,128)(2,1)S(1)}, u32[]{:S(2)}, u32[]{:S(2)}) collective-permute-start(bf16[64,3072]{1,0:T(8,128)(2,1)S(1)} %constant_dynamic-slice_fusion), channel_id=1, source_target_pairs={{0,8},{2,10},{4,12},{6,14},{8,0},{10,2},{12,4},{14,6},{16,24},{18,... | collective-permute-start | bytes 1179656 | tf_op jit(solution)/shard_map/ppermute | solution.py:359
  6.7 2.8 %shard_map.157 = (bf16[832,256]{1,0:T(8,128)(2,1)}, bf16[832,256]{1,0:T(8,128)(2,1)}, bf16[832,256]{1,0:T(8,128)(2,1)}, bf16[832,256]{1,0:T(8,128)(2,1)}) custom-call(s32[1]{0:T(128)} %bitcast.member_ref, bf16[192,1024]{1,0:T(8,128)(2,1)} %refs_0_.1, bf16[192,1024]{1,0:T(8,128)(2,1)} %refs_1_.1, bf16[192,1024]{1,0:T(8,128)(2,1)} %refs_2_.1, ...), custom_call_target="tpu_custom_call" | custom-call | tf_op jit(solution)/shard_map/pallas_call | solution.py:235
  9.5 1.5 collective-permute-start.8
  11.0 4.1 %collective-permute-done.refs_1_ = bf16[64,3072]{1,0:T(8,128)(2,1)S(1)} collective-permute-done((bf16[64,3072]{1,0:T(8,128)(2,1)S(1)}, bf16[64,3072]{1,0:T(8,128)(2,1)S(1)}, u32[]{:S(2)}, u32[]{:S(2)}) %collective-permute-start) | collective-permute-done | bytes 393248 | tf_op jit(solution)/shard_map/ppermute | solution.py:359
  15.9 4.0 %collective-permute-start.2 = (bf16[832,256]{1,0:T(8,128)(2,1)}, bf16[832,256]{1,0:T(8,128)(2,1)S(1)}, u32[]{:S(2)}, u32[]{:S(2)}) collective-permute-start(bf16[832,256]{1,0:T(8,128)(2,1)} %get-tuple-element.47), channel_id=1, source_target_pairs={{0,8},{2,10},{4,12},{6,14},{8,0},{10,2},{12,4},{14,6},{16,24},{18,... | collective-permute-start | bytes 1277960 | tf_op jit(solution)/shard_map/ppermute | solution.py:359
  22.6 4.5 %collective-permute-start.11 = (bf16[832,256]{1,0:T(8,128)(2,1)}, bf16[832,256]{1,0:T(8,128)(2,1)S(1)}, u32[]{:S(2)}, u32[]{:S(2)}) collective-permute-start(bf16[832,256]{1,0:T(8,128)(2,1)} %get-tuple-element.53), channel_id=1, source_target_pairs={{0,16},{2,18},{4,20},{6,22},{8,24},{10,26},{12,28},{14,30},{16,0},... | collective-permute-start | bytes 1277960 | tf_op jit(solution)/shard_map/ppermute | solution.py:359
  28.5 2.6 %collective-permute-done.2.refs_13_.refs_12_ = bf16[832,256]{1,0:T(8,128)(2,1)S(1)} collective-permute-done((bf16[832,256]{1,0:T(8,128)(2,1)}, bf16[832,256]{1,0:T(8,128)(2,1)S(1)}, u32[]{:S(2)}, u32[]{:S(2)}) %collective-permute-start.2) | collective-permute-done | bytes 426016 | tf_op jit(solution)/shard_map/ppermute | solution.py:359
  32.6 7.7 %collective-permute-done.6 = bf16[64,3072]{1,0:T(8,128)(2,1)} collective-permute-done((bf16[64,3072]{1,0:T(8,128)(2,1)S(1)}, bf16[64,3072]{1,0:T(8,128)(2,1)}, u32[]{:S(2)}, u32[]{:S(2)}) %collective-permute-start.6) | collective-permute-done | bytes 393248 | tf_op jit(solution)/shard_map/ppermute | solution.py:359
  41.3 1.6 collective-permute-start.7
  42.9 3.1 %collective-permute-start.19 = (bf16[832,256]{1,0:T(8,128)(2,1)S(1)}, bf16[832,256]{1,0:T(8,128)(2,1)S(1)}, u32[]{:S(2)}, u32[]{:S(2)}) collective-permute-start(bf16[832,256]{1,0:T(8,128)(2,1)S(1)} %copy-done.37), channel_id=1, source_target_pairs={{0,24},{2,26},{4,28},{6,30},{8,16},{10,18},{12,20},{14,22},{16,8},... | collective-permute-start | bytes 1277960 | tf_op jit(solution)/shard_map/ppermute | solution.py:359
  46.0 14.9 %collective-permute-done.11.refs_17_.refs_16_ = bf16[832,256]{1,0:T(8,128)(2,1)S(1)} collective-permute-done((bf16[832,256]{1,0:T(8,128)(2,1)}, bf16[832,256]{1,0:T(8,128)(2,1)S(1)}, u32[]{:S(2)}, u32[]{:S(2)}) %collective-permute-start.11) | collective-permute-done | bytes 426016 | tf_op jit(solution)/shard_map/ppermute | solution.py:359
  60.9 3.2 %collective-permute-done.9 = bf16[64,3072]{1,0:T(8,128)(2,1)S(1)} collective-permute-done((bf16[64,3072]{1,0:T(8,128)(2,1)}, bf16[64,3072]{1,0:T(8,128)(2,1)S(1)}, u32[]{:S(2)}, u32[]{:S(2)}) %collective-permute-start.9) | collective-permute-done | bytes 393248 | tf_op jit(solution)/shard_map/ppermute | solution.py:359
  64.2 1.5 collective-permute-start.12
  65.7 1.6 collective-permute-start.10
  67.8 9.2 %collective-permute-done.12.refs_18_.refs_17_ = bf16[832,256]{1,0:T(8,128)(2,1)} collective-permute-done((bf16[832,256]{1,0:T(8,128)(2,1)S(1)}, bf16[832,256]{1,0:T(8,128)(2,1)}, u32[]{:S(2)}, u32[]{:S(2)}) %collective-permute-start.12) | collective-permute-done | bytes 426016 | tf_op jit(solution)/shard_map/ppermute | solution.py:365
  77.7 1.6 collective-permute-start.5
  79.2 2.7 %collective-permute-done.20.refs_22_.refs_21_ = bf16[832,256]{1,0:T(8,128)(2,1)} collective-permute-done((bf16[832,256]{1,0:T(8,128)(2,1)S(1)}, bf16[832,256]{1,0:T(8,128)(2,1)}, u32[]{:S(2)}, u32[]{:S(2)}) %collective-permute-start.20) | collective-permute-done | bytes 426016 | tf_op jit(solution)/shard_map/ppermute | solution.py:365
  82.0 7.2 %collective-permute-done.5.refs_2_ = bf16[64,3072]{1,0:T(8,128)(2,1)S(1)} collective-permute-done((bf16[64,3072]{1,0:T(8,128)(2,1)S(1)}, bf16[64,3072]{1,0:T(8,128)(2,1)S(1)}, u32[]{:S(2)}, u32[]{:S(2)}) %collective-permute-start.5) | collective-permute-done | bytes 393248 | tf_op jit(solution)/shard_map/ppermute | solution.py:368
  93.8 8.5 %shard_map.158 = (bf16[256,256]{1,0:T(8,128)(2,1)}, bf16[256,256]{1,0:T(8,128)(2,1)}, bf16[128,512]{1,0:T(8,128)(2,1)}, bf16[128,512]{1,0:T(8,128)(2,1)}, bf16[1...) custom-call(s32[23]{0:T(128)} %stack.156.where_ref, bf16[128,3072]{1,0:T(8,128)(2,1)} %copy-done.1, ...), custom_call_target="tpu_custom_call" | custom-call | flops 2415919104 | bytes 4718592 | tf_op jit(solution)/shard_map/pallas_call | solution.py:107
  102.3 2.4 %collective-permute-start.30 = (bf16[128,512]{1,0:T(8,128)(2,1)}, bf16[128,512]{1,0:T(8,128)(2,1)S(1)}, u32[]{:S(2)}, u32[]{:S(2)}) collective-permute-start(bf16[128,512]{1,0:T(8,128)(2,1)} %get-tuple-element.68.refs_3_), channel_id=1, source_target_pairs={{0,8},{2,10},{4,12},{6,14},{8,0},{10,2},{12,4},{14,6},{16,24},{18,... | collective-permute-start | bytes 393224 | tf_op jit(solution)/shard_map/ppermute | solution.py:438
  105.2 1.9 %collective-permute-start.32 = (bf16[128,512]{1,0:T(8,128)(2,1)}, bf16[128,512]{1,0:T(8,128)(2,1)S(1)}, u32[]{:S(2)}, u32[]{:S(2)}) collective-permute-start(bf16[128,512]{1,0:T(8,128)(2,1)} %get-tuple-element.70.refs_5_), channel_id=1, source_target_pairs={{0,24},{2,26},{4,28},{6,30},{8,16},{10,18},{12,20},{14,22},{16,8},... | collective-permute-start | bytes 393224 | tf_op jit(solution)/shard_map/ppermute | solution.py:438
  109.3 10.7 %shard_map.159 = (bf16[256,256]{1,0:T(8,128)(2,1)}, bf16[256,256]{1,0:T(8,128)(2,1)}, bf16[256,256]{1,0:T(8,128)(2,1)}, bf16[256,256]{1,0:T(8,128)(2,1)}) custom-call(s32[21]{0:T(128)} %stack.153.where_ref, bf16[256,256]{1,0:T(8,128)(2,1)} %get-tuple-element.65.refs_0_, bf16[256,256]{1,0:T(8,128)(2,1)} %get-tuple-element.66.refs_1_, ...), custom_call_target="tpu_custom_call" | custom-call | flops 1342177280 | bytes 2097152 | tf_op jit(solution)/shard_map/pallas_call | solution.py:192
  120.5 1.6 collective-permute-start.33
  122.1 3.3 %collective-permute-start.23 = (bf16[256,256]{1,0:T(8,128)(2,1)}, bf16[256,256]{1,0:T(8,128)(2,1)S(1)}, u32[]{:S(2)}, u32[]{:S(2)}) collective-permute-start(bf16[256,256]{1,0:T(8,128)(2,1)} %get-tuple-element.72), channel_id=1, source_target_pairs={{0,8},{2,10},{4,12},{6,14},{8,0},{10,2},{12,4},{14,6},{16,24},{18,... | collective-permute-start | bytes 393224 | tf_op jit(solution)/shard_map/ppermute | solution.py:438
  125.4 2.3 %collective-permute-start.25 = (bf16[256,256]{1,0:T(8,128)(2,1)}, bf16[256,256]{1,0:T(8,128)(2,1)}, u32[]{:S(2)}, u32[]{:S(2)}) collective-permute-start(bf16[256,256]{1,0:T(8,128)(2,1)} %get-tuple-element.74), channel_id=1, source_target_pairs={{0,24},{2,26},{4,28},{6,30},{8,16},{10,18},{12,20},{14,22},{16,8},... | collective-permute-start | bytes 393224 | tf_op jit(solution)/shard_map/ppermute | solution.py:438
  127.7 2.2 %collective-permute-done.23.refs_1_ = bf16[256,256]{1,0:T(8,128)(2,1)S(1)} collective-permute-done((bf16[256,256]{1,0:T(8,128)(2,1)}, bf16[256,256]{1,0:T(8,128)(2,1)S(1)}, u32[]{:S(2)}, u32[]{:S(2)}) %collective-permute-start.23) | collective-permute-done | bytes 131104 | tf_op jit(solution)/shard_map/ppermute | solution.py:438
  129.9 8.1 %collective-permute-done.24.refs_2_ = bf16[256,256]{1,0:T(8,128)(2,1)S(1)} collective-permute-done((bf16[256,256]{1,0:T(8,128)(2,1)}, bf16[256,256]{1,0:T(8,128)(2,1)S(1)}, u32[]{:S(2)}, u32[]{:S(2)}) %collective-permute-start.24) | collective-permute-done | bytes 131104 | tf_op jit(solution)/shard_map/ppermute | solution.py:438
  143.4 5.6 %shard_map.160 = (f32[128,768]{1,0:T(8,128)}, bf16[128,768]{1,0:T(8,128)(2,1)}, bf16[128,768]{1,0:T(8,128)(2,1)}, bf16[128,768]{1,0:T(8,128)(2,1)}) custom-call(s32[12]{0:T(128)} %stack.136.where_ref, bf16[256,256]{1,0:T(8,128)(2,1)} %get-tuple-element.71.refs_0_, bf16[256,256]{1,0:T(8,128)(2,1)} %copy-done.32, bf16[256,256]{1,0:T(8,128)(2,1)} %copy-done.33, ...), custom_call_target="tpu_custom_call" | custom-call | flops 805306368 | bytes 3145728 | tf_op jit(solution)/shard_map/pallas_call | solution.py:304
  149.0 1.6 collective-permute-start.36
  150.6 1.8 %collective-permute-start.38 = (bf16[128,768]{1,0:T(8,128)(2,1)}, bf16[128,768]{1,0:T(8,128)(2,1)S(1)}, u32[]{:S(2)}, u32[]{:S(2)}) collective-permute-start(bf16[128,768]{1,0:T(8,128)(2,1)} %get-tuple-element.85), channel_id=1, source_target_pairs={{0,9},{1,8},{2,11},{3,10},{4,13},{5,12},{6,15},{7,14},{8,1},{9,0},... | collective-permute-start | bytes 589832 | tf_op jit(solution)/shard_map/ppermute | solution.py:376
  152.7 1.9 %shard_map.161 = (bf16[128,1024]{1,0:T(8,128)(2,1)}, bf16[128,1024]{1,0:T(8,128)(2,1)}) custom-call(s32[1]{0:T(128)} %bitcast.member_ref, bf16[128,512]{1,0:T(8,128)(2,1)} %get-tuple-element.86.refs_2_.refs_0_, bf16[128,512]{1,0:T(8,128)(2,1)} %copy-done.29, bf16[128,512]{1,0:T(8,128)(2,1)} %copy-done.30, bf16[128,512]{1,0:T(8,128)(2,1)} %copy-done.31), custom_call_target="tpu_custom_call" | custom-call | tf_op jit(solution)/shard_map/pallas_call | solution.py:259
  154.6 5.8 %collective-permute-done.36 = bf16[128,768]{1,0:T(8,128)(2,1)S(1)} collective-permute-done((bf16[128,768]{1,0:T(8,128)(2,1)}, bf16[128,768]{1,0:T(8,128)(2,1)S(1)}, u32[]{:S(2)}, u32[]{:S(2)}) %collective-permute-start.36) | collective-permute-done | bytes 196640 | tf_op jit(solution)/shard_map/ppermute | solution.py:368
  (143 shorter events, 27.3 us)
Async XLA Ops:
  2.9 12.2 %collective-permute-start = (bf16[64,3072]{1,0:T(8,128)(2,1)S(1)}, bf16[64,3072]{1,0:T(8,128)(2,1)S(1)}, u32[]{:S(2)}, u32[]{:S(2)}) collective-permute-start(bf16[64,3072]{1,0:T(8,128)(2,1)S(1)} %constant_dynamic-slice_fusion), channel_id=1, source_target_pairs={{0,8},{2,10},{4,12},{6,14},{8,0},{10,2},{12,4},{14,6},{16,24},{18,... | collective-permute-start | bytes 1179656 | tf_op jit(solution)/shard_map/ppermute | solution.py:359
  6.0 9.1 %collective-permute-start.1 = (bf16[64,3072]{1,0:T(8,128)(2,1)S(1)}, bf16[64,3072]{1,0:T(8,128)(2,1)S(1)}, u32[]{:S(2)}, u32[]{:S(2)}) collective-permute-start(bf16[64,3072]{1,0:T(8,128)(2,1)S(1)} %constant_dynamic-slice_fusion), channel_id=1, source_target_pairs={{8,16},{10,18},{12,20},{14,22},{16,8},{18,10},{20,12},{22,14},{9,1... | collective-permute-start | bytes 1179656 | tf_op jit(solution)/shard_map/ppermute | solution.py:359
  9.5 17.6 %collective-permute-start.8 = (bf16[832,256]{1,0:T(8,128)(2,1)}, bf16[832,256]{1,0:T(8,128)(2,1)S(1)}, u32[]{:S(2)}, u32[]{:S(2)}) collective-permute-start(bf16[832,256]{1,0:T(8,128)(2,1)} %get-tuple-element.55.refs_9_.refs_8_), channel_id=1, source_target_pairs={{0,4},{2,6},{4,0},{6,2},{8,12},{10,14},{12,8},{14,10},{16,20},{18,... | collective-permute-start | bytes 1277960 | tf_op jit(solution)/shard_map/ppermute | solution.py:365
  15.9 15.2 %collective-permute-start.2 = (bf16[832,256]{1,0:T(8,128)(2,1)}, bf16[832,256]{1,0:T(8,128)(2,1)S(1)}, u32[]{:S(2)}, u32[]{:S(2)}) collective-permute-start(bf16[832,256]{1,0:T(8,128)(2,1)} %get-tuple-element.47), channel_id=1, source_target_pairs={{0,8},{2,10},{4,12},{6,14},{8,0},{10,2},{12,4},{14,6},{16,24},{18,... | collective-permute-start | bytes 1277960 | tf_op jit(solution)/shard_map/ppermute | solution.py:359
  19.9 7.3 %collective-permute-start.3 = (bf16[64,3072]{1,0:T(8,128)(2,1)}, bf16[64,3072]{1,0:T(8,128)(2,1)}, u32[]{:S(2)}, u32[]{:S(2)}) collective-permute-start(bf16[64,3072]{1,0:T(8,128)(2,1)} %copy-done.24), channel_id=1, source_target_pairs={{8,16},{10,18},{12,20},{14,22},{16,8},{18,10},{20,12},{22,14},{9,1... | collective-permute-start | bytes 1179656 | tf_op jit(solution)/shard_map/ppermute | solution.py:359
  21.3 19.0 %collective-permute-start.6 = (bf16[64,3072]{1,0:T(8,128)(2,1)S(1)}, bf16[64,3072]{1,0:T(8,128)(2,1)}, u32[]{:S(2)}, u32[]{:S(2)}) collective-permute-start(bf16[64,3072]{1,0:T(8,128)(2,1)S(1)} %collective-permute-done.1), channel_id=1, source_target_pairs={{8,0},{10,2},{12,4},{14,6},{16,24},{18,26},{20,28},{22,30},{9,1},{... | collective-permute-start | bytes 1179656 | tf_op jit(solution)/shard_map/ppermute | solution.py:359
  22.6 38.3 %collective-permute-start.11 = (bf16[832,256]{1,0:T(8,128)(2,1)}, bf16[832,256]{1,0:T(8,128)(2,1)S(1)}, u32[]{:S(2)}, u32[]{:S(2)}) collective-permute-start(bf16[832,256]{1,0:T(8,128)(2,1)} %get-tuple-element.53), channel_id=1, source_target_pairs={{0,16},{2,18},{4,20},{6,22},{8,24},{10,26},{12,28},{14,30},{16,0},... | collective-permute-start | bytes 1277960 | tf_op jit(solution)/shard_map/ppermute | solution.py:359
  27.2 37.0 %collective-permute-start.9 = (bf16[64,3072]{1,0:T(8,128)(2,1)}, bf16[64,3072]{1,0:T(8,128)(2,1)S(1)}, u32[]{:S(2)}, u32[]{:S(2)}) collective-permute-start(bf16[64,3072]{1,0:T(8,128)(2,1)} %collective-permute-done.3), channel_id=1, source_target_pairs={{8,0},{10,2},{12,4},{14,6},{16,24},{18,26},{20,28},{22,30},{9,1},{... | collective-permute-start | bytes 1179656 | tf_op jit(solution)/shard_map/ppermute | solution.py:359
  31.1 33.1 %collective-permute-start.4 = (bf16[832,256]{1,0:T(8,128)(2,1)S(1)}, bf16[832,256]{1,0:T(8,128)(2,1)S(1)}, u32[]{:S(2)}, u32[]{:S(2)}) collective-permute-start(bf16[832,256]{1,0:T(8,128)(2,1)S(1)} %collective-permute-done.2.refs_13_.refs_12_), channel_id=1, source_target_pairs={{0,4},{2,6},{4,0},{6,2},{8,12},{10,14},{12,8},{14,10},{16,20},{18,... | collective-permute-start | bytes 1277960 | tf_op jit(solution)/shard_map/ppermute | solution.py:365
  41.3 36.2 %collective-permute-start.7 = (bf16[64,3072]{1,0:T(8,128)(2,1)S(1)}, bf16[64,3072]{1,0:T(8,128)(2,1)S(1)}, u32[]{:S(2)}, u32[]{:S(2)}) collective-permute-start(bf16[64,3072]{1,0:T(8,128)(2,1)S(1)} %broadcast_select_fusion.1.refs_3_), channel_id=1, source_target_pairs={{0,1},{1,0},{2,3},{3,2},{4,5},{5,4},{6,7},{7,6},{8,9},{9,8},{10,11... | collective-permute-start | bytes 1179656 | tf_op jit(solution)/shard_map/ppermute | solution.py:368
  42.9 24.4 %collective-permute-start.19 = (bf16[832,256]{1,0:T(8,128)(2,1)S(1)}, bf16[832,256]{1,0:T(8,128)(2,1)S(1)}, u32[]{:S(2)}, u32[]{:S(2)}) collective-permute-start(bf16[832,256]{1,0:T(8,128)(2,1)S(1)} %copy-done.37), channel_id=1, source_target_pairs={{0,24},{2,26},{4,28},{6,30},{8,16},{10,18},{12,20},{14,22},{16,8},... | collective-permute-start | bytes 1277960 | tf_op jit(solution)/shard_map/ppermute | solution.py:359
  64.2 12.9 %collective-permute-start.12 = (bf16[832,256]{1,0:T(8,128)(2,1)S(1)}, bf16[832,256]{1,0:T(8,128)(2,1)}, u32[]{:S(2)}, u32[]{:S(2)}) collective-permute-start(bf16[832,256]{1,0:T(8,128)(2,1)S(1)} %collective-permute-done.11.refs_17_.refs_16_), channel_id=1, source_target_pairs={{0,4},{2,6},{4,0},{6,2},{8,12},{10,14},{12,8},{14,10},{16,20},{18,... | collective-permute-start | bytes 1277960 | tf_op jit(solution)/shard_map/ppermute | solution.py:365
  65.7 11.9 %collective-permute-start.10 = (bf16[64,3072]{1,0:T(8,128)(2,1)S(1)}, bf16[64,3072]{1,0:T(8,128)(2,1)S(1)}, u32[]{:S(2)}, u32[]{:S(2)}) collective-permute-start(bf16[64,3072]{1,0:T(8,128)(2,1)S(1)} %broadcast_select_fusion.refs_5_), channel_id=1, source_target_pairs={{0,1},{1,0},{2,3},{3,2},{4,5},{5,4},{6,7},{7,6},{8,9},{9,8},{10,11... | collective-permute-start | bytes 1179656 | tf_op jit(solution)/shard_map/ppermute | solution.py:368
  67.3 14.6 %collective-permute-start.20 = (bf16[832,256]{1,0:T(8,128)(2,1)S(1)}, bf16[832,256]{1,0:T(8,128)(2,1)}, u32[]{:S(2)}, u32[]{:S(2)}) collective-permute-start(bf16[832,256]{1,0:T(8,128)(2,1)S(1)} %collective-permute-done.19.refs_21_.refs_20_), channel_id=1, source_target_pairs={{0,4},{2,6},{4,0},{6,2},{8,12},{10,14},{12,8},{14,10},{16,20},{18,... | collective-permute-start | bytes 1277960 | tf_op jit(solution)/shard_map/ppermute | solution.py:365
  77.0 12.2 %collective-permute-start.13 = (bf16[832,256]{1,0:T(8,128)(2,1)S(1)}, bf16[832,256]{1,0:T(8,128)(2,1)S(1)}, u32[]{:S(2)}, u32[]{:S(2)}) collective-permute-start(bf16[832,256]{1,0:T(8,128)(2,1)S(1)} %copy-done.2), channel_id=1, source_target_pairs={{0,2},{2,0},{4,6},{6,4},{8,10},{10,8},{12,14},{14,12},{16,18},{18,... | collective-permute-start | bytes 1277960 | tf_op jit(solution)/shard_map/ppermute | solution.py:365
  77.0 12.7 %collective-permute-start.14 = (bf16[832,256]{1,0:T(8,128)(2,1)S(1)}, bf16[832,256]{1,0:T(8,128)(2,1)S(1)}, u32[]{:S(2)}, u32[]{:S(2)}) collective-permute-start(bf16[832,256]{1,0:T(8,128)(2,1)S(1)} %collective-permute-done.8.refs_10_.refs_9_), channel_id=1, source_target_pairs={{0,2},{2,0},{4,6},{6,4},{8,10},{10,8},{12,14},{14,12},{16,18},{18,... | collective-permute-start | bytes 1277960 | tf_op jit(solution)/shard_map/ppermute | solution.py:365
  77.5 12.3 %collective-permute-start.15 = (bf16[832,256]{1,0:T(8,128)(2,1)S(1)}, bf16[832,256]{1,0:T(8,128)(2,1)S(1)}, u32[]{:S(2)}, u32[]{:S(2)}) collective-permute-start(bf16[832,256]{1,0:T(8,128)(2,1)S(1)} %collective-permute-done.2.refs_13_.refs_12_), channel_id=1, source_target_pairs={{0,2},{2,0},{4,6},{6,4},{8,10},{10,8},{12,14},{14,12},{16,18},{18,... | collective-permute-start | bytes 1277960 | tf_op jit(solution)/shard_map/ppermute | solution.py:365
  77.7 11.5 %collective-permute-start.5 = (bf16[64,3072]{1,0:T(8,128)(2,1)S(1)}, bf16[64,3072]{1,0:T(8,128)(2,1)S(1)}, u32[]{:S(2)}, u32[]{:S(2)}) collective-permute-start(bf16[64,3072]{1,0:T(8,128)(2,1)S(1)} %copy-done.25), channel_id=1, source_target_pairs={{0,1},{1,0},{2,3},{3,2},{4,5},{5,4},{6,7},{7,6},{8,9},{9,8},{10,11... | collective-permute-start | bytes 1179656 | tf_op jit(solution)/shard_map/ppermute | solution.py:368
  82.0 8.3 %collective-permute-start.16 = (bf16[832,256]{1,0:T(8,128)(2,1)S(1)}, bf16[832,256]{1,0:T(8,128)(2,1)S(1)}, u32[]{:S(2)}, u32[]{:S(2)}) collective-permute-start(bf16[832,256]{1,0:T(8,128)(2,1)S(1)} %collective-permute-done.4.refs_14_.refs_13_), channel_id=1, source_target_pairs={{0,2},{2,0},{4,6},{6,4},{8,10},{10,8},{12,14},{14,12},{16,18},{18,... | collective-permute-start | bytes 1277960 | tf_op jit(solution)/shard_map/ppermute | solution.py:365
  89.8 3.2 %collective-permute-start.22 = (bf16[832,256]{1,0:T(8,128)(2,1)}, bf16[832,256]{1,0:T(8,128)(2,1)S(1)}, u32[]{:S(2)}, u32[]{:S(2)}) collective-permute-start(bf16[832,256]{1,0:T(8,128)(2,1)} %collective-permute-done.20.refs_22_.refs_21_), channel_id=1, source_target_pairs={{0,2},{2,0},{4,6},{6,4},{8,10},{10,8},{12,14},{14,12},{16,18},{18,... | collective-permute-start | bytes 1277960 | tf_op jit(solution)/shard_map/ppermute | solution.py:365
  91.4 28.6 %collective-permute-start.29 = (bf16[192,1024]{1,0:T(8,128)(2,1)}, bf16[192,1024]{1,0:T(8,128)(2,1)}, u32[]{:S(2)}, u32[]{:S(2)}) collective-permute-start(bf16[192,1024]{1,0:T(8,128)(2,1)} %bitcast.32.refs_4_), channel_id=1, source_target_pairs={{0,16},{2,18},{4,20},{6,22},{8,24},{10,26},{12,28},{14,30},{16,0},... | collective-permute-start | bytes 1179656 | tf_op jit(solution)/shard_map/ppermute | solution.py:359
  102.3 17.7 %collective-permute-start.30 = (bf16[128,512]{1,0:T(8,128)(2,1)}, bf16[128,512]{1,0:T(8,128)(2,1)S(1)}, u32[]{:S(2)}, u32[]{:S(2)}) collective-permute-start(bf16[128,512]{1,0:T(8,128)(2,1)} %get-tuple-element.68.refs_3_), channel_id=1, source_target_pairs={{0,8},{2,10},{4,12},{6,14},{8,0},{10,2},{12,4},{14,6},{16,24},{18,... | collective-permute-start | bytes 393224 | tf_op jit(solution)/shard_map/ppermute | solution.py:438
  104.7 15.8 %collective-permute-start.31 = (bf16[128,512]{1,0:T(8,128)(2,1)}, bf16[128,512]{1,0:T(8,128)(2,1)S(1)}, u32[]{:S(2)}, u32[]{:S(2)}) collective-permute-start(bf16[128,512]{1,0:T(8,128)(2,1)} %get-tuple-element.69.refs_4_), channel_id=1, source_target_pairs={{0,16},{2,18},{4,20},{6,22},{8,24},{10,26},{12,28},{14,30},{16,0},... | collective-permute-start | bytes 393224 | tf_op jit(solution)/shard_map/ppermute | solution.py:438
  105.2 15.3 %collective-permute-start.32 = (bf16[128,512]{1,0:T(8,128)(2,1)}, bf16[128,512]{1,0:T(8,128)(2,1)S(1)}, u32[]{:S(2)}, u32[]{:S(2)}) collective-permute-start(bf16[128,512]{1,0:T(8,128)(2,1)} %get-tuple-element.70.refs_5_), channel_id=1, source_target_pairs={{0,24},{2,26},{4,28},{6,30},{8,16},{10,18},{12,20},{14,22},{16,8},... | collective-permute-start | bytes 393224 | tf_op jit(solution)/shard_map/ppermute | solution.py:438
  107.8 31.4 %collective-permute-start.26 = (bf16[192,1024]{1,0:T(8,128)(2,1)}, bf16[192,1024]{1,0:T(8,128)(2,1)S(1)}, u32[]{:S(2)}, u32[]{:S(2)}) collective-permute-start(bf16[192,1024]{1,0:T(8,128)(2,1)} %bitcast.32.refs_4_), channel_id=1, source_target_pairs={{0,4},{2,6},{4,0},{6,2},{8,12},{10,14},{12,8},{14,10},{16,20},{18,... | collective-permute-start | bytes 1179656 | tf_op jit(solution)/shard_map/ppermute | solution.py:365
  120.5 18.7 %collective-permute-start.33 = (bf16[192,1024]{1,0:T(8,128)(2,1)}, bf16[192,1024]{1,0:T(8,128)(2,1)S(1)}, u32[]{:S(2)}, u32[]{:S(2)}) collective-permute-start(bf16[192,1024]{1,0:T(8,128)(2,1)} %collective-permute-done.29.refs_8_), channel_id=1, source_target_pairs={{0,4},{2,6},{4,0},{6,2},{8,12},{10,14},{12,8},{14,10},{16,20},{18,... | collective-permute-start | bytes 1179656 | tf_op jit(solution)/shard_map/ppermute | solution.py:365
  122.1 7.8 %collective-permute-start.23 = (bf16[256,256]{1,0:T(8,128)(2,1)}, bf16[256,256]{1,0:T(8,128)(2,1)S(1)}, u32[]{:S(2)}, u32[]{:S(2)}) collective-permute-start(bf16[256,256]{1,0:T(8,128)(2,1)} %get-tuple-element.72), channel_id=1, source_target_pairs={{0,8},{2,10},{4,12},{6,14},{8,0},{10,2},{12,4},{14,6},{16,24},{18,... | collective-permute-start | bytes 393224 | tf_op jit(solution)/shard_map/ppermute | solution.py:438
  125.3 12.7 %collective-permute-start.24 = (bf16[256,256]{1,0:T(8,128)(2,1)}, bf16[256,256]{1,0:T(8,128)(2,1)S(1)}, u32[]{:S(2)}, u32[]{:S(2)}) collective-permute-start(bf16[256,256]{1,0:T(8,128)(2,1)} %get-tuple-element.73), channel_id=1, source_target_pairs={{0,16},{2,18},{4,20},{6,22},{8,24},{10,26},{12,28},{14,30},{16,0},... | collective-permute-start | bytes 393224 | tf_op jit(solution)/shard_map/ppermute | solution.py:438
  125.4 13.3 %collective-permute-start.25 = (bf16[256,256]{1,0:T(8,128)(2,1)}, bf16[256,256]{1,0:T(8,128)(2,1)}, u32[]{:S(2)}, u32[]{:S(2)}) collective-permute-start(bf16[256,256]{1,0:T(8,128)(2,1)} %get-tuple-element.74), channel_id=1, source_target_pairs={{0,24},{2,26},{4,28},{6,30},{8,16},{10,18},{12,20},{14,22},{16,8},... | collective-permute-start | bytes 393224 | tf_op jit(solution)/shard_map/ppermute | solution.py:438
  149.0 11.4 %collective-permute-start.36 = (bf16[128,768]{1,0:T(8,128)(2,1)}, bf16[128,768]{1,0:T(8,128)(2,1)S(1)}, u32[]{:S(2)}, u32[]{:S(2)}) collective-permute-start(bf16[128,768]{1,0:T(8,128)(2,1)} %get-tuple-element.83), channel_id=1, source_target_pairs={{0,1},{1,0},{2,3},{3,2},{4,5},{5,4},{6,7},{7,6},{8,9},{9,8},{10,11... | collective-permute-start | bytes 589832 | tf_op jit(solution)/shard_map/ppermute | solution.py:368
  150.6 10.8 %collective-permute-start.38 = (bf16[128,768]{1,0:T(8,128)(2,1)}, bf16[128,768]{1,0:T(8,128)(2,1)S(1)}, u32[]{:S(2)}, u32[]{:S(2)}) collective-permute-start(bf16[128,768]{1,0:T(8,128)(2,1)} %get-tuple-element.85), channel_id=1, source_target_pairs={{0,9},{1,8},{2,11},{3,10},{4,13},{5,12},{6,15},{7,14},{8,1},{9,0},... | collective-permute-start | bytes 589832 | tf_op jit(solution)/shard_map/ppermute | solution.py:376
  152.4 9.4 %collective-permute-start.37 = (bf16[128,768]{1,0:T(8,128)(2,1)}, bf16[128,768]{1,0:T(8,128)(2,1)S(1)}, u32[]{:S(2)}, u32[]{:S(2)}) collective-permute-start(bf16[128,768]{1,0:T(8,128)(2,1)} %get-tuple-element.84), channel_id=1, source_target_pairs={{0,8},{1,9},{2,10},{3,11},{4,12},{5,13},{6,14},{7,15},{8,0},{9,1},... | collective-permute-start | bytes 589832 | tf_op jit(solution)/shard_map/ppermute | solution.py:376
  (45 other events, 599.0 us)

commit v5 on v2

v5 whole, which is shorter than its diff:
```python
import functools
import math

import jax
import jax.numpy as jnp
from jax import lax
from jax.experimental import pallas as pl
from jax.experimental.pallas import tpu as pltpu
from jax.sharding import PartitionSpec as P

INNER = 4
VMEM_BYTES = 60 * 1024 * 1024


def modulate(image, mod_shift, mod_scale):
    values = image.astype(jnp.float32)
    center = jnp.mean(values, axis=-1, keepdims=True)
    spread = jnp.mean(jnp.square(values - center), axis=-1, keepdims=True)
    normed = (values - center) * lax.rsqrt(spread + 1e-06)
    return ((1.0 + mod_scale) * normed + mod_shift).astype(jnp.bfloat16)


def after(x, *deps):
    return lax.optimization_barrier((x,) + deps)[0]


def nt_dot(a, b):
    return lax.dot_general(a, b, (((1,), (1,)), ((), ())), preferred_element_type=jnp.float32)


def norm_heads(x, gain):
    power = jnp.mean(x * x, axis=-1, keepdims=True)
    return (x * lax.rsqrt(power + 1e-06) * gain).astype(jnp.bfloat16)


def patch_kernel(depth, n_pieces, counts, where_ref, *refs):
    n_patches = len(counts)
    tk_ref, tv_ref, qg_ref, kg_ref = refs[:4]
    shares, refs = refs[4 : 4 + sum(counts)], refs[4 + sum(counts) :]
    pieces, refs = refs[:n_pieces], refs[n_pieces:]
    outs, (x_ref, held, scores, expos, x_sem, w_sem, k_sem) = refs[:n_patches], refs[n_patches:]
    rows, width = outs[0].shape[0] // 2, outs[0].shape[1] // 2
    head_size = qg_ref.shape[1]
    groups = [slice(g * rows, (g + 1) * rows) for g in range(n_patches)]
    owns, x_copies, at = [], [], 1 + n_pieces
    for g, count in enumerate(counts):
        owns.append(where_ref[at])
        for i in range(count):
            share = shares[len(x_copies)]
            first = pl.multiple_of(g * rows + where_ref[at + 1 + i], 16)
            x_copies.append(
                pltpu.make_async_copy(
                    share, x_ref.at[pl.ds(first, share.shape[0])], x_sem.at[len(x_copies)]
                )
            )
        at += 1 + count
    parts = ((pl.ds(0, 3 * depth), w_sem), (pl.ds(3 * depth, 2 * rows), k_sem))
    w_copies, k_copies = [
        [
            pltpu.make_async_copy(piece.at[part], held.at[where_ref[1 + i], part], sem.at[i])
            for i, piece in enumerate(pieces)
        ]
        for part, sem in parts
    ]
    for copy in x_copies + w_copies + k_copies:
        copy.start()
    for copy in x_copies:
        copy.wait()

    chunk = INNER * depth
    proj = [jnp.zeros((n_patches * rows, width), jnp.float32) for _ in range(3)]
    if chunk % 128 == 0:
        for first in range(0, n_pieces, INNER):
            for copy in w_copies[first : first + INNER]:
                copy.wait()
            place = where_ref[1 + first] // INNER
            part = x_ref[:, pl.ds(pl.multiple_of(place * chunk, 128), chunk)]
            for i in range(3):
                weight = held[pl.ds(place * INNER, INNER), i * depth : (i + 1) * depth, :]
                proj[i] += jnp.dot(
                    part, weight.reshape(chunk, width), preferred_element_type=jnp.float32
                )
    else:
        for copy in w_copies:
            copy.wait()
        for i in range(3):
            weight = held[:, i * depth : (i + 1) * depth, :]
            proj[i] += jnp.dot(
                x_ref[...],
                weight.reshape(n_pieces * depth, width),
                preferred_element_type=jnp.float32,
            )
    q_proj, k_proj, v_proj = proj
    for copy in k_copies:
        copy.wait()

    v_new = v_proj.astype(jnp.bfloat16)
    k0, v0 = 3 * depth, 3 * depth + rows
    scale = math.log2(math.e) / math.sqrt(head_size)
    own_cols = [pl.ds(pl.multiple_of(own * rows, 128), rows) for own in owns]
    for h in range(width // head_size):
        cols = slice(h * head_size, (h + 1) * head_size)
        beside = slice(width + cols.start, width + cols.stop)
        query = norm_heads(q_proj[:, cols], qg_ref[...])
        key = norm_heads(k_proj[:, cols], kg_ref[...])
        value = v_new[:, cols]
        keys = held[:, k0 : k0 + rows, cols].reshape(n_pieces * rows, head_size)
        values = held[:, v0 : v0 + rows, cols].reshape(n_pieces * rows, head_size)
        scores[h] = nt_dot(query, keys)
        for g, group in enumerate(groups):
            scores[h, group, own_cols[g]] = nt_dot(query[group], key[group])
            outs[g][:rows, beside] = key[group]
            outs[g][rows:, beside] = value[group]
        text_s = nt_dot(query, tk_ref[:, cols])
        image_s = scores[h]
        largest = jnp.maximum(
            jnp.max(text_s, axis=-1, keepdims=True), jnp.max(image_s, axis=-1, keepdims=True)
        )
        text_e = jnp.exp2((text_s - largest) * scale)
        image_e = jnp.exp2((image_s - largest) * scale)
        total = jnp.sum(text_e, axis=-1, keepdims=True) + jnp.sum(image_e, axis=-1, keepdims=True)
        expos[h] = image_e.astype(jnp.bfloat16)
        fresh_mix = []
        for g, group in enumerate(groups):
            fresh_mix.append(
                jnp.dot(
                    expos[h, group, own_cols[g]], value[group], preferred_element_type=jnp.float32
                )
            )
            expos[h, group, own_cols[g]] = jnp.zeros((rows, rows), jnp.bfloat16)
        mixture = (
            jnp.dot(text_e.astype(jnp.bfloat16), tv_ref[:, cols], preferred_element_type=jnp.float32)
            + jnp.dot(expos[h], values, preferred_element_type=jnp.float32)
            + jnp.concatenate(fresh_mix, axis=0)
        )
        attended = (mixture / total).astype(jnp.bfloat16)
        for g, group in enumerate(groups):
            first = pl.multiple_of(lax.rem(owns[g] // INNER, 2) * rows, 16)
            for out in outs[g // 2 * 2 : g // 2 * 2 + 2]:
                out[pl.ds(first, rows), cols] = attended[group]


def attend_patches(where, patches, text_keys, text_values, query_gain, key_gain, pieces, depth):
    shares = [x for patch in patches for x in patch]
    model_width, width = shares[0].shape[1], pieces[0].shape[1]
    rows = sum(x.shape[0] for x in patches[0])
    n, n_pieces, texts, head_size = len(patches), len(pieces), text_keys.shape[0], query_gain.shape[0]
    heads, n_keys = width // head_size, n_pieces * rows
    whole = lambda i, w: (0, 0)
    return pl.pallas_call(
        functools.partial(patch_kernel, depth, n_pieces, [len(x) for x in patches]),
        grid_spec=pltpu.PrefetchScalarGridSpec(
            num_scalar_prefetch=1,
            grid=(1,),
            in_specs=[pl.BlockSpec((texts, width), lambda i, w: (0, w[0]))] * 2
            + [pl.BlockSpec((1, head_size), whole)] * 2
            + [pl.BlockSpec(memory_space=pl.ANY)] * (len(shares) + n_pieces),
            out_specs=[pl.BlockSpec((2 * rows, 2 * width), whole)] * n,
            scratch_shapes=[
                pltpu.VMEM((n * rows, model_width), jnp.bfloat16),
                pltpu.VMEM((n_pieces,) + pieces[0].shape, jnp.bfloat16),
                pltpu.VMEM((heads, n * rows, n_keys), jnp.float32),
                pltpu.VMEM((heads, n * rows, n_keys), jnp.bfloat16),
                pltpu.SemaphoreType.DMA((len(shares),)),
                pltpu.SemaphoreType.DMA((n_pieces,)),
                pltpu.SemaphoreType.DMA((n_pieces,)),
            ],
        ),
        out_shape=[jax.ShapeDtypeStruct((2 * rows, 2 * width), jnp.bfloat16)] * n,
        compiler_params=pltpu.CompilerParams(vmem_limit_bytes=VMEM_BYTES),
        cost_estimate=pl.CostEstimate(
            flops=2 * n * rows * (model_width * 3 * width + 2 * (texts + n_keys) * width),
            bytes_accessed=2 * n_pieces * pieces[0].size,
            transcendentals=n * rows * (texts + n_keys) * heads,
        ),
    )(
        where,
        text_keys,
        text_values,
        query_gain.reshape(1, -1),
        key_gain.reshape(1, -1),
        *shares,
        *pieces,
    )


def deal_kernel(n_arrays, team, member_ref, *refs):
    arrays, outs = refs[:n_arrays], refs[n_arrays:]
    width = outs[0].shape[1]
    for k in range(team):
        at = member_ref[0] ^ k
        cols = pl.ds(pl.multiple_of(at * width, 128), width)
        first = 0
        for x in arrays:
            rows = x.shape[0]
            outs[k][first : first + rows, :] = x[:, cols]
            first += rows


def deal(member, arrays, team):
    width = arrays[0].shape[1] // team
    shape = jax.ShapeDtypeStruct((sum(x.shape[0] for x in arrays), width), jnp.bfloat16)
    return pl.pallas_call(
        functools.partial(deal_kernel, len(arrays), team),
        in_specs=[pl.BlockSpec(memory_space=pltpu.SMEM)]
        + [pl.BlockSpec(memory_space=pltpu.VMEM)] * len(arrays),
        out_specs=[pl.BlockSpec(memory_space=pltpu.VMEM)] * team,
        out_shape=[shape] * team,
        compiler_params=pltpu.CompilerParams(vmem_limit_bytes=VMEM_BYTES),
    )(member.reshape(1), *arrays)


def collect_kernel(team, member_ref, *refs):
    packs, (key_ref, value_ref) = refs[:team], refs[team:]
    rows, width = key_ref.shape[0], key_ref.shape[1] // team
    for s in range(team):
        at = member_ref[0] ^ s
        cols = pl.ds(pl.multiple_of(at * width, 128), width)
        key_ref[:, cols] = packs[s][:rows, width:]
        value_ref[:, cols] = packs[s][rows:, width:]


def collect(member, packs):
    team = len(packs)
    rows, width = packs[0].shape[0] // 2, packs[0].shape[1] // 2
    shape = jax.ShapeDtypeStruct((rows, width * team), jnp.bfloat16)
    return pl.pallas_call(
        functools.partial(collect_kernel, team),
        in_specs=[pl.BlockSpec(memory_space=pltpu.SMEM)]
        + [pl.BlockSpec(memory_space=pltpu.VMEM)] * team,
        out_specs=[pl.BlockSpec(memory_space=pltpu.VMEM)] * 2,
        out_shape=[shape, shape],
        compiler_params=pltpu.CompilerParams(vmem_limit_bytes=VMEM_BYTES),
    )(member.reshape(1), *packs)


def project_kernel(n_packs, n_pieces, n_shares, where_ref, *refs):
    packs, pieces = refs[:n_packs], refs[n_packs : n_packs + n_pieces]
    refs = refs[n_packs + n_pieces :]
    outs, held, sems = refs[:-2], refs[-2], refs[-1]
    rows, width = packs[0].shape[0] // 2, packs[0].shape[1]
    depth = held.shape[1]
    copies = [
        pltpu.make_async_copy(piece, held.at[where_ref[2 + n_shares + i]], sems.at[i])
        for i, piece in enumerate(pieces)
    ]
    for copy in copies:
        copy.start()
    own = pl.multiple_of(where_ref[1] * rows, 16)
    other = pl.multiple_of((1 - where_ref[1]) * rows, 16)
    attended = [
        jnp.concatenate([x[pl.ds(own, rows), :], x[pl.ds(other, rows), :]], axis=0) for x in packs
    ]
    for copy in copies:
        copy.wait()
    for i in reversed(range(n_shares)):
        block = pl.ds(where_ref[2 + i] * INNER, INNER)
        total = jnp.zeros((2 * rows, INNER * depth), jnp.float32)
        for s in range(n_packs):
            cols = pl.ds(pl.multiple_of((where_ref[0] ^ s) * width, 128), width)
            total += nt_dot(attended[s], held[block, :, cols].reshape(INNER * depth, width))
        outs[2 * i][...] = total[:rows].astype(outs[2 * i].dtype)
        outs[2 * i + 1][...] = total[rows:].astype(outs[2 * i + 1].dtype)


def project(where, packs, pieces, n_shares):
    rows, width = packs[0].shape[0] // 2, packs[0].shape[1] // 2
    depth, local_width = pieces[0].shape
    block = INNER * depth
    whole = lambda i, w: (0, 0)
    types = [jnp.float32] + [jnp.bfloat16] * (2 * n_shares - 1)
    return pl.pallas_call(
        functools.partial(project_kernel, len(packs), len(pieces), n_shares),
        grid_spec=pltpu.PrefetchScalarGridSpec(
            num_scalar_prefetch=1,
            grid=(1,),
            in_specs=[pl.BlockSpec((2 * rows, width), whole)] * len(packs)
            + [pl.BlockSpec(memory_space=pl.ANY)] * len(pieces),
            out_specs=[pl.BlockSpec((rows, block), whole)] * len(types),
            scratch_shapes=[
                pltpu.VMEM((len(pieces), depth, local_width), jnp.bfloat16),
                pltpu.SemaphoreType.DMA((len(pieces),)),
            ],
        ),
        out_shape=[jax.ShapeDtypeStruct((rows, block), t) for t in types],
        compiler_params=pltpu.CompilerParams(vmem_limit_bytes=VMEM_BYTES),
        cost_estimate=pl.CostEstimate(
            flops=4 * rows * block * n_shares * local_width,
            bytes_accessed=2 * block * n_shares * local_width,
            transcendentals=0,
        ),
    )(where, *packs, *pieces)


def on_device(
    image,
    mod_shift,
    mod_scale,
    mod_gate,
    w_query,
    w_key,
    w_value,
    query_gain,
    key_gain,
    text_keys,
    text_values,
    stale_keys,
    stale_values,
    w_out,
):
    head_size = query_gain.shape[0]
    rows, model_width = image.shape
    depth, local_width = w_query.shape
    heads = local_width // head_size
    patches = lax.axis_size("patch")
    fsdp = lax.axis_size("fsdp")
    outer = patches // INNER
    team = math.gcd(outer, heads)
    width = local_width // team
    assert outer == 2 * fsdp and team > 1 and team & (team - 1) == 0 and outer & (outer - 1) == 0
    me = lax.axis_index("patch")
    mine = lax.axis_index("fsdp")
    place, seat = me // INNER, me % INNER
    member, parity = place % team, place % 2
    def over_outer(x, pairs):
        pairs = [(a * INNER + k, b * INNER + k) for a, b in pairs for k in range(INNER)]
        return lax.ppermute(x, "patch", pairs)

    def to_partner(x, bits):
        return over_outer(x, [(z, z ^ bits) for z in range(outer)])

    def flip(x, bits):
        return lax.ppermute(x, "patch", [(p, p ^ bits) for p in range(patches)])

    def along_fsdp(x, step):
        return lax.ppermute(x, "fsdp", [(i, (i + step) % fsdp) for i in range(fsdp)])

    def along_both(x, bits, step):
        pairs = [
            (p * fsdp + f, (p ^ (bits * INNER)) * fsdp + (f + step) % fsdp)
            for p in range(patches)
            for f in range(fsdp)
        ]
        return lax.ppermute(x, ("patch", "fsdp"), pairs)

    def spread(piece, side, *deps):
        return [piece, side, flip(after(piece, *deps), 1), flip(after(side, *deps), 1)]

    def shares_of(got):
        return [got] + [along_fsdp(got, i) for i in range(1, fsdp)]

    def seats_of(position):
        return [position * INNER + (seat ^ bits) for bits in (0, 2, 1, 3)]

    modded = modulate(image, mod_shift, mod_scale)
    share = rows // fsdp
    part = lax.dynamic_slice_in_dim(modded, mine * share, share, axis=0)
    dealt = deal(member, (w_query, w_key, w_value, stale_keys, stale_values), team)
    pieces, sides = {0: dealt[0]}, {}
    row_shares = {}
    if outer == 4 and team == 4:
        ends = [(1, 0), (2, 3)]
        middle = [(1, 2), (2, 1)]
        inside = jnp.logical_or(place == 1, place == 2)
        near = to_partner(part, 1)
        across = over_outer(part, middle)
        sides[0] = flip(pieces[0], 2)
        far = over_outer(near, middle)
        pieces[2] = to_partner(after(dealt[2], near, across), 2)
        pieces[1] = to_partner(after(dealt[1], near, across), 1)
        end_across = over_outer(across, ends)
        end_far = over_outer(after(far, sides[0]), ends)
        sides[1] = flip(after(pieces[1], far), 2)
        pieces[3] = to_partner(after(dealt[3], far), 3)
        sides[2] = flip(after(pieces[2], end_far, sides[1]), 2)
        row_shares[1] = shares_of(after(near, pieces[1]))
        row_shares[2] = shares_of(jnp.where(inside, far, end_across))
        row_shares[3] = shares_of(jnp.where(inside, across, end_far))
        late = [sides[2], row_shares[1][-1]]
    else:
        for k in range(1, team):
            row_shares[k] = shares_of(to_partner(part, k))
        for k in range(1, outer):
            pieces[k] = to_partner(dealt[k % team], k)
        late = []
    for k in range(outer):
        if k not in sides:
            sides[k] = flip(pieces[k], 2)
    out_piece = after(w_out.T, sides[outer - 1])
    out_pieces = [out_piece] + [to_partner(out_piece, 2 * k) for k in range(1, fsdp)]

    origins = [o for k in range(outer) for o in seats_of(place ^ k)]
    pieces = [x for k in range(outer) for x in spread(pieces[k], sides[k], *late)]
    patch_rows = [[modded]] + [row_shares[k] for k in range(1, team)]
    where = [member] + origins
    for k in range(team):
        where.append((place ^ k) * INNER + seat)
        where += [((mine + (fsdp - i)) % fsdp) * share for i in range(fsdp)] if k else [0 * mine]
    messages = attend_patches(
        jnp.stack(where).astype(jnp.int32),
        patch_rows,
        text_keys,
        text_values,
        query_gain,
        key_gain,
        pieces,
        depth,
    )

    def give(x, bits):
        return lax.ppermute(x, "patch", [(p, p ^ (bits * INNER)) for p in range(patches)])

    packs = [messages[0]] + [give(messages[k], k) for k in range(1, team)]
    out_sides = [flip(out_pieces[0], 2)]
    out_sides += [flip(after(piece, messages[0]), 2) for piece in out_pieces[1:]]
    out_pieces = [x for p, q in zip(out_pieces, out_sides) for x in spread(p, q, *packs[1:])]
    out_places = [o for k in range(fsdp) for o in seats_of((place ^ (2 * k)) // 2)]
    where = [member, parity] + [(mine + i) % fsdp for i in range(fsdp)] + out_places
    where = jnp.stack(where).astype(jnp.int32)
    partial = project(where, packs, out_pieces, fsdp)
    own, partner = partial[0], [along_both(partial[1], 1, 0)]
    for i in range(1, fsdp):
        own = own + along_fsdp(partial[2 * i], i).astype(jnp.float32)
        partner.append(along_both(partial[2 * i + 1], 1, i))
    other = sum(x.astype(jnp.float32) for x in partner)
    summed = jnp.where(
        parity == 0,
        jnp.concatenate([own, other], axis=1),
        jnp.concatenate([other, own], axis=1),
    )
    key_out, value_out = collect(member, [after(packs[0], partial[0])] + packs[1:])

    out_share = model_width // fsdp
    col_start = mine * out_share
    image_part = lax.dynamic_slice_in_dim(image, col_start, out_share, 1).astype(jnp.float32)
    gate_part = lax.dynamic_slice_in_dim(mod_gate, col_start, out_share, 0)
    hidden = (image_part + gate_part * summed).astype(jnp.bfloat16)
    return (hidden, key_out, value_out)


def solution(mesh):
    return jax.shard_map(
        on_device,
        mesh=mesh,
        in_specs=(
            P("patch", None),
            P(),
            P(),
            P(),
            P("patch", "fsdp"),
            P("patch", "fsdp"),
            P("patch", "fsdp"),
            P(),
            P(),
            P(None, "fsdp"),
            P(None, "fsdp"),
            P("patch", "fsdp"),
            P("patch", "fsdp"),
            P("fsdp", "patch"),
        ),
        out_specs=(P("patch", "fsdp"), P("patch", "fsdp"), P("patch", "fsdp")),
        check_vma=False,
    )
```

time: 165 us -> 160 us (0.970)
  starting transfers between devices: 48.1 us -> 45 us
  waiting for transfers between devices: 82.9 us -> 80.2 us
  Pallas kernels: 24.9 us -> 27.2 us
    ppermute x9, waiting for transfers between devices: 46.7 us -> 40.7 us  [over_outer(): return lax.ppermute(x, 'patch', pairs)]
    ppermute x6 -> x3, starting transfers between devices: 9.02 us -> 4.39 us  [give(): lax.ppermute(x, 'patch', [(p, p ^ bits * INNER) for p in range(patches)])]
    ppermute x18, waiting for transfers between devices: 8.18 us -> 4.38 us  [flip(): return lax.ppermute(x, 'patch', [(p, p ^ bits) for p in range(patches)])]
    ppermute x2, waiting for transfers between devices: 0.84 us -> 4.54 us  [along_both(): return lax.ppermute(x, ('patch', 'fsdp'), pairs)]
    pallas_call x1, Pallas kernels: 14.6 us -> 16.7 us  [attend_patches(): pl.pallas_call(functools.partial(patch_kernel, depth, n_pieces, [len(x) f...]
    ppermute x2, starting transfers between devices: 2.75 us -> 4.8 us  [along_both(): return lax.ppermute(x, ('patch', 'fsdp'), pairs)]
    ppermute x6 -> x3, waiting for transfers between devices: 15.6 us -> 17.3 us  [give(): lax.ppermute(x, 'patch', [(p, p ^ bits * INNER) for p in range(patches)])]
  transfers between devices with their start and end apart: 39 -> 36, of which waited for: 14 -> 19; matrix products, arithmetic and copies ran while one was open for 1% -> 1% of each run, Pallas kernels for 12% -> 13%
where the time goes in v5:
time: 160 us
  waiting for transfers between devices  80.2 us (50%)
  starting transfers between devices  45 us (28%)
  Pallas kernels  27.2 us (17%)
  local copies, waits for them, and re-layouts  3.38 us (2%)
  other arithmetic  3.22 us (2%)
    ppermute x9, waiting for transfers between devices, over_outer(): return lax.ppermute(x, 'patch', pairs)  40.7 us
    ppermute x9, starting transfers between devices, over_outer(): return lax.ppermute(x, 'patch', pairs)  19.1 us
    ppermute x3, waiting for transfers between devices, give(): lax.ppermute(x, 'patch', [(p, p ^ bits * INNER) for p in range(patches)])  17.3 us
    pallas_call x1, Pallas kernels, attend_patches(): pl.pallas_call(functools.partial(patch_kernel, depth, n_pieces, [len(x) f...  16.7 us
    ppermute x4, waiting for transfers between devices, along_fsdp(): lax.ppermute(x, 'fsdp', [(i, (i + step) % fsdp) for i in range(fsdp)])  13.2 us
    ppermute x18, starting transfers between devices, flip(): return lax.ppermute(x, 'patch', [(p, p ^ bits) for p in range(patches)])  10.9 us
    ppermute x4, starting transfers between devices, along_fsdp(): lax.ppermute(x, 'fsdp', [(i, (i + step) % fsdp) for i in range(fsdp)])  5.8 us
    pallas_call x1, Pallas kernels, project(): pl.pallas_call(functools.partial(project_kernel, len(packs), len(pieces),...  5.63 us
  transfers between devices with their start and end apart: 36, of which 19 were waited for; matrix products, arithmetic and copies ran while one was open for 1% of the time, Pallas kernels for 13%

profile of v5, /device:TPU:0, one launch (start us, length us, event | category | flops | bytes accessed | tf_op | source)
XLA Modules:
  0.0 160.0 jit_solution(6910472962036703505)
XLA Ops:
  0.7 1.4 convert_reduce_fusion
  2.9 3.1 %collective-permute-start = (bf16[64,3072]{1,0:T(8,128)(2,1)S(1)}, bf16[64,3072]{1,0:T(8,128)(2,1)}, u32[]{:S(2)}, u32[]{:S(2)}) collective-permute-start(bf16[64,3072]{1,0:T(8,128)(2,1)S(1)} %constant_dynamic-slice_fusion), channel_id=1, source_target_pairs={{0,8},{2,10},{4,12},{6,14},{8,0},{10,2},{12,4},{14,6},{16,24},{18,... | collective-permute-start | bytes 1179656 | tf_op jit(solution)/shard_map/ppermute | solution.py:327
  6.7 2.8 %shard_map.157 = (bf16[832,256]{1,0:T(8,128)(2,1)}, bf16[832,256]{1,0:T(8,128)(2,1)}, bf16[832,256]{1,0:T(8,128)(2,1)}, bf16[832,256]{1,0:T(8,128)(2,1)}) custom-call(s32[1]{0:T(128)} %bitcast.member_ref, bf16[192,1024]{1,0:T(8,128)(2,1)} %refs_0_.2, bf16[192,1024]{1,0:T(8,128)(2,1)} %refs_1_.2, bf16[192,1024]{1,0:T(8,128)(2,1)} %refs_2_.1, ...), custom_call_target="tpu_custom_call" | custom-call | tf_op jit(solution)/shard_map/pallas_call | solution.py:203
  9.5 5.7 %collective-permute-done.refs_5_ = bf16[64,3072]{1,0:T(8,128)(2,1)} collective-permute-done((bf16[64,3072]{1,0:T(8,128)(2,1)S(1)}, bf16[64,3072]{1,0:T(8,128)(2,1)}, u32[]{:S(2)}, u32[]{:S(2)}) %collective-permute-start) | collective-permute-done | bytes 393248 | tf_op jit(solution)/shard_map/ppermute | solution.py:327
  15.2 4.7 %collective-permute-start.2 = (bf16[832,256]{1,0:T(8,128)(2,1)}, bf16[832,256]{1,0:T(8,128)(2,1)}, u32[]{:S(2)}, u32[]{:S(2)}) collective-permute-start(bf16[832,256]{1,0:T(8,128)(2,1)} %get-tuple-element.40), channel_id=1, source_target_pairs={{0,8},{2,10},{4,12},{6,14},{8,0},{10,2},{12,4},{14,6},{16,24},{18,... | collective-permute-start | bytes 1277960 | tf_op jit(solution)/shard_map/ppermute | solution.py:327
  19.9 1.5 collective-permute-start.7
  22.1 2.8 %collective-permute-start.10 = (bf16[832,256]{1,0:T(8,128)(2,1)}, bf16[832,256]{1,0:T(8,128)(2,1)}, u32[]{:S(2)}, u32[]{:S(2)}) collective-permute-start(bf16[832,256]{1,0:T(8,128)(2,1)} %get-tuple-element.45), channel_id=1, source_target_pairs={{0,16},{2,18},{4,20},{6,22},{8,24},{10,26},{12,28},{14,30},{16,0},... | collective-permute-start | bytes 1277960 | tf_op jit(solution)/shard_map/ppermute | solution.py:327
  24.8 5.6 %collective-permute-done.2.refs_15_ = bf16[832,256]{1,0:T(8,128)(2,1)} collective-permute-done((bf16[832,256]{1,0:T(8,128)(2,1)}, bf16[832,256]{1,0:T(8,128)(2,1)}, u32[]{:S(2)}, u32[]{:S(2)}) %collective-permute-start.2) | collective-permute-done | bytes 426016 | tf_op jit(solution)/shard_map/ppermute | solution.py:327
  30.5 1.5 collective-permute-start.11
  35.4 2.7 %collective-permute-start.19 = (bf16[832,256]{1,0:T(8,128)(2,1)}, bf16[832,256]{1,0:T(8,128)(2,1)}, u32[]{:S(2)}, u32[]{:S(2)}) collective-permute-start(bf16[832,256]{1,0:T(8,128)(2,1)} %get-tuple-element.55), channel_id=1, source_target_pairs={{0,24},{2,26},{4,28},{6,30},{8,16},{10,18},{12,20},{14,22},{16,8},... | collective-permute-start | bytes 1277960 | tf_op jit(solution)/shard_map/ppermute | solution.py:327
  38.1 24.4 %collective-permute-done.10.refs_19_ = bf16[832,256]{1,0:T(8,128)(2,1)} collective-permute-done((bf16[832,256]{1,0:T(8,128)(2,1)}, bf16[832,256]{1,0:T(8,128)(2,1)}, u32[]{:S(2)}, u32[]{:S(2)}) %collective-permute-start.10) | collective-permute-done | bytes 426016 | tf_op jit(solution)/shard_map/ppermute | solution.py:327
  62.5 1.5 collective-permute-start.3
  64.0 2.0 %collective-permute-done.8 = bf16[64,3072]{1,0:T(8,128)(2,1)S(1)} collective-permute-done((bf16[64,3072]{1,0:T(8,128)(2,1)S(1)}, bf16[64,3072]{1,0:T(8,128)(2,1)S(1)}, u32[]{:S(2)}, u32[]{:S(2)}) %collective-permute-start.8) | collective-permute-done | bytes 393248 | tf_op jit(solution)/shard_map/ppermute | solution.py:327
  67.2 3.0 %collective-permute-done.5 = bf16[64,3072]{1,0:T(8,128)(2,1)S(1)} collective-permute-done((bf16[64,3072]{1,0:T(8,128)(2,1)S(1)}, bf16[64,3072]{1,0:T(8,128)(2,1)S(1)}, u32[]{:S(2)}, u32[]{:S(2)}) %collective-permute-start.5) | collective-permute-done | bytes 393248 | tf_op jit(solution)/shard_map/ppermute | solution.py:327
  70.3 1.6 collective-permute-start.6
  73.1 1.5 collective-permute-done.3.refs_6_
  75.4 1.5 collective-permute-done.12.refs_20_
  77.5 1.3 collective-permute-done.6.refs_8_
  78.8 1.5 collective-permute-start.9
  81.3 7.7 %collective-permute-done.9.refs_10_ = bf16[64,3072]{1,0:T(8,128)(2,1)S(1)} collective-permute-done((bf16[64,3072]{1,0:T(8,128)(2,1)S(1)}, bf16[64,3072]{1,0:T(8,128)(2,1)S(1)}, u32[]{:S(2)}, u32[]{:S(2)}) %collective-permute-start.9) | collective-permute-done | bytes 393248 | tf_op jit(solution)/shard_map/ppermute | solution.py:336
  90.5 2.0 %collective-permute-start.29 = (bf16[192,1024]{1,0:T(8,128)(2,1)S(1)}, bf16[192,1024]{1,0:T(8,128)(2,1)S(1)}, u32[]{:S(2)}, u32[]{:S(2)}) collective-permute-start(bf16[192,1024]{1,0:T(8,128)(2,1)S(1)} %bitcast.34), channel_id=1, source_target_pairs={{0,16},{2,18},{4,20},{6,22},{8,24},{10,26},{12,28},{14,30},{16,0},... | collective-permute-start | bytes 1179656 | tf_op jit(solution)/shard_map/ppermute | solution.py:327
  93.2 1.8 %collective-permute-start.26 = (bf16[192,1024]{1,0:T(8,128)(2,1)S(1)}, bf16[192,1024]{1,0:T(8,128)(2,1)S(1)}, u32[]{:S(2)}, u32[]{:S(2)}) collective-permute-start(bf16[192,1024]{1,0:T(8,128)(2,1)S(1)} %bitcast.35), channel_id=1, source_target_pairs={{0,4},{2,6},{4,0},{6,2},{8,12},{10,14},{12,8},{14,10},{16,20},{18,... | collective-permute-start | bytes 1179656 | tf_op jit(solution)/shard_map/ppermute | solution.py:333
  95.1 16.7 %shard_map.158 = (bf16[256,512]{1,0:T(8,128)(2,1)}, bf16[256,512]{1,0:T(8,128)(2,1)}, bf16[256,512]{1,0:T(8,128)(2,1)}, bf16[256,512]{1,0:T(8,128)(2,1)}) custom-call(s32[28]{0:T(128)} %stack.136.where_ref, bf16[512,1024]{1,0:T(8,128)(2,1)} %refs_0_.3, bf16[512,1024]{1,0:T(8,128)(2,1)} %refs_1_.3, f32[1,128]{1,0:T(1,128)} %bitcast.37, f32[1,128]{1,0:T(1,128)} %bitcast.38, ...), custom_call_target="tpu_custom_call" | custom-call | flops 3758096384 | bytes 6815744 | tf_op jit(solution)/shard_map/pallas_call | solution.py:150
  112.7 2.7 %collective-permute-start.24 = (bf16[256,512]{1,0:T(8,128)(2,1)}, bf16[256,512]{1,0:T(8,128)(2,1)S(1)}, u32[]{:S(2)}, u32[]{:S(2)}) collective-permute-start(bf16[256,512]{1,0:T(8,128)(2,1)} %get-tuple-element.60), channel_id=1, source_target_pairs={{0,16},{2,18},{4,20},{6,22},{8,24},{10,26},{12,28},{14,30},{16,0},... | collective-permute-start | bytes 786440 | tf_op jit(solution)/shard_map/ppermute | solution.py:411
  115.4 1.6 %collective-permute-start.25 = (bf16[256,512]{1,0:T(8,128)(2,1)}, bf16[256,512]{1,0:T(8,128)(2,1)S(1)}, u32[]{:S(2)}, u32[]{:S(2)}) collective-permute-start(bf16[256,512]{1,0:T(8,128)(2,1)} %get-tuple-element.61), channel_id=1, source_target_pairs={{0,24},{2,26},{4,28},{6,30},{8,16},{10,18},{12,20},{14,22},{16,8},... | collective-permute-start | bytes 786440 | tf_op jit(solution)/shard_map/ppermute | solution.py:411
  117.0 8.1 %collective-permute-done.23.refs_1_ = bf16[256,512]{1,0:T(8,128)(2,1)S(1)} collective-permute-done((bf16[256,512]{1,0:T(8,128)(2,1)}, bf16[256,512]{1,0:T(8,128)(2,1)S(1)}, u32[]{:S(2)}, u32[]{:S(2)}) %collective-permute-start.23) | collective-permute-done | bytes 262176 | tf_op jit(solution)/shard_map/ppermute | solution.py:411
  125.1 9.2 %collective-permute-done.24.refs_2_ = bf16[256,512]{1,0:T(8,128)(2,1)S(1)} collective-permute-done((bf16[256,512]{1,0:T(8,128)(2,1)}, bf16[256,512]{1,0:T(8,128)(2,1)S(1)}, u32[]{:S(2)}, u32[]{:S(2)}) %collective-permute-start.24) | collective-permute-done | bytes 262176 | tf_op jit(solution)/shard_map/ppermute | solution.py:411
  138.0 5.6 %shard_map.159 = (f32[128,768]{1,0:T(8,128)}, bf16[128,768]{1,0:T(8,128)(2,1)}, bf16[128,768]{1,0:T(8,128)(2,1)}, bf16[128,768]{1,0:T(8,128)(2,1)}) custom-call(s32[12]{0:T(128)} %stack.117.where_ref, bf16[256,512]{1,0:T(8,128)(2,1)} %get-tuple-element.72.refs_0_, bf16[256,512]{1,0:T(8,128)(2,1)} %copy-done.2, bf16[256,512]{1,0:T(8,128)(2,1)} %copy-done.3, ...), custom_call_target="tpu_custom_call" | custom-call | flops 805306368 | bytes 3145728 | tf_op jit(solution)/shard_map/pallas_call | solution.py:272
  145.0 4.7 %collective-permute-start.35 = (bf16[128,768]{1,0:T(8,128)(2,1)}, bf16[128,768]{1,0:T(8,128)(2,1)S(1)}, u32[]{:S(2)}, u32[]{:S(2)}) collective-permute-start(bf16[128,768]{1,0:T(8,128)(2,1)} %get-tuple-element.71), channel_id=1, source_target_pairs={{0,9},{1,8},{2,11},{3,10},{4,13},{5,12},{6,15},{7,14},{8,1},{9,0},... | collective-permute-start | bytes 589832 | tf_op jit(solution)/shard_map/ppermute | solution.py:344
  149.8 2.0 %shard_map.160 = (bf16[128,1024]{1,0:T(8,128)(2,1)}, bf16[128,1024]{1,0:T(8,128)(2,1)}) custom-call(s32[1]{0:T(128)} %bitcast.member_ref, bf16[256,512]{1,0:T(8,128)(2,1)} %get-tuple-element.72.refs_0_, bf16[256,512]{1,0:T(8,128)(2,1)} %copy-done.2, bf16[256,512]{1,0:T(8,128)(2,1)} %copy-done.3, bf16[256,512]{1,0:T(8,128)(2,1)} %copy-done.4), custom_call_target="tpu_custom_call" | custom-call | tf_op jit(solution)/shard_map/pallas_call | solution.py:227
  151.8 2.6 %collective-permute-done.33 = bf16[128,768]{1,0:T(8,128)(2,1)S(1)} collective-permute-done((bf16[128,768]{1,0:T(8,128)(2,1)}, bf16[128,768]{1,0:T(8,128)(2,1)S(1)}, u32[]{:S(2)}, u32[]{:S(2)}) %collective-permute-start.33) | collective-permute-done | bytes 196640 | tf_op jit(solution)/shard_map/ppermute | solution.py:336
  155.6 3.4 %collective-permute-done.34 = bf16[128,768]{1,0:T(8,128)(2,1)S(1)} collective-permute-done((bf16[128,768]{1,0:T(8,128)(2,1)}, bf16[128,768]{1,0:T(8,128)(2,1)S(1)}, u32[]{:S(2)}, u32[]{:S(2)}) %collective-permute-start.34) | collective-permute-done | bytes 196640 | tf_op jit(solution)/shard_map/ppermute | solution.py:344
  (111 shorter events, 20.6 us)
Async XLA Ops:
  2.9 12.3 %collective-permute-start = (bf16[64,3072]{1,0:T(8,128)(2,1)S(1)}, bf16[64,3072]{1,0:T(8,128)(2,1)}, u32[]{:S(2)}, u32[]{:S(2)}) collective-permute-start(bf16[64,3072]{1,0:T(8,128)(2,1)S(1)} %constant_dynamic-slice_fusion), channel_id=1, source_target_pairs={{0,8},{2,10},{4,12},{6,14},{8,0},{10,2},{12,4},{14,6},{16,24},{18,... | collective-permute-start | bytes 1179656 | tf_op jit(solution)/shard_map/ppermute | solution.py:327
  6.0 9.2 %collective-permute-start.1 = (bf16[64,3072]{1,0:T(8,128)(2,1)S(1)}, bf16[64,3072]{1,0:T(8,128)(2,1)S(1)}, u32[]{:S(2)}, u32[]{:S(2)}) collective-permute-start(bf16[64,3072]{1,0:T(8,128)(2,1)S(1)} %constant_dynamic-slice_fusion), channel_id=1, source_target_pairs={{8,16},{10,18},{12,20},{14,22},{16,8},{18,10},{20,12},{22,14},{9,1... | collective-permute-start | bytes 1179656 | tf_op jit(solution)/shard_map/ppermute | solution.py:327
  15.2 15.2 %collective-permute-start.2 = (bf16[832,256]{1,0:T(8,128)(2,1)}, bf16[832,256]{1,0:T(8,128)(2,1)}, u32[]{:S(2)}, u32[]{:S(2)}) collective-permute-start(bf16[832,256]{1,0:T(8,128)(2,1)} %get-tuple-element.40), channel_id=1, source_target_pairs={{0,8},{2,10},{4,12},{6,14},{8,0},{10,2},{12,4},{14,6},{16,24},{18,... | collective-permute-start | bytes 1277960 | tf_op jit(solution)/shard_map/ppermute | solution.py:327
  19.9 12.1 %collective-permute-start.7 = (bf16[832,256]{1,0:T(8,128)(2,1)}, bf16[832,256]{1,0:T(8,128)(2,1)S(1)}, u32[]{:S(2)}, u32[]{:S(2)}) collective-permute-start(bf16[832,256]{1,0:T(8,128)(2,1)} %get-tuple-element.48.refs_11_), channel_id=1, source_target_pairs={{0,4},{2,6},{4,0},{6,2},{8,12},{10,14},{12,8},{14,10},{16,20},{18,... | collective-permute-start | bytes 1277960 | tf_op jit(solution)/shard_map/ppermute | solution.py:333
  21.4 3.4 %collective-permute-start.4 = (bf16[64,3072]{1,0:T(8,128)(2,1)}, bf16[64,3072]{1,0:T(8,128)(2,1)S(1)}, u32[]{:S(2)}, u32[]{:S(2)}) collective-permute-start(bf16[64,3072]{1,0:T(8,128)(2,1)} %collective-permute-done.refs_5_), channel_id=1, source_target_pairs={{8,16},{10,18},{12,20},{14,22},{16,8},{18,10},{20,12},{22,14},{9,1... | collective-permute-start | bytes 1179656 | tf_op jit(solution)/shard_map/ppermute | solution.py:327
  22.1 40.4 %collective-permute-start.10 = (bf16[832,256]{1,0:T(8,128)(2,1)}, bf16[832,256]{1,0:T(8,128)(2,1)}, u32[]{:S(2)}, u32[]{:S(2)}) collective-permute-start(bf16[832,256]{1,0:T(8,128)(2,1)} %get-tuple-element.45), channel_id=1, source_target_pairs={{0,16},{2,18},{4,20},{6,22},{8,24},{10,26},{12,28},{14,30},{16,0},... | collective-permute-start | bytes 1277960 | tf_op jit(solution)/shard_map/ppermute | solution.py:327
  30.5 35.5 %collective-permute-start.11 = (bf16[832,256]{1,0:T(8,128)(2,1)}, bf16[832,256]{1,0:T(8,128)(2,1)}, u32[]{:S(2)}, u32[]{:S(2)}) collective-permute-start(bf16[832,256]{1,0:T(8,128)(2,1)} %collective-permute-done.2.refs_15_), channel_id=1, source_target_pairs={{0,4},{2,6},{4,0},{6,2},{8,12},{10,14},{12,8},{14,10},{16,20},{18,... | collective-permute-start | bytes 1277960 | tf_op jit(solution)/shard_map/ppermute | solution.py:333
  32.8 33.3 %collective-permute-start.8 = (bf16[64,3072]{1,0:T(8,128)(2,1)S(1)}, bf16[64,3072]{1,0:T(8,128)(2,1)S(1)}, u32[]{:S(2)}, u32[]{:S(2)}) collective-permute-start(bf16[64,3072]{1,0:T(8,128)(2,1)S(1)} %collective-permute-done.4), channel_id=1, source_target_pairs={{8,0},{10,2},{12,4},{14,6},{16,24},{18,26},{20,28},{22,30},{9,1},{... | collective-permute-start | bytes 1179656 | tf_op jit(solution)/shard_map/ppermute | solution.py:327
  34.0 36.2 %collective-permute-start.5 = (bf16[64,3072]{1,0:T(8,128)(2,1)S(1)}, bf16[64,3072]{1,0:T(8,128)(2,1)S(1)}, u32[]{:S(2)}, u32[]{:S(2)}) collective-permute-start(bf16[64,3072]{1,0:T(8,128)(2,1)S(1)} %collective-permute-done.1), channel_id=1, source_target_pairs={{8,0},{10,2},{12,4},{14,6},{16,24},{18,26},{20,28},{22,30},{9,1},{... | collective-permute-start | bytes 1179656 | tf_op jit(solution)/shard_map/ppermute | solution.py:327
  35.4 36.5 %collective-permute-start.19 = (bf16[832,256]{1,0:T(8,128)(2,1)}, bf16[832,256]{1,0:T(8,128)(2,1)}, u32[]{:S(2)}, u32[]{:S(2)}) collective-permute-start(bf16[832,256]{1,0:T(8,128)(2,1)} %get-tuple-element.55), channel_id=1, source_target_pairs={{0,24},{2,26},{4,28},{6,30},{8,16},{10,18},{12,20},{14,22},{16,8},... | collective-permute-start | bytes 1277960 | tf_op jit(solution)/shard_map/ppermute | solution.py:327
  62.5 12.1 %collective-permute-start.3 = (bf16[64,3072]{1,0:T(8,128)(2,1)}, bf16[64,3072]{1,0:T(8,128)(2,1)S(1)}, u32[]{:S(2)}, u32[]{:S(2)}) collective-permute-start(bf16[64,3072]{1,0:T(8,128)(2,1)} %collective-permute-done.refs_5_), channel_id=1, source_target_pairs={{0,1},{1,0},{2,3},{3,2},{4,5},{5,4},{6,7},{7,6},{8,9},{9,8},{10,11... | collective-permute-start | bytes 1179656 | tf_op jit(solution)/shard_map/ppermute | solution.py:336
  66.0 10.8 %collective-permute-start.12 = (bf16[832,256]{1,0:T(8,128)(2,1)}, bf16[832,256]{1,0:T(8,128)(2,1)}, u32[]{:S(2)}, u32[]{:S(2)}) collective-permute-start(bf16[832,256]{1,0:T(8,128)(2,1)} %collective-permute-done.10.refs_19_), channel_id=1, source_target_pairs={{0,4},{2,6},{4,0},{6,2},{8,12},{10,14},{12,8},{14,10},{16,20},{18,... | collective-permute-start | bytes 1277960 | tf_op jit(solution)/shard_map/ppermute | solution.py:333
  70.3 8.6 %collective-permute-start.6 = (bf16[64,3072]{1,0:T(8,128)(2,1)S(1)}, bf16[64,3072]{1,0:T(8,128)(2,1)S(1)}, u32[]{:S(2)}, u32[]{:S(2)}) collective-permute-start(bf16[64,3072]{1,0:T(8,128)(2,1)S(1)} %broadcast_select_fusion.1.refs_7_), channel_id=1, source_target_pairs={{0,1},{1,0},{2,3},{3,2},{4,5},{5,4},{6,7},{7,6},{8,9},{9,8},{10,11... | collective-permute-start | bytes 1179656 | tf_op jit(solution)/shard_map/ppermute | solution.py:336
  71.8 9.5 %collective-permute-start.20 = (bf16[832,256]{1,0:T(8,128)(2,1)}, bf16[832,256]{1,0:T(8,128)(2,1)S(1)}, u32[]{:S(2)}, u32[]{:S(2)}) collective-permute-start(bf16[832,256]{1,0:T(8,128)(2,1)} %collective-permute-done.19.refs_23_), channel_id=1, source_target_pairs={{0,4},{2,6},{4,0},{6,2},{8,12},{10,14},{12,8},{14,10},{16,20},{18,... | collective-permute-start | bytes 1277960 | tf_op jit(solution)/shard_map/ppermute | solution.py:333
  76.9 12.2 %collective-permute-start.13 = (bf16[832,256]{1,0:T(8,128)(2,1)S(1)}, bf16[832,256]{1,0:T(8,128)(2,1)S(1)}, u32[]{:S(2)}, u32[]{:S(2)}) collective-permute-start(bf16[832,256]{1,0:T(8,128)(2,1)S(1)} %copy-done.16), channel_id=1, source_target_pairs={{0,2},{2,0},{4,6},{6,4},{8,10},{10,8},{12,14},{14,12},{16,18},{18,... | collective-permute-start | bytes 1277960 | tf_op jit(solution)/shard_map/ppermute | solution.py:333
  76.9 12.7 %collective-permute-start.14 = (bf16[832,256]{1,0:T(8,128)(2,1)S(1)}, bf16[832,256]{1,0:T(8,128)(2,1)S(1)}, u32[]{:S(2)}, u32[]{:S(2)}) collective-permute-start(bf16[832,256]{1,0:T(8,128)(2,1)S(1)} %copy-done.18), channel_id=1, source_target_pairs={{0,2},{2,0},{4,6},{6,4},{8,10},{10,8},{12,14},{14,12},{16,18},{18,... | collective-permute-start | bytes 1277960 | tf_op jit(solution)/shard_map/ppermute | solution.py:333
  77.4 12.3 %collective-permute-start.15 = (bf16[832,256]{1,0:T(8,128)(2,1)}, bf16[832,256]{1,0:T(8,128)(2,1)S(1)}, u32[]{:S(2)}, u32[]{:S(2)}) collective-permute-start(bf16[832,256]{1,0:T(8,128)(2,1)} %collective-permute-done.2.refs_15_), channel_id=1, source_target_pairs={{0,2},{2,0},{4,6},{6,4},{8,10},{10,8},{12,14},{14,12},{16,18},{18,... | collective-permute-start | bytes 1277960 | tf_op jit(solution)/shard_map/ppermute | solution.py:333
  78.8 10.2 %collective-permute-start.9 = (bf16[64,3072]{1,0:T(8,128)(2,1)S(1)}, bf16[64,3072]{1,0:T(8,128)(2,1)S(1)}, u32[]{:S(2)}, u32[]{:S(2)}) collective-permute-start(bf16[64,3072]{1,0:T(8,128)(2,1)S(1)} %broadcast_select_fusion.refs_9_), channel_id=1, source_target_pairs={{0,1},{1,0},{2,3},{3,2},{4,5},{5,4},{6,7},{7,6},{8,9},{9,8},{10,11... | collective-permute-start | bytes 1179656 | tf_op jit(solution)/shard_map/ppermute | solution.py:336
  81.3 8.8 %collective-permute-start.16 = (bf16[832,256]{1,0:T(8,128)(2,1)}, bf16[832,256]{1,0:T(8,128)(2,1)}, u32[]{:S(2)}, u32[]{:S(2)}) collective-permute-start(bf16[832,256]{1,0:T(8,128)(2,1)} %collective-permute-done.11.refs_16_), channel_id=1, source_target_pairs={{0,2},{2,0},{4,6},{6,4},{8,10},{10,8},{12,14},{14,12},{16,18},{18,... | collective-permute-start | bytes 1277960 | tf_op jit(solution)/shard_map/ppermute | solution.py:333
  89.0 4.1 %collective-permute-start.17 = (bf16[832,256]{1,0:T(8,128)(2,1)}, bf16[832,256]{1,0:T(8,128)(2,1)}, u32[]{:S(2)}, u32[]{:S(2)}) collective-permute-start(bf16[832,256]{1,0:T(8,128)(2,1)} %collective-permute-done.10.refs_19_), channel_id=1, source_target_pairs={{0,2},{2,0},{4,6},{6,4},{8,10},{10,8},{12,14},{14,12},{16,18},{18,... | collective-permute-start | bytes 1277960 | tf_op jit(solution)/shard_map/ppermute | solution.py:333
  89.1 6.0 %collective-permute-start.18 = (bf16[832,256]{1,0:T(8,128)(2,1)}, bf16[832,256]{1,0:T(8,128)(2,1)}, u32[]{:S(2)}, u32[]{:S(2)}) collective-permute-start(bf16[832,256]{1,0:T(8,128)(2,1)} %collective-permute-done.12.refs_20_), channel_id=1, source_target_pairs={{0,2},{2,0},{4,6},{6,4},{8,10},{10,8},{12,14},{14,12},{16,18},{18,... | collective-permute-start | bytes 1277960 | tf_op jit(solution)/shard_map/ppermute | solution.py:333
  89.6 5.5 %collective-permute-start.21 = (bf16[832,256]{1,0:T(8,128)(2,1)}, bf16[832,256]{1,0:T(8,128)(2,1)}, u32[]{:S(2)}, u32[]{:S(2)}) collective-permute-start(bf16[832,256]{1,0:T(8,128)(2,1)} %collective-permute-done.19.refs_23_), channel_id=1, source_target_pairs={{0,2},{2,0},{4,6},{6,4},{8,10},{10,8},{12,14},{14,12},{16,18},{18,... | collective-permute-start | bytes 1277960 | tf_op jit(solution)/shard_map/ppermute | solution.py:333
  89.7 5.4 %collective-permute-start.22 = (bf16[832,256]{1,0:T(8,128)(2,1)S(1)}, bf16[832,256]{1,0:T(8,128)(2,1)}, u32[]{:S(2)}, u32[]{:S(2)}) collective-permute-start(bf16[832,256]{1,0:T(8,128)(2,1)S(1)} %collective-permute-done.20.refs_24_), channel_id=1, source_target_pairs={{0,2},{2,0},{4,6},{6,4},{8,10},{10,8},{12,14},{14,12},{16,18},{18,... | collective-permute-start | bytes 1277960 | tf_op jit(solution)/shard_map/ppermute | solution.py:333
  90.5 21.2 %collective-permute-start.29 = (bf16[192,1024]{1,0:T(8,128)(2,1)S(1)}, bf16[192,1024]{1,0:T(8,128)(2,1)S(1)}, u32[]{:S(2)}, u32[]{:S(2)}) collective-permute-start(bf16[192,1024]{1,0:T(8,128)(2,1)S(1)} %bitcast.34), channel_id=1, source_target_pairs={{0,16},{2,18},{4,20},{6,22},{8,24},{10,26},{12,28},{14,30},{16,0},... | collective-permute-start | bytes 1179656 | tf_op jit(solution)/shard_map/ppermute | solution.py:327
  93.2 41.2 %collective-permute-start.26 = (bf16[192,1024]{1,0:T(8,128)(2,1)S(1)}, bf16[192,1024]{1,0:T(8,128)(2,1)S(1)}, u32[]{:S(2)}, u32[]{:S(2)}) collective-permute-start(bf16[192,1024]{1,0:T(8,128)(2,1)S(1)} %bitcast.35), channel_id=1, source_target_pairs={{0,4},{2,6},{4,0},{6,2},{8,12},{10,14},{12,8},{14,10},{16,20},{18,... | collective-permute-start | bytes 1179656 | tf_op jit(solution)/shard_map/ppermute | solution.py:333
  111.7 23.2 %collective-permute-start.30 = (bf16[192,1024]{1,0:T(8,128)(2,1)S(1)}, bf16[192,1024]{1,0:T(8,128)(2,1)S(1)}, u32[]{:S(2)}, u32[]{:S(2)}) collective-permute-start(bf16[192,1024]{1,0:T(8,128)(2,1)S(1)} %collective-permute-done.29.refs_8_), channel_id=1, source_target_pairs={{0,4},{2,6},{4,0},{6,2},{8,12},{10,14},{12,8},{14,10},{16,20},{18,... | collective-permute-start | bytes 1179656 | tf_op jit(solution)/shard_map/ppermute | solution.py:333
  112.6 12.5 %collective-permute-start.23 = (bf16[256,512]{1,0:T(8,128)(2,1)}, bf16[256,512]{1,0:T(8,128)(2,1)S(1)}, u32[]{:S(2)}, u32[]{:S(2)}) collective-permute-start(bf16[256,512]{1,0:T(8,128)(2,1)} %get-tuple-element.59), channel_id=1, source_target_pairs={{0,8},{2,10},{4,12},{6,14},{8,0},{10,2},{12,4},{14,6},{16,24},{18,... | collective-permute-start | bytes 786440 | tf_op jit(solution)/shard_map/ppermute | solution.py:411
  112.7 21.6 %collective-permute-start.24 = (bf16[256,512]{1,0:T(8,128)(2,1)}, bf16[256,512]{1,0:T(8,128)(2,1)S(1)}, u32[]{:S(2)}, u32[]{:S(2)}) collective-permute-start(bf16[256,512]{1,0:T(8,128)(2,1)} %get-tuple-element.60), channel_id=1, source_target_pairs={{0,16},{2,18},{4,20},{6,22},{8,24},{10,26},{12,28},{14,30},{16,0},... | collective-permute-start | bytes 786440 | tf_op jit(solution)/shard_map/ppermute | solution.py:411
  115.4 18.9 %collective-permute-start.25 = (bf16[256,512]{1,0:T(8,128)(2,1)}, bf16[256,512]{1,0:T(8,128)(2,1)S(1)}, u32[]{:S(2)}, u32[]{:S(2)}) collective-permute-start(bf16[256,512]{1,0:T(8,128)(2,1)} %get-tuple-element.61), channel_id=1, source_target_pairs={{0,24},{2,26},{4,28},{6,30},{8,16},{10,18},{12,20},{14,22},{16,8},... | collective-permute-start | bytes 786440 | tf_op jit(solution)/shard_map/ppermute | solution.py:411
  143.6 10.8 %collective-permute-start.33 = (bf16[128,768]{1,0:T(8,128)(2,1)}, bf16[128,768]{1,0:T(8,128)(2,1)S(1)}, u32[]{:S(2)}, u32[]{:S(2)}) collective-permute-start(bf16[128,768]{1,0:T(8,128)(2,1)} %get-tuple-element.69), channel_id=1, source_target_pairs={{0,1},{1,0},{2,3},{3,2},{4,5},{5,4},{6,7},{7,6},{8,9},{9,8},{10,11... | collective-permute-start | bytes 589832 | tf_op jit(solution)/shard_map/ppermute | solution.py:336
  145.0 10.7 %collective-permute-start.35 = (bf16[128,768]{1,0:T(8,128)(2,1)}, bf16[128,768]{1,0:T(8,128)(2,1)S(1)}, u32[]{:S(2)}, u32[]{:S(2)}) collective-permute-start(bf16[128,768]{1,0:T(8,128)(2,1)} %get-tuple-element.71), channel_id=1, source_target_pairs={{0,9},{1,8},{2,11},{3,10},{4,13},{5,12},{6,15},{7,14},{8,1},{9,0},... | collective-permute-start | bytes 589832 | tf_op jit(solution)/shard_map/ppermute | solution.py:344
  149.7 9.4 %collective-permute-start.34 = (bf16[128,768]{1,0:T(8,128)(2,1)}, bf16[128,768]{1,0:T(8,128)(2,1)S(1)}, u32[]{:S(2)}, u32[]{:S(2)}) collective-permute-start(bf16[128,768]{1,0:T(8,128)(2,1)} %get-tuple-element.70), channel_id=1, source_target_pairs={{0,8},{1,9},{2,10},{3,11},{4,12},{5,13},{6,14},{7,15},{8,0},{9,1},... | collective-permute-start | bytes 589832 | tf_op jit(solution)/shard_map/ppermute | solution.py:344
  (30 other events, 306.2 us)

commit v6 on v5

--- a/solution.py
+++ b/solution.py
@@ -33,36 +33,34 @@
     return (x * lax.rsqrt(power + 1e-06) * gain).astype(jnp.bfloat16)
 
 
-def patch_kernel(depth, n_pieces, counts, where_ref, *refs):
-    n_patches = len(counts)
+def patch_kernel(depth, n_pieces, cuts, where_ref, *refs):
+    n_patches = len(cuts)
     tk_ref, tv_ref, qg_ref, kg_ref = refs[:4]
-    shares, refs = refs[4 : 4 + sum(counts)], refs[4 + sum(counts) :]
+    n_rows = 1 + max(i for cut in cuts for i, _, _ in cut)
+    arrays, refs = refs[4 : 4 + n_rows], refs[4 + n_rows :]
     pieces, refs = refs[:n_pieces], refs[n_pieces:]
-    outs, (x_ref, held, scores, expos, x_sem, w_sem, k_sem) = refs[:n_patches], refs[n_patches:]
+    outs, (x_ref, held, scores, expos, x_sem, w_sem) = refs[:n_patches], refs[n_patches:]
     rows, width = outs[0].shape[0] // 2, outs[0].shape[1] // 2
     head_size = qg_ref.shape[1]
     groups = [slice(g * rows, (g + 1) * rows) for g in range(n_patches)]
     owns, x_copies, at = [], [], 1 + n_pieces
-    for g, count in enumerate(counts):
+    for g, cut in enumerate(cuts):
         owns.append(where_ref[at])
-        for i in range(count):
-            share = shares[len(x_copies)]
+        for i, (array, start, length) in enumerate(cut):
             first = pl.multiple_of(g * rows + where_ref[at + 1 + i], 16)
             x_copies.append(
                 pltpu.make_async_copy(
-                    share, x_ref.at[pl.ds(first, share.shape[0])], x_sem.at[len(x_copies)]
+                    arrays[array].at[pl.ds(start, length)],
+                    x_ref.at[pl.ds(first, length)],
+                    x_sem.at[len(x_copies)],
                 )
             )
-        at += 1 + count
-    parts = ((pl.ds(0, 3 * depth), w_sem), (pl.ds(3 * depth, 2 * rows), k_sem))
-    w_copies, k_copies = [
-        [
-            pltpu.make_async_copy(piece.at[part], held.at[where_ref[1 + i], part], sem.at[i])
-            for i, piece in enumerate(pieces)
-        ]
-        for part, sem in parts
+        at += 1 + len(cut)
+    w_copies = [
+        pltpu.make_async_copy(piece, held.at[where_ref[1 + i]], w_sem.at[i])
+        for i, piece in enumerate(pieces)
     ]
-    for copy in x_copies + w_copies + k_copies:
+    for copy in x_copies + w_copies:
         copy.start()
     for copy in x_copies:
         copy.wait()
@@ -91,8 +89,6 @@
                 preferred_element_type=jnp.float32,
             )
     q_proj, k_proj, v_proj = proj
-    for copy in k_copies:
-        copy.wait()
 
     v_new = v_proj.astype(jnp.bfloat16)
     k0, v0 = 3 * depth, 3 * depth + rows
@@ -141,28 +137,34 @@
 
 
 def attend_patches(where, patches, text_keys, text_values, query_gain, key_gain, pieces, depth):
-    shares = [x for patch in patches for x in patch]
-    model_width, width = shares[0].shape[1], pieces[0].shape[1]
-    rows = sum(x.shape[0] for x in patches[0])
+    arrays, cuts, (rows, model_width), width = [], [], patches[0][0].shape, pieces[0].shape[1]
+    for patch in patches:
+        cuts.append([])
+        for x in patch:
+            x, start = x if isinstance(x, tuple) else (x, 0)
+            held = [i for i, y in enumerate(arrays) if y is x]
+            if not held:
+                arrays.append(x)
+            place = held[0] if held else len(arrays) - 1
+            cuts[-1].append((place, start, rows // len(patch)))
     n, n_pieces, texts, head_size = len(patches), len(pieces), text_keys.shape[0], query_gain.shape[0]
     heads, n_keys = width // head_size, n_pieces * rows
     whole = lambda i, w: (0, 0)
     return pl.pallas_call(
-        functools.partial(patch_kernel, depth, n_pieces, [len(x) for x in patches]),
+        functools.partial(patch_kernel, depth, n_pieces, cuts),
         grid_spec=pltpu.PrefetchScalarGridSpec(
             num_scalar_prefetch=1,
             grid=(1,),
             in_specs=[pl.BlockSpec((texts, width), lambda i, w: (0, w[0]))] * 2
             + [pl.BlockSpec((1, head_size), whole)] * 2
-            + [pl.BlockSpec(memory_space=pl.ANY)] * (len(shares) + n_pieces),
+            + [pl.BlockSpec(memory_space=pl.ANY)] * (len(arrays) + n_pieces),
             out_specs=[pl.BlockSpec((2 * rows, 2 * width), whole)] * n,
             scratch_shapes=[
                 pltpu.VMEM((n * rows, model_width), jnp.bfloat16),
                 pltpu.VMEM((n_pieces,) + pieces[0].shape, jnp.bfloat16),
                 pltpu.VMEM((heads, n * rows, n_keys), jnp.float32),
                 pltpu.VMEM((heads, n * rows, n_keys), jnp.bfloat16),
-                pltpu.SemaphoreType.DMA((len(shares),)),
-                pltpu.SemaphoreType.DMA((n_pieces,)),
+                pltpu.SemaphoreType.DMA((sum(len(cut) for cut in cuts),)),
                 pltpu.SemaphoreType.DMA((n_pieces,)),
             ],
         ),
@@ -179,7 +181,7 @@
         text_values,
         query_gain.reshape(1, -1),
         key_gain.reshape(1, -1),
-        *shares,
+        *arrays,
         *pieces,
     )
 
@@ -368,21 +370,22 @@
         far = over_outer(near, middle)
         pieces[2] = to_partner(after(dealt[2], near, across), 2)
         pieces[1] = to_partner(after(dealt[1], near, across), 1)
-        end_across = over_outer(across, ends)
-        end_far = over_outer(after(far, sides[0]), ends)
+        row_shares[1] = shares_of(after(near, sides[0]))
+        end_across = over_outer(after(across, pieces[1]), ends)
+        end_far = over_outer(after(far, row_shares[1][-1]), ends)
         sides[1] = flip(after(pieces[1], far), 2)
         pieces[3] = to_partner(after(dealt[3], far), 3)
-        sides[2] = flip(after(pieces[2], end_far, sides[1]), 2)
-        row_shares[1] = shares_of(after(near, pieces[1]))
         row_shares[2] = shares_of(jnp.where(inside, far, end_across))
         row_shares[3] = shares_of(jnp.where(inside, across, end_far))
-        late = [sides[2], row_shares[1][-1]]
+        sides[2] = flip(after(pieces[2], end_far, sides[1]), 2)
+        late = [sides[2], row_shares[2][-1]]
+        later = [row_shares[3][-1]]
     else:
         for k in range(1, team):
             row_shares[k] = shares_of(to_partner(part, k))
         for k in range(1, outer):
             pieces[k] = to_partner(dealt[k % team], k)
-        late = []
+        late = later = []
     for k in range(outer):
         if k not in sides:
             sides[k] = flip(pieces[k], 2)
@@ -390,7 +393,8 @@
     out_pieces = [out_piece] + [to_partner(out_piece, 2 * k) for k in range(1, fsdp)]
 
     origins = [o for k in range(outer) for o in seats_of(place ^ k)]
-    pieces = [x for k in range(outer) for x in spread(pieces[k], sides[k], *late)]
+    deps = lambda k: late if k < 2 else later
+    pieces = [x for k in range(outer) for x in spread(pieces[k], sides[k], *deps(k))]
     patch_rows = [[modded]] + [row_shares[k] for k in range(1, team)]
     where = [member] + origins
     for k in range(team):

time: 160 us -> 161 us (level)
  starting transfers between devices: 45 us -> 53 us
  waiting for transfers between devices: 80.2 us -> 73.7 us
    ppermute x9, starting transfers between devices: 19.1 us -> 29.2 us  [over_outer(): return lax.ppermute(x, 'patch', pairs)]
    ppermute x9, waiting for transfers between devices: 40.7 us -> 35.7 us  [over_outer(): return lax.ppermute(x, 'patch', pairs)]
    ppermute x18, starting transfers between devices: 10.9 us -> 8.67 us  [flip(): return lax.ppermute(x, 'patch', [(p, p ^ bits) for p in range(patches)])]
    ppermute x18, waiting for transfers between devices: 4.38 us -> 2.2 us  [flip(): return lax.ppermute(x, 'patch', [(p, p ^ bits) for p in range(patches)])]
  transfers between devices with their start and end apart: 36 -> 36, of which waited for: 19 -> 17; matrix products, arithmetic and copies ran while one was open for 1% -> 2% of each run, Pallas kernels for 13% -> 11%
where the time goes in v6:
time: 161 us; the launch traced here: 160 us
  waiting for transfers between devices  73.7 us (46%)
  starting transfers between devices  53 us (33%)
  Pallas kernels  26.4 us (16%)
  local copies, waits for them, and re-layouts  4.19 us (3%)
  other arithmetic  2.04 us (1%)
    ppermute x9, waiting for transfers between devices, over_outer(): return lax.ppermute(x, 'patch', pairs)  35.7 us
    ppermute x9, starting transfers between devices, over_outer(): return lax.ppermute(x, 'patch', pairs)  29.2 us
    ppermute x3, waiting for transfers between devices, give(): lax.ppermute(x, 'patch', [(p, p ^ bits * INNER) for p in range(patches)])  17.4 us
    pallas_call x1, Pallas kernels, attend_patches(): pl.pallas_call(functools.partial(patch_kernel, depth, n_pieces, cuts), gr...  15.8 us
    ppermute x4, waiting for transfers between devices, along_fsdp(): lax.ppermute(x, 'fsdp', [(i, (i + step) % fsdp) for i in range(fsdp)])  13.8 us
    ppermute x18, starting transfers between devices, flip(): return lax.ppermute(x, 'patch', [(p, p ^ bits) for p in range(patches)])  8.67 us
    ppermute x4, starting transfers between devices, along_fsdp(): lax.ppermute(x, 'fsdp', [(i, (i + step) % fsdp) for i in range(fsdp)])  6.22 us
    pallas_call x1, Pallas kernels, project(): pl.pallas_call(functools.partial(project_kernel, len(packs), len(pieces),...  5.64 us
  transfers between devices with their start and end apart: 36, of which 17 were waited for; matrix products, arithmetic and copies ran while one was open for 2% of the time, Pallas kernels for 11%

profile of v6, /device:TPU:0, one launch (start us, length us, event | category | flops | bytes accessed | tf_op | source)
XLA Modules:
  0.0 160.3 jit_solution(13756220117940409110)
XLA Ops:
  0.7 2.9 %shard_map.157 = (bf16[832,256]{1,0:T(8,128)(2,1)}, bf16[832,256]{1,0:T(8,128)(2,1)}, bf16[832,256]{1,0:T(8,128)(2,1)}, bf16[832,256]{1,0:T(8,128)(2,1)}) custom-call(s32[1]{0:T(128)} %bitcast.member_ref, bf16[192,1024]{1,0:T(8,128)(2,1)} %refs_0_.2, bf16[192,1024]{1,0:T(8,128)(2,1)} %refs_1_.2, bf16[192,1024]{1,0:T(8,128)(2,1)} %refs_2_.1, ...), custom_call_target="tpu_custom_call" | custom-call | tf_op jit(solution)/shard_map/pallas_call | solution.py:205
  3.6 3.0 %collective-permute-start.1 = (bf16[832,256]{1,0:T(8,128)(2,1)}, bf16[832,256]{1,0:T(8,128)(2,1)}, u32[]{:S(2)}, u32[]{:S(2)}) collective-permute-start(bf16[832,256]{1,0:T(8,128)(2,1)} %get-tuple-element.50.refs_11_), channel_id=1, source_target_pairs={{0,4},{2,6},{4,0},{6,2},{8,12},{10,14},{12,8},{14,10},{16,20},{18,... | collective-permute-start | bytes 1277960 | tf_op jit(solution)/shard_map/ppermute | solution.py:335
  7.6 1.6 %collective-permute-start = (bf16[64,3072]{1,0:T(8,128)(2,1)S(1)}, bf16[64,3072]{1,0:T(8,128)(2,1)S(1)}, u32[]{:S(2)}, u32[]{:S(2)}) collective-permute-start(bf16[64,3072]{1,0:T(8,128)(2,1)S(1)} %constant_dynamic-slice_fusion), channel_id=1, source_target_pairs={{0,8},{2,10},{4,12},{6,14},{8,0},{10,2},{12,4},{14,6},{16,24},{18,... | collective-permute-start | bytes 1179656 | tf_op jit(solution)/shard_map/ppermute | solution.py:329
  9.9 8.3 %collective-permute-done.refs_5_ = bf16[64,3072]{1,0:T(8,128)(2,1)S(1)} collective-permute-done((bf16[64,3072]{1,0:T(8,128)(2,1)S(1)}, bf16[64,3072]{1,0:T(8,128)(2,1)S(1)}, u32[]{:S(2)}, u32[]{:S(2)}) %collective-permute-start) | collective-permute-done | bytes 393248 | tf_op jit(solution)/shard_map/ppermute | solution.py:329
  18.9 1.6 collective-permute-start.2
  20.5 4.4 %collective-permute-start.5 = (bf16[832,256]{1,0:T(8,128)(2,1)}, bf16[832,256]{1,0:T(8,128)(2,1)}, u32[]{:S(2)}, u32[]{:S(2)}) collective-permute-start(bf16[832,256]{1,0:T(8,128)(2,1)} %get-tuple-element.43), channel_id=1, source_target_pairs={{0,8},{2,10},{4,12},{6,14},{8,0},{10,2},{12,4},{14,6},{16,24},{18,... | collective-permute-start | bytes 1277960 | tf_op jit(solution)/shard_map/ppermute | solution.py:329
  24.8 3.8 %collective-permute-done.2.refs_6_ = bf16[64,3072]{1,0:T(8,128)(2,1)S(1)} collective-permute-done((bf16[64,3072]{1,0:T(8,128)(2,1)S(1)}, bf16[64,3072]{1,0:T(8,128)(2,1)S(1)}, u32[]{:S(2)}, u32[]{:S(2)}) %collective-permute-start.2) | collective-permute-done | bytes 393248 | tf_op jit(solution)/shard_map/ppermute | solution.py:338
  29.4 1.3 collective-permute-start.8
  30.7 5.0 %collective-permute-start.10 = (bf16[832,256]{1,0:T(8,128)(2,1)}, bf16[832,256]{1,0:T(8,128)(2,1)S(1)}, u32[]{:S(2)}, u32[]{:S(2)}) collective-permute-start(bf16[832,256]{1,0:T(8,128)(2,1)} %get-tuple-element.47), channel_id=1, source_target_pairs={{0,16},{2,18},{4,20},{6,22},{8,24},{10,26},{12,28},{14,30},{16,0},... | collective-permute-start | bytes 1277960 | tf_op jit(solution)/shard_map/ppermute | solution.py:329
  35.7 1.7 %collective-permute-start.19 = (bf16[832,256]{1,0:T(8,128)(2,1)}, bf16[832,256]{1,0:T(8,128)(2,1)S(1)}, u32[]{:S(2)}, u32[]{:S(2)}) collective-permute-start(bf16[832,256]{1,0:T(8,128)(2,1)} %get-tuple-element.57), channel_id=1, source_target_pairs={{0,24},{2,26},{4,28},{6,30},{8,16},{10,18},{12,20},{14,22},{16,8},... | collective-permute-start | bytes 1277960 | tf_op jit(solution)/shard_map/ppermute | solution.py:329
  37.4 1.3 collective-permute-start.6
  39.2 8.9 %collective-permute-done.8 = bf16[64,3072]{1,0:T(8,128)(2,1)S(1)} collective-permute-done((bf16[64,3072]{1,0:T(8,128)(2,1)S(1)}, bf16[64,3072]{1,0:T(8,128)(2,1)S(1)}, u32[]{:S(2)}, u32[]{:S(2)}) %collective-permute-start.8) | collective-permute-done | bytes 393248 | tf_op jit(solution)/shard_map/ppermute | solution.py:329
  48.2 1.6 collective-permute-start.9
  49.7 4.5 %collective-permute-done.19.refs_23_ = bf16[832,256]{1,0:T(8,128)(2,1)S(1)} collective-permute-done((bf16[832,256]{1,0:T(8,128)(2,1)}, bf16[832,256]{1,0:T(8,128)(2,1)S(1)}, u32[]{:S(2)}, u32[]{:S(2)}) %collective-permute-start.19) | collective-permute-done | bytes 426016 | tf_op jit(solution)/shard_map/ppermute | solution.py:329
  54.7 8.6 %collective-permute-done.10.refs_19_ = bf16[832,256]{1,0:T(8,128)(2,1)S(1)} collective-permute-done((bf16[832,256]{1,0:T(8,128)(2,1)}, bf16[832,256]{1,0:T(8,128)(2,1)S(1)}, u32[]{:S(2)}, u32[]{:S(2)}) %collective-permute-start.10) | collective-permute-done | bytes 426016 | tf_op jit(solution)/shard_map/ppermute | solution.py:329
  63.9 4.6 %collective-permute-done.6 = bf16[64,3072]{1,0:T(8,128)(2,1)S(1)} collective-permute-done((bf16[64,3072]{1,0:T(8,128)(2,1)S(1)}, bf16[64,3072]{1,0:T(8,128)(2,1)S(1)}, u32[]{:S(2)}, u32[]{:S(2)}) %collective-permute-start.6) | collective-permute-done | bytes 393248 | tf_op jit(solution)/shard_map/ppermute | solution.py:329
  68.6 1.6 collective-permute-start.7
  70.7 7.4 %collective-permute-done.7.refs_8_ = bf16[64,3072]{1,0:T(8,128)(2,1)S(1)} collective-permute-done((bf16[64,3072]{1,0:T(8,128)(2,1)S(1)}, bf16[64,3072]{1,0:T(8,128)(2,1)S(1)}, u32[]{:S(2)}, u32[]{:S(2)}) %collective-permute-start.7) | collective-permute-done | bytes 393248 | tf_op jit(solution)/shard_map/ppermute | solution.py:338
  81.5 12.6 %collective-permute-start.29 = (bf16[192,1024]{1,0:T(8,128)(2,1)S(1)}, bf16[192,1024]{1,0:T(8,128)(2,1)S(1)}, u32[]{:S(2)}, u32[]{:S(2)}) collective-permute-start(bf16[192,1024]{1,0:T(8,128)(2,1)S(1)} %bitcast.34), channel_id=1, source_target_pairs={{0,16},{2,18},{4,20},{6,22},{8,24},{10,26},{12,28},{14,30},{16,0},... | collective-permute-start | bytes 1179656 | tf_op jit(solution)/shard_map/ppermute | solution.py:329
  95.3 15.8 %shard_map.158 = (bf16[256,512]{1,0:T(8,128)(2,1)}, bf16[256,512]{1,0:T(8,128)(2,1)}, bf16[256,512]{1,0:T(8,128)(2,1)}, bf16[256,512]{1,0:T(8,128)(2,1)}) custom-call(s32[28]{0:T(128)} %stack.136.where_ref, bf16[512,1024]{1,0:T(8,128)(2,1)} %refs_0_.3, bf16[512,1024]{1,0:T(8,128)(2,1)} %refs_1_.3, f32[1,128]{1,0:T(1,128)} %bitcast.37, f32[1,128]{1,0:T(1,128)} %bitcast.38, ...), custom_call_target="tpu_custom_call" | custom-call | flops 3758096384 | bytes 6815744 | tf_op jit(solution)/shard_map/pallas_call | solution.py:153
  113.0 2.9 %collective-permute-start.24 = (bf16[256,512]{1,0:T(8,128)(2,1)}, bf16[256,512]{1,0:T(8,128)(2,1)S(1)}, u32[]{:S(2)}, u32[]{:S(2)}) collective-permute-start(bf16[256,512]{1,0:T(8,128)(2,1)} %get-tuple-element.62), channel_id=1, source_target_pairs={{0,16},{2,18},{4,20},{6,22},{8,24},{10,26},{12,28},{14,30},{16,0},... | collective-permute-start | bytes 786440 | tf_op jit(solution)/shard_map/ppermute | solution.py:415
  115.9 1.3 collective-permute-start.25
  117.2 8.0 %collective-permute-done.23.refs_1_ = bf16[256,512]{1,0:T(8,128)(2,1)S(1)} collective-permute-done((bf16[256,512]{1,0:T(8,128)(2,1)}, bf16[256,512]{1,0:T(8,128)(2,1)S(1)}, u32[]{:S(2)}, u32[]{:S(2)}) %collective-permute-start.23) | collective-permute-done | bytes 262176 | tf_op jit(solution)/shard_map/ppermute | solution.py:415
  125.2 9.4 %collective-permute-done.24.refs_2_ = bf16[256,512]{1,0:T(8,128)(2,1)S(1)} collective-permute-done((bf16[256,512]{1,0:T(8,128)(2,1)}, bf16[256,512]{1,0:T(8,128)(2,1)S(1)}, u32[]{:S(2)}, u32[]{:S(2)}) %collective-permute-start.24) | collective-permute-done | bytes 262176 | tf_op jit(solution)/shard_map/ppermute | solution.py:415
  138.2 5.6 %shard_map.159 = (f32[128,768]{1,0:T(8,128)}, bf16[128,768]{1,0:T(8,128)(2,1)}, bf16[128,768]{1,0:T(8,128)(2,1)}, bf16[128,768]{1,0:T(8,128)(2,1)}) custom-call(s32[12]{0:T(128)} %stack.117.where_ref, bf16[256,512]{1,0:T(8,128)(2,1)} %get-tuple-element.74.refs_0_, bf16[256,512]{1,0:T(8,128)(2,1)} %copy-done.2, bf16[256,512]{1,0:T(8,128)(2,1)} %copy-done.3, ...), custom_call_target="tpu_custom_call" | custom-call | flops 805306368 | bytes 3145728 | tf_op jit(solution)/shard_map/pallas_call | solution.py:274
  143.9 1.6 collective-permute-start.33
  145.5 4.4 %collective-permute-start.35 = (bf16[128,768]{1,0:T(8,128)(2,1)}, bf16[128,768]{1,0:T(8,128)(2,1)S(1)}, u32[]{:S(2)}, u32[]{:S(2)}) collective-permute-start(bf16[128,768]{1,0:T(8,128)(2,1)} %get-tuple-element.73), channel_id=1, source_target_pairs={{0,9},{1,8},{2,11},{3,10},{4,13},{5,12},{6,15},{7,14},{8,1},{9,0},... | collective-permute-start | bytes 589832 | tf_op jit(solution)/shard_map/ppermute | solution.py:346
  150.0 2.0 %shard_map.160 = (bf16[128,1024]{1,0:T(8,128)(2,1)}, bf16[128,1024]{1,0:T(8,128)(2,1)}) custom-call(s32[1]{0:T(128)} %bitcast.member_ref, bf16[256,512]{1,0:T(8,128)(2,1)} %get-tuple-element.74.refs_0_, bf16[256,512]{1,0:T(8,128)(2,1)} %copy-done.2, bf16[256,512]{1,0:T(8,128)(2,1)} %copy-done.3, bf16[256,512]{1,0:T(8,128)(2,1)} %copy-done.4), custom_call_target="tpu_custom_call" | custom-call | tf_op jit(solution)/shard_map/pallas_call | solution.py:229
  152.1 2.6 %collective-permute-done.33 = bf16[128,768]{1,0:T(8,128)(2,1)S(1)} collective-permute-done((bf16[128,768]{1,0:T(8,128)(2,1)}, bf16[128,768]{1,0:T(8,128)(2,1)S(1)}, u32[]{:S(2)}, u32[]{:S(2)}) %collective-permute-start.33) | collective-permute-done | bytes 196640 | tf_op jit(solution)/shard_map/ppermute | solution.py:338
  154.7 1.1 collective-permute-done.35
  155.9 3.4 %collective-permute-done.34 = bf16[128,768]{1,0:T(8,128)(2,1)S(1)} collective-permute-done((bf16[128,768]{1,0:T(8,128)(2,1)}, bf16[128,768]{1,0:T(8,128)(2,1)S(1)}, u32[]{:S(2)}, u32[]{:S(2)}) %collective-permute-start.34) | collective-permute-done | bytes 196640 | tf_op jit(solution)/shard_map/ppermute | solution.py:346
  159.4 0.9 fusion.8
  (115 shorter events, 15.6 us)
Async XLA Ops:
  3.6 15.3 %collective-permute-start.1 = (bf16[832,256]{1,0:T(8,128)(2,1)}, bf16[832,256]{1,0:T(8,128)(2,1)}, u32[]{:S(2)}, u32[]{:S(2)}) collective-permute-start(bf16[832,256]{1,0:T(8,128)(2,1)} %get-tuple-element.50.refs_11_), channel_id=1, source_target_pairs={{0,4},{2,6},{4,0},{6,2},{8,12},{10,14},{12,8},{14,10},{16,20},{18,... | collective-permute-start | bytes 1277960 | tf_op jit(solution)/shard_map/ppermute | solution.py:335
  7.6 10.6 %collective-permute-start = (bf16[64,3072]{1,0:T(8,128)(2,1)S(1)}, bf16[64,3072]{1,0:T(8,128)(2,1)S(1)}, u32[]{:S(2)}, u32[]{:S(2)}) collective-permute-start(bf16[64,3072]{1,0:T(8,128)(2,1)S(1)} %constant_dynamic-slice_fusion), channel_id=1, source_target_pairs={{0,8},{2,10},{4,12},{6,14},{8,0},{10,2},{12,4},{14,6},{16,24},{18,... | collective-permute-start | bytes 1179656 | tf_op jit(solution)/shard_map/ppermute | solution.py:329
  9.2 11.3 %collective-permute-start.4 = (bf16[64,3072]{1,0:T(8,128)(2,1)S(1)}, bf16[64,3072]{1,0:T(8,128)(2,1)S(1)}, u32[]{:S(2)}, u32[]{:S(2)}) collective-permute-start(bf16[64,3072]{1,0:T(8,128)(2,1)S(1)} %constant_dynamic-slice_fusion), channel_id=1, source_target_pairs={{8,16},{10,18},{12,20},{14,22},{16,8},{18,10},{20,12},{22,14},{9,1... | collective-permute-start | bytes 1179656 | tf_op jit(solution)/shard_map/ppermute | solution.py:329
  18.2 6.6 %collective-permute-start.3 = (bf16[64,3072]{1,0:T(8,128)(2,1)S(1)}, bf16[64,3072]{1,0:T(8,128)(2,1)S(1)}, u32[]{:S(2)}, u32[]{:S(2)}) collective-permute-start(bf16[64,3072]{1,0:T(8,128)(2,1)S(1)} %collective-permute-done.refs_5_), channel_id=1, source_target_pairs={{8,16},{10,18},{12,20},{14,22},{16,8},{18,10},{20,12},{22,14},{9,1... | collective-permute-start | bytes 1179656 | tf_op jit(solution)/shard_map/ppermute | solution.py:329
  18.9 9.7 %collective-permute-start.2 = (bf16[64,3072]{1,0:T(8,128)(2,1)S(1)}, bf16[64,3072]{1,0:T(8,128)(2,1)S(1)}, u32[]{:S(2)}, u32[]{:S(2)}) collective-permute-start(bf16[64,3072]{1,0:T(8,128)(2,1)S(1)} %collective-permute-done.refs_5_), channel_id=1, source_target_pairs={{0,1},{1,0},{2,3},{3,2},{4,5},{5,4},{6,7},{7,6},{8,9},{9,8},{10,11... | collective-permute-start | bytes 1179656 | tf_op jit(solution)/shard_map/ppermute | solution.py:338
  20.5 16.9 %collective-permute-start.5 = (bf16[832,256]{1,0:T(8,128)(2,1)}, bf16[832,256]{1,0:T(8,128)(2,1)}, u32[]{:S(2)}, u32[]{:S(2)}) collective-permute-start(bf16[832,256]{1,0:T(8,128)(2,1)} %get-tuple-element.43), channel_id=1, source_target_pairs={{0,8},{2,10},{4,12},{6,14},{8,0},{10,2},{12,4},{14,6},{16,24},{18,... | collective-permute-start | bytes 1277960 | tf_op jit(solution)/shard_map/ppermute | solution.py:329
  29.4 18.7 %collective-permute-start.8 = (bf16[64,3072]{1,0:T(8,128)(2,1)S(1)}, bf16[64,3072]{1,0:T(8,128)(2,1)S(1)}, u32[]{:S(2)}, u32[]{:S(2)}) collective-permute-start(bf16[64,3072]{1,0:T(8,128)(2,1)S(1)} %collective-permute-done.3), channel_id=1, source_target_pairs={{8,0},{10,2},{12,4},{14,6},{16,24},{18,26},{20,28},{22,30},{9,1},{... | collective-permute-start | bytes 1179656 | tf_op jit(solution)/shard_map/ppermute | solution.py:329
  30.7 32.7 %collective-permute-start.10 = (bf16[832,256]{1,0:T(8,128)(2,1)}, bf16[832,256]{1,0:T(8,128)(2,1)S(1)}, u32[]{:S(2)}, u32[]{:S(2)}) collective-permute-start(bf16[832,256]{1,0:T(8,128)(2,1)} %get-tuple-element.47), channel_id=1, source_target_pairs={{0,16},{2,18},{4,20},{6,22},{8,24},{10,26},{12,28},{14,30},{16,0},... | collective-permute-start | bytes 1277960 | tf_op jit(solution)/shard_map/ppermute | solution.py:329
  35.7 18.6 %collective-permute-start.19 = (bf16[832,256]{1,0:T(8,128)(2,1)}, bf16[832,256]{1,0:T(8,128)(2,1)S(1)}, u32[]{:S(2)}, u32[]{:S(2)}) collective-permute-start(bf16[832,256]{1,0:T(8,128)(2,1)} %get-tuple-element.57), channel_id=1, source_target_pairs={{0,24},{2,26},{4,28},{6,30},{8,16},{10,18},{12,20},{14,22},{16,8},... | collective-permute-start | bytes 1277960 | tf_op jit(solution)/shard_map/ppermute | solution.py:329
  37.4 31.1 %collective-permute-start.6 = (bf16[64,3072]{1,0:T(8,128)(2,1)S(1)}, bf16[64,3072]{1,0:T(8,128)(2,1)S(1)}, u32[]{:S(2)}, u32[]{:S(2)}) collective-permute-start(bf16[64,3072]{1,0:T(8,128)(2,1)S(1)} %collective-permute-done.4), channel_id=1, source_target_pairs={{8,0},{10,2},{12,4},{14,6},{16,24},{18,26},{20,28},{22,30},{9,1},{... | collective-permute-start | bytes 1179656 | tf_op jit(solution)/shard_map/ppermute | solution.py:329
  38.6 24.7 %collective-permute-start.11 = (bf16[832,256]{1,0:T(8,128)(2,1)}, bf16[832,256]{1,0:T(8,128)(2,1)}, u32[]{:S(2)}, u32[]{:S(2)}) collective-permute-start(bf16[832,256]{1,0:T(8,128)(2,1)} %collective-permute-done.5.refs_15_), channel_id=1, source_target_pairs={{0,4},{2,6},{4,0},{6,2},{8,12},{10,14},{12,8},{14,10},{16,20},{18,... | collective-permute-start | bytes 1277960 | tf_op jit(solution)/shard_map/ppermute | solution.py:335
  48.2 22.0 %collective-permute-start.9 = (bf16[64,3072]{1,0:T(8,128)(2,1)S(1)}, bf16[64,3072]{1,0:T(8,128)(2,1)S(1)}, u32[]{:S(2)}, u32[]{:S(2)}) collective-permute-start(bf16[64,3072]{1,0:T(8,128)(2,1)S(1)} %broadcast_select_fusion.refs_9_), channel_id=1, source_target_pairs={{0,1},{1,0},{2,3},{3,2},{4,5},{5,4},{6,7},{7,6},{8,9},{9,8},{10,11... | collective-permute-start | bytes 1179656 | tf_op jit(solution)/shard_map/ppermute | solution.py:338
  54.2 16.4 %collective-permute-start.20 = (bf16[832,256]{1,0:T(8,128)(2,1)S(1)}, bf16[832,256]{1,0:T(8,128)(2,1)S(1)}, u32[]{:S(2)}, u32[]{:S(2)}) collective-permute-start(bf16[832,256]{1,0:T(8,128)(2,1)S(1)} %collective-permute-done.19.refs_23_), channel_id=1, source_target_pairs={{0,4},{2,6},{4,0},{6,2},{8,12},{10,14},{12,8},{14,10},{16,20},{18,... | collective-permute-start | bytes 1277960 | tf_op jit(solution)/shard_map/ppermute | solution.py:335
  63.4 15.5 %collective-permute-start.12 = (bf16[832,256]{1,0:T(8,128)(2,1)S(1)}, bf16[832,256]{1,0:T(8,128)(2,1)}, u32[]{:S(2)}, u32[]{:S(2)}) collective-permute-start(bf16[832,256]{1,0:T(8,128)(2,1)S(1)} %collective-permute-done.10.refs_19_), channel_id=1, source_target_pairs={{0,4},{2,6},{4,0},{6,2},{8,12},{10,14},{12,8},{14,10},{16,20},{18,... | collective-permute-start | bytes 1277960 | tf_op jit(solution)/shard_map/ppermute | solution.py:335
  68.6 9.5 %collective-permute-start.7 = (bf16[64,3072]{1,0:T(8,128)(2,1)S(1)}, bf16[64,3072]{1,0:T(8,128)(2,1)S(1)}, u32[]{:S(2)}, u32[]{:S(2)}) collective-permute-start(bf16[64,3072]{1,0:T(8,128)(2,1)S(1)} %broadcast_select_fusion.1.refs_7_), channel_id=1, source_target_pairs={{0,1},{1,0},{2,3},{3,2},{4,5},{5,4},{6,7},{7,6},{8,9},{9,8},{10,11... | collective-permute-start | bytes 1179656 | tf_op jit(solution)/shard_map/ppermute | solution.py:338
  70.1 9.3 %collective-permute-start.17 = (bf16[832,256]{1,0:T(8,128)(2,1)S(1)}, bf16[832,256]{1,0:T(8,128)(2,1)S(1)}, u32[]{:S(2)}, u32[]{:S(2)}) collective-permute-start(bf16[832,256]{1,0:T(8,128)(2,1)S(1)} %collective-permute-done.10.refs_19_), channel_id=1, source_target_pairs={{0,2},{2,0},{4,6},{6,4},{8,10},{10,8},{12,14},{14,12},{16,18},{18,... | collective-permute-start | bytes 1277960 | tf_op jit(solution)/shard_map/ppermute | solution.py:335
  70.1 9.3 %collective-permute-start.21 = (bf16[832,256]{1,0:T(8,128)(2,1)S(1)}, bf16[832,256]{1,0:T(8,128)(2,1)S(1)}, u32[]{:S(2)}, u32[]{:S(2)}) collective-permute-start(bf16[832,256]{1,0:T(8,128)(2,1)S(1)} %collective-permute-done.19.refs_23_), channel_id=1, source_target_pairs={{0,2},{2,0},{4,6},{6,4},{8,10},{10,8},{12,14},{14,12},{16,18},{18,... | collective-permute-start | bytes 1277960 | tf_op jit(solution)/shard_map/ppermute | solution.py:335
  70.6 9.3 %collective-permute-start.22 = (bf16[832,256]{1,0:T(8,128)(2,1)S(1)}, bf16[832,256]{1,0:T(8,128)(2,1)S(1)}, u32[]{:S(2)}, u32[]{:S(2)}) collective-permute-start(bf16[832,256]{1,0:T(8,128)(2,1)S(1)} %collective-permute-done.20.refs_24_), channel_id=1, source_target_pairs={{0,2},{2,0},{4,6},{6,4},{8,10},{10,8},{12,14},{14,12},{16,18},{18,... | collective-permute-start | bytes 1277960 | tf_op jit(solution)/shard_map/ppermute | solution.py:335
  78.9 15.9 %collective-permute-start.14 = (bf16[832,256]{1,0:T(8,128)(2,1)}, bf16[832,256]{1,0:T(8,128)(2,1)}, u32[]{:S(2)}, u32[]{:S(2)}) collective-permute-start(bf16[832,256]{1,0:T(8,128)(2,1)} %collective-permute-done.1.refs_12_), channel_id=1, source_target_pairs={{0,2},{2,0},{4,6},{6,4},{8,10},{10,8},{12,14},{14,12},{16,18},{18,... | collective-permute-start | bytes 1277960 | tf_op jit(solution)/shard_map/ppermute | solution.py:335
  79.4 15.9 %collective-permute-start.15 = (bf16[832,256]{1,0:T(8,128)(2,1)}, bf16[832,256]{1,0:T(8,128)(2,1)}, u32[]{:S(2)}, u32[]{:S(2)}) collective-permute-start(bf16[832,256]{1,0:T(8,128)(2,1)} %collective-permute-done.5.refs_15_), channel_id=1, source_target_pairs={{0,2},{2,0},{4,6},{6,4},{8,10},{10,8},{12,14},{14,12},{16,18},{18,... | collective-permute-start | bytes 1277960 | tf_op jit(solution)/shard_map/ppermute | solution.py:335
  79.5 15.8 %collective-permute-start.16 = (bf16[832,256]{1,0:T(8,128)(2,1)}, bf16[832,256]{1,0:T(8,128)(2,1)}, u32[]{:S(2)}, u32[]{:S(2)}) collective-permute-start(bf16[832,256]{1,0:T(8,128)(2,1)} %collective-permute-done.11.refs_16_), channel_id=1, source_target_pairs={{0,2},{2,0},{4,6},{6,4},{8,10},{10,8},{12,14},{14,12},{16,18},{18,... | collective-permute-start | bytes 1277960 | tf_op jit(solution)/shard_map/ppermute | solution.py:335
  79.9 15.4 %collective-permute-start.18 = (bf16[832,256]{1,0:T(8,128)(2,1)}, bf16[832,256]{1,0:T(8,128)(2,1)}, u32[]{:S(2)}, u32[]{:S(2)}) collective-permute-start(bf16[832,256]{1,0:T(8,128)(2,1)} %collective-permute-done.12.refs_20_), channel_id=1, source_target_pairs={{0,2},{2,0},{4,6},{6,4},{8,10},{10,8},{12,14},{14,12},{16,18},{18,... | collective-permute-start | bytes 1277960 | tf_op jit(solution)/shard_map/ppermute | solution.py:335
  81.5 30.5 %collective-permute-start.29 = (bf16[192,1024]{1,0:T(8,128)(2,1)S(1)}, bf16[192,1024]{1,0:T(8,128)(2,1)S(1)}, u32[]{:S(2)}, u32[]{:S(2)}) collective-permute-start(bf16[192,1024]{1,0:T(8,128)(2,1)S(1)} %bitcast.34), channel_id=1, source_target_pairs={{0,16},{2,18},{4,20},{6,22},{8,24},{10,26},{12,28},{14,30},{16,0},... | collective-permute-start | bytes 1179656 | tf_op jit(solution)/shard_map/ppermute | solution.py:329
  94.8 39.9 %collective-permute-start.26 = (bf16[192,1024]{1,0:T(8,128)(2,1)S(1)}, bf16[192,1024]{1,0:T(8,128)(2,1)S(1)}, u32[]{:S(2)}, u32[]{:S(2)}) collective-permute-start(bf16[192,1024]{1,0:T(8,128)(2,1)S(1)} %bitcast.35), channel_id=1, source_target_pairs={{0,4},{2,6},{4,0},{6,2},{8,12},{10,14},{12,8},{14,10},{16,20},{18,... | collective-permute-start | bytes 1179656 | tf_op jit(solution)/shard_map/ppermute | solution.py:335
  111.9 23.3 %collective-permute-start.30 = (bf16[192,1024]{1,0:T(8,128)(2,1)S(1)}, bf16[192,1024]{1,0:T(8,128)(2,1)S(1)}, u32[]{:S(2)}, u32[]{:S(2)}) collective-permute-start(bf16[192,1024]{1,0:T(8,128)(2,1)S(1)} %collective-permute-done.29.refs_8_), channel_id=1, source_target_pairs={{0,4},{2,6},{4,0},{6,2},{8,12},{10,14},{12,8},{14,10},{16,20},{18,... | collective-permute-start | bytes 1179656 | tf_op jit(solution)/shard_map/ppermute | solution.py:335
  112.8 12.4 %collective-permute-start.23 = (bf16[256,512]{1,0:T(8,128)(2,1)}, bf16[256,512]{1,0:T(8,128)(2,1)S(1)}, u32[]{:S(2)}, u32[]{:S(2)}) collective-permute-start(bf16[256,512]{1,0:T(8,128)(2,1)} %get-tuple-element.61), channel_id=1, source_target_pairs={{0,8},{2,10},{4,12},{6,14},{8,0},{10,2},{12,4},{14,6},{16,24},{18,... | collective-permute-start | bytes 786440 | tf_op jit(solution)/shard_map/ppermute | solution.py:415
  113.0 21.6 %collective-permute-start.24 = (bf16[256,512]{1,0:T(8,128)(2,1)}, bf16[256,512]{1,0:T(8,128)(2,1)S(1)}, u32[]{:S(2)}, u32[]{:S(2)}) collective-permute-start(bf16[256,512]{1,0:T(8,128)(2,1)} %get-tuple-element.62), channel_id=1, source_target_pairs={{0,16},{2,18},{4,20},{6,22},{8,24},{10,26},{12,28},{14,30},{16,0},... | collective-permute-start | bytes 786440 | tf_op jit(solution)/shard_map/ppermute | solution.py:415
  115.9 18.7 %collective-permute-start.25 = (bf16[256,512]{1,0:T(8,128)(2,1)}, bf16[256,512]{1,0:T(8,128)(2,1)S(1)}, u32[]{:S(2)}, u32[]{:S(2)}) collective-permute-start(bf16[256,512]{1,0:T(8,128)(2,1)} %get-tuple-element.63), channel_id=1, source_target_pairs={{0,24},{2,26},{4,28},{6,30},{8,16},{10,18},{12,20},{14,22},{16,8},... | collective-permute-start | bytes 786440 | tf_op jit(solution)/shard_map/ppermute | solution.py:415
  135.2 2.9 %collective-permute-start.32 = (bf16[192,1024]{1,0:T(8,128)(2,1)S(1)}, bf16[192,1024]{1,0:T(8,128)(2,1)}, u32[]{:S(2)}, u32[]{:S(2)}) collective-permute-start(bf16[192,1024]{1,0:T(8,128)(2,1)S(1)} %collective-permute-done.30.refs_9_), channel_id=1, source_target_pairs={{0,2},{2,0},{4,6},{6,4},{8,10},{10,8},{12,14},{14,12},{16,18},{18,... | collective-permute-start | bytes 1179656 | tf_op jit(solution)/shard_map/ppermute | solution.py:335
  143.9 10.8 %collective-permute-start.33 = (bf16[128,768]{1,0:T(8,128)(2,1)}, bf16[128,768]{1,0:T(8,128)(2,1)S(1)}, u32[]{:S(2)}, u32[]{:S(2)}) collective-permute-start(bf16[128,768]{1,0:T(8,128)(2,1)} %get-tuple-element.71), channel_id=1, source_target_pairs={{0,1},{1,0},{2,3},{3,2},{4,5},{5,4},{6,7},{7,6},{8,9},{9,8},{10,11... | collective-permute-start | bytes 589832 | tf_op jit(solution)/shard_map/ppermute | solution.py:338
  145.5 10.4 %collective-permute-start.35 = (bf16[128,768]{1,0:T(8,128)(2,1)}, bf16[128,768]{1,0:T(8,128)(2,1)S(1)}, u32[]{:S(2)}, u32[]{:S(2)}) collective-permute-start(bf16[128,768]{1,0:T(8,128)(2,1)} %get-tuple-element.73), channel_id=1, source_target_pairs={{0,9},{1,8},{2,11},{3,10},{4,13},{5,12},{6,15},{7,14},{8,1},{9,0},... | collective-permute-start | bytes 589832 | tf_op jit(solution)/shard_map/ppermute | solution.py:346
  149.9 9.4 %collective-permute-start.34 = (bf16[128,768]{1,0:T(8,128)(2,1)}, bf16[128,768]{1,0:T(8,128)(2,1)S(1)}, u32[]{:S(2)}, u32[]{:S(2)}) collective-permute-start(bf16[128,768]{1,0:T(8,128)(2,1)} %get-tuple-element.72), channel_id=1, source_target_pairs={{0,8},{1,9},{2,10},{3,11},{4,12},{5,13},{6,14},{7,15},{8,0},{9,1},... | collective-permute-start | bytes 589832 | tf_op jit(solution)/shard_map/ppermute | solution.py:346
  (32 other events, 410.8 us)

commit v7 on v6

--- a/solution.py
+++ b/solution.py
@@ -374,7 +374,7 @@
         end_across = over_outer(after(across, pieces[1]), ends)
         end_far = over_outer(after(far, row_shares[1][-1]), ends)
         sides[1] = flip(after(pieces[1], far), 2)
-        pieces[3] = to_partner(after(dealt[3], far), 3)
+        pieces[3] = to_partner(after(dealt[3], far, pieces[2]), 3)
         row_shares[2] = shares_of(jnp.where(inside, far, end_across))
         row_shares[3] = shares_of(jnp.where(inside, across, end_far))
         sides[2] = flip(after(pieces[2], end_far, sides[1]), 2)

time: 161 us -> 152 us (0.944)
  starting transfers between devices: 53 us -> 37.1 us
  waiting for transfers between devices: 73.7 us -> 81 us
    ppermute x9, starting transfers between devices: 29.2 us -> 13.8 us  [over_outer(): return lax.ppermute(x, 'patch', pairs)]
    ppermute x9, waiting for transfers between devices: 35.7 us -> 39.5 us  [over_outer(): return lax.ppermute(x, 'patch', pairs)]
    ppermute x18, waiting for transfers between devices: 2.2 us -> 4.47 us  [flip(): return lax.ppermute(x, 'patch', [(p, p ^ bits) for p in range(patches)])]
  transfers between devices with their start and end apart: 36 -> 36, of which waited for: 17 -> 20; matrix products, arithmetic and copies ran while one was open for 2% -> 2% of each run, Pallas kernels for 11% -> 12%
where the time goes in v7:
time: 152 us
  waiting for transfers between devices  81 us (53%)
  starting transfers between devices  37.1 us (24%)
  Pallas kernels  26.4 us (17%)
  local copies, waits for them, and re-layouts  4.16 us (3%)
  other arithmetic  2.04 us (1%)
    ppermute x9, waiting for transfers between devices, over_outer(): return lax.ppermute(x, 'patch', pairs)  39.5 us
    ppermute x3, waiting for transfers between devices, give(): lax.ppermute(x, 'patch', [(p, p ^ bits * INNER) for p in range(patches)])  17.7 us
    pallas_call x1, Pallas kernels, attend_patches(): pl.pallas_call(functools.partial(patch_kernel, depth, n_pieces, cuts), gr...  15.8 us
    ppermute x4, waiting for transfers between devices, along_fsdp(): lax.ppermute(x, 'fsdp', [(i, (i + step) % fsdp) for i in range(fsdp)])  15.4 us
    ppermute x9, starting transfers between devices, over_outer(): return lax.ppermute(x, 'patch', pairs)  13.8 us
    ppermute x18, starting transfers between devices, flip(): return lax.ppermute(x, 'patch', [(p, p ^ bits) for p in range(patches)])  8.64 us
    pallas_call x1, Pallas kernels, project(): pl.pallas_call(functools.partial(project_kernel, len(packs), len(pieces),...  5.65 us
    ppermute x2, starting transfers between devices, along_both(): return lax.ppermute(x, ('patch', 'fsdp'), pairs)  5.45 us
  transfers between devices with their start and end apart: 36, of which 20 were waited for; matrix products, arithmetic and copies ran while one was open for 2% of the time, Pallas kernels for 12%

profile of v7, /device:TPU:0, one launch (start us, length us, event | category | flops | bytes accessed | tf_op | source)
XLA Modules:
  0.0 151.7 jit_solution(13449065850078026055)
XLA Ops:
  0.7 2.9 %shard_map.157 = (bf16[832,256]{1,0:T(8,128)(2,1)}, bf16[832,256]{1,0:T(8,128)(2,1)}, bf16[832,256]{1,0:T(8,128)(2,1)}, bf16[832,256]{1,0:T(8,128)(2,1)}) custom-call(s32[1]{0:T(128)} %bitcast.member_ref, bf16[192,1024]{1,0:T(8,128)(2,1)} %refs_0_.2, bf16[192,1024]{1,0:T(8,128)(2,1)} %refs_1_.2, bf16[192,1024]{1,0:T(8,128)(2,1)} %refs_2_.1, ...), custom_call_target="tpu_custom_call" | custom-call | tf_op jit(solution)/shard_map/pallas_call | solution.py:205
  3.5 3.0 %collective-permute-start.1 = (bf16[832,256]{1,0:T(8,128)(2,1)}, bf16[832,256]{1,0:T(8,128)(2,1)S(1)}, u32[]{:S(2)}, u32[]{:S(2)}) collective-permute-start(bf16[832,256]{1,0:T(8,128)(2,1)} %get-tuple-element.50.refs_11_), channel_id=1, source_target_pairs={{0,4},{2,6},{4,0},{6,2},{8,12},{10,14},{12,8},{14,10},{16,20},{18,... | collective-permute-start | bytes 1277960 | tf_op jit(solution)/shard_map/ppermute | solution.py:335
  7.5 1.6 %collective-permute-start = (bf16[64,3072]{1,0:T(8,128)(2,1)S(1)}, bf16[64,3072]{1,0:T(8,128)(2,1)S(1)}, u32[]{:S(2)}, u32[]{:S(2)}) collective-permute-start(bf16[64,3072]{1,0:T(8,128)(2,1)S(1)} %constant_dynamic-slice_fusion), channel_id=1, source_target_pairs={{0,8},{2,10},{4,12},{6,14},{8,0},{10,2},{12,4},{14,6},{16,24},{18,... | collective-permute-start | bytes 1179656 | tf_op jit(solution)/shard_map/ppermute | solution.py:329
  9.9 8.3 %collective-permute-done.refs_5_ = bf16[64,3072]{1,0:T(8,128)(2,1)S(1)} collective-permute-done((bf16[64,3072]{1,0:T(8,128)(2,1)S(1)}, bf16[64,3072]{1,0:T(8,128)(2,1)S(1)}, u32[]{:S(2)}, u32[]{:S(2)}) %collective-permute-start) | collective-permute-done | bytes 393248 | tf_op jit(solution)/shard_map/ppermute | solution.py:329
  18.9 1.6 %collective-permute-start.2 = (bf16[64,3072]{1,0:T(8,128)(2,1)S(1)}, bf16[64,3072]{1,0:T(8,128)(2,1)S(1)}, u32[]{:S(2)}, u32[]{:S(2)}) collective-permute-start(bf16[64,3072]{1,0:T(8,128)(2,1)S(1)} %collective-permute-done.refs_5_), channel_id=1, source_target_pairs={{0,1},{1,0},{2,3},{3,2},{4,5},{5,4},{6,7},{7,6},{8,9},{9,8},{10,11... | collective-permute-start | bytes 1179656 | tf_op jit(solution)/shard_map/ppermute | solution.py:338
  20.5 4.4 %collective-permute-start.5 = (bf16[832,256]{1,0:T(8,128)(2,1)}, bf16[832,256]{1,0:T(8,128)(2,1)}, u32[]{:S(2)}, u32[]{:S(2)}) collective-permute-start(bf16[832,256]{1,0:T(8,128)(2,1)} %get-tuple-element.43), channel_id=1, source_target_pairs={{0,8},{2,10},{4,12},{6,14},{8,0},{10,2},{12,4},{14,6},{16,24},{18,... | collective-permute-start | bytes 1277960 | tf_op jit(solution)/shard_map/ppermute | solution.py:329
  24.8 3.8 %collective-permute-done.2.refs_6_ = bf16[64,3072]{1,0:T(8,128)(2,1)S(1)} collective-permute-done((bf16[64,3072]{1,0:T(8,128)(2,1)S(1)}, bf16[64,3072]{1,0:T(8,128)(2,1)S(1)}, u32[]{:S(2)}, u32[]{:S(2)}) %collective-permute-start.2) | collective-permute-done | bytes 393248 | tf_op jit(solution)/shard_map/ppermute | solution.py:338
  29.4 1.3 collective-permute-start.8
  30.7 7.8 %collective-permute-done.5.refs_15_ = bf16[832,256]{1,0:T(8,128)(2,1)} collective-permute-done((bf16[832,256]{1,0:T(8,128)(2,1)}, bf16[832,256]{1,0:T(8,128)(2,1)}, u32[]{:S(2)}, u32[]{:S(2)}) %collective-permute-start.5) | collective-permute-done | bytes 426016 | tf_op jit(solution)/shard_map/ppermute | solution.py:329
  38.5 1.3 collective-permute-start.6
  40.4 8.8 %collective-permute-done.10.refs_19_ = bf16[832,256]{1,0:T(8,128)(2,1)} collective-permute-done((bf16[832,256]{1,0:T(8,128)(2,1)}, bf16[832,256]{1,0:T(8,128)(2,1)}, u32[]{:S(2)}, u32[]{:S(2)}) %collective-permute-start.10) | collective-permute-done | bytes 426016 | tf_op jit(solution)/shard_map/ppermute | solution.py:329
  49.2 3.8 %collective-permute-start.19 = (bf16[832,256]{1,0:T(8,128)(2,1)}, bf16[832,256]{1,0:T(8,128)(2,1)S(1)}, u32[]{:S(2)}, u32[]{:S(2)}) collective-permute-start(bf16[832,256]{1,0:T(8,128)(2,1)} %get-tuple-element.57), channel_id=1, source_target_pairs={{0,24},{2,26},{4,28},{6,30},{8,16},{10,18},{12,20},{14,22},{16,8},... | collective-permute-start | bytes 1277960 | tf_op jit(solution)/shard_map/ppermute | solution.py:329
  53.1 9.3 %collective-permute-done.8 = bf16[64,3072]{1,0:T(8,128)(2,1)S(1)} collective-permute-done((bf16[64,3072]{1,0:T(8,128)(2,1)S(1)}, bf16[64,3072]{1,0:T(8,128)(2,1)S(1)}, u32[]{:S(2)}, u32[]{:S(2)}) %collective-permute-start.8) | collective-permute-done | bytes 393248 | tf_op jit(solution)/shard_map/ppermute | solution.py:329
  62.5 2.2 %collective-permute-start.9 = (bf16[64,3072]{1,0:T(8,128)(2,1)S(1)}, bf16[64,3072]{1,0:T(8,128)(2,1)S(1)}, u32[]{:S(2)}, u32[]{:S(2)}) collective-permute-start(bf16[64,3072]{1,0:T(8,128)(2,1)S(1)} %broadcast_select_fusion.refs_9_), channel_id=1, source_target_pairs={{0,1},{1,0},{2,3},{3,2},{4,5},{5,4},{6,7},{7,6},{8,9},{9,8},{10,11... | collective-permute-start | bytes 1179656 | tf_op jit(solution)/shard_map/ppermute | solution.py:338
  65.2 3.0 %collective-permute-done.6 = bf16[64,3072]{1,0:T(8,128)(2,1)S(1)} collective-permute-done((bf16[64,3072]{1,0:T(8,128)(2,1)S(1)}, bf16[64,3072]{1,0:T(8,128)(2,1)S(1)}, u32[]{:S(2)}, u32[]{:S(2)}) %collective-permute-start.6) | collective-permute-done | bytes 393248 | tf_op jit(solution)/shard_map/ppermute | solution.py:329
  69.4 4.3 %collective-permute-done.9.refs_10_ = bf16[64,3072]{1,0:T(8,128)(2,1)S(1)} collective-permute-done((bf16[64,3072]{1,0:T(8,128)(2,1)S(1)}, bf16[64,3072]{1,0:T(8,128)(2,1)S(1)}, u32[]{:S(2)}, u32[]{:S(2)}) %collective-permute-start.9) | collective-permute-done | bytes 393248 | tf_op jit(solution)/shard_map/ppermute | solution.py:338
  74.3 4.6 %collective-permute-done.7.refs_8_ = bf16[64,3072]{1,0:T(8,128)(2,1)S(1)} collective-permute-done((bf16[64,3072]{1,0:T(8,128)(2,1)S(1)}, bf16[64,3072]{1,0:T(8,128)(2,1)S(1)}, u32[]{:S(2)}, u32[]{:S(2)}) %collective-permute-start.7) | collective-permute-done | bytes 393248 | tf_op jit(solution)/shard_map/ppermute | solution.py:338
  80.1 2.0 %collective-permute-done.20.refs_24_ = bf16[832,256]{1,0:T(8,128)(2,1)S(1)} collective-permute-done((bf16[832,256]{1,0:T(8,128)(2,1)S(1)}, bf16[832,256]{1,0:T(8,128)(2,1)S(1)}, u32[]{:S(2)}, u32[]{:S(2)}) %collective-permute-start.20) | collective-permute-done | bytes 426016 | tf_op jit(solution)/shard_map/ppermute | solution.py:335
  83.6 0.8 copy-done.24
  86.1 15.8 %shard_map.158 = (bf16[256,512]{1,0:T(8,128)(2,1)}, bf16[256,512]{1,0:T(8,128)(2,1)}, bf16[256,512]{1,0:T(8,128)(2,1)}, bf16[256,512]{1,0:T(8,128)(2,1)}) custom-call(s32[28]{0:T(128)} %stack.136.where_ref, bf16[512,1024]{1,0:T(8,128)(2,1)} %refs_0_.3, bf16[512,1024]{1,0:T(8,128)(2,1)} %refs_1_.3, f32[1,128]{1,0:T(1,128)} %bitcast.37, f32[1,128]{1,0:T(1,128)} %bitcast.38, ...), custom_call_target="tpu_custom_call" | custom-call | flops 3758096384 | bytes 6815744 | tf_op jit(solution)/shard_map/pallas_call | solution.py:153
  102.0 2.1 %collective-permute-done.29.refs_8_ = bf16[192,1024]{1,0:T(8,128)(2,1)S(1)} collective-permute-done((bf16[192,1024]{1,0:T(8,128)(2,1)S(1)}, bf16[192,1024]{1,0:T(8,128)(2,1)S(1)}, u32[]{:S(2)}, u32[]{:S(2)}) %collective-permute-start.29) | collective-permute-done | bytes 393248 | tf_op jit(solution)/shard_map/ppermute | solution.py:329
  105.0 2.3 %collective-permute-start.24 = (bf16[256,512]{1,0:T(8,128)(2,1)}, bf16[256,512]{1,0:T(8,128)(2,1)S(1)}, u32[]{:S(2)}, u32[]{:S(2)}) collective-permute-start(bf16[256,512]{1,0:T(8,128)(2,1)} %get-tuple-element.62), channel_id=1, source_target_pairs={{0,16},{2,18},{4,20},{6,22},{8,24},{10,26},{12,28},{14,30},{16,0},... | collective-permute-start | bytes 786440 | tf_op jit(solution)/shard_map/ppermute | solution.py:415
  107.3 1.6 %collective-permute-start.25 = (bf16[256,512]{1,0:T(8,128)(2,1)}, bf16[256,512]{1,0:T(8,128)(2,1)S(1)}, u32[]{:S(2)}, u32[]{:S(2)}) collective-permute-start(bf16[256,512]{1,0:T(8,128)(2,1)} %get-tuple-element.63), channel_id=1, source_target_pairs={{0,24},{2,26},{4,28},{6,30},{8,16},{10,18},{12,20},{14,22},{16,8},... | collective-permute-start | bytes 786440 | tf_op jit(solution)/shard_map/ppermute | solution.py:415
  109.0 8.4 %collective-permute-done.23.refs_1_ = bf16[256,512]{1,0:T(8,128)(2,1)S(1)} collective-permute-done((bf16[256,512]{1,0:T(8,128)(2,1)}, bf16[256,512]{1,0:T(8,128)(2,1)S(1)}, u32[]{:S(2)}, u32[]{:S(2)}) %collective-permute-start.23) | collective-permute-done | bytes 262176 | tf_op jit(solution)/shard_map/ppermute | solution.py:415
  117.4 9.2 %collective-permute-done.24.refs_2_ = bf16[256,512]{1,0:T(8,128)(2,1)S(1)} collective-permute-done((bf16[256,512]{1,0:T(8,128)(2,1)}, bf16[256,512]{1,0:T(8,128)(2,1)S(1)}, u32[]{:S(2)}, u32[]{:S(2)}) %collective-permute-start.24) | collective-permute-done | bytes 262176 | tf_op jit(solution)/shard_map/ppermute | solution.py:415
  130.3 5.7 %shard_map.159 = (f32[128,768]{1,0:T(8,128)}, bf16[128,768]{1,0:T(8,128)(2,1)}, bf16[128,768]{1,0:T(8,128)(2,1)}, bf16[128,768]{1,0:T(8,128)(2,1)}) custom-call(s32[12]{0:T(128)} %stack.117.where_ref, bf16[256,512]{1,0:T(8,128)(2,1)} %get-tuple-element.74.refs_0_, bf16[256,512]{1,0:T(8,128)(2,1)} %copy-done.2, bf16[256,512]{1,0:T(8,128)(2,1)} %copy-done.3, ...), custom_call_target="tpu_custom_call" | custom-call | flops 805306368 | bytes 3145728 | tf_op jit(solution)/shard_map/pallas_call | solution.py:274
  136.6 5.5 %collective-permute-start.35 = (bf16[128,768]{1,0:T(8,128)(2,1)}, bf16[128,768]{1,0:T(8,128)(2,1)S(1)}, u32[]{:S(2)}, u32[]{:S(2)}) collective-permute-start(bf16[128,768]{1,0:T(8,128)(2,1)} %get-tuple-element.73), channel_id=1, source_target_pairs={{0,9},{1,8},{2,11},{3,10},{4,13},{5,12},{6,15},{7,14},{8,1},{9,0},... | collective-permute-start | bytes 589832 | tf_op jit(solution)/shard_map/ppermute | solution.py:346
  142.0 2.0 %shard_map.160 = (bf16[128,1024]{1,0:T(8,128)(2,1)}, bf16[128,1024]{1,0:T(8,128)(2,1)}) custom-call(s32[1]{0:T(128)} %bitcast.member_ref, bf16[256,512]{1,0:T(8,128)(2,1)} %get-tuple-element.74.refs_0_, bf16[256,512]{1,0:T(8,128)(2,1)} %copy-done.2, bf16[256,512]{1,0:T(8,128)(2,1)} %copy-done.3, bf16[256,512]{1,0:T(8,128)(2,1)} %copy-done.4), custom_call_target="tpu_custom_call" | custom-call | tf_op jit(solution)/shard_map/pallas_call | solution.py:229
  144.1 2.7 %collective-permute-done.33 = bf16[128,768]{1,0:T(8,128)(2,1)S(1)} collective-permute-done((bf16[128,768]{1,0:T(8,128)(2,1)}, bf16[128,768]{1,0:T(8,128)(2,1)S(1)}, u32[]{:S(2)}, u32[]{:S(2)}) %collective-permute-start.33) | collective-permute-done | bytes 196640 | tf_op jit(solution)/shard_map/ppermute | solution.py:338
  146.8 1.2 collective-permute-done.35
  148.0 2.8 %collective-permute-done.34 = bf16[128,768]{1,0:T(8,128)(2,1)S(1)} collective-permute-done((bf16[128,768]{1,0:T(8,128)(2,1)}, bf16[128,768]{1,0:T(8,128)(2,1)S(1)}, u32[]{:S(2)}, u32[]{:S(2)}) %collective-permute-start.34) | collective-permute-done | bytes 196640 | tf_op jit(solution)/shard_map/ppermute | solution.py:346
  150.8 0.9 fusion.8
  (117 shorter events, 15.6 us)
Async XLA Ops:
  3.5 15.3 %collective-permute-start.1 = (bf16[832,256]{1,0:T(8,128)(2,1)}, bf16[832,256]{1,0:T(8,128)(2,1)S(1)}, u32[]{:S(2)}, u32[]{:S(2)}) collective-permute-start(bf16[832,256]{1,0:T(8,128)(2,1)} %get-tuple-element.50.refs_11_), channel_id=1, source_target_pairs={{0,4},{2,6},{4,0},{6,2},{8,12},{10,14},{12,8},{14,10},{16,20},{18,... | collective-permute-start | bytes 1277960 | tf_op jit(solution)/shard_map/ppermute | solution.py:335
  7.5 10.6 %collective-permute-start = (bf16[64,3072]{1,0:T(8,128)(2,1)S(1)}, bf16[64,3072]{1,0:T(8,128)(2,1)S(1)}, u32[]{:S(2)}, u32[]{:S(2)}) collective-permute-start(bf16[64,3072]{1,0:T(8,128)(2,1)S(1)} %constant_dynamic-slice_fusion), channel_id=1, source_target_pairs={{0,8},{2,10},{4,12},{6,14},{8,0},{10,2},{12,4},{14,6},{16,24},{18,... | collective-permute-start | bytes 1179656 | tf_op jit(solution)/shard_map/ppermute | solution.py:329
  9.2 11.3 %collective-permute-start.4 = (bf16[64,3072]{1,0:T(8,128)(2,1)S(1)}, bf16[64,3072]{1,0:T(8,128)(2,1)S(1)}, u32[]{:S(2)}, u32[]{:S(2)}) collective-permute-start(bf16[64,3072]{1,0:T(8,128)(2,1)S(1)} %constant_dynamic-slice_fusion), channel_id=1, source_target_pairs={{8,16},{10,18},{12,20},{14,22},{16,8},{18,10},{20,12},{22,14},{9,1... | collective-permute-start | bytes 1179656 | tf_op jit(solution)/shard_map/ppermute | solution.py:329
  18.2 6.6 %collective-permute-start.3 = (bf16[64,3072]{1,0:T(8,128)(2,1)S(1)}, bf16[64,3072]{1,0:T(8,128)(2,1)S(1)}, u32[]{:S(2)}, u32[]{:S(2)}) collective-permute-start(bf16[64,3072]{1,0:T(8,128)(2,1)S(1)} %collective-permute-done.refs_5_), channel_id=1, source_target_pairs={{8,16},{10,18},{12,20},{14,22},{16,8},{18,10},{20,12},{22,14},{9,1... | collective-permute-start | bytes 1179656 | tf_op jit(solution)/shard_map/ppermute | solution.py:329
  18.9 9.7 %collective-permute-start.2 = (bf16[64,3072]{1,0:T(8,128)(2,1)S(1)}, bf16[64,3072]{1,0:T(8,128)(2,1)S(1)}, u32[]{:S(2)}, u32[]{:S(2)}) collective-permute-start(bf16[64,3072]{1,0:T(8,128)(2,1)S(1)} %collective-permute-done.refs_5_), channel_id=1, source_target_pairs={{0,1},{1,0},{2,3},{3,2},{4,5},{5,4},{6,7},{7,6},{8,9},{9,8},{10,11... | collective-permute-start | bytes 1179656 | tf_op jit(solution)/shard_map/ppermute | solution.py:338
  20.5 18.1 %collective-permute-start.5 = (bf16[832,256]{1,0:T(8,128)(2,1)}, bf16[832,256]{1,0:T(8,128)(2,1)}, u32[]{:S(2)}, u32[]{:S(2)}) collective-permute-start(bf16[832,256]{1,0:T(8,128)(2,1)} %get-tuple-element.43), channel_id=1, source_target_pairs={{0,8},{2,10},{4,12},{6,14},{8,0},{10,2},{12,4},{14,6},{16,24},{18,... | collective-permute-start | bytes 1277960 | tf_op jit(solution)/shard_map/ppermute | solution.py:329
  24.8 24.4 %collective-permute-start.10 = (bf16[832,256]{1,0:T(8,128)(2,1)}, bf16[832,256]{1,0:T(8,128)(2,1)}, u32[]{:S(2)}, u32[]{:S(2)}) collective-permute-start(bf16[832,256]{1,0:T(8,128)(2,1)} %get-tuple-element.47), channel_id=1, source_target_pairs={{0,16},{2,18},{4,20},{6,22},{8,24},{10,26},{12,28},{14,30},{16,0},... | collective-permute-start | bytes 1277960 | tf_op jit(solution)/shard_map/ppermute | solution.py:329
  29.4 33.0 %collective-permute-start.8 = (bf16[64,3072]{1,0:T(8,128)(2,1)S(1)}, bf16[64,3072]{1,0:T(8,128)(2,1)S(1)}, u32[]{:S(2)}, u32[]{:S(2)}) collective-permute-start(bf16[64,3072]{1,0:T(8,128)(2,1)S(1)} %collective-permute-done.3), channel_id=1, source_target_pairs={{8,0},{10,2},{12,4},{14,6},{16,24},{18,26},{20,28},{22,30},{9,1},{... | collective-permute-start | bytes 1179656 | tf_op jit(solution)/shard_map/ppermute | solution.py:329
  38.5 29.7 %collective-permute-start.6 = (bf16[64,3072]{1,0:T(8,128)(2,1)S(1)}, bf16[64,3072]{1,0:T(8,128)(2,1)S(1)}, u32[]{:S(2)}, u32[]{:S(2)}) collective-permute-start(bf16[64,3072]{1,0:T(8,128)(2,1)S(1)} %collective-permute-done.4), channel_id=1, source_target_pairs={{8,0},{10,2},{12,4},{14,6},{16,24},{18,26},{20,28},{22,30},{9,1},{... | collective-permute-start | bytes 1179656 | tf_op jit(solution)/shard_map/ppermute | solution.py:329
  39.8 24.8 %collective-permute-start.11 = (bf16[832,256]{1,0:T(8,128)(2,1)}, bf16[832,256]{1,0:T(8,128)(2,1)}, u32[]{:S(2)}, u32[]{:S(2)}) collective-permute-start(bf16[832,256]{1,0:T(8,128)(2,1)} %collective-permute-done.5.refs_15_), channel_id=1, source_target_pairs={{0,4},{2,6},{4,0},{6,2},{8,12},{10,14},{12,8},{14,10},{16,20},{18,... | collective-permute-start | bytes 1277960 | tf_op jit(solution)/shard_map/ppermute | solution.py:335
  49.2 19.6 %collective-permute-start.19 = (bf16[832,256]{1,0:T(8,128)(2,1)}, bf16[832,256]{1,0:T(8,128)(2,1)S(1)}, u32[]{:S(2)}, u32[]{:S(2)}) collective-permute-start(bf16[832,256]{1,0:T(8,128)(2,1)} %get-tuple-element.57), channel_id=1, source_target_pairs={{0,24},{2,26},{4,28},{6,30},{8,16},{10,18},{12,20},{14,22},{16,8},... | collective-permute-start | bytes 1277960 | tf_op jit(solution)/shard_map/ppermute | solution.py:329
  62.5 11.3 %collective-permute-start.9 = (bf16[64,3072]{1,0:T(8,128)(2,1)S(1)}, bf16[64,3072]{1,0:T(8,128)(2,1)S(1)}, u32[]{:S(2)}, u32[]{:S(2)}) collective-permute-start(bf16[64,3072]{1,0:T(8,128)(2,1)S(1)} %broadcast_select_fusion.refs_9_), channel_id=1, source_target_pairs={{0,1},{1,0},{2,3},{3,2},{4,5},{5,4},{6,7},{7,6},{8,9},{9,8},{10,11... | collective-permute-start | bytes 1179656 | tf_op jit(solution)/shard_map/ppermute | solution.py:338
  64.7 14.9 %collective-permute-start.12 = (bf16[832,256]{1,0:T(8,128)(2,1)}, bf16[832,256]{1,0:T(8,128)(2,1)}, u32[]{:S(2)}, u32[]{:S(2)}) collective-permute-start(bf16[832,256]{1,0:T(8,128)(2,1)} %collective-permute-done.10.refs_19_), channel_id=1, source_target_pairs={{0,4},{2,6},{4,0},{6,2},{8,12},{10,14},{12,8},{14,10},{16,20},{18,... | collective-permute-start | bytes 1277960 | tf_op jit(solution)/shard_map/ppermute | solution.py:335
  68.3 10.5 %collective-permute-start.7 = (bf16[64,3072]{1,0:T(8,128)(2,1)S(1)}, bf16[64,3072]{1,0:T(8,128)(2,1)S(1)}, u32[]{:S(2)}, u32[]{:S(2)}) collective-permute-start(bf16[64,3072]{1,0:T(8,128)(2,1)S(1)} %broadcast_select_fusion.1.refs_7_), channel_id=1, source_target_pairs={{0,1},{1,0},{2,3},{3,2},{4,5},{5,4},{6,7},{7,6},{8,9},{9,8},{10,11... | collective-permute-start | bytes 1179656 | tf_op jit(solution)/shard_map/ppermute | solution.py:338
  68.9 13.2 %collective-permute-start.20 = (bf16[832,256]{1,0:T(8,128)(2,1)S(1)}, bf16[832,256]{1,0:T(8,128)(2,1)S(1)}, u32[]{:S(2)}, u32[]{:S(2)}) collective-permute-start(bf16[832,256]{1,0:T(8,128)(2,1)S(1)} %collective-permute-done.19.refs_23_), channel_id=1, source_target_pairs={{0,4},{2,6},{4,0},{6,2},{8,12},{10,14},{12,8},{14,10},{16,20},{18,... | collective-permute-start | bytes 1277960 | tf_op jit(solution)/shard_map/ppermute | solution.py:335
  73.7 8.4 %collective-permute-start.17 = (bf16[832,256]{1,0:T(8,128)(2,1)}, bf16[832,256]{1,0:T(8,128)(2,1)S(1)}, u32[]{:S(2)}, u32[]{:S(2)}) collective-permute-start(bf16[832,256]{1,0:T(8,128)(2,1)} %collective-permute-done.10.refs_19_), channel_id=1, source_target_pairs={{0,2},{2,0},{4,6},{6,4},{8,10},{10,8},{12,14},{14,12},{16,18},{18,... | collective-permute-start | bytes 1277960 | tf_op jit(solution)/shard_map/ppermute | solution.py:335
  73.7 8.9 %collective-permute-start.21 = (bf16[832,256]{1,0:T(8,128)(2,1)S(1)}, bf16[832,256]{1,0:T(8,128)(2,1)S(1)}, u32[]{:S(2)}, u32[]{:S(2)}) collective-permute-start(bf16[832,256]{1,0:T(8,128)(2,1)S(1)} %collective-permute-done.19.refs_23_), channel_id=1, source_target_pairs={{0,2},{2,0},{4,6},{6,4},{8,10},{10,8},{12,14},{14,12},{16,18},{18,... | collective-permute-start | bytes 1277960 | tf_op jit(solution)/shard_map/ppermute | solution.py:335
  79.6 3.1 %collective-permute-start.13 = (bf16[832,256]{1,0:T(8,128)(2,1)S(1)}, bf16[832,256]{1,0:T(8,128)(2,1)S(1)}, u32[]{:S(2)}, u32[]{:S(2)}) collective-permute-start(bf16[832,256]{1,0:T(8,128)(2,1)S(1)} %copy-done.16), channel_id=1, source_target_pairs={{0,2},{2,0},{4,6},{6,4},{8,10},{10,8},{12,14},{14,12},{16,18},{18,... | collective-permute-start | bytes 1277960 | tf_op jit(solution)/shard_map/ppermute | solution.py:335
  79.6 3.6 %collective-permute-start.14 = (bf16[832,256]{1,0:T(8,128)(2,1)S(1)}, bf16[832,256]{1,0:T(8,128)(2,1)S(1)}, u32[]{:S(2)}, u32[]{:S(2)}) collective-permute-start(bf16[832,256]{1,0:T(8,128)(2,1)S(1)} %copy-done.18), channel_id=1, source_target_pairs={{0,2},{2,0},{4,6},{6,4},{8,10},{10,8},{12,14},{14,12},{16,18},{18,... | collective-permute-start | bytes 1277960 | tf_op jit(solution)/shard_map/ppermute | solution.py:335
  82.2 3.4 %collective-permute-start.16 = (bf16[832,256]{1,0:T(8,128)(2,1)}, bf16[832,256]{1,0:T(8,128)(2,1)}, u32[]{:S(2)}, u32[]{:S(2)}) collective-permute-start(bf16[832,256]{1,0:T(8,128)(2,1)} %collective-permute-done.11.refs_16_), channel_id=1, source_target_pairs={{0,2},{2,0},{4,6},{6,4},{8,10},{10,8},{12,14},{14,12},{16,18},{18,... | collective-permute-start | bytes 1277960 | tf_op jit(solution)/shard_map/ppermute | solution.py:335
  82.7 3.4 %collective-permute-start.18 = (bf16[832,256]{1,0:T(8,128)(2,1)}, bf16[832,256]{1,0:T(8,128)(2,1)}, u32[]{:S(2)}, u32[]{:S(2)}) collective-permute-start(bf16[832,256]{1,0:T(8,128)(2,1)} %collective-permute-done.12.refs_20_), channel_id=1, source_target_pairs={{0,2},{2,0},{4,6},{6,4},{8,10},{10,8},{12,14},{14,12},{16,18},{18,... | collective-permute-start | bytes 1277960 | tf_op jit(solution)/shard_map/ppermute | solution.py:335
  82.7 3.3 %collective-permute-start.22 = (bf16[832,256]{1,0:T(8,128)(2,1)S(1)}, bf16[832,256]{1,0:T(8,128)(2,1)}, u32[]{:S(2)}, u32[]{:S(2)}) collective-permute-start(bf16[832,256]{1,0:T(8,128)(2,1)S(1)} %collective-permute-done.20.refs_24_), channel_id=1, source_target_pairs={{0,2},{2,0},{4,6},{6,4},{8,10},{10,8},{12,14},{14,12},{16,18},{18,... | collective-permute-start | bytes 1277960 | tf_op jit(solution)/shard_map/ppermute | solution.py:335
  84.4 19.7 %collective-permute-start.29 = (bf16[192,1024]{1,0:T(8,128)(2,1)S(1)}, bf16[192,1024]{1,0:T(8,128)(2,1)S(1)}, u32[]{:S(2)}, u32[]{:S(2)}) collective-permute-start(bf16[192,1024]{1,0:T(8,128)(2,1)S(1)} %bitcast.34), channel_id=1, source_target_pairs={{0,16},{2,18},{4,20},{6,22},{8,24},{10,26},{12,28},{14,30},{16,0},... | collective-permute-start | bytes 1179656 | tf_op jit(solution)/shard_map/ppermute | solution.py:329
  85.0 41.7 %collective-permute-start.26 = (bf16[192,1024]{1,0:T(8,128)(2,1)S(1)}, bf16[192,1024]{1,0:T(8,128)(2,1)S(1)}, u32[]{:S(2)}, u32[]{:S(2)}) collective-permute-start(bf16[192,1024]{1,0:T(8,128)(2,1)S(1)} %bitcast.35), channel_id=1, source_target_pairs={{0,4},{2,6},{4,0},{6,2},{8,12},{10,14},{12,8},{14,10},{16,20},{18,... | collective-permute-start | bytes 1179656 | tf_op jit(solution)/shard_map/ppermute | solution.py:335
  104.1 23.2 %collective-permute-start.30 = (bf16[192,1024]{1,0:T(8,128)(2,1)S(1)}, bf16[192,1024]{1,0:T(8,128)(2,1)S(1)}, u32[]{:S(2)}, u32[]{:S(2)}) collective-permute-start(bf16[192,1024]{1,0:T(8,128)(2,1)S(1)} %collective-permute-done.29.refs_8_), channel_id=1, source_target_pairs={{0,4},{2,6},{4,0},{6,2},{8,12},{10,14},{12,8},{14,10},{16,20},{18,... | collective-permute-start | bytes 1179656 | tf_op jit(solution)/shard_map/ppermute | solution.py:335
  104.6 12.8 %collective-permute-start.23 = (bf16[256,512]{1,0:T(8,128)(2,1)}, bf16[256,512]{1,0:T(8,128)(2,1)S(1)}, u32[]{:S(2)}, u32[]{:S(2)}) collective-permute-start(bf16[256,512]{1,0:T(8,128)(2,1)} %get-tuple-element.61), channel_id=1, source_target_pairs={{0,8},{2,10},{4,12},{6,14},{8,0},{10,2},{12,4},{14,6},{16,24},{18,... | collective-permute-start | bytes 786440 | tf_op jit(solution)/shard_map/ppermute | solution.py:415
  105.0 21.6 %collective-permute-start.24 = (bf16[256,512]{1,0:T(8,128)(2,1)}, bf16[256,512]{1,0:T(8,128)(2,1)S(1)}, u32[]{:S(2)}, u32[]{:S(2)}) collective-permute-start(bf16[256,512]{1,0:T(8,128)(2,1)} %get-tuple-element.62), channel_id=1, source_target_pairs={{0,16},{2,18},{4,20},{6,22},{8,24},{10,26},{12,28},{14,30},{16,0},... | collective-permute-start | bytes 786440 | tf_op jit(solution)/shard_map/ppermute | solution.py:415
  107.3 19.3 %collective-permute-start.25 = (bf16[256,512]{1,0:T(8,128)(2,1)}, bf16[256,512]{1,0:T(8,128)(2,1)S(1)}, u32[]{:S(2)}, u32[]{:S(2)}) collective-permute-start(bf16[256,512]{1,0:T(8,128)(2,1)} %get-tuple-element.63), channel_id=1, source_target_pairs={{0,24},{2,26},{4,28},{6,30},{8,16},{10,18},{12,20},{14,22},{16,8},... | collective-permute-start | bytes 786440 | tf_op jit(solution)/shard_map/ppermute | solution.py:415
  127.3 2.9 %collective-permute-start.32 = (bf16[192,1024]{1,0:T(8,128)(2,1)S(1)}, bf16[192,1024]{1,0:T(8,128)(2,1)}, u32[]{:S(2)}, u32[]{:S(2)}) collective-permute-start(bf16[192,1024]{1,0:T(8,128)(2,1)S(1)} %collective-permute-done.30.refs_9_), channel_id=1, source_target_pairs={{0,2},{2,0},{4,6},{6,4},{8,10},{10,8},{12,14},{14,12},{16,18},{18,... | collective-permute-start | bytes 1179656 | tf_op jit(solution)/shard_map/ppermute | solution.py:335
  136.0 10.8 %collective-permute-start.33 = (bf16[128,768]{1,0:T(8,128)(2,1)}, bf16[128,768]{1,0:T(8,128)(2,1)S(1)}, u32[]{:S(2)}, u32[]{:S(2)}) collective-permute-start(bf16[128,768]{1,0:T(8,128)(2,1)} %get-tuple-element.71), channel_id=1, source_target_pairs={{0,1},{1,0},{2,3},{3,2},{4,5},{5,4},{6,7},{7,6},{8,9},{9,8},{10,11... | collective-permute-start | bytes 589832 | tf_op jit(solution)/shard_map/ppermute | solution.py:338
  136.6 11.4 %collective-permute-start.35 = (bf16[128,768]{1,0:T(8,128)(2,1)}, bf16[128,768]{1,0:T(8,128)(2,1)S(1)}, u32[]{:S(2)}, u32[]{:S(2)}) collective-permute-start(bf16[128,768]{1,0:T(8,128)(2,1)} %get-tuple-element.73), channel_id=1, source_target_pairs={{0,9},{1,8},{2,11},{3,10},{4,13},{5,12},{6,15},{7,14},{8,1},{9,0},... | collective-permute-start | bytes 589832 | tf_op jit(solution)/shard_map/ppermute | solution.py:346
  142.0 8.7 %collective-permute-start.34 = (bf16[128,768]{1,0:T(8,128)(2,1)}, bf16[128,768]{1,0:T(8,128)(2,1)S(1)}, u32[]{:S(2)}, u32[]{:S(2)}) collective-permute-start(bf16[128,768]{1,0:T(8,128)(2,1)} %get-tuple-element.72), channel_id=1, source_target_pairs={{0,8},{1,9},{2,10},{3,11},{4,12},{5,13},{6,14},{7,15},{8,0},{9,1},... | collective-permute-start | bytes 589832 | tf_op jit(solution)/shard_map/ppermute | solution.py:346
  (33 other events, 343.2 us)

commit v8 on v7

--- a/solution.py
+++ b/solution.py
@@ -60,10 +60,12 @@
         pltpu.make_async_copy(piece, held.at[where_ref[1 + i]], w_sem.at[i])
         for i, piece in enumerate(pieces)
     ]
-    for copy in x_copies + w_copies:
+    for copy in x_copies + w_copies[:INNER]:
         copy.start()
     for copy in x_copies:
         copy.wait()
+    for copy in w_copies[INNER:]:
+        copy.start()
 
     chunk = INNER * depth
     proj = [jnp.zeros((n_patches * rows, width), jnp.float32) for _ in range(3)]
@@ -376,8 +378,8 @@
         sides[1] = flip(after(pieces[1], far), 2)
         pieces[3] = to_partner(after(dealt[3], far, pieces[2]), 3)
         row_shares[2] = shares_of(jnp.where(inside, far, end_across))
-        row_shares[3] = shares_of(jnp.where(inside, across, end_far))
-        sides[2] = flip(after(pieces[2], end_far, sides[1]), 2)
+        row_shares[3] = shares_of(after(jnp.where(inside, across, end_far), row_shares[2][-1]))
+        sides[2] = flip(pieces[2], 2)
         late = [sides[2], row_shares[2][-1]]
         later = [row_shares[3][-1]]
     else:

time: 152 us -> 155 us (1.020)
  starting transfers between devices: 37.1 us -> 52.8 us
  waiting for transfers between devices: 81 us -> 67.7 us
    ppermute x9, starting transfers between devices: 13.8 us -> 26.4 us  [over_outer(): return lax.ppermute(x, 'patch', pairs)]
    ppermute x4, waiting for transfers between devices: 15.4 us -> 6.74 us  [along_fsdp(): lax.ppermute(x, 'fsdp', [(i, (i + step) % fsdp) for i in range(fsdp)])]
    ppermute x9, waiting for transfers between devices: 39.5 us -> 33.2 us  [over_outer(): return lax.ppermute(x, 'patch', pairs)]
    ppermute x2, waiting for transfers between devices: 3.98 us -> 6.66 us  [along_both(): return lax.ppermute(x, ('patch', 'fsdp'), pairs)]
    ppermute x18, starting transfers between devices: 8.64 us -> 11.1 us  [flip(): return lax.ppermute(x, 'patch', [(p, p ^ bits) for p in range(patches)])]
  transfers between devices with their start and end apart: 36 -> 36, of which waited for: 20 -> 15; matrix products, arithmetic and copies ran while one was open for 2% -> 1% of each run, Pallas kernels for 12% -> 13%
where the time goes in v8:
time: 155 us; the launch traced here: 154 us
  waiting for transfers between devices  67.7 us (44%)
  starting transfers between devices  52.8 us (34%)
  Pallas kernels  26.1 us (17%)
  local copies, waits for them, and re-layouts  3.52 us (2%)
  other arithmetic  3.23 us (2%)
    ppermute x9, waiting for transfers between devices, over_outer(): return lax.ppermute(x, 'patch', pairs)  33.2 us
    ppermute x9, starting transfers between devices, over_outer(): return lax.ppermute(x, 'patch', pairs)  26.4 us
    ppermute x3, waiting for transfers between devices, give(): lax.ppermute(x, 'patch', [(p, p ^ bits * INNER) for p in range(patches)])  17.2 us
    pallas_call x1, Pallas kernels, attend_patches(): pl.pallas_call(functools.partial(patch_kernel, depth, n_pieces, cuts), gr...  15.6 us
    ppermute x18, starting transfers between devices, flip(): return lax.ppermute(x, 'patch', [(p, p ^ bits) for p in range(patches)])  11.1 us
    ppermute x4, waiting for transfers between devices, along_fsdp(): lax.ppermute(x, 'fsdp', [(i, (i + step) % fsdp) for i in range(fsdp)])  6.74 us
    ppermute x2, waiting for transfers between devices, along_both(): return lax.ppermute(x, ('patch', 'fsdp'), pairs)  6.66 us
    ppermute x2, starting transfers between devices, along_both(): return lax.ppermute(x, ('patch', 'fsdp'), pairs)  5.69 us
  transfers between devices with their start and end apart: 36, of which 15 were waited for; matrix products, arithmetic and copies ran while one was open for 1% of the time, Pallas kernels for 13%

profile of v8, /device:TPU:0, one launch (start us, length us, event | category | flops | bytes accessed | tf_op | source)
XLA Modules:
  0.0 154.4 jit_solution(9915796387230013254)
XLA Ops:
  0.7 1.4 convert_reduce_fusion
  2.9 3.1 %collective-permute-start = (bf16[64,3072]{1,0:T(8,128)(2,1)S(1)}, bf16[64,3072]{1,0:T(8,128)(2,1)S(1)}, u32[]{:S(2)}, u32[]{:S(2)}) collective-permute-start(bf16[64,3072]{1,0:T(8,128)(2,1)S(1)} %constant_dynamic-slice_fusion), channel_id=1, source_target_pairs={{0,8},{2,10},{4,12},{6,14},{8,0},{10,2},{12,4},{14,6},{16,24},{18,... | collective-permute-start | bytes 1179656 | tf_op jit(solution)/shard_map/ppermute | solution.py:331
  6.7 2.8 %shard_map.157 = (bf16[832,256]{1,0:T(8,128)(2,1)}, bf16[832,256]{1,0:T(8,128)(2,1)}, bf16[832,256]{1,0:T(8,128)(2,1)}, bf16[832,256]{1,0:T(8,128)(2,1)}) custom-call(s32[1]{0:T(128)} %bitcast.member_ref, bf16[192,1024]{1,0:T(8,128)(2,1)} %refs_0_.2, bf16[192,1024]{1,0:T(8,128)(2,1)} %refs_1_.2, bf16[192,1024]{1,0:T(8,128)(2,1)} %refs_2_.1, ...), custom_call_target="tpu_custom_call" | custom-call | tf_op jit(solution)/shard_map/pallas_call | solution.py:207
  9.5 1.5 collective-permute-start.1
  11.0 4.1 %collective-permute-done.refs_5_ = bf16[64,3072]{1,0:T(8,128)(2,1)S(1)} collective-permute-done((bf16[64,3072]{1,0:T(8,128)(2,1)S(1)}, bf16[64,3072]{1,0:T(8,128)(2,1)S(1)}, u32[]{:S(2)}, u32[]{:S(2)}) %collective-permute-start) | collective-permute-done | bytes 393248 | tf_op jit(solution)/shard_map/ppermute | solution.py:331
  15.1 4.8 %collective-permute-start.5 = (bf16[832,256]{1,0:T(8,128)(2,1)}, bf16[832,256]{1,0:T(8,128)(2,1)}, u32[]{:S(2)}, u32[]{:S(2)}) collective-permute-start(bf16[832,256]{1,0:T(8,128)(2,1)} %get-tuple-element.43), channel_id=1, source_target_pairs={{0,8},{2,10},{4,12},{6,14},{8,0},{10,2},{12,4},{14,6},{16,24},{18,... | collective-permute-start | bytes 1277960 | tf_op jit(solution)/shard_map/ppermute | solution.py:331
  21.8 1.6 %collective-permute-start.2 = (bf16[64,3072]{1,0:T(8,128)(2,1)S(1)}, bf16[64,3072]{1,0:T(8,128)(2,1)S(1)}, u32[]{:S(2)}, u32[]{:S(2)}) collective-permute-start(bf16[64,3072]{1,0:T(8,128)(2,1)S(1)} %collective-permute-done.refs_5_), channel_id=1, source_target_pairs={{0,1},{1,0},{2,3},{3,2},{4,5},{5,4},{6,7},{7,6},{8,9},{9,8},{10,11... | collective-permute-start | bytes 1179656 | tf_op jit(solution)/shard_map/ppermute | solution.py:340
  23.3 13.7 %collective-permute-done.5.refs_15_ = bf16[832,256]{1,0:T(8,128)(2,1)} collective-permute-done((bf16[832,256]{1,0:T(8,128)(2,1)}, bf16[832,256]{1,0:T(8,128)(2,1)}, u32[]{:S(2)}, u32[]{:S(2)}) %collective-permute-start.5) | collective-permute-done | bytes 426016 | tf_op jit(solution)/shard_map/ppermute | solution.py:331
  38.3 1.3 collective-permute-start.8
  39.6 1.6 %collective-permute-start.14 = (bf16[832,256]{1,0:T(8,128)(2,1)}, bf16[832,256]{1,0:T(8,128)(2,1)S(1)}, u32[]{:S(2)}, u32[]{:S(2)}) collective-permute-start(bf16[832,256]{1,0:T(8,128)(2,1)} %collective-permute-done.5.refs_15_), channel_id=1, source_target_pairs={{0,4},{2,6},{4,0},{6,2},{8,12},{10,14},{12,8},{14,10},{16,20},{18,... | collective-permute-start | bytes 1277960 | tf_op jit(solution)/shard_map/ppermute | solution.py:337
  41.2 1.8 %collective-permute-done.10.refs_19_ = bf16[832,256]{1,0:T(8,128)(2,1)} collective-permute-done((bf16[832,256]{1,0:T(8,128)(2,1)}, bf16[832,256]{1,0:T(8,128)(2,1)}, u32[]{:S(2)}, u32[]{:S(2)}) %collective-permute-start.10) | collective-permute-done | bytes 426016 | tf_op jit(solution)/shard_map/ppermute | solution.py:331
  43.0 7.3 %collective-permute-start.19 = (bf16[832,256]{1,0:T(8,128)(2,1)}, bf16[832,256]{1,0:T(8,128)(2,1)}, u32[]{:S(2)}, u32[]{:S(2)}) collective-permute-start(bf16[832,256]{1,0:T(8,128)(2,1)} %get-tuple-element.57), channel_id=1, source_target_pairs={{0,24},{2,26},{4,28},{6,30},{8,16},{10,18},{12,20},{14,22},{16,8},... | collective-permute-start | bytes 1277960 | tf_op jit(solution)/shard_map/ppermute | solution.py:331
  50.3 1.5 collective-permute-start.11
  51.8 8.5 %collective-permute-done.6 = bf16[64,3072]{1,0:T(8,128)(2,1)S(1)} collective-permute-done((bf16[64,3072]{1,0:T(8,128)(2,1)S(1)}, bf16[64,3072]{1,0:T(8,128)(2,1)S(1)}, u32[]{:S(2)}, u32[]{:S(2)}) %collective-permute-start.6) | collective-permute-done | bytes 393248 | tf_op jit(solution)/shard_map/ppermute | solution.py:331
  60.3 1.6 %collective-permute-start.7 = (bf16[64,3072]{1,0:T(8,128)(2,1)S(1)}, bf16[64,3072]{1,0:T(8,128)(2,1)S(1)}, u32[]{:S(2)}, u32[]{:S(2)}) collective-permute-start(bf16[64,3072]{1,0:T(8,128)(2,1)S(1)} %broadcast_select_fusion.1.refs_7_), channel_id=1, source_target_pairs={{0,1},{1,0},{2,3},{3,2},{4,5},{5,4},{6,7},{7,6},{8,9},{9,8},{10,11... | collective-permute-start | bytes 1179656 | tf_op jit(solution)/shard_map/ppermute | solution.py:340
  61.9 5.2 %collective-permute-done.8 = bf16[64,3072]{1,0:T(8,128)(2,1)S(1)} collective-permute-done((bf16[64,3072]{1,0:T(8,128)(2,1)S(1)}, bf16[64,3072]{1,0:T(8,128)(2,1)S(1)}, u32[]{:S(2)}, u32[]{:S(2)}) %collective-permute-start.8) | collective-permute-done | bytes 393248 | tf_op jit(solution)/shard_map/ppermute | solution.py:331
  67.1 2.5 %collective-permute-done.7.refs_8_ = bf16[64,3072]{1,0:T(8,128)(2,1)S(1)} collective-permute-done((bf16[64,3072]{1,0:T(8,128)(2,1)S(1)}, bf16[64,3072]{1,0:T(8,128)(2,1)S(1)}, u32[]{:S(2)}, u32[]{:S(2)}) %collective-permute-start.7) | collective-permute-done | bytes 393248 | tf_op jit(solution)/shard_map/ppermute | solution.py:340
  69.7 1.5 collective-permute-start.9
  71.2 1.5 collective-permute-start.20
  73.4 4.2 %collective-permute-done.9.refs_10_ = bf16[64,3072]{1,0:T(8,128)(2,1)} collective-permute-done((bf16[64,3072]{1,0:T(8,128)(2,1)S(1)}, bf16[64,3072]{1,0:T(8,128)(2,1)}, u32[]{:S(2)}, u32[]{:S(2)}) %collective-permute-start.9) | collective-permute-done | bytes 393248 | tf_op jit(solution)/shard_map/ppermute | solution.py:340
  77.5 2.1 %collective-permute-done.20.refs_24_ = bf16[832,256]{1,0:T(8,128)(2,1)} collective-permute-done((bf16[832,256]{1,0:T(8,128)(2,1)}, bf16[832,256]{1,0:T(8,128)(2,1)}, u32[]{:S(2)}, u32[]{:S(2)}) %collective-permute-start.20) | collective-permute-done | bytes 426016 | tf_op jit(solution)/shard_map/ppermute | solution.py:337
  81.9 6.2 %collective-permute-start.29 = (bf16[192,1024]{1,0:T(8,128)(2,1)S(1)}, bf16[192,1024]{1,0:T(8,128)(2,1)S(1)}, u32[]{:S(2)}, u32[]{:S(2)}) collective-permute-start(bf16[192,1024]{1,0:T(8,128)(2,1)S(1)} %bitcast.34), channel_id=1, source_target_pairs={{0,16},{2,18},{4,20},{6,22},{8,24},{10,26},{12,28},{14,30},{16,0},... | collective-permute-start | bytes 1179656 | tf_op jit(solution)/shard_map/ppermute | solution.py:331
  88.7 1.3 collective-permute-start.26
  90.8 15.6 %shard_map.158 = (bf16[256,512]{1,0:T(8,128)(2,1)}, bf16[256,512]{1,0:T(8,128)(2,1)}, bf16[256,512]{1,0:T(8,128)(2,1)}, bf16[256,512]{1,0:T(8,128)(2,1)}) custom-call(s32[28]{0:T(128)} %stack.136.where_ref, bf16[512,1024]{1,0:T(8,128)(2,1)} %refs_0_.3, bf16[512,1024]{1,0:T(8,128)(2,1)} %refs_1_.3, f32[1,128]{1,0:T(1,128)} %bitcast.37, f32[1,128]{1,0:T(1,128)} %bitcast.38, ...), custom_call_target="tpu_custom_call" | custom-call | flops 3758096384 | bytes 6815744 | tf_op jit(solution)/shard_map/pallas_call | solution.py:155
  108.3 3.4 %collective-permute-start.25 = (bf16[256,512]{1,0:T(8,128)(2,1)}, bf16[256,512]{1,0:T(8,128)(2,1)S(1)}, u32[]{:S(2)}, u32[]{:S(2)}) collective-permute-start(bf16[256,512]{1,0:T(8,128)(2,1)} %get-tuple-element.63), channel_id=1, source_target_pairs={{0,24},{2,26},{4,28},{6,30},{8,16},{10,18},{12,20},{14,22},{16,8},... | collective-permute-start | bytes 786440 | tf_op jit(solution)/shard_map/ppermute | solution.py:417
  111.8 8.2 %collective-permute-done.23.refs_1_ = bf16[256,512]{1,0:T(8,128)(2,1)S(1)} collective-permute-done((bf16[256,512]{1,0:T(8,128)(2,1)}, bf16[256,512]{1,0:T(8,128)(2,1)S(1)}, u32[]{:S(2)}, u32[]{:S(2)}) %collective-permute-start.23) | collective-permute-done | bytes 262176 | tf_op jit(solution)/shard_map/ppermute | solution.py:417
  119.9 9.0 %collective-permute-done.24.refs_2_ = bf16[256,512]{1,0:T(8,128)(2,1)S(1)} collective-permute-done((bf16[256,512]{1,0:T(8,128)(2,1)}, bf16[256,512]{1,0:T(8,128)(2,1)S(1)}, u32[]{:S(2)}, u32[]{:S(2)}) %collective-permute-start.24) | collective-permute-done | bytes 262176 | tf_op jit(solution)/shard_map/ppermute | solution.py:417
  132.6 5.6 %shard_map.159 = (f32[128,768]{1,0:T(8,128)}, bf16[128,768]{1,0:T(8,128)(2,1)}, bf16[128,768]{1,0:T(8,128)(2,1)}, bf16[128,768]{1,0:T(8,128)(2,1)}) custom-call(s32[12]{0:T(128)} %stack.117.where_ref, bf16[256,512]{1,0:T(8,128)(2,1)} %get-tuple-element.74.refs_0_, bf16[256,512]{1,0:T(8,128)(2,1)} %copy-done.2, bf16[256,512]{1,0:T(8,128)(2,1)} %copy-done.3, ...), custom_call_target="tpu_custom_call" | custom-call | flops 805306368 | bytes 3145728 | tf_op jit(solution)/shard_map/pallas_call | solution.py:276
  139.0 5.7 %collective-permute-start.35 = (bf16[128,768]{1,0:T(8,128)(2,1)}, bf16[128,768]{1,0:T(8,128)(2,1)S(1)}, u32[]{:S(2)}, u32[]{:S(2)}) collective-permute-start(bf16[128,768]{1,0:T(8,128)(2,1)} %get-tuple-element.73), channel_id=1, source_target_pairs={{0,9},{1,8},{2,11},{3,10},{4,13},{5,12},{6,15},{7,14},{8,1},{9,0},... | collective-permute-start | bytes 589832 | tf_op jit(solution)/shard_map/ppermute | solution.py:348
  144.7 2.0 %shard_map.160 = (bf16[128,1024]{1,0:T(8,128)(2,1)}, bf16[128,1024]{1,0:T(8,128)(2,1)}) custom-call(s32[1]{0:T(128)} %bitcast.member_ref, bf16[256,512]{1,0:T(8,128)(2,1)} %get-tuple-element.74.refs_0_, bf16[256,512]{1,0:T(8,128)(2,1)} %copy-done.2, bf16[256,512]{1,0:T(8,128)(2,1)} %copy-done.3, bf16[256,512]{1,0:T(8,128)(2,1)} %copy-done.4), custom_call_target="tpu_custom_call" | custom-call | tf_op jit(solution)/shard_map/pallas_call | solution.py:231
  146.7 3.9 %collective-permute-done.35 = bf16[128,768]{1,0:T(8,128)(2,1)S(1)} collective-permute-done((bf16[128,768]{1,0:T(8,128)(2,1)}, bf16[128,768]{1,0:T(8,128)(2,1)S(1)}, u32[]{:S(2)}, u32[]{:S(2)}) %collective-permute-start.35) | collective-permute-done | bytes 196640 | tf_op jit(solution)/shard_map/ppermute | solution.py:348
  150.6 2.8 %collective-permute-done.34 = bf16[128,768]{1,0:T(8,128)(2,1)S(1)} collective-permute-done((bf16[128,768]{1,0:T(8,128)(2,1)}, bf16[128,768]{1,0:T(8,128)(2,1)S(1)}, u32[]{:S(2)}, u32[]{:S(2)}) %collective-permute-start.34) | collective-permute-done | bytes 196640 | tf_op jit(solution)/shard_map/ppermute | solution.py:348
  (115 shorter events, 16.3 us)
Async XLA Ops:
  2.9 12.2 %collective-permute-start = (bf16[64,3072]{1,0:T(8,128)(2,1)S(1)}, bf16[64,3072]{1,0:T(8,128)(2,1)S(1)}, u32[]{:S(2)}, u32[]{:S(2)}) collective-permute-start(bf16[64,3072]{1,0:T(8,128)(2,1)S(1)} %constant_dynamic-slice_fusion), channel_id=1, source_target_pairs={{0,8},{2,10},{4,12},{6,14},{8,0},{10,2},{12,4},{14,6},{16,24},{18,... | collective-permute-start | bytes 1179656 | tf_op jit(solution)/shard_map/ppermute | solution.py:331
  6.0 9.1 %collective-permute-start.4 = (bf16[64,3072]{1,0:T(8,128)(2,1)S(1)}, bf16[64,3072]{1,0:T(8,128)(2,1)S(1)}, u32[]{:S(2)}, u32[]{:S(2)}) collective-permute-start(bf16[64,3072]{1,0:T(8,128)(2,1)S(1)} %constant_dynamic-slice_fusion), channel_id=1, source_target_pairs={{8,16},{10,18},{12,20},{14,22},{16,8},{18,10},{20,12},{22,14},{9,1... | collective-permute-start | bytes 1179656 | tf_op jit(solution)/shard_map/ppermute | solution.py:331
  9.5 12.2 %collective-permute-start.1 = (bf16[832,256]{1,0:T(8,128)(2,1)}, bf16[832,256]{1,0:T(8,128)(2,1)S(1)}, u32[]{:S(2)}, u32[]{:S(2)}) collective-permute-start(bf16[832,256]{1,0:T(8,128)(2,1)} %get-tuple-element.49.refs_11_), channel_id=1, source_target_pairs={{0,4},{2,6},{4,0},{6,2},{8,12},{10,14},{12,8},{14,10},{16,20},{18,... | collective-permute-start | bytes 1277960 | tf_op jit(solution)/shard_map/ppermute | solution.py:337
  15.1 21.9 %collective-permute-start.5 = (bf16[832,256]{1,0:T(8,128)(2,1)}, bf16[832,256]{1,0:T(8,128)(2,1)}, u32[]{:S(2)}, u32[]{:S(2)}) collective-permute-start(bf16[832,256]{1,0:T(8,128)(2,1)} %get-tuple-element.43), channel_id=1, source_target_pairs={{0,8},{2,10},{4,12},{6,14},{8,0},{10,2},{12,4},{14,6},{16,24},{18,... | collective-permute-start | bytes 1277960 | tf_op jit(solution)/shard_map/ppermute | solution.py:331
  19.9 23.1 %collective-permute-start.10 = (bf16[832,256]{1,0:T(8,128)(2,1)}, bf16[832,256]{1,0:T(8,128)(2,1)}, u32[]{:S(2)}, u32[]{:S(2)}) collective-permute-start(bf16[832,256]{1,0:T(8,128)(2,1)} %get-tuple-element.48), channel_id=1, source_target_pairs={{0,16},{2,18},{4,20},{6,22},{8,24},{10,26},{12,28},{14,30},{16,0},... | collective-permute-start | bytes 1277960 | tf_op jit(solution)/shard_map/ppermute | solution.py:331
  21.1 17.2 %collective-permute-start.3 = (bf16[64,3072]{1,0:T(8,128)(2,1)S(1)}, bf16[64,3072]{1,0:T(8,128)(2,1)S(1)}, u32[]{:S(2)}, u32[]{:S(2)}) collective-permute-start(bf16[64,3072]{1,0:T(8,128)(2,1)S(1)} %collective-permute-done.refs_5_), channel_id=1, source_target_pairs={{8,16},{10,18},{12,20},{14,22},{16,8},{18,10},{20,12},{22,14},{9,1... | collective-permute-start | bytes 1179656 | tf_op jit(solution)/shard_map/ppermute | solution.py:331
  21.8 16.5 %collective-permute-start.2 = (bf16[64,3072]{1,0:T(8,128)(2,1)S(1)}, bf16[64,3072]{1,0:T(8,128)(2,1)S(1)}, u32[]{:S(2)}, u32[]{:S(2)}) collective-permute-start(bf16[64,3072]{1,0:T(8,128)(2,1)S(1)} %collective-permute-done.refs_5_), channel_id=1, source_target_pairs={{0,1},{1,0},{2,3},{3,2},{4,5},{5,4},{6,7},{7,6},{8,9},{9,8},{10,11... | collective-permute-start | bytes 1179656 | tf_op jit(solution)/shard_map/ppermute | solution.py:340
  37.0 23.3 %collective-permute-start.6 = (bf16[64,3072]{1,0:T(8,128)(2,1)S(1)}, bf16[64,3072]{1,0:T(8,128)(2,1)S(1)}, u32[]{:S(2)}, u32[]{:S(2)}) collective-permute-start(bf16[64,3072]{1,0:T(8,128)(2,1)S(1)} %collective-permute-done.4), channel_id=1, source_target_pairs={{8,0},{10,2},{12,4},{14,6},{16,24},{18,26},{20,28},{22,30},{9,1},{... | collective-permute-start | bytes 1179656 | tf_op jit(solution)/shard_map/ppermute | solution.py:331
  38.3 28.7 %collective-permute-start.8 = (bf16[64,3072]{1,0:T(8,128)(2,1)S(1)}, bf16[64,3072]{1,0:T(8,128)(2,1)S(1)}, u32[]{:S(2)}, u32[]{:S(2)}) collective-permute-start(bf16[64,3072]{1,0:T(8,128)(2,1)S(1)} %collective-permute-done.3), channel_id=1, source_target_pairs={{8,0},{10,2},{12,4},{14,6},{16,24},{18,26},{20,28},{22,30},{9,1},{... | collective-permute-start | bytes 1179656 | tf_op jit(solution)/shard_map/ppermute | solution.py:331
  39.6 33.7 %collective-permute-start.14 = (bf16[832,256]{1,0:T(8,128)(2,1)}, bf16[832,256]{1,0:T(8,128)(2,1)S(1)}, u32[]{:S(2)}, u32[]{:S(2)}) collective-permute-start(bf16[832,256]{1,0:T(8,128)(2,1)} %collective-permute-done.5.refs_15_), channel_id=1, source_target_pairs={{0,4},{2,6},{4,0},{6,2},{8,12},{10,14},{12,8},{14,10},{16,20},{18,... | collective-permute-start | bytes 1277960 | tf_op jit(solution)/shard_map/ppermute | solution.py:337
  43.0 28.2 %collective-permute-start.19 = (bf16[832,256]{1,0:T(8,128)(2,1)}, bf16[832,256]{1,0:T(8,128)(2,1)}, u32[]{:S(2)}, u32[]{:S(2)}) collective-permute-start(bf16[832,256]{1,0:T(8,128)(2,1)} %get-tuple-element.57), channel_id=1, source_target_pairs={{0,24},{2,26},{4,28},{6,30},{8,16},{10,18},{12,20},{14,22},{16,8},... | collective-permute-start | bytes 1277960 | tf_op jit(solution)/shard_map/ppermute | solution.py:331
  50.3 22.4 %collective-permute-start.11 = (bf16[832,256]{1,0:T(8,128)(2,1)}, bf16[832,256]{1,0:T(8,128)(2,1)}, u32[]{:S(2)}, u32[]{:S(2)}) collective-permute-start(bf16[832,256]{1,0:T(8,128)(2,1)} %collective-permute-done.10.refs_19_), channel_id=1, source_target_pairs={{0,4},{2,6},{4,0},{6,2},{8,12},{10,14},{12,8},{14,10},{16,20},{18,... | collective-permute-start | bytes 1277960 | tf_op jit(solution)/shard_map/ppermute | solution.py:337
  60.3 9.3 %collective-permute-start.7 = (bf16[64,3072]{1,0:T(8,128)(2,1)S(1)}, bf16[64,3072]{1,0:T(8,128)(2,1)S(1)}, u32[]{:S(2)}, u32[]{:S(2)}) collective-permute-start(bf16[64,3072]{1,0:T(8,128)(2,1)S(1)} %broadcast_select_fusion.1.refs_7_), channel_id=1, source_target_pairs={{0,1},{1,0},{2,3},{3,2},{4,5},{5,4},{6,7},{7,6},{8,9},{9,8},{10,11... | collective-permute-start | bytes 1179656 | tf_op jit(solution)/shard_map/ppermute | solution.py:340
  69.7 7.9 %collective-permute-start.9 = (bf16[64,3072]{1,0:T(8,128)(2,1)S(1)}, bf16[64,3072]{1,0:T(8,128)(2,1)}, u32[]{:S(2)}, u32[]{:S(2)}) collective-permute-start(bf16[64,3072]{1,0:T(8,128)(2,1)S(1)} %broadcast_select_fusion.refs_9_), channel_id=1, source_target_pairs={{0,1},{1,0},{2,3},{3,2},{4,5},{5,4},{6,7},{7,6},{8,9},{9,8},{10,11... | collective-permute-start | bytes 1179656 | tf_op jit(solution)/shard_map/ppermute | solution.py:340
  71.2 8.4 %collective-permute-start.20 = (bf16[832,256]{1,0:T(8,128)(2,1)}, bf16[832,256]{1,0:T(8,128)(2,1)}, u32[]{:S(2)}, u32[]{:S(2)}) collective-permute-start(bf16[832,256]{1,0:T(8,128)(2,1)} %collective-permute-done.19.refs_23_), channel_id=1, source_target_pairs={{0,4},{2,6},{4,0},{6,2},{8,12},{10,14},{12,8},{14,10},{16,20},{18,... | collective-permute-start | bytes 1277960 | tf_op jit(solution)/shard_map/ppermute | solution.py:337
  72.7 6.9 %collective-permute-start.12 = (bf16[832,256]{1,0:T(8,128)(2,1)S(1)}, bf16[832,256]{1,0:T(8,128)(2,1)S(1)}, u32[]{:S(2)}, u32[]{:S(2)}) collective-permute-start(bf16[832,256]{1,0:T(8,128)(2,1)S(1)} %copy-done.16), channel_id=1, source_target_pairs={{0,2},{2,0},{4,6},{6,4},{8,10},{10,8},{12,14},{14,12},{16,18},{18,... | collective-permute-start | bytes 1277960 | tf_op jit(solution)/shard_map/ppermute | solution.py:337
  72.8 7.3 %collective-permute-start.13 = (bf16[832,256]{1,0:T(8,128)(2,1)S(1)}, bf16[832,256]{1,0:T(8,128)(2,1)S(1)}, u32[]{:S(2)}, u32[]{:S(2)}) collective-permute-start(bf16[832,256]{1,0:T(8,128)(2,1)S(1)} %copy-done.18), channel_id=1, source_target_pairs={{0,2},{2,0},{4,6},{6,4},{8,10},{10,8},{12,14},{14,12},{16,18},{18,... | collective-permute-start | bytes 1277960 | tf_op jit(solution)/shard_map/ppermute | solution.py:337
  73.3 6.9 %collective-permute-start.15 = (bf16[832,256]{1,0:T(8,128)(2,1)}, bf16[832,256]{1,0:T(8,128)(2,1)S(1)}, u32[]{:S(2)}, u32[]{:S(2)}) collective-permute-start(bf16[832,256]{1,0:T(8,128)(2,1)} %collective-permute-done.5.refs_15_), channel_id=1, source_target_pairs={{0,2},{2,0},{4,6},{6,4},{8,10},{10,8},{12,14},{14,12},{16,18},{18,... | collective-permute-start | bytes 1277960 | tf_op jit(solution)/shard_map/ppermute | solution.py:337
  77.5 3.1 %collective-permute-start.16 = (bf16[832,256]{1,0:T(8,128)(2,1)S(1)}, bf16[832,256]{1,0:T(8,128)(2,1)S(1)}, u32[]{:S(2)}, u32[]{:S(2)}) collective-permute-start(bf16[832,256]{1,0:T(8,128)(2,1)S(1)} %collective-permute-done.14.refs_16_), channel_id=1, source_target_pairs={{0,2},{2,0},{4,6},{6,4},{8,10},{10,8},{12,14},{14,12},{16,18},{18,... | collective-permute-start | bytes 1277960 | tf_op jit(solution)/shard_map/ppermute | solution.py:337
  79.6 9.1 %collective-permute-start.17 = (bf16[832,256]{1,0:T(8,128)(2,1)}, bf16[832,256]{1,0:T(8,128)(2,1)}, u32[]{:S(2)}, u32[]{:S(2)}) collective-permute-start(bf16[832,256]{1,0:T(8,128)(2,1)} %collective-permute-done.10.refs_19_), channel_id=1, source_target_pairs={{0,2},{2,0},{4,6},{6,4},{8,10},{10,8},{12,14},{14,12},{16,18},{18,... | collective-permute-start | bytes 1277960 | tf_op jit(solution)/shard_map/ppermute | solution.py:337
  79.6 10.4 %collective-permute-start.18 = (bf16[832,256]{1,0:T(8,128)(2,1)}, bf16[832,256]{1,0:T(8,128)(2,1)S(1)}, u32[]{:S(2)}, u32[]{:S(2)}) collective-permute-start(bf16[832,256]{1,0:T(8,128)(2,1)} %collective-permute-done.11.refs_20_), channel_id=1, source_target_pairs={{0,2},{2,0},{4,6},{6,4},{8,10},{10,8},{12,14},{14,12},{16,18},{18,... | collective-permute-start | bytes 1277960 | tf_op jit(solution)/shard_map/ppermute | solution.py:337
  80.1 9.9 %collective-permute-start.21 = (bf16[832,256]{1,0:T(8,128)(2,1)}, bf16[832,256]{1,0:T(8,128)(2,1)}, u32[]{:S(2)}, u32[]{:S(2)}) collective-permute-start(bf16[832,256]{1,0:T(8,128)(2,1)} %collective-permute-done.19.refs_23_), channel_id=1, source_target_pairs={{0,2},{2,0},{4,6},{6,4},{8,10},{10,8},{12,14},{14,12},{16,18},{18,... | collective-permute-start | bytes 1277960 | tf_op jit(solution)/shard_map/ppermute | solution.py:337
  80.2 9.8 %collective-permute-start.22 = (bf16[832,256]{1,0:T(8,128)(2,1)}, bf16[832,256]{1,0:T(8,128)(2,1)}, u32[]{:S(2)}, u32[]{:S(2)}) collective-permute-start(bf16[832,256]{1,0:T(8,128)(2,1)} %collective-permute-done.20.refs_24_), channel_id=1, source_target_pairs={{0,2},{2,0},{4,6},{6,4},{8,10},{10,8},{12,14},{14,12},{16,18},{18,... | collective-permute-start | bytes 1277960 | tf_op jit(solution)/shard_map/ppermute | solution.py:337
  81.9 24.6 %collective-permute-start.29 = (bf16[192,1024]{1,0:T(8,128)(2,1)S(1)}, bf16[192,1024]{1,0:T(8,128)(2,1)S(1)}, u32[]{:S(2)}, u32[]{:S(2)}) collective-permute-start(bf16[192,1024]{1,0:T(8,128)(2,1)S(1)} %bitcast.34), channel_id=1, source_target_pairs={{0,16},{2,18},{4,20},{6,22},{8,24},{10,26},{12,28},{14,30},{16,0},... | collective-permute-start | bytes 1179656 | tf_op jit(solution)/shard_map/ppermute | solution.py:331
  88.7 40.3 %collective-permute-start.26 = (bf16[192,1024]{1,0:T(8,128)(2,1)S(1)}, bf16[192,1024]{1,0:T(8,128)(2,1)S(1)}, u32[]{:S(2)}, u32[]{:S(2)}) collective-permute-start(bf16[192,1024]{1,0:T(8,128)(2,1)S(1)} %bitcast.35), channel_id=1, source_target_pairs={{0,4},{2,6},{4,0},{6,2},{8,12},{10,14},{12,8},{14,10},{16,20},{18,... | collective-permute-start | bytes 1179656 | tf_op jit(solution)/shard_map/ppermute | solution.py:337
  106.5 23.2 %collective-permute-start.30 = (bf16[192,1024]{1,0:T(8,128)(2,1)S(1)}, bf16[192,1024]{1,0:T(8,128)(2,1)S(1)}, u32[]{:S(2)}, u32[]{:S(2)}) collective-permute-start(bf16[192,1024]{1,0:T(8,128)(2,1)S(1)} %collective-permute-done.29.refs_8_), channel_id=1, source_target_pairs={{0,4},{2,6},{4,0},{6,2},{8,12},{10,14},{12,8},{14,10},{16,20},{18,... | collective-permute-start | bytes 1179656 | tf_op jit(solution)/shard_map/ppermute | solution.py:337
  107.4 12.6 %collective-permute-start.23 = (bf16[256,512]{1,0:T(8,128)(2,1)}, bf16[256,512]{1,0:T(8,128)(2,1)S(1)}, u32[]{:S(2)}, u32[]{:S(2)}) collective-permute-start(bf16[256,512]{1,0:T(8,128)(2,1)} %get-tuple-element.61), channel_id=1, source_target_pairs={{0,8},{2,10},{4,12},{6,14},{8,0},{10,2},{12,4},{14,6},{16,24},{18,... | collective-permute-start | bytes 786440 | tf_op jit(solution)/shard_map/ppermute | solution.py:417
  107.4 21.6 %collective-permute-start.24 = (bf16[256,512]{1,0:T(8,128)(2,1)}, bf16[256,512]{1,0:T(8,128)(2,1)S(1)}, u32[]{:S(2)}, u32[]{:S(2)}) collective-permute-start(bf16[256,512]{1,0:T(8,128)(2,1)} %get-tuple-element.62), channel_id=1, source_target_pairs={{0,16},{2,18},{4,20},{6,22},{8,24},{10,26},{12,28},{14,30},{16,0},... | collective-permute-start | bytes 786440 | tf_op jit(solution)/shard_map/ppermute | solution.py:417
  108.3 20.6 %collective-permute-start.25 = (bf16[256,512]{1,0:T(8,128)(2,1)}, bf16[256,512]{1,0:T(8,128)(2,1)S(1)}, u32[]{:S(2)}, u32[]{:S(2)}) collective-permute-start(bf16[256,512]{1,0:T(8,128)(2,1)} %get-tuple-element.63), channel_id=1, source_target_pairs={{0,24},{2,26},{4,28},{6,30},{8,16},{10,18},{12,20},{14,22},{16,8},... | collective-permute-start | bytes 786440 | tf_op jit(solution)/shard_map/ppermute | solution.py:417
  138.3 8.4 %collective-permute-start.33 = (bf16[128,768]{1,0:T(8,128)(2,1)}, bf16[128,768]{1,0:T(8,128)(2,1)S(1)}, u32[]{:S(2)}, u32[]{:S(2)}) collective-permute-start(bf16[128,768]{1,0:T(8,128)(2,1)} %get-tuple-element.71), channel_id=1, source_target_pairs={{0,1},{1,0},{2,3},{3,2},{4,5},{5,4},{6,7},{7,6},{8,9},{9,8},{10,11... | collective-permute-start | bytes 589832 | tf_op jit(solution)/shard_map/ppermute | solution.py:340
  139.0 11.6 %collective-permute-start.35 = (bf16[128,768]{1,0:T(8,128)(2,1)}, bf16[128,768]{1,0:T(8,128)(2,1)S(1)}, u32[]{:S(2)}, u32[]{:S(2)}) collective-permute-start(bf16[128,768]{1,0:T(8,128)(2,1)} %get-tuple-element.73), channel_id=1, source_target_pairs={{0,9},{1,8},{2,11},{3,10},{4,13},{5,12},{6,15},{7,14},{8,1},{9,0},... | collective-permute-start | bytes 589832 | tf_op jit(solution)/shard_map/ppermute | solution.py:348
  144.7 8.7 %collective-permute-start.34 = (bf16[128,768]{1,0:T(8,128)(2,1)}, bf16[128,768]{1,0:T(8,128)(2,1)S(1)}, u32[]{:S(2)}, u32[]{:S(2)}) collective-permute-start(bf16[128,768]{1,0:T(8,128)(2,1)} %get-tuple-element.72), channel_id=1, source_target_pairs={{0,8},{1,9},{2,10},{3,11},{4,12},{5,13},{6,14},{7,15},{8,0},{9,1},... | collective-permute-start | bytes 589832 | tf_op jit(solution)/shard_map/ppermute | solution.py:348
  (32 other events, 300.8 us)

commit v9 on v8

--- a/solution.py
+++ b/solution.py
@@ -370,7 +370,7 @@
         across = over_outer(part, middle)
         sides[0] = flip(pieces[0], 2)
         far = over_outer(near, middle)
-        pieces[2] = to_partner(after(dealt[2], near, across), 2)
+        pieces[2] = to_partner(after(dealt[2], far), 2)
         pieces[1] = to_partner(after(dealt[1], near, across), 1)
         row_shares[1] = shares_of(after(near, sides[0]))
         end_across = over_outer(after(across, pieces[1]), ends)

time: 155 us -> 151 us (0.974)
  starting transfers between devices: 52.8 us -> 44.4 us
  waiting for transfers between devices: 67.7 us -> 72.7 us
    ppermute x9, starting transfers between devices: 26.4 us -> 17 us  [over_outer(): return lax.ppermute(x, 'patch', pairs)]
    ppermute x9, waiting for transfers between devices: 33.2 us -> 37.9 us  [over_outer(): return lax.ppermute(x, 'patch', pairs)]
  transfers between devices with their start and end apart: 36 -> 36, of which waited for: 15 -> 16; matrix products, arithmetic and copies ran while one was open for 1% -> 1% of each run, Pallas kernels for 13% -> 14%
where the time goes in v9:
time: 151 us
  waiting for transfers between devices  72.7 us (48%)
  starting transfers between devices  44.4 us (29%)
  Pallas kernels  26.1 us (17%)
  local copies, waits for them, and re-layouts  3.51 us (2%)
  other arithmetic  3.23 us (2%)
    ppermute x9, waiting for transfers between devices, over_outer(): return lax.ppermute(x, 'patch', pairs)  37.9 us
    ppermute x3, waiting for transfers between devices, give(): lax.ppermute(x, 'patch', [(p, p ^ bits * INNER) for p in range(patches)])  17.2 us
    ppermute x9, starting transfers between devices, over_outer(): return lax.ppermute(x, 'patch', pairs)  17 us
    pallas_call x1, Pallas kernels, attend_patches(): pl.pallas_call(functools.partial(patch_kernel, depth, n_pieces, cuts), gr...  15.6 us
    ppermute x18, starting transfers between devices, flip(): return lax.ppermute(x, 'patch', [(p, p ^ bits) for p in range(patches)])  11.9 us
    ppermute x2, waiting for transfers between devices, along_both(): return lax.ppermute(x, ('patch', 'fsdp'), pairs)  6.67 us
    ppermute x4, waiting for transfers between devices, along_fsdp(): lax.ppermute(x, 'fsdp', [(i, (i + step) % fsdp) for i in range(fsdp)])  6.44 us
    ppermute x4, starting transfers between devices, along_fsdp(): lax.ppermute(x, 'fsdp', [(i, (i + step) % fsdp) for i in range(fsdp)])  5.78 us
  transfers between devices with their start and end apart: 36, of which 16 were waited for; matrix products, arithmetic and copies ran while one was open for 1% of the time, Pallas kernels for 14%

profile of v9, /device:TPU:0, one launch (start us, length us, event | category | flops | bytes accessed | tf_op | source)
XLA Modules:
  0.0 151.0 jit_solution(8360239152627538326)
XLA Ops:
  2.9 3.1 %collective-permute-start = (bf16[64,3072]{1,0:T(8,128)(2,1)S(1)}, bf16[64,3072]{1,0:T(8,128)(2,1)}, u32[]{:S(2)}, u32[]{:S(2)}) collective-permute-start(bf16[64,3072]{1,0:T(8,128)(2,1)S(1)} %constant_dynamic-slice_fusion), channel_id=1, source_target_pairs={{0,8},{2,10},{4,12},{6,14},{8,0},{10,2},{12,4},{14,6},{16,24},{18,... | collective-permute-start | bytes 1179656 | tf_op jit(solution)/shard_map/ppermute | solution.py:331
  6.7 2.8 %shard_map.157 = (bf16[832,256]{1,0:T(8,128)(2,1)}, bf16[832,256]{1,0:T(8,128)(2,1)}, bf16[832,256]{1,0:T(8,128)(2,1)}, bf16[832,256]{1,0:T(8,128)(2,1)}) custom-call(s32[1]{0:T(128)} %bitcast.member_ref, bf16[192,1024]{1,0:T(8,128)(2,1)} %refs_0_.2, bf16[192,1024]{1,0:T(8,128)(2,1)} %refs_1_.2, bf16[192,1024]{1,0:T(8,128)(2,1)} %refs_2_.1, ...), custom_call_target="tpu_custom_call" | custom-call | tf_op jit(solution)/shard_map/pallas_call | solution.py:207
  9.5 1.5 %collective-permute-start.1 = (bf16[832,256]{1,0:T(8,128)(2,1)}, bf16[832,256]{1,0:T(8,128)(2,1)S(1)}, u32[]{:S(2)}, u32[]{:S(2)}) collective-permute-start(bf16[832,256]{1,0:T(8,128)(2,1)} %get-tuple-element.49.refs_11_), channel_id=1, source_target_pairs={{0,4},{2,6},{4,0},{6,2},{8,12},{10,14},{12,8},{14,10},{16,20},{18,... | collective-permute-start | bytes 1277960 | tf_op jit(solution)/shard_map/ppermute | solution.py:337
  11.0 4.2 %collective-permute-done.refs_5_ = bf16[64,3072]{1,0:T(8,128)(2,1)} collective-permute-done((bf16[64,3072]{1,0:T(8,128)(2,1)S(1)}, bf16[64,3072]{1,0:T(8,128)(2,1)}, u32[]{:S(2)}, u32[]{:S(2)}) %collective-permute-start) | collective-permute-done | bytes 393248 | tf_op jit(solution)/shard_map/ppermute | solution.py:331
  15.2 4.7 %collective-permute-start.5 = (bf16[832,256]{1,0:T(8,128)(2,1)}, bf16[832,256]{1,0:T(8,128)(2,1)}, u32[]{:S(2)}, u32[]{:S(2)}) collective-permute-start(bf16[832,256]{1,0:T(8,128)(2,1)} %get-tuple-element.43), channel_id=1, source_target_pairs={{0,8},{2,10},{4,12},{6,14},{8,0},{10,2},{12,4},{14,6},{16,24},{18,... | collective-permute-start | bytes 1277960 | tf_op jit(solution)/shard_map/ppermute | solution.py:331
  21.0 1.5 collective-permute-start.2
  22.5 6.6 %collective-permute-done.5.refs_15_ = bf16[832,256]{1,0:T(8,128)(2,1)} collective-permute-done((bf16[832,256]{1,0:T(8,128)(2,1)}, bf16[832,256]{1,0:T(8,128)(2,1)}, u32[]{:S(2)}, u32[]{:S(2)}) %collective-permute-start.5) | collective-permute-done | bytes 426016 | tf_op jit(solution)/shard_map/ppermute | solution.py:331
  30.5 3.6 %collective-permute-start.10 = (bf16[832,256]{1,0:T(8,128)(2,1)}, bf16[832,256]{1,0:T(8,128)(2,1)}, u32[]{:S(2)}, u32[]{:S(2)}) collective-permute-start(bf16[832,256]{1,0:T(8,128)(2,1)} %get-tuple-element.48), channel_id=1, source_target_pairs={{0,16},{2,18},{4,20},{6,22},{8,24},{10,26},{12,28},{14,30},{16,0},... | collective-permute-start | bytes 1277960 | tf_op jit(solution)/shard_map/ppermute | solution.py:331
  35.4 1.6 %collective-permute-start.14 = (bf16[832,256]{1,0:T(8,128)(2,1)}, bf16[832,256]{1,0:T(8,128)(2,1)S(1)}, u32[]{:S(2)}, u32[]{:S(2)}) collective-permute-start(bf16[832,256]{1,0:T(8,128)(2,1)} %collective-permute-done.5.refs_15_), channel_id=1, source_target_pairs={{0,4},{2,6},{4,0},{6,2},{8,12},{10,14},{12,8},{14,10},{16,20},{18,... | collective-permute-start | bytes 1277960 | tf_op jit(solution)/shard_map/ppermute | solution.py:337
  36.9 6.1 %collective-permute-done.6 = bf16[64,3072]{1,0:T(8,128)(2,1)S(1)} collective-permute-done((bf16[64,3072]{1,0:T(8,128)(2,1)S(1)}, bf16[64,3072]{1,0:T(8,128)(2,1)S(1)}, u32[]{:S(2)}, u32[]{:S(2)}) %collective-permute-start.6) | collective-permute-done | bytes 393248 | tf_op jit(solution)/shard_map/ppermute | solution.py:331
  43.1 1.6 %collective-permute-start.7 = (bf16[64,3072]{1,0:T(8,128)(2,1)S(1)}, bf16[64,3072]{1,0:T(8,128)(2,1)S(1)}, u32[]{:S(2)}, u32[]{:S(2)}) collective-permute-start(bf16[64,3072]{1,0:T(8,128)(2,1)S(1)} %broadcast_select_fusion.1.refs_7_), channel_id=1, source_target_pairs={{0,1},{1,0},{2,3},{3,2},{4,5},{5,4},{6,7},{7,6},{8,9},{9,8},{10,11... | collective-permute-start | bytes 1179656 | tf_op jit(solution)/shard_map/ppermute | solution.py:340
  44.7 7.1 %collective-permute-done.10.refs_19_ = bf16[832,256]{1,0:T(8,128)(2,1)} collective-permute-done((bf16[832,256]{1,0:T(8,128)(2,1)}, bf16[832,256]{1,0:T(8,128)(2,1)}, u32[]{:S(2)}, u32[]{:S(2)}) %collective-permute-start.10) | collective-permute-done | bytes 426016 | tf_op jit(solution)/shard_map/ppermute | solution.py:331
  51.8 1.5 collective-permute-start.19
  53.3 1.5 %collective-permute-start.11 = (bf16[832,256]{1,0:T(8,128)(2,1)}, bf16[832,256]{1,0:T(8,128)(2,1)}, u32[]{:S(2)}, u32[]{:S(2)}) collective-permute-start(bf16[832,256]{1,0:T(8,128)(2,1)} %collective-permute-done.10.refs_19_), channel_id=1, source_target_pairs={{0,4},{2,6},{4,0},{6,2},{8,12},{10,14},{12,8},{14,10},{16,20},{18,... | collective-permute-start | bytes 1277960 | tf_op jit(solution)/shard_map/ppermute | solution.py:337
  54.8 12.2 %collective-permute-done.8 = bf16[64,3072]{1,0:T(8,128)(2,1)S(1)} collective-permute-done((bf16[64,3072]{1,0:T(8,128)(2,1)S(1)}, bf16[64,3072]{1,0:T(8,128)(2,1)S(1)}, u32[]{:S(2)}, u32[]{:S(2)}) %collective-permute-start.8) | collective-permute-done | bytes 393248 | tf_op jit(solution)/shard_map/ppermute | solution.py:331
  67.1 1.6 %collective-permute-start.9 = (bf16[64,3072]{1,0:T(8,128)(2,1)S(1)}, bf16[64,3072]{1,0:T(8,128)(2,1)}, u32[]{:S(2)}, u32[]{:S(2)}) collective-permute-start(bf16[64,3072]{1,0:T(8,128)(2,1)S(1)} %broadcast_select_fusion.refs_9_), channel_id=1, source_target_pairs={{0,1},{1,0},{2,3},{3,2},{4,5},{5,4},{6,7},{7,6},{8,9},{9,8},{10,11... | collective-permute-start | bytes 1179656 | tf_op jit(solution)/shard_map/ppermute | solution.py:340
  68.7 1.6 %collective-permute-start.20 = (bf16[832,256]{1,0:T(8,128)(2,1)}, bf16[832,256]{1,0:T(8,128)(2,1)}, u32[]{:S(2)}, u32[]{:S(2)}) collective-permute-start(bf16[832,256]{1,0:T(8,128)(2,1)} %collective-permute-done.19.refs_23_), channel_id=1, source_target_pairs={{0,4},{2,6},{4,0},{6,2},{8,12},{10,14},{12,8},{14,10},{16,20},{18,... | collective-permute-start | bytes 1277960 | tf_op jit(solution)/shard_map/ppermute | solution.py:337
  70.9 6.4 %collective-permute-done.9.refs_10_ = bf16[64,3072]{1,0:T(8,128)(2,1)} collective-permute-done((bf16[64,3072]{1,0:T(8,128)(2,1)S(1)}, bf16[64,3072]{1,0:T(8,128)(2,1)}, u32[]{:S(2)}, u32[]{:S(2)}) %collective-permute-start.9) | collective-permute-done | bytes 393248 | tf_op jit(solution)/shard_map/ppermute | solution.py:340
  77.3 2.2 %collective-permute-done.20.refs_24_ = bf16[832,256]{1,0:T(8,128)(2,1)} collective-permute-done((bf16[832,256]{1,0:T(8,128)(2,1)}, bf16[832,256]{1,0:T(8,128)(2,1)}, u32[]{:S(2)}, u32[]{:S(2)}) %collective-permute-start.20) | collective-permute-done | bytes 426016 | tf_op jit(solution)/shard_map/ppermute | solution.py:337
  82.8 1.5 %collective-permute-start.26 = (bf16[192,1024]{1,0:T(8,128)(2,1)S(1)}, bf16[192,1024]{1,0:T(8,128)(2,1)S(1)}, u32[]{:S(2)}, u32[]{:S(2)}) collective-permute-start(bf16[192,1024]{1,0:T(8,128)(2,1)S(1)} %bitcast.35), channel_id=1, source_target_pairs={{0,4},{2,6},{4,0},{6,2},{8,12},{10,14},{12,8},{14,10},{16,20},{18,... | collective-permute-start | bytes 1179656 | tf_op jit(solution)/shard_map/ppermute | solution.py:337
  85.1 15.6 %shard_map.158 = (bf16[256,512]{1,0:T(8,128)(2,1)}, bf16[256,512]{1,0:T(8,128)(2,1)}, bf16[256,512]{1,0:T(8,128)(2,1)}, bf16[256,512]{1,0:T(8,128)(2,1)}) custom-call(s32[28]{0:T(128)} %stack.136.where_ref, bf16[512,1024]{1,0:T(8,128)(2,1)} %refs_0_.3, bf16[512,1024]{1,0:T(8,128)(2,1)} %refs_1_.3, f32[1,128]{1,0:T(1,128)} %bitcast.37, f32[1,128]{1,0:T(1,128)} %bitcast.38, ...), custom_call_target="tpu_custom_call" | custom-call | flops 3758096384 | bytes 6815744 | tf_op jit(solution)/shard_map/pallas_call | solution.py:155
  100.7 1.6 %collective-permute-done.29.refs_8_ = bf16[192,1024]{1,0:T(8,128)(2,1)S(1)} collective-permute-done((bf16[192,1024]{1,0:T(8,128)(2,1)S(1)}, bf16[192,1024]{1,0:T(8,128)(2,1)S(1)}, u32[]{:S(2)}, u32[]{:S(2)}) %collective-permute-start.29) | collective-permute-done | bytes 393248 | tf_op jit(solution)/shard_map/ppermute | solution.py:331
  102.3 1.5 %collective-permute-start.30 = (bf16[192,1024]{1,0:T(8,128)(2,1)S(1)}, bf16[192,1024]{1,0:T(8,128)(2,1)S(1)}, u32[]{:S(2)}, u32[]{:S(2)}) collective-permute-start(bf16[192,1024]{1,0:T(8,128)(2,1)S(1)} %collective-permute-done.29.refs_8_), channel_id=1, source_target_pairs={{0,4},{2,6},{4,0},{6,2},{8,12},{10,14},{12,8},{14,10},{16,20},{18,... | collective-permute-start | bytes 1179656 | tf_op jit(solution)/shard_map/ppermute | solution.py:337
  103.8 1.9 %collective-permute-start.24 = (bf16[256,512]{1,0:T(8,128)(2,1)}, bf16[256,512]{1,0:T(8,128)(2,1)S(1)}, u32[]{:S(2)}, u32[]{:S(2)}) collective-permute-start(bf16[256,512]{1,0:T(8,128)(2,1)} %get-tuple-element.62), channel_id=1, source_target_pairs={{0,16},{2,18},{4,20},{6,22},{8,24},{10,26},{12,28},{14,30},{16,0},... | collective-permute-start | bytes 786440 | tf_op jit(solution)/shard_map/ppermute | solution.py:417
  105.8 2.5 %collective-permute-start.25 = (bf16[256,512]{1,0:T(8,128)(2,1)}, bf16[256,512]{1,0:T(8,128)(2,1)S(1)}, u32[]{:S(2)}, u32[]{:S(2)}) collective-permute-start(bf16[256,512]{1,0:T(8,128)(2,1)} %get-tuple-element.63), channel_id=1, source_target_pairs={{0,24},{2,26},{4,28},{6,30},{8,16},{10,18},{12,20},{14,22},{16,8},... | collective-permute-start | bytes 786440 | tf_op jit(solution)/shard_map/ppermute | solution.py:417
  108.2 8.4 %collective-permute-done.23.refs_1_ = bf16[256,512]{1,0:T(8,128)(2,1)S(1)} collective-permute-done((bf16[256,512]{1,0:T(8,128)(2,1)}, bf16[256,512]{1,0:T(8,128)(2,1)S(1)}, u32[]{:S(2)}, u32[]{:S(2)}) %collective-permute-start.23) | collective-permute-done | bytes 262176 | tf_op jit(solution)/shard_map/ppermute | solution.py:417
  116.6 8.8 %collective-permute-done.24.refs_2_ = bf16[256,512]{1,0:T(8,128)(2,1)S(1)} collective-permute-done((bf16[256,512]{1,0:T(8,128)(2,1)}, bf16[256,512]{1,0:T(8,128)(2,1)S(1)}, u32[]{:S(2)}, u32[]{:S(2)}) %collective-permute-start.24) | collective-permute-done | bytes 262176 | tf_op jit(solution)/shard_map/ppermute | solution.py:417
  129.1 5.6 %shard_map.159 = (f32[128,768]{1,0:T(8,128)}, bf16[128,768]{1,0:T(8,128)(2,1)}, bf16[128,768]{1,0:T(8,128)(2,1)}, bf16[128,768]{1,0:T(8,128)(2,1)}) custom-call(s32[12]{0:T(128)} %stack.117.where_ref, bf16[256,512]{1,0:T(8,128)(2,1)} %get-tuple-element.74.refs_0_, bf16[256,512]{1,0:T(8,128)(2,1)} %copy-done.2, bf16[256,512]{1,0:T(8,128)(2,1)} %copy-done.3, ...), custom_call_target="tpu_custom_call" | custom-call | flops 805306368 | bytes 3145728 | tf_op jit(solution)/shard_map/pallas_call | solution.py:276
  136.0 5.3 %collective-permute-start.35 = (bf16[128,768]{1,0:T(8,128)(2,1)}, bf16[128,768]{1,0:T(8,128)(2,1)S(1)}, u32[]{:S(2)}, u32[]{:S(2)}) collective-permute-start(bf16[128,768]{1,0:T(8,128)(2,1)} %get-tuple-element.73), channel_id=1, source_target_pairs={{0,9},{1,8},{2,11},{3,10},{4,13},{5,12},{6,15},{7,14},{8,1},{9,0},... | collective-permute-start | bytes 589832 | tf_op jit(solution)/shard_map/ppermute | solution.py:348
  141.3 2.0 %shard_map.160 = (bf16[128,1024]{1,0:T(8,128)(2,1)}, bf16[128,1024]{1,0:T(8,128)(2,1)}) custom-call(s32[1]{0:T(128)} %bitcast.member_ref, bf16[256,512]{1,0:T(8,128)(2,1)} %get-tuple-element.74.refs_0_, bf16[256,512]{1,0:T(8,128)(2,1)} %copy-done.2, bf16[256,512]{1,0:T(8,128)(2,1)} %copy-done.3, bf16[256,512]{1,0:T(8,128)(2,1)} %copy-done.4), custom_call_target="tpu_custom_call" | custom-call | tf_op jit(solution)/shard_map/pallas_call | solution.py:231
  143.4 3.9 %collective-permute-done.35 = bf16[128,768]{1,0:T(8,128)(2,1)S(1)} collective-permute-done((bf16[128,768]{1,0:T(8,128)(2,1)}, bf16[128,768]{1,0:T(8,128)(2,1)S(1)}, u32[]{:S(2)}, u32[]{:S(2)}) %collective-permute-start.35) | collective-permute-done | bytes 196640 | tf_op jit(solution)/shard_map/ppermute | solution.py:348
  147.2 2.8 %collective-permute-done.34 = bf16[128,768]{1,0:T(8,128)(2,1)S(1)} collective-permute-done((bf16[128,768]{1,0:T(8,128)(2,1)}, bf16[128,768]{1,0:T(8,128)(2,1)S(1)}, u32[]{:S(2)}, u32[]{:S(2)}) %collective-permute-start.34) | collective-permute-done | bytes 196640 | tf_op jit(solution)/shard_map/ppermute | solution.py:348
  (115 shorter events, 17.1 us)
Async XLA Ops:
  2.9 12.3 %collective-permute-start = (bf16[64,3072]{1,0:T(8,128)(2,1)S(1)}, bf16[64,3072]{1,0:T(8,128)(2,1)}, u32[]{:S(2)}, u32[]{:S(2)}) collective-permute-start(bf16[64,3072]{1,0:T(8,128)(2,1)S(1)} %constant_dynamic-slice_fusion), channel_id=1, source_target_pairs={{0,8},{2,10},{4,12},{6,14},{8,0},{10,2},{12,4},{14,6},{16,24},{18,... | collective-permute-start | bytes 1179656 | tf_op jit(solution)/shard_map/ppermute | solution.py:331
  6.0 9.2 %collective-permute-start.4 = (bf16[64,3072]{1,0:T(8,128)(2,1)S(1)}, bf16[64,3072]{1,0:T(8,128)(2,1)S(1)}, u32[]{:S(2)}, u32[]{:S(2)}) collective-permute-start(bf16[64,3072]{1,0:T(8,128)(2,1)S(1)} %constant_dynamic-slice_fusion), channel_id=1, source_target_pairs={{8,16},{10,18},{12,20},{14,22},{16,8},{18,10},{20,12},{22,14},{9,1... | collective-permute-start | bytes 1179656 | tf_op jit(solution)/shard_map/ppermute | solution.py:331
  9.5 11.5 %collective-permute-start.1 = (bf16[832,256]{1,0:T(8,128)(2,1)}, bf16[832,256]{1,0:T(8,128)(2,1)S(1)}, u32[]{:S(2)}, u32[]{:S(2)}) collective-permute-start(bf16[832,256]{1,0:T(8,128)(2,1)} %get-tuple-element.49.refs_11_), channel_id=1, source_target_pairs={{0,4},{2,6},{4,0},{6,2},{8,12},{10,14},{12,8},{14,10},{16,20},{18,... | collective-permute-start | bytes 1277960 | tf_op jit(solution)/shard_map/ppermute | solution.py:337
  15.2 13.9 %collective-permute-start.5 = (bf16[832,256]{1,0:T(8,128)(2,1)}, bf16[832,256]{1,0:T(8,128)(2,1)}, u32[]{:S(2)}, u32[]{:S(2)}) collective-permute-start(bf16[832,256]{1,0:T(8,128)(2,1)} %get-tuple-element.43), channel_id=1, source_target_pairs={{0,8},{2,10},{4,12},{6,14},{8,0},{10,2},{12,4},{14,6},{16,24},{18,... | collective-permute-start | bytes 1277960 | tf_op jit(solution)/shard_map/ppermute | solution.py:331
  19.9 10.6 %collective-permute-start.3 = (bf16[64,3072]{1,0:T(8,128)(2,1)}, bf16[64,3072]{1,0:T(8,128)(2,1)S(1)}, u32[]{:S(2)}, u32[]{:S(2)}) collective-permute-start(bf16[64,3072]{1,0:T(8,128)(2,1)} %collective-permute-done.refs_5_), channel_id=1, source_target_pairs={{8,16},{10,18},{12,20},{14,22},{16,8},{18,10},{20,12},{22,14},{9,1... | collective-permute-start | bytes 1179656 | tf_op jit(solution)/shard_map/ppermute | solution.py:331
  21.0 13.0 %collective-permute-start.2 = (bf16[64,3072]{1,0:T(8,128)(2,1)}, bf16[64,3072]{1,0:T(8,128)(2,1)S(1)}, u32[]{:S(2)}, u32[]{:S(2)}) collective-permute-start(bf16[64,3072]{1,0:T(8,128)(2,1)} %collective-permute-done.refs_5_), channel_id=1, source_target_pairs={{0,1},{1,0},{2,3},{3,2},{4,5},{5,4},{6,7},{7,6},{8,9},{9,8},{10,11... | collective-permute-start | bytes 1179656 | tf_op jit(solution)/shard_map/ppermute | solution.py:340
  29.1 13.9 %collective-permute-start.6 = (bf16[64,3072]{1,0:T(8,128)(2,1)S(1)}, bf16[64,3072]{1,0:T(8,128)(2,1)S(1)}, u32[]{:S(2)}, u32[]{:S(2)}) collective-permute-start(bf16[64,3072]{1,0:T(8,128)(2,1)S(1)} %collective-permute-done.4), channel_id=1, source_target_pairs={{8,0},{10,2},{12,4},{14,6},{16,24},{18,26},{20,28},{22,30},{9,1},{... | collective-permute-start | bytes 1179656 | tf_op jit(solution)/shard_map/ppermute | solution.py:331
  30.5 21.3 %collective-permute-start.10 = (bf16[832,256]{1,0:T(8,128)(2,1)}, bf16[832,256]{1,0:T(8,128)(2,1)}, u32[]{:S(2)}, u32[]{:S(2)}) collective-permute-start(bf16[832,256]{1,0:T(8,128)(2,1)} %get-tuple-element.48), channel_id=1, source_target_pairs={{0,16},{2,18},{4,20},{6,22},{8,24},{10,26},{12,28},{14,30},{16,0},... | collective-permute-start | bytes 1277960 | tf_op jit(solution)/shard_map/ppermute | solution.py:331
  34.1 33.0 %collective-permute-start.8 = (bf16[64,3072]{1,0:T(8,128)(2,1)S(1)}, bf16[64,3072]{1,0:T(8,128)(2,1)S(1)}, u32[]{:S(2)}, u32[]{:S(2)}) collective-permute-start(bf16[64,3072]{1,0:T(8,128)(2,1)S(1)} %collective-permute-done.3), channel_id=1, source_target_pairs={{8,0},{10,2},{12,4},{14,6},{16,24},{18,26},{20,28},{22,30},{9,1},{... | collective-permute-start | bytes 1179656 | tf_op jit(solution)/shard_map/ppermute | solution.py:331
  35.4 35.4 %collective-permute-start.14 = (bf16[832,256]{1,0:T(8,128)(2,1)}, bf16[832,256]{1,0:T(8,128)(2,1)S(1)}, u32[]{:S(2)}, u32[]{:S(2)}) collective-permute-start(bf16[832,256]{1,0:T(8,128)(2,1)} %collective-permute-done.5.refs_15_), channel_id=1, source_target_pairs={{0,4},{2,6},{4,0},{6,2},{8,12},{10,14},{12,8},{14,10},{16,20},{18,... | collective-permute-start | bytes 1277960 | tf_op jit(solution)/shard_map/ppermute | solution.py:337
  43.1 24.0 %collective-permute-start.7 = (bf16[64,3072]{1,0:T(8,128)(2,1)S(1)}, bf16[64,3072]{1,0:T(8,128)(2,1)S(1)}, u32[]{:S(2)}, u32[]{:S(2)}) collective-permute-start(bf16[64,3072]{1,0:T(8,128)(2,1)S(1)} %broadcast_select_fusion.1.refs_7_), channel_id=1, source_target_pairs={{0,1},{1,0},{2,3},{3,2},{4,5},{5,4},{6,7},{7,6},{8,9},{9,8},{10,11... | collective-permute-start | bytes 1179656 | tf_op jit(solution)/shard_map/ppermute | solution.py:340
  51.8 16.9 %collective-permute-start.19 = (bf16[832,256]{1,0:T(8,128)(2,1)S(1)}, bf16[832,256]{1,0:T(8,128)(2,1)}, u32[]{:S(2)}, u32[]{:S(2)}) collective-permute-start(bf16[832,256]{1,0:T(8,128)(2,1)S(1)} %copy-done.25), channel_id=1, source_target_pairs={{0,24},{2,26},{4,28},{6,30},{8,16},{10,18},{12,20},{14,22},{16,8},... | collective-permute-start | bytes 1277960 | tf_op jit(solution)/shard_map/ppermute | solution.py:331
  53.3 15.4 %collective-permute-start.11 = (bf16[832,256]{1,0:T(8,128)(2,1)}, bf16[832,256]{1,0:T(8,128)(2,1)}, u32[]{:S(2)}, u32[]{:S(2)}) collective-permute-start(bf16[832,256]{1,0:T(8,128)(2,1)} %collective-permute-done.10.refs_19_), channel_id=1, source_target_pairs={{0,4},{2,6},{4,0},{6,2},{8,12},{10,14},{12,8},{14,10},{16,20},{18,... | collective-permute-start | bytes 1277960 | tf_op jit(solution)/shard_map/ppermute | solution.py:337
  67.1 10.2 %collective-permute-start.9 = (bf16[64,3072]{1,0:T(8,128)(2,1)S(1)}, bf16[64,3072]{1,0:T(8,128)(2,1)}, u32[]{:S(2)}, u32[]{:S(2)}) collective-permute-start(bf16[64,3072]{1,0:T(8,128)(2,1)S(1)} %broadcast_select_fusion.refs_9_), channel_id=1, source_target_pairs={{0,1},{1,0},{2,3},{3,2},{4,5},{5,4},{6,7},{7,6},{8,9},{9,8},{10,11... | collective-permute-start | bytes 1179656 | tf_op jit(solution)/shard_map/ppermute | solution.py:340
  68.7 10.8 %collective-permute-start.20 = (bf16[832,256]{1,0:T(8,128)(2,1)}, bf16[832,256]{1,0:T(8,128)(2,1)}, u32[]{:S(2)}, u32[]{:S(2)}) collective-permute-start(bf16[832,256]{1,0:T(8,128)(2,1)} %collective-permute-done.19.refs_23_), channel_id=1, source_target_pairs={{0,4},{2,6},{4,0},{6,2},{8,12},{10,14},{12,8},{14,10},{16,20},{18,... | collective-permute-start | bytes 1277960 | tf_op jit(solution)/shard_map/ppermute | solution.py:337
  70.3 9.2 %collective-permute-start.12 = (bf16[832,256]{1,0:T(8,128)(2,1)S(1)}, bf16[832,256]{1,0:T(8,128)(2,1)S(1)}, u32[]{:S(2)}, u32[]{:S(2)}) collective-permute-start(bf16[832,256]{1,0:T(8,128)(2,1)S(1)} %copy-done.16), channel_id=1, source_target_pairs={{0,2},{2,0},{4,6},{6,4},{8,10},{10,8},{12,14},{14,12},{16,18},{18,... | collective-permute-start | bytes 1277960 | tf_op jit(solution)/shard_map/ppermute | solution.py:337
  70.3 9.7 %collective-permute-start.13 = (bf16[832,256]{1,0:T(8,128)(2,1)S(1)}, bf16[832,256]{1,0:T(8,128)(2,1)S(1)}, u32[]{:S(2)}, u32[]{:S(2)}) collective-permute-start(bf16[832,256]{1,0:T(8,128)(2,1)S(1)} %copy-done.18), channel_id=1, source_target_pairs={{0,2},{2,0},{4,6},{6,4},{8,10},{10,8},{12,14},{14,12},{16,18},{18,... | collective-permute-start | bytes 1277960 | tf_op jit(solution)/shard_map/ppermute | solution.py:337
  70.8 9.3 %collective-permute-start.15 = (bf16[832,256]{1,0:T(8,128)(2,1)}, bf16[832,256]{1,0:T(8,128)(2,1)S(1)}, u32[]{:S(2)}, u32[]{:S(2)}) collective-permute-start(bf16[832,256]{1,0:T(8,128)(2,1)} %collective-permute-done.5.refs_15_), channel_id=1, source_target_pairs={{0,2},{2,0},{4,6},{6,4},{8,10},{10,8},{12,14},{14,12},{16,18},{18,... | collective-permute-start | bytes 1277960 | tf_op jit(solution)/shard_map/ppermute | solution.py:337
  77.3 3.2 %collective-permute-start.16 = (bf16[832,256]{1,0:T(8,128)(2,1)S(1)}, bf16[832,256]{1,0:T(8,128)(2,1)S(1)}, u32[]{:S(2)}, u32[]{:S(2)}) collective-permute-start(bf16[832,256]{1,0:T(8,128)(2,1)S(1)} %collective-permute-done.14.refs_16_), channel_id=1, source_target_pairs={{0,2},{2,0},{4,6},{6,4},{8,10},{10,8},{12,14},{14,12},{16,18},{18,... | collective-permute-start | bytes 1277960 | tf_op jit(solution)/shard_map/ppermute | solution.py:337
  79.5 3.2 %collective-permute-start.17 = (bf16[832,256]{1,0:T(8,128)(2,1)}, bf16[832,256]{1,0:T(8,128)(2,1)}, u32[]{:S(2)}, u32[]{:S(2)}) collective-permute-start(bf16[832,256]{1,0:T(8,128)(2,1)} %collective-permute-done.10.refs_19_), channel_id=1, source_target_pairs={{0,2},{2,0},{4,6},{6,4},{8,10},{10,8},{12,14},{14,12},{16,18},{18,... | collective-permute-start | bytes 1277960 | tf_op jit(solution)/shard_map/ppermute | solution.py:337
  79.5 4.7 %collective-permute-start.18 = (bf16[832,256]{1,0:T(8,128)(2,1)}, bf16[832,256]{1,0:T(8,128)(2,1)S(1)}, u32[]{:S(2)}, u32[]{:S(2)}) collective-permute-start(bf16[832,256]{1,0:T(8,128)(2,1)} %collective-permute-done.11.refs_20_), channel_id=1, source_target_pairs={{0,2},{2,0},{4,6},{6,4},{8,10},{10,8},{12,14},{14,12},{16,18},{18,... | collective-permute-start | bytes 1277960 | tf_op jit(solution)/shard_map/ppermute | solution.py:337
  80.0 4.2 %collective-permute-start.21 = (bf16[832,256]{1,0:T(8,128)(2,1)}, bf16[832,256]{1,0:T(8,128)(2,1)}, u32[]{:S(2)}, u32[]{:S(2)}) collective-permute-start(bf16[832,256]{1,0:T(8,128)(2,1)} %collective-permute-done.19.refs_23_), channel_id=1, source_target_pairs={{0,2},{2,0},{4,6},{6,4},{8,10},{10,8},{12,14},{14,12},{16,18},{18,... | collective-permute-start | bytes 1277960 | tf_op jit(solution)/shard_map/ppermute | solution.py:337
  80.1 4.2 %collective-permute-start.22 = (bf16[832,256]{1,0:T(8,128)(2,1)}, bf16[832,256]{1,0:T(8,128)(2,1)}, u32[]{:S(2)}, u32[]{:S(2)}) collective-permute-start(bf16[832,256]{1,0:T(8,128)(2,1)} %collective-permute-done.20.refs_24_), channel_id=1, source_target_pairs={{0,2},{2,0},{4,6},{6,4},{8,10},{10,8},{12,14},{14,12},{16,18},{18,... | collective-permute-start | bytes 1277960 | tf_op jit(solution)/shard_map/ppermute | solution.py:337
  81.8 20.6 %collective-permute-start.29 = (bf16[192,1024]{1,0:T(8,128)(2,1)S(1)}, bf16[192,1024]{1,0:T(8,128)(2,1)S(1)}, u32[]{:S(2)}, u32[]{:S(2)}) collective-permute-start(bf16[192,1024]{1,0:T(8,128)(2,1)S(1)} %bitcast.34), channel_id=1, source_target_pairs={{0,16},{2,18},{4,20},{6,22},{8,24},{10,26},{12,28},{14,30},{16,0},... | collective-permute-start | bytes 1179656 | tf_op jit(solution)/shard_map/ppermute | solution.py:331
  82.8 42.7 %collective-permute-start.26 = (bf16[192,1024]{1,0:T(8,128)(2,1)S(1)}, bf16[192,1024]{1,0:T(8,128)(2,1)S(1)}, u32[]{:S(2)}, u32[]{:S(2)}) collective-permute-start(bf16[192,1024]{1,0:T(8,128)(2,1)S(1)} %bitcast.35), channel_id=1, source_target_pairs={{0,4},{2,6},{4,0},{6,2},{8,12},{10,14},{12,8},{14,10},{16,20},{18,... | collective-permute-start | bytes 1179656 | tf_op jit(solution)/shard_map/ppermute | solution.py:337
  102.3 23.8 %collective-permute-start.30 = (bf16[192,1024]{1,0:T(8,128)(2,1)S(1)}, bf16[192,1024]{1,0:T(8,128)(2,1)S(1)}, u32[]{:S(2)}, u32[]{:S(2)}) collective-permute-start(bf16[192,1024]{1,0:T(8,128)(2,1)S(1)} %collective-permute-done.29.refs_8_), channel_id=1, source_target_pairs={{0,4},{2,6},{4,0},{6,2},{8,12},{10,14},{12,8},{14,10},{16,20},{18,... | collective-permute-start | bytes 1179656 | tf_op jit(solution)/shard_map/ppermute | solution.py:337
  103.8 12.7 %collective-permute-start.23 = (bf16[256,512]{1,0:T(8,128)(2,1)}, bf16[256,512]{1,0:T(8,128)(2,1)S(1)}, u32[]{:S(2)}, u32[]{:S(2)}) collective-permute-start(bf16[256,512]{1,0:T(8,128)(2,1)} %get-tuple-element.61), channel_id=1, source_target_pairs={{0,8},{2,10},{4,12},{6,14},{8,0},{10,2},{12,4},{14,6},{16,24},{18,... | collective-permute-start | bytes 786440 | tf_op jit(solution)/shard_map/ppermute | solution.py:417
  103.8 21.6 %collective-permute-start.24 = (bf16[256,512]{1,0:T(8,128)(2,1)}, bf16[256,512]{1,0:T(8,128)(2,1)S(1)}, u32[]{:S(2)}, u32[]{:S(2)}) collective-permute-start(bf16[256,512]{1,0:T(8,128)(2,1)} %get-tuple-element.62), channel_id=1, source_target_pairs={{0,16},{2,18},{4,20},{6,22},{8,24},{10,26},{12,28},{14,30},{16,0},... | collective-permute-start | bytes 786440 | tf_op jit(solution)/shard_map/ppermute | solution.py:417
  105.8 19.7 %collective-permute-start.25 = (bf16[256,512]{1,0:T(8,128)(2,1)}, bf16[256,512]{1,0:T(8,128)(2,1)S(1)}, u32[]{:S(2)}, u32[]{:S(2)}) collective-permute-start(bf16[256,512]{1,0:T(8,128)(2,1)} %get-tuple-element.63), channel_id=1, source_target_pairs={{0,24},{2,26},{4,28},{6,30},{8,16},{10,18},{12,20},{14,22},{16,8},... | collective-permute-start | bytes 786440 | tf_op jit(solution)/shard_map/ppermute | solution.py:417
  134.7 8.6 %collective-permute-start.33 = (bf16[128,768]{1,0:T(8,128)(2,1)}, bf16[128,768]{1,0:T(8,128)(2,1)S(1)}, u32[]{:S(2)}, u32[]{:S(2)}) collective-permute-start(bf16[128,768]{1,0:T(8,128)(2,1)} %get-tuple-element.71), channel_id=1, source_target_pairs={{0,1},{1,0},{2,3},{3,2},{4,5},{5,4},{6,7},{7,6},{8,9},{9,8},{10,11... | collective-permute-start | bytes 589832 | tf_op jit(solution)/shard_map/ppermute | solution.py:340
  136.0 11.2 %collective-permute-start.35 = (bf16[128,768]{1,0:T(8,128)(2,1)}, bf16[128,768]{1,0:T(8,128)(2,1)S(1)}, u32[]{:S(2)}, u32[]{:S(2)}) collective-permute-start(bf16[128,768]{1,0:T(8,128)(2,1)} %get-tuple-element.73), channel_id=1, source_target_pairs={{0,9},{1,8},{2,11},{3,10},{4,13},{5,12},{6,15},{7,14},{8,1},{9,0},... | collective-permute-start | bytes 589832 | tf_op jit(solution)/shard_map/ppermute | solution.py:348
  141.3 8.8 %collective-permute-start.34 = (bf16[128,768]{1,0:T(8,128)(2,1)}, bf16[128,768]{1,0:T(8,128)(2,1)S(1)}, u32[]{:S(2)}, u32[]{:S(2)}) collective-permute-start(bf16[128,768]{1,0:T(8,128)(2,1)} %get-tuple-element.72), channel_id=1, source_target_pairs={{0,8},{1,9},{2,10},{3,11},{4,12},{5,13},{6,14},{7,15},{8,0},{9,1},... | collective-permute-start | bytes 589832 | tf_op jit(solution)/shard_map/ppermute | solution.py:348
  (32 other events, 324.0 us)

commit v10 on v9

--- a/solution.py
+++ b/solution.py
@@ -419,7 +419,7 @@
     packs = [messages[0]] + [give(messages[k], k) for k in range(1, team)]
     out_sides = [flip(out_pieces[0], 2)]
     out_sides += [flip(after(piece, messages[0]), 2) for piece in out_pieces[1:]]
-    out_pieces = [x for p, q in zip(out_pieces, out_sides) for x in spread(p, q, *packs[1:])]
+    out_pieces = [x for p, q in zip(out_pieces, out_sides) for x in spread(p, q, *packs[1:3])]
     out_places = [o for k in range(fsdp) for o in seats_of((place ^ (2 * k)) // 2)]
     where = [member, parity] + [(mine + i) % fsdp for i in range(fsdp)] + out_places
     where = jnp.stack(where).astype(jnp.int32)

time: 151 us -> 151 us (level)
  starting transfers between devices: 44.4 us -> 41.5 us
  waiting for transfers between devices: 72.7 us -> 74.5 us
    ppermute x3, waiting for transfers between devices: 17.2 us -> 21.2 us  [give(): lax.ppermute(x, 'patch', [(p, p ^ bits * INNER) for p in range(patches)])]
    ppermute x2, waiting for transfers between devices: 6.67 us -> 2.86 us  [along_both(): return lax.ppermute(x, ('patch', 'fsdp'), pairs)]
    ppermute x4, waiting for transfers between devices: 6.44 us -> 9.92 us  [along_fsdp(): lax.ppermute(x, 'fsdp', [(i, (i + step) % fsdp) for i in range(fsdp)])]
    ppermute x18, waiting for transfers between devices: 4.53 us -> 2.7 us  [flip(): return lax.ppermute(x, 'patch', [(p, p ^ bits) for p in range(patches)])]
  transfers between devices with their start and end apart: 36 -> 36, of which waited for: 16 -> 15; matrix products, arithmetic and copies ran while one was open for 1% -> 1% of each run, Pallas kernels for 14% -> 14%
where the time goes in v10:
time: 151 us
  waiting for transfers between devices  74.5 us (49%)
  starting transfers between devices  41.5 us (27%)
  Pallas kernels  26.1 us (17%)
  local copies, waits for them, and re-layouts  4.23 us (3%)
  other arithmetic  3.23 us (2%)
    ppermute x9, waiting for transfers between devices, over_outer(): return lax.ppermute(x, 'patch', pairs)  37.9 us
    ppermute x3, waiting for transfers between devices, give(): lax.ppermute(x, 'patch', [(p, p ^ bits * INNER) for p in range(patches)])  21.2 us
    ppermute x9, starting transfers between devices, over_outer(): return lax.ppermute(x, 'patch', pairs)  17 us
    pallas_call x1, Pallas kernels, attend_patches(): pl.pallas_call(functools.partial(patch_kernel, depth, n_pieces, cuts), gr...  15.6 us
    ppermute x18, starting transfers between devices, flip(): return lax.ppermute(x, 'patch', [(p, p ^ bits) for p in range(patches)])  11.9 us
    ppermute x4, waiting for transfers between devices, along_fsdp(): lax.ppermute(x, 'fsdp', [(i, (i + step) % fsdp) for i in range(fsdp)])  9.92 us
    pallas_call x1, Pallas kernels, project(): pl.pallas_call(functools.partial(project_kernel, len(packs), len(pieces),...  5.63 us
    ppermute x4, starting transfers between devices, along_fsdp(): lax.ppermute(x, 'fsdp', [(i, (i + step) % fsdp) for i in range(fsdp)])  5.33 us
  transfers between devices with their start and end apart: 36, of which 15 were waited for; matrix products, arithmetic and copies ran while one was open for 1% of the time, Pallas kernels for 14%

profile of v10, /device:TPU:0, one launch (start us, length us, event | category | flops | bytes accessed | tf_op | source)
XLA Modules:
  0.0 150.7 jit_solution(2917033591851349301)
XLA Ops:
  2.9 3.1 %collective-permute-start = (bf16[64,3072]{1,0:T(8,128)(2,1)S(1)}, bf16[64,3072]{1,0:T(8,128)(2,1)}, u32[]{:S(2)}, u32[]{:S(2)}) collective-permute-start(bf16[64,3072]{1,0:T(8,128)(2,1)S(1)} %constant_dynamic-slice_fusion), channel_id=1, source_target_pairs={{0,8},{2,10},{4,12},{6,14},{8,0},{10,2},{12,4},{14,6},{16,24},{18,... | collective-permute-start | bytes 1179656 | tf_op jit(solution)/shard_map/ppermute | solution.py:331
  6.7 2.8 %shard_map.157 = (bf16[832,256]{1,0:T(8,128)(2,1)}, bf16[832,256]{1,0:T(8,128)(2,1)}, bf16[832,256]{1,0:T(8,128)(2,1)}, bf16[832,256]{1,0:T(8,128)(2,1)}) custom-call(s32[1]{0:T(128)} %bitcast.member_ref, bf16[192,1024]{1,0:T(8,128)(2,1)} %refs_0_.2, bf16[192,1024]{1,0:T(8,128)(2,1)} %refs_1_.2, bf16[192,1024]{1,0:T(8,128)(2,1)} %refs_2_.1, ...), custom_call_target="tpu_custom_call" | custom-call | tf_op jit(solution)/shard_map/pallas_call | solution.py:207
  9.5 1.5 %collective-permute-start.1 = (bf16[832,256]{1,0:T(8,128)(2,1)}, bf16[832,256]{1,0:T(8,128)(2,1)S(1)}, u32[]{:S(2)}, u32[]{:S(2)}) collective-permute-start(bf16[832,256]{1,0:T(8,128)(2,1)} %get-tuple-element.49.refs_11_), channel_id=1, source_target_pairs={{0,4},{2,6},{4,0},{6,2},{8,12},{10,14},{12,8},{14,10},{16,20},{18,... | collective-permute-start | bytes 1277960 | tf_op jit(solution)/shard_map/ppermute | solution.py:337
  11.0 4.2 %collective-permute-done.refs_5_ = bf16[64,3072]{1,0:T(8,128)(2,1)} collective-permute-done((bf16[64,3072]{1,0:T(8,128)(2,1)S(1)}, bf16[64,3072]{1,0:T(8,128)(2,1)}, u32[]{:S(2)}, u32[]{:S(2)}) %collective-permute-start) | collective-permute-done | bytes 393248 | tf_op jit(solution)/shard_map/ppermute | solution.py:331
  15.2 4.7 %collective-permute-start.5 = (bf16[832,256]{1,0:T(8,128)(2,1)}, bf16[832,256]{1,0:T(8,128)(2,1)}, u32[]{:S(2)}, u32[]{:S(2)}) collective-permute-start(bf16[832,256]{1,0:T(8,128)(2,1)} %get-tuple-element.43), channel_id=1, source_target_pairs={{0,8},{2,10},{4,12},{6,14},{8,0},{10,2},{12,4},{14,6},{16,24},{18,... | collective-permute-start | bytes 1277960 | tf_op jit(solution)/shard_map/ppermute | solution.py:331
  21.0 1.5 collective-permute-start.2
  22.5 6.6 %collective-permute-done.5.refs_15_ = bf16[832,256]{1,0:T(8,128)(2,1)} collective-permute-done((bf16[832,256]{1,0:T(8,128)(2,1)}, bf16[832,256]{1,0:T(8,128)(2,1)}, u32[]{:S(2)}, u32[]{:S(2)}) %collective-permute-start.5) | collective-permute-done | bytes 426016 | tf_op jit(solution)/shard_map/ppermute | solution.py:331
  30.5 3.6 %collective-permute-start.10 = (bf16[832,256]{1,0:T(8,128)(2,1)}, bf16[832,256]{1,0:T(8,128)(2,1)}, u32[]{:S(2)}, u32[]{:S(2)}) collective-permute-start(bf16[832,256]{1,0:T(8,128)(2,1)} %get-tuple-element.48), channel_id=1, source_target_pairs={{0,16},{2,18},{4,20},{6,22},{8,24},{10,26},{12,28},{14,30},{16,0},... | collective-permute-start | bytes 1277960 | tf_op jit(solution)/shard_map/ppermute | solution.py:331
  35.4 1.6 %collective-permute-start.14 = (bf16[832,256]{1,0:T(8,128)(2,1)}, bf16[832,256]{1,0:T(8,128)(2,1)S(1)}, u32[]{:S(2)}, u32[]{:S(2)}) collective-permute-start(bf16[832,256]{1,0:T(8,128)(2,1)} %collective-permute-done.5.refs_15_), channel_id=1, source_target_pairs={{0,4},{2,6},{4,0},{6,2},{8,12},{10,14},{12,8},{14,10},{16,20},{18,... | collective-permute-start | bytes 1277960 | tf_op jit(solution)/shard_map/ppermute | solution.py:337
  36.9 6.1 %collective-permute-done.6 = bf16[64,3072]{1,0:T(8,128)(2,1)S(1)} collective-permute-done((bf16[64,3072]{1,0:T(8,128)(2,1)S(1)}, bf16[64,3072]{1,0:T(8,128)(2,1)S(1)}, u32[]{:S(2)}, u32[]{:S(2)}) %collective-permute-start.6) | collective-permute-done | bytes 393248 | tf_op jit(solution)/shard_map/ppermute | solution.py:331
  43.1 1.6 %collective-permute-start.7 = (bf16[64,3072]{1,0:T(8,128)(2,1)S(1)}, bf16[64,3072]{1,0:T(8,128)(2,1)S(1)}, u32[]{:S(2)}, u32[]{:S(2)}) collective-permute-start(bf16[64,3072]{1,0:T(8,128)(2,1)S(1)} %broadcast_select_fusion.1.refs_7_), channel_id=1, source_target_pairs={{0,1},{1,0},{2,3},{3,2},{4,5},{5,4},{6,7},{7,6},{8,9},{9,8},{10,11... | collective-permute-start | bytes 1179656 | tf_op jit(solution)/shard_map/ppermute | solution.py:340
  44.7 7.1 %collective-permute-done.10.refs_19_ = bf16[832,256]{1,0:T(8,128)(2,1)} collective-permute-done((bf16[832,256]{1,0:T(8,128)(2,1)}, bf16[832,256]{1,0:T(8,128)(2,1)}, u32[]{:S(2)}, u32[]{:S(2)}) %collective-permute-start.10) | collective-permute-done | bytes 426016 | tf_op jit(solution)/shard_map/ppermute | solution.py:331
  51.8 1.5 %collective-permute-start.19 = (bf16[832,256]{1,0:T(8,128)(2,1)S(1)}, bf16[832,256]{1,0:T(8,128)(2,1)}, u32[]{:S(2)}, u32[]{:S(2)}) collective-permute-start(bf16[832,256]{1,0:T(8,128)(2,1)S(1)} %copy-done.25), channel_id=1, source_target_pairs={{0,24},{2,26},{4,28},{6,30},{8,16},{10,18},{12,20},{14,22},{16,8},... | collective-permute-start | bytes 1277960 | tf_op jit(solution)/shard_map/ppermute | solution.py:331
  53.3 1.5 %collective-permute-start.11 = (bf16[832,256]{1,0:T(8,128)(2,1)}, bf16[832,256]{1,0:T(8,128)(2,1)}, u32[]{:S(2)}, u32[]{:S(2)}) collective-permute-start(bf16[832,256]{1,0:T(8,128)(2,1)} %collective-permute-done.10.refs_19_), channel_id=1, source_target_pairs={{0,4},{2,6},{4,0},{6,2},{8,12},{10,14},{12,8},{14,10},{16,20},{18,... | collective-permute-start | bytes 1277960 | tf_op jit(solution)/shard_map/ppermute | solution.py:337
  54.8 12.2 %collective-permute-done.8 = bf16[64,3072]{1,0:T(8,128)(2,1)S(1)} collective-permute-done((bf16[64,3072]{1,0:T(8,128)(2,1)S(1)}, bf16[64,3072]{1,0:T(8,128)(2,1)S(1)}, u32[]{:S(2)}, u32[]{:S(2)}) %collective-permute-start.8) | collective-permute-done | bytes 393248 | tf_op jit(solution)/shard_map/ppermute | solution.py:331
  67.1 1.6 %collective-permute-start.9 = (bf16[64,3072]{1,0:T(8,128)(2,1)S(1)}, bf16[64,3072]{1,0:T(8,128)(2,1)}, u32[]{:S(2)}, u32[]{:S(2)}) collective-permute-start(bf16[64,3072]{1,0:T(8,128)(2,1)S(1)} %broadcast_select_fusion.refs_9_), channel_id=1, source_target_pairs={{0,1},{1,0},{2,3},{3,2},{4,5},{5,4},{6,7},{7,6},{8,9},{9,8},{10,11... | collective-permute-start | bytes 1179656 | tf_op jit(solution)/shard_map/ppermute | solution.py:340
  68.7 1.6 %collective-permute-start.20 = (bf16[832,256]{1,0:T(8,128)(2,1)}, bf16[832,256]{1,0:T(8,128)(2,1)}, u32[]{:S(2)}, u32[]{:S(2)}) collective-permute-start(bf16[832,256]{1,0:T(8,128)(2,1)} %collective-permute-done.19.refs_23_), channel_id=1, source_target_pairs={{0,4},{2,6},{4,0},{6,2},{8,12},{10,14},{12,8},{14,10},{16,20},{18,... | collective-permute-start | bytes 1277960 | tf_op jit(solution)/shard_map/ppermute | solution.py:337
  70.9 6.4 %collective-permute-done.9.refs_10_ = bf16[64,3072]{1,0:T(8,128)(2,1)} collective-permute-done((bf16[64,3072]{1,0:T(8,128)(2,1)S(1)}, bf16[64,3072]{1,0:T(8,128)(2,1)}, u32[]{:S(2)}, u32[]{:S(2)}) %collective-permute-start.9) | collective-permute-done | bytes 393248 | tf_op jit(solution)/shard_map/ppermute | solution.py:340
  77.3 2.2 %collective-permute-done.20.refs_24_ = bf16[832,256]{1,0:T(8,128)(2,1)} collective-permute-done((bf16[832,256]{1,0:T(8,128)(2,1)}, bf16[832,256]{1,0:T(8,128)(2,1)}, u32[]{:S(2)}, u32[]{:S(2)}) %collective-permute-start.20) | collective-permute-done | bytes 426016 | tf_op jit(solution)/shard_map/ppermute | solution.py:337
  82.8 1.5 %collective-permute-start.26 = (bf16[192,1024]{1,0:T(8,128)(2,1)S(1)}, bf16[192,1024]{1,0:T(8,128)(2,1)S(1)}, u32[]{:S(2)}, u32[]{:S(2)}) collective-permute-start(bf16[192,1024]{1,0:T(8,128)(2,1)S(1)} %bitcast.35), channel_id=1, source_target_pairs={{0,4},{2,6},{4,0},{6,2},{8,12},{10,14},{12,8},{14,10},{16,20},{18,... | collective-permute-start | bytes 1179656 | tf_op jit(solution)/shard_map/ppermute | solution.py:337
  85.1 15.6 %shard_map.158 = (bf16[256,512]{1,0:T(8,128)(2,1)}, bf16[256,512]{1,0:T(8,128)(2,1)}, bf16[256,512]{1,0:T(8,128)(2,1)}, bf16[256,512]{1,0:T(8,128)(2,1)}) custom-call(s32[28]{0:T(128)} %stack.136.where_ref, bf16[512,1024]{1,0:T(8,128)(2,1)} %refs_0_.3, bf16[512,1024]{1,0:T(8,128)(2,1)} %refs_1_.3, f32[1,128]{1,0:T(1,128)} %bitcast.37, f32[1,128]{1,0:T(1,128)} %bitcast.38, ...), custom_call_target="tpu_custom_call" | custom-call | flops 3758096384 | bytes 6815744 | tf_op jit(solution)/shard_map/pallas_call | solution.py:155
  100.7 1.6 %collective-permute-done.29.refs_8_ = bf16[192,1024]{1,0:T(8,128)(2,1)S(1)} collective-permute-done((bf16[192,1024]{1,0:T(8,128)(2,1)S(1)}, bf16[192,1024]{1,0:T(8,128)(2,1)S(1)}, u32[]{:S(2)}, u32[]{:S(2)}) %collective-permute-start.29) | collective-permute-done | bytes 393248 | tf_op jit(solution)/shard_map/ppermute | solution.py:331
  102.3 1.5 %collective-permute-start.30 = (bf16[192,1024]{1,0:T(8,128)(2,1)S(1)}, bf16[192,1024]{1,0:T(8,128)(2,1)S(1)}, u32[]{:S(2)}, u32[]{:S(2)}) collective-permute-start(bf16[192,1024]{1,0:T(8,128)(2,1)S(1)} %collective-permute-done.29.refs_8_), channel_id=1, source_target_pairs={{0,4},{2,6},{4,0},{6,2},{8,12},{10,14},{12,8},{14,10},{16,20},{18,... | collective-permute-start | bytes 1179656 | tf_op jit(solution)/shard_map/ppermute | solution.py:337
  103.8 1.9 %collective-permute-start.24 = (bf16[256,512]{1,0:T(8,128)(2,1)}, bf16[256,512]{1,0:T(8,128)(2,1)S(1)}, u32[]{:S(2)}, u32[]{:S(2)}) collective-permute-start(bf16[256,512]{1,0:T(8,128)(2,1)} %get-tuple-element.62), channel_id=1, source_target_pairs={{0,16},{2,18},{4,20},{6,22},{8,24},{10,26},{12,28},{14,30},{16,0},... | collective-permute-start | bytes 786440 | tf_op jit(solution)/shard_map/ppermute | solution.py:417
  105.8 10.7 %collective-permute-done.23.refs_1_ = bf16[256,512]{1,0:T(8,128)(2,1)S(1)} collective-permute-done((bf16[256,512]{1,0:T(8,128)(2,1)}, bf16[256,512]{1,0:T(8,128)(2,1)S(1)}, u32[]{:S(2)}, u32[]{:S(2)}) %collective-permute-start.23) | collective-permute-done | bytes 262176 | tf_op jit(solution)/shard_map/ppermute | solution.py:417
  116.4 2.2 %collective-permute-done.24.refs_2_ = bf16[256,512]{1,0:T(8,128)(2,1)S(1)} collective-permute-done((bf16[256,512]{1,0:T(8,128)(2,1)}, bf16[256,512]{1,0:T(8,128)(2,1)S(1)}, u32[]{:S(2)}, u32[]{:S(2)}) %collective-permute-start.24) | collective-permute-done | bytes 262176 | tf_op jit(solution)/shard_map/ppermute | solution.py:417
  121.7 8.3 %collective-permute-done.25.refs_3_ = bf16[256,512]{1,0:T(8,128)(2,1)S(1)} collective-permute-done((bf16[256,512]{1,0:T(8,128)(2,1)}, bf16[256,512]{1,0:T(8,128)(2,1)S(1)}, u32[]{:S(2)}, u32[]{:S(2)}) %collective-permute-start.25) | collective-permute-done | bytes 262176 | tf_op jit(solution)/shard_map/ppermute | solution.py:417
  130.9 5.6 %shard_map.159 = (f32[128,768]{1,0:T(8,128)}, bf16[128,768]{1,0:T(8,128)(2,1)}, bf16[128,768]{1,0:T(8,128)(2,1)}, bf16[128,768]{1,0:T(8,128)(2,1)}) custom-call(s32[12]{0:T(128)} %stack.117.where_ref, bf16[256,512]{1,0:T(8,128)(2,1)} %get-tuple-element.74.refs_0_, bf16[256,512]{1,0:T(8,128)(2,1)} %copy-done.2, bf16[256,512]{1,0:T(8,128)(2,1)} %copy-done.3, ...), custom_call_target="tpu_custom_call" | custom-call | flops 805306368 | bytes 3145728 | tf_op jit(solution)/shard_map/pallas_call | solution.py:276
  137.3 3.8 %collective-permute-start.35 = (bf16[128,768]{1,0:T(8,128)(2,1)}, bf16[128,768]{1,0:T(8,128)(2,1)S(1)}, u32[]{:S(2)}, u32[]{:S(2)}) collective-permute-start(bf16[128,768]{1,0:T(8,128)(2,1)} %get-tuple-element.73), channel_id=1, source_target_pairs={{0,9},{1,8},{2,11},{3,10},{4,13},{5,12},{6,15},{7,14},{8,1},{9,0},... | collective-permute-start | bytes 589832 | tf_op jit(solution)/shard_map/ppermute | solution.py:348
  141.3 2.0 %shard_map.160 = (bf16[128,1024]{1,0:T(8,128)(2,1)}, bf16[128,1024]{1,0:T(8,128)(2,1)}) custom-call(s32[1]{0:T(128)} %bitcast.member_ref, bf16[256,512]{1,0:T(8,128)(2,1)} %get-tuple-element.74.refs_0_, bf16[256,512]{1,0:T(8,128)(2,1)} %copy-done.2, bf16[256,512]{1,0:T(8,128)(2,1)} %copy-done.3, bf16[256,512]{1,0:T(8,128)(2,1)} %copy-done.4), custom_call_target="tpu_custom_call" | custom-call | tf_op jit(solution)/shard_map/pallas_call | solution.py:231
  143.3 3.5 %collective-permute-done.33 = bf16[128,768]{1,0:T(8,128)(2,1)S(1)} collective-permute-done((bf16[128,768]{1,0:T(8,128)(2,1)}, bf16[128,768]{1,0:T(8,128)(2,1)S(1)}, u32[]{:S(2)}, u32[]{:S(2)}) %collective-permute-start.33) | collective-permute-done | bytes 196640 | tf_op jit(solution)/shard_map/ppermute | solution.py:340
  147.2 2.5 %collective-permute-done.34 = bf16[128,768]{1,0:T(8,128)(2,1)S(1)} collective-permute-done((bf16[128,768]{1,0:T(8,128)(2,1)}, bf16[128,768]{1,0:T(8,128)(2,1)S(1)}, u32[]{:S(2)}, u32[]{:S(2)}) %collective-permute-start.34) | collective-permute-done | bytes 196640 | tf_op jit(solution)/shard_map/ppermute | solution.py:348
  (115 shorter events, 17.5 us)
Async XLA Ops:
  2.9 12.3 %collective-permute-start = (bf16[64,3072]{1,0:T(8,128)(2,1)S(1)}, bf16[64,3072]{1,0:T(8,128)(2,1)}, u32[]{:S(2)}, u32[]{:S(2)}) collective-permute-start(bf16[64,3072]{1,0:T(8,128)(2,1)S(1)} %constant_dynamic-slice_fusion), channel_id=1, source_target_pairs={{0,8},{2,10},{4,12},{6,14},{8,0},{10,2},{12,4},{14,6},{16,24},{18,... | collective-permute-start | bytes 1179656 | tf_op jit(solution)/shard_map/ppermute | solution.py:331
  6.0 9.2 %collective-permute-start.4 = (bf16[64,3072]{1,0:T(8,128)(2,1)S(1)}, bf16[64,3072]{1,0:T(8,128)(2,1)S(1)}, u32[]{:S(2)}, u32[]{:S(2)}) collective-permute-start(bf16[64,3072]{1,0:T(8,128)(2,1)S(1)} %constant_dynamic-slice_fusion), channel_id=1, source_target_pairs={{8,16},{10,18},{12,20},{14,22},{16,8},{18,10},{20,12},{22,14},{9,1... | collective-permute-start | bytes 1179656 | tf_op jit(solution)/shard_map/ppermute | solution.py:331
  9.5 11.5 %collective-permute-start.1 = (bf16[832,256]{1,0:T(8,128)(2,1)}, bf16[832,256]{1,0:T(8,128)(2,1)S(1)}, u32[]{:S(2)}, u32[]{:S(2)}) collective-permute-start(bf16[832,256]{1,0:T(8,128)(2,1)} %get-tuple-element.49.refs_11_), channel_id=1, source_target_pairs={{0,4},{2,6},{4,0},{6,2},{8,12},{10,14},{12,8},{14,10},{16,20},{18,... | collective-permute-start | bytes 1277960 | tf_op jit(solution)/shard_map/ppermute | solution.py:337
  15.2 13.9 %collective-permute-start.5 = (bf16[832,256]{1,0:T(8,128)(2,1)}, bf16[832,256]{1,0:T(8,128)(2,1)}, u32[]{:S(2)}, u32[]{:S(2)}) collective-permute-start(bf16[832,256]{1,0:T(8,128)(2,1)} %get-tuple-element.43), channel_id=1, source_target_pairs={{0,8},{2,10},{4,12},{6,14},{8,0},{10,2},{12,4},{14,6},{16,24},{18,... | collective-permute-start | bytes 1277960 | tf_op jit(solution)/shard_map/ppermute | solution.py:331
  19.9 10.6 %collective-permute-start.3 = (bf16[64,3072]{1,0:T(8,128)(2,1)}, bf16[64,3072]{1,0:T(8,128)(2,1)S(1)}, u32[]{:S(2)}, u32[]{:S(2)}) collective-permute-start(bf16[64,3072]{1,0:T(8,128)(2,1)} %collective-permute-done.refs_5_), channel_id=1, source_target_pairs={{8,16},{10,18},{12,20},{14,22},{16,8},{18,10},{20,12},{22,14},{9,1... | collective-permute-start | bytes 1179656 | tf_op jit(solution)/shard_map/ppermute | solution.py:331
  21.0 13.0 %collective-permute-start.2 = (bf16[64,3072]{1,0:T(8,128)(2,1)}, bf16[64,3072]{1,0:T(8,128)(2,1)S(1)}, u32[]{:S(2)}, u32[]{:S(2)}) collective-permute-start(bf16[64,3072]{1,0:T(8,128)(2,1)} %collective-permute-done.refs_5_), channel_id=1, source_target_pairs={{0,1},{1,0},{2,3},{3,2},{4,5},{5,4},{6,7},{7,6},{8,9},{9,8},{10,11... | collective-permute-start | bytes 1179656 | tf_op jit(solution)/shard_map/ppermute | solution.py:340
  29.1 13.9 %collective-permute-start.6 = (bf16[64,3072]{1,0:T(8,128)(2,1)S(1)}, bf16[64,3072]{1,0:T(8,128)(2,1)S(1)}, u32[]{:S(2)}, u32[]{:S(2)}) collective-permute-start(bf16[64,3072]{1,0:T(8,128)(2,1)S(1)} %collective-permute-done.4), channel_id=1, source_target_pairs={{8,0},{10,2},{12,4},{14,6},{16,24},{18,26},{20,28},{22,30},{9,1},{... | collective-permute-start | bytes 1179656 | tf_op jit(solution)/shard_map/ppermute | solution.py:331
  30.5 21.3 %collective-permute-start.10 = (bf16[832,256]{1,0:T(8,128)(2,1)}, bf16[832,256]{1,0:T(8,128)(2,1)}, u32[]{:S(2)}, u32[]{:S(2)}) collective-permute-start(bf16[832,256]{1,0:T(8,128)(2,1)} %get-tuple-element.48), channel_id=1, source_target_pairs={{0,16},{2,18},{4,20},{6,22},{8,24},{10,26},{12,28},{14,30},{16,0},... | collective-permute-start | bytes 1277960 | tf_op jit(solution)/shard_map/ppermute | solution.py:331
  34.1 33.0 %collective-permute-start.8 = (bf16[64,3072]{1,0:T(8,128)(2,1)S(1)}, bf16[64,3072]{1,0:T(8,128)(2,1)S(1)}, u32[]{:S(2)}, u32[]{:S(2)}) collective-permute-start(bf16[64,3072]{1,0:T(8,128)(2,1)S(1)} %collective-permute-done.3), channel_id=1, source_target_pairs={{8,0},{10,2},{12,4},{14,6},{16,24},{18,26},{20,28},{22,30},{9,1},{... | collective-permute-start | bytes 1179656 | tf_op jit(solution)/shard_map/ppermute | solution.py:331
  35.4 35.4 %collective-permute-start.14 = (bf16[832,256]{1,0:T(8,128)(2,1)}, bf16[832,256]{1,0:T(8,128)(2,1)S(1)}, u32[]{:S(2)}, u32[]{:S(2)}) collective-permute-start(bf16[832,256]{1,0:T(8,128)(2,1)} %collective-permute-done.5.refs_15_), channel_id=1, source_target_pairs={{0,4},{2,6},{4,0},{6,2},{8,12},{10,14},{12,8},{14,10},{16,20},{18,... | collective-permute-start | bytes 1277960 | tf_op jit(solution)/shard_map/ppermute | solution.py:337
  43.1 24.0 %collective-permute-start.7 = (bf16[64,3072]{1,0:T(8,128)(2,1)S(1)}, bf16[64,3072]{1,0:T(8,128)(2,1)S(1)}, u32[]{:S(2)}, u32[]{:S(2)}) collective-permute-start(bf16[64,3072]{1,0:T(8,128)(2,1)S(1)} %broadcast_select_fusion.1.refs_7_), channel_id=1, source_target_pairs={{0,1},{1,0},{2,3},{3,2},{4,5},{5,4},{6,7},{7,6},{8,9},{9,8},{10,11... | collective-permute-start | bytes 1179656 | tf_op jit(solution)/shard_map/ppermute | solution.py:340
  51.8 16.9 %collective-permute-start.19 = (bf16[832,256]{1,0:T(8,128)(2,1)S(1)}, bf16[832,256]{1,0:T(8,128)(2,1)}, u32[]{:S(2)}, u32[]{:S(2)}) collective-permute-start(bf16[832,256]{1,0:T(8,128)(2,1)S(1)} %copy-done.25), channel_id=1, source_target_pairs={{0,24},{2,26},{4,28},{6,30},{8,16},{10,18},{12,20},{14,22},{16,8},... | collective-permute-start | bytes 1277960 | tf_op jit(solution)/shard_map/ppermute | solution.py:331
  53.3 15.4 %collective-permute-start.11 = (bf16[832,256]{1,0:T(8,128)(2,1)}, bf16[832,256]{1,0:T(8,128)(2,1)}, u32[]{:S(2)}, u32[]{:S(2)}) collective-permute-start(bf16[832,256]{1,0:T(8,128)(2,1)} %collective-permute-done.10.refs_19_), channel_id=1, source_target_pairs={{0,4},{2,6},{4,0},{6,2},{8,12},{10,14},{12,8},{14,10},{16,20},{18,... | collective-permute-start | bytes 1277960 | tf_op jit(solution)/shard_map/ppermute | solution.py:337
  67.1 10.2 %collective-permute-start.9 = (bf16[64,3072]{1,0:T(8,128)(2,1)S(1)}, bf16[64,3072]{1,0:T(8,128)(2,1)}, u32[]{:S(2)}, u32[]{:S(2)}) collective-permute-start(bf16[64,3072]{1,0:T(8,128)(2,1)S(1)} %broadcast_select_fusion.refs_9_), channel_id=1, source_target_pairs={{0,1},{1,0},{2,3},{3,2},{4,5},{5,4},{6,7},{7,6},{8,9},{9,8},{10,11... | collective-permute-start | bytes 1179656 | tf_op jit(solution)/shard_map/ppermute | solution.py:340
  68.7 10.8 %collective-permute-start.20 = (bf16[832,256]{1,0:T(8,128)(2,1)}, bf16[832,256]{1,0:T(8,128)(2,1)}, u32[]{:S(2)}, u32[]{:S(2)}) collective-permute-start(bf16[832,256]{1,0:T(8,128)(2,1)} %collective-permute-done.19.refs_23_), channel_id=1, source_target_pairs={{0,4},{2,6},{4,0},{6,2},{8,12},{10,14},{12,8},{14,10},{16,20},{18,... | collective-permute-start | bytes 1277960 | tf_op jit(solution)/shard_map/ppermute | solution.py:337
  70.3 9.2 %collective-permute-start.12 = (bf16[832,256]{1,0:T(8,128)(2,1)S(1)}, bf16[832,256]{1,0:T(8,128)(2,1)S(1)}, u32[]{:S(2)}, u32[]{:S(2)}) collective-permute-start(bf16[832,256]{1,0:T(8,128)(2,1)S(1)} %copy-done.16), channel_id=1, source_target_pairs={{0,2},{2,0},{4,6},{6,4},{8,10},{10,8},{12,14},{14,12},{16,18},{18,... | collective-permute-start | bytes 1277960 | tf_op jit(solution)/shard_map/ppermute | solution.py:337
  70.3 9.7 %collective-permute-start.13 = (bf16[832,256]{1,0:T(8,128)(2,1)S(1)}, bf16[832,256]{1,0:T(8,128)(2,1)S(1)}, u32[]{:S(2)}, u32[]{:S(2)}) collective-permute-start(bf16[832,256]{1,0:T(8,128)(2,1)S(1)} %copy-done.18), channel_id=1, source_target_pairs={{0,2},{2,0},{4,6},{6,4},{8,10},{10,8},{12,14},{14,12},{16,18},{18,... | collective-permute-start | bytes 1277960 | tf_op jit(solution)/shard_map/ppermute | solution.py:337
  70.8 9.3 %collective-permute-start.15 = (bf16[832,256]{1,0:T(8,128)(2,1)}, bf16[832,256]{1,0:T(8,128)(2,1)S(1)}, u32[]{:S(2)}, u32[]{:S(2)}) collective-permute-start(bf16[832,256]{1,0:T(8,128)(2,1)} %collective-permute-done.5.refs_15_), channel_id=1, source_target_pairs={{0,2},{2,0},{4,6},{6,4},{8,10},{10,8},{12,14},{14,12},{16,18},{18,... | collective-permute-start | bytes 1277960 | tf_op jit(solution)/shard_map/ppermute | solution.py:337
  79.5 4.7 %collective-permute-start.18 = (bf16[832,256]{1,0:T(8,128)(2,1)}, bf16[832,256]{1,0:T(8,128)(2,1)S(1)}, u32[]{:S(2)}, u32[]{:S(2)}) collective-permute-start(bf16[832,256]{1,0:T(8,128)(2,1)} %collective-permute-done.11.refs_20_), channel_id=1, source_target_pairs={{0,2},{2,0},{4,6},{6,4},{8,10},{10,8},{12,14},{14,12},{16,18},{18,... | collective-permute-start | bytes 1277960 | tf_op jit(solution)/shard_map/ppermute | solution.py:337
  81.8 20.6 %collective-permute-start.29 = (bf16[192,1024]{1,0:T(8,128)(2,1)S(1)}, bf16[192,1024]{1,0:T(8,128)(2,1)S(1)}, u32[]{:S(2)}, u32[]{:S(2)}) collective-permute-start(bf16[192,1024]{1,0:T(8,128)(2,1)S(1)} %bitcast.34), channel_id=1, source_target_pairs={{0,16},{2,18},{4,20},{6,22},{8,24},{10,26},{12,28},{14,30},{16,0},... | collective-permute-start | bytes 1179656 | tf_op jit(solution)/shard_map/ppermute | solution.py:331
  82.8 35.9 %collective-permute-start.26 = (bf16[192,1024]{1,0:T(8,128)(2,1)S(1)}, bf16[192,1024]{1,0:T(8,128)(2,1)S(1)}, u32[]{:S(2)}, u32[]{:S(2)}) collective-permute-start(bf16[192,1024]{1,0:T(8,128)(2,1)S(1)} %bitcast.35), channel_id=1, source_target_pairs={{0,4},{2,6},{4,0},{6,2},{8,12},{10,14},{12,8},{14,10},{16,20},{18,... | collective-permute-start | bytes 1179656 | tf_op jit(solution)/shard_map/ppermute | solution.py:337
  102.3 16.9 %collective-permute-start.30 = (bf16[192,1024]{1,0:T(8,128)(2,1)S(1)}, bf16[192,1024]{1,0:T(8,128)(2,1)S(1)}, u32[]{:S(2)}, u32[]{:S(2)}) collective-permute-start(bf16[192,1024]{1,0:T(8,128)(2,1)S(1)} %collective-permute-done.29.refs_8_), channel_id=1, source_target_pairs={{0,4},{2,6},{4,0},{6,2},{8,12},{10,14},{12,8},{14,10},{16,20},{18,... | collective-permute-start | bytes 1179656 | tf_op jit(solution)/shard_map/ppermute | solution.py:337
  103.8 12.6 %collective-permute-start.23 = (bf16[256,512]{1,0:T(8,128)(2,1)}, bf16[256,512]{1,0:T(8,128)(2,1)S(1)}, u32[]{:S(2)}, u32[]{:S(2)}) collective-permute-start(bf16[256,512]{1,0:T(8,128)(2,1)} %get-tuple-element.61), channel_id=1, source_target_pairs={{0,8},{2,10},{4,12},{6,14},{8,0},{10,2},{12,4},{14,6},{16,24},{18,... | collective-permute-start | bytes 786440 | tf_op jit(solution)/shard_map/ppermute | solution.py:417
  103.8 14.8 %collective-permute-start.24 = (bf16[256,512]{1,0:T(8,128)(2,1)}, bf16[256,512]{1,0:T(8,128)(2,1)S(1)}, u32[]{:S(2)}, u32[]{:S(2)}) collective-permute-start(bf16[256,512]{1,0:T(8,128)(2,1)} %get-tuple-element.62), channel_id=1, source_target_pairs={{0,16},{2,18},{4,20},{6,22},{8,24},{10,26},{12,28},{14,30},{16,0},... | collective-permute-start | bytes 786440 | tf_op jit(solution)/shard_map/ppermute | solution.py:417
  118.6 11.4 %collective-permute-start.27 = (bf16[192,1024]{1,0:T(8,128)(2,1)S(1)}, bf16[192,1024]{1,0:T(8,128)(2,1)S(1)}, u32[]{:S(2)}, u32[]{:S(2)}) collective-permute-start(bf16[192,1024]{1,0:T(8,128)(2,1)S(1)} %bitcast.36), channel_id=1, source_target_pairs={{0,2},{2,0},{4,6},{6,4},{8,10},{10,8},{12,14},{14,12},{16,18},{18,... | collective-permute-start | bytes 1179656 | tf_op jit(solution)/shard_map/ppermute | solution.py:337
  118.6 11.4 %collective-permute-start.28 = (bf16[192,1024]{1,0:T(8,128)(2,1)S(1)}, bf16[192,1024]{1,0:T(8,128)(2,1)}, u32[]{:S(2)}, u32[]{:S(2)}) collective-permute-start(bf16[192,1024]{1,0:T(8,128)(2,1)S(1)} %collective-permute-done.26.refs_5_), channel_id=1, source_target_pairs={{0,2},{2,0},{4,6},{6,4},{8,10},{10,8},{12,14},{14,12},{16,18},{18,... | collective-permute-start | bytes 1179656 | tf_op jit(solution)/shard_map/ppermute | solution.py:337
  119.1 10.9 %collective-permute-start.31 = (bf16[192,1024]{1,0:T(8,128)(2,1)S(1)}, bf16[192,1024]{1,0:T(8,128)(2,1)}, u32[]{:S(2)}, u32[]{:S(2)}) collective-permute-start(bf16[192,1024]{1,0:T(8,128)(2,1)S(1)} %collective-permute-done.29.refs_8_), channel_id=1, source_target_pairs={{0,2},{2,0},{4,6},{6,4},{8,10},{10,8},{12,14},{14,12},{16,18},{18,... | collective-permute-start | bytes 1179656 | tf_op jit(solution)/shard_map/ppermute | solution.py:337
  119.2 10.9 %collective-permute-start.32 = (bf16[192,1024]{1,0:T(8,128)(2,1)S(1)}, bf16[192,1024]{1,0:T(8,128)(2,1)}, u32[]{:S(2)}, u32[]{:S(2)}) collective-permute-start(bf16[192,1024]{1,0:T(8,128)(2,1)S(1)} %collective-permute-done.30.refs_9_), channel_id=1, source_target_pairs={{0,2},{2,0},{4,6},{6,4},{8,10},{10,8},{12,14},{14,12},{16,18},{18,... | collective-permute-start | bytes 1179656 | tf_op jit(solution)/shard_map/ppermute | solution.py:337
  119.6 10.4 %collective-permute-start.25 = (bf16[256,512]{1,0:T(8,128)(2,1)}, bf16[256,512]{1,0:T(8,128)(2,1)S(1)}, u32[]{:S(2)}, u32[]{:S(2)}) collective-permute-start(bf16[256,512]{1,0:T(8,128)(2,1)} %get-tuple-element.63), channel_id=1, source_target_pairs={{0,24},{2,26},{4,28},{6,30},{8,16},{10,18},{12,20},{14,22},{16,8},... | collective-permute-start | bytes 786440 | tf_op jit(solution)/shard_map/ppermute | solution.py:417
  136.5 10.3 %collective-permute-start.33 = (bf16[128,768]{1,0:T(8,128)(2,1)}, bf16[128,768]{1,0:T(8,128)(2,1)S(1)}, u32[]{:S(2)}, u32[]{:S(2)}) collective-permute-start(bf16[128,768]{1,0:T(8,128)(2,1)} %get-tuple-element.71), channel_id=1, source_target_pairs={{0,1},{1,0},{2,3},{3,2},{4,5},{5,4},{6,7},{7,6},{8,9},{9,8},{10,11... | collective-permute-start | bytes 589832 | tf_op jit(solution)/shard_map/ppermute | solution.py:340
  137.3 9.9 %collective-permute-start.35 = (bf16[128,768]{1,0:T(8,128)(2,1)}, bf16[128,768]{1,0:T(8,128)(2,1)S(1)}, u32[]{:S(2)}, u32[]{:S(2)}) collective-permute-start(bf16[128,768]{1,0:T(8,128)(2,1)} %get-tuple-element.73), channel_id=1, source_target_pairs={{0,9},{1,8},{2,11},{3,10},{4,13},{5,12},{6,15},{7,14},{8,1},{9,0},... | collective-permute-start | bytes 589832 | tf_op jit(solution)/shard_map/ppermute | solution.py:348
  141.2 8.5 %collective-permute-start.34 = (bf16[128,768]{1,0:T(8,128)(2,1)}, bf16[128,768]{1,0:T(8,128)(2,1)S(1)}, u32[]{:S(2)}, u32[]{:S(2)}) collective-permute-start(bf16[128,768]{1,0:T(8,128)(2,1)} %get-tuple-element.72), channel_id=1, source_target_pairs={{0,8},{1,9},{2,10},{3,11},{4,12},{5,13},{6,14},{7,15},{8,0},{9,1},... | collective-permute-start | bytes 589832 | tf_op jit(solution)/shard_map/ppermute | solution.py:348
  (32 other events, 359.9 us)
